TPU v7x, 32 devices: a whole 2x2x4 slice. The times are simulated.
32 devices in a mesh: grp: 2 (over y), row: 4 (over x, core), col: 4 (over z).
Axes of the slice: x: 2, y: 2, z: 4, core: 2. Of those that a mesh axis runs over, the one named last changes fastest.
Arguments:
- left_act: bfloat16 [512, 2048], P(('grp', 'row', 'col')), parts along dimension 0, may hold values from -15 to 15
- right_act: bfloat16 [512, 2048], P(('grp', 'col', 'row')), parts along dimension 0, may hold values from -15 to 15
- row_mask: int32 [128], P('grp'), parts along dimension 0, may hold values 0 or 1
- res_mask: int32 [512], P('grp'), parts along dimension 0, may hold values 0 or 1
- out_weight: bfloat16 [1024, 128], replicated, may hold values from -0.1875 to 0.1875
- cotangent: bfloat16 [512, 256, 128], P(('grp', 'row'), 'col'), parts along dimension 0, may hold values from -1 to 1
Outputs:
- pair_out: bfloat16 [512, 256, 128], P(('grp', 'row'), 'col'), parts along dimension 0
- grad_left: float32 [512, 2048], P(('grp', 'row', 'col')), parts along dimension 0
- grad_right: float32 [512, 2048], P(('grp', 'col', 'row')), parts along dimension 0
- grad_weight: float32 [2048, 128], P(('grp', 'row', 'col')), parts along dimension 0
There are 2 independent parts, one for each index of `grp`. A program takes and returns all parts, laid end to end along the dimension named above; an argument that names none is the same for every part. Nothing has to cross between parts.
All inputs are finite; a program needn't handle non-finite values.
Results may differ from a plain program's by a relative error of at most 0.0085.
Values may be sent and summed in bfloat16 or wider, within the bound.
No kernel may reach another device: no remote copies, remote signals or barrier semaphores. Data moves between devices by JAX's collectives and lax.ppermute only.
A program may use at most 128 MiB of HBM per device.

v0:
```python
import jax
import jax.numpy as jnp
from jax import lax
from jax.sharding import PartitionSpec as P


def shards(left_act, right_act, row_mask, res_mask, out_weight, cotangent):
    col_count = lax.axis_size("col")
    row_count = lax.axis_size("row")
    seq_keep = row_mask.astype(jnp.float32)
    res_keep = res_mask.astype(jnp.float32)
    row_width = left_act.shape[1]
    sequences = seq_keep.shape[0]
    channels = row_width // sequences
    pair_width = out_weight.shape[1]
    weight_cube = out_weight.reshape(channels, channels, pair_width)
    chan_keep = jnp.repeat(seq_keep, channels)
    left_all = lax.all_gather(left_act, "col", axis=0, tiled=True)
    right_all = lax.all_gather(right_act, "row", axis=0, tiled=True)
    i_rows = left_all.shape[0]
    j_rows = right_all.shape[0]
    i_keep = lax.dynamic_slice_in_dim(res_keep, lax.axis_index("row") * i_rows, i_rows)
    j_keep = lax.dynamic_slice_in_dim(res_keep, lax.axis_index("col") * j_rows, j_rows)
    left_masked = left_all * (i_keep[:, None] * chan_keep[None, :]).astype(jnp.bfloat16)
    right_masked = right_all * (j_keep[:, None] * chan_keep[None, :]).astype(jnp.bfloat16)
    valid_rows = jnp.sum(seq_keep)
    block_rows = min(i_rows, 16)
    block_count = i_rows // block_rows
    wide_block = block_rows * channels
    right_wide = (
        right_masked.reshape(j_rows, sequences, channels)
        .transpose(1, 0, 2)
        .reshape(sequences, j_rows * channels)
    )
    left_wide = (
        left_masked.reshape(block_count, block_rows, sequences, channels)
        .transpose(0, 2, 1, 3)
        .reshape(block_count, sequences, wide_block)
    )
    grad_split = cotangent.reshape(block_count, block_rows, j_rows, pair_width)
    keep_split = i_keep.reshape(block_count, block_rows)

    def outer_of(left_block):
        products = lax.dot_general(
            left_block, right_wide, (((0,), (0,)), ((), ())), preferred_element_type=jnp.float32
        )
        return products.astype(jnp.bfloat16).reshape(block_rows, channels, j_rows, channels)

    def counts_of(keep_block):
        return jnp.maximum(valid_rows * keep_block[:, None] * j_keep[None, :], 1.0)[:, :, None]

    def forward_part(outer_block, pair_count):
        projected = jnp.einsum(
            "icje,cep->ijp", outer_block, weight_cube, preferred_element_type=jnp.float32
        )
        return (projected / pair_count).astype(jnp.bfloat16)

    def backward_part(state_carry, outer_block, pair_count, left_block, grad_block):
        grad_w, grad_r = state_carry
        scaled = (grad_block.astype(jnp.float32) / pair_count).astype(jnp.bfloat16)
        grad_w = grad_w + jnp.einsum(
            "icje,ijp->cep", outer_block, scaled, preferred_element_type=jnp.float32
        )
        inner_grad = jnp.einsum(
            "ijp,cep->icje", scaled, weight_cube, preferred_element_type=jnp.float32
        )
        inner_wide = inner_grad.astype(jnp.bfloat16).reshape(wide_block, j_rows * channels)
        part_left = lax.dot_general(
            right_wide, inner_wide, (((1,), (1,)), ((), ())), preferred_element_type=jnp.float32
        )
        grad_r = grad_r + jnp.dot(left_block, inner_wide, preferred_element_type=jnp.float32)
        return ((grad_w, grad_r), part_left)

    start_carry = (
        jnp.zeros((channels, channels, pair_width), jnp.float32),
        jnp.zeros((sequences, j_rows * channels), jnp.float32),
    )

    def joint_step(state_carry, pieces):
        left_block, keep_block, grad_block = pieces
        outer_block = outer_of(left_block)
        pair_count = counts_of(keep_block)
        new_carry, part_left = backward_part(
            state_carry, outer_block, pair_count, left_block, grad_block
        )
        return (new_carry, (forward_part(outer_block, pair_count), part_left))

    final_carry, stacked = lax.scan(joint_step, start_carry, (left_wide, keep_split, grad_split))
    pair_blocks, left_parts = stacked
    pair_out = pair_blocks.reshape(i_rows, j_rows, pair_width)
    grad_cube, grad_r = final_carry
    grad_w = grad_cube.reshape(channels * channels, pair_width)
    left_rows_out = (
        left_parts.reshape(block_count, sequences, block_rows, channels)
        .transpose(0, 2, 1, 3)
        .reshape(i_rows, row_width)
    )
    right_rows_out = (
        grad_r.reshape(sequences, j_rows, channels).transpose(1, 0, 2).reshape(j_rows, row_width)
    )
    left_sum = lax.psum_scatter(
        left_rows_out.astype(jnp.bfloat16), "col", scatter_dimension=0, tiled=True
    ).astype(jnp.float32)
    right_sum = lax.psum_scatter(
        right_rows_out.astype(jnp.bfloat16), "row", scatter_dimension=0, tiled=True
    ).astype(jnp.float32)
    own_left = left_act.shape[0]
    left_first = (lax.axis_index("row") * col_count + lax.axis_index("col")) * own_left
    left_keep = lax.dynamic_slice_in_dim(res_keep, left_first, own_left)
    grad_left = left_sum * (left_keep[:, None] * chan_keep[None, :])
    own_right = right_act.shape[0]
    right_first = (lax.axis_index("col") * row_count + lax.axis_index("row")) * own_right
    right_keep = lax.dynamic_slice_in_dim(res_keep, right_first, own_right)
    grad_right = right_sum * (right_keep[:, None] * chan_keep[None, :])
    grad_weight = lax.psum_scatter(grad_w, ("row", "col"), scatter_dimension=0, tiled=True)
    return (pair_out, grad_left, grad_right, grad_weight)


def solution(mesh):
    placed = (
        P(("grp", "row", "col"), None),
        P(("grp", "col", "row"), None),
        P("grp"),
        P("grp"),
        P(),
        P(("grp", "row"), "col", None),
    )
    return jax.shard_map(
        shards,
        mesh=mesh,
        in_specs=placed,
        out_specs=(
            P(("grp", "row"), "col", None),
            P(("grp", "row", "col"), None),
            P(("grp", "col", "row"), None),
            P(("grp", "row", "col"), None),
        ),
        check_vma=False,
    )
```

profile of v0, /device:TPU:0, one launch (start us, length us, event | category | flops | bytes accessed | tf_op | source)
XLA Modules:
  0.0 330.5 jit_solution(8853170975604748920)
XLA Ops:
  10.0 15.8 %all_gather.6 = bf16[64,2048]{1,0:T(8,128)(2,1)S(1)} all-gather(bf16[16,2048]{1,0:T(8,128)(2,1)} %param.8), channel_id=1, replica_groups=mesh['grp'=2,'row'=4,'col'=4] {'col'}, dimensions={0}, use_global_device_ids=true | all-gather | bytes 327680 | tf_op jit(solution)/shard_map/all_gather | solution.py:18
  25.8 6.0 %all_gather.7 = bf16[64,2048]{1,0:T(8,128)(2,1)S(1)} all-gather(bf16[16,2048]{1,0:T(8,128)(2,1)} %param.9), channel_id=1, replica_groups=mesh['grp'=2,'row'=4,'col'=4] {'row'}, dimensions={0}, use_global_device_ids=true | all-gather | bytes 327680 | tf_op jit(solution)/shard_map/all_gather | solution.py:19
  35.2 183.1 %while.17 = (s32[]{:T(128)}, f32[32,32,128]{2,1,0:T(8,128)}, f32[64,2048]{1,0:T(8,128)S(1)}, bf16[4,16,64,128]{3,2,1,0:T(8,128)(2,1)}, bf16[4,64,512]{2,1,0:T(8,...) while((s32[]{:T(128)}, f32[32,32,128]{2,1,0:T(8,128)}, ...), condition=%wide.region_2.3_spmd.clone, body=%wide.region_1.2_spmd.clone.sunk | while | flops 1211631616 | bytes 48253616 | solution.py:88
  40.4 8.4 %copy.65 = bf16[16,32,64,32]{3,2,1,0:T(8,128)(2,1)} copy(bf16[16,32,64,32]{2,3,1,0:T(8,128)(2,1)} %convert_bitcast_fusion.3) | data formatting | bytes 4194304 | tf_op jit(solution)/shard_map/while/body/eval_jaxpr/convert_element_type | solution.py:67
  48.8 11.1 %reshape.115 = bf16[512,2048]{1,0:T(8,128)(2,1)S(1)} reshape(bf16[16,32,64,32]{3,2,1,0:T(8,128)(2,1)} %copy.65) | data formatting | bytes 4194304 | tf_op jit(solution)/shard_map/while/body/eval_jaxpr/reshape | solution.py:67
  62.6 8.1 %reshape.114 = bf16[16,32,64,32]{3,2,1,0:T(8,128)(2,1)} reshape(bf16[512,2048]{1,0:T(8,128)(2,1)S(1)} %convolution_convert_fusion.2) | data formatting | bytes 4194304 | tf_op jit(solution)/shard_map/while/body/eval_jaxpr/reshape | solution.py:47
  70.7 6.0 %fusion.69 = bf16[4,16,64,128]{3,2,1,0:T(8,128)(2,1)} fusion(bf16[4,16,64,128]{3,2,1,0:T(8,128)(2,1)} %get-tuple-element.270, s32[]{:T(128)} %get-tuple-element.267, bf16[16,32,64,32]{3,2,1,0:T(8,128)(2,1)} %reshape.114, bf16[32,32,128]{2,1,0:T(8,128)(2,1)S(1)} %get-tuple-element.292, f32[16,64]{1,0:T(8,128)S(1)} %multiply_maximum_fusion.2), kind=kOutput, calls=%fused_computation.9.clone.1 | convolution fusion | flops 268697600 | bytes 8917504 | tf_op jit(solution)/shard_map/while/body/eval_jaxpr/icje,cep->ijp/dot_general | solution.py:53
  81.8 4.3 %convert_bitcast_fusion.3 = bf16[16,32,64,32]{2,3,1,0:T(8,128)(2,1)} fusion(bf16[32,32,128]{2,1,0:T(8,128)(2,1)S(1)} %get-tuple-element.292, f32[16,64]{1,0:T(8,128)S(1)} %multiply_maximum_fusion.2, bf16[4,16,64,128]{3,2,1,0:T(8,128)(2,1)} %get-tuple-element.288, s32[]{:T(128)} %get-tuple-element.267), kind=kOutput, calls=%fused_computation.clone.1 | convolution fusion | flops 269877248 | bytes 2626048 | tf_op jit(solution)/shard_map/while/body/eval_jaxpr/ijp,cep->icje/dot_general | solution.py:64
  86.1 8.4 %copy.65 = bf16[16,32,64,32]{3,2,1,0:T(8,128)(2,1)} copy(bf16[16,32,64,32]{2,3,1,0:T(8,128)(2,1)} %convert_bitcast_fusion.3) | data formatting | bytes 4194304 | tf_op jit(solution)/shard_map/while/body/eval_jaxpr/convert_element_type | solution.py:67
  94.6 11.1 %reshape.115 = bf16[512,2048]{1,0:T(8,128)(2,1)S(1)} reshape(bf16[16,32,64,32]{3,2,1,0:T(8,128)(2,1)} %copy.65) | data formatting | bytes 4194304 | tf_op jit(solution)/shard_map/while/body/eval_jaxpr/reshape | solution.py:67
  108.3 8.1 %reshape.114 = bf16[16,32,64,32]{3,2,1,0:T(8,128)(2,1)} reshape(bf16[512,2048]{1,0:T(8,128)(2,1)S(1)} %convolution_convert_fusion.2) | data formatting | bytes 4194304 | tf_op jit(solution)/shard_map/while/body/eval_jaxpr/reshape | solution.py:47
  116.4 6.0 %fusion.69 = bf16[4,16,64,128]{3,2,1,0:T(8,128)(2,1)} fusion(bf16[4,16,64,128]{3,2,1,0:T(8,128)(2,1)} %get-tuple-element.270, s32[]{:T(128)} %get-tuple-element.267, bf16[16,32,64,32]{3,2,1,0:T(8,128)(2,1)} %reshape.114, bf16[32,32,128]{2,1,0:T(8,128)(2,1)S(1)} %get-tuple-element.292, f32[16,64]{1,0:T(8,128)S(1)} %multiply_maximum_fusion.2), kind=kOutput, calls=%fused_computation.9.clone.1 | convolution fusion | flops 268697600 | bytes 8917504 | tf_op jit(solution)/shard_map/while/body/eval_jaxpr/icje,cep->ijp/dot_general | solution.py:53
  127.6 4.3 %convert_bitcast_fusion.3 = bf16[16,32,64,32]{2,3,1,0:T(8,128)(2,1)} fusion(bf16[32,32,128]{2,1,0:T(8,128)(2,1)S(1)} %get-tuple-element.292, f32[16,64]{1,0:T(8,128)S(1)} %multiply_maximum_fusion.2, bf16[4,16,64,128]{3,2,1,0:T(8,128)(2,1)} %get-tuple-element.288, s32[]{:T(128)} %get-tuple-element.267), kind=kOutput, calls=%fused_computation.clone.1 | convolution fusion | flops 269877248 | bytes 2626048 | tf_op jit(solution)/shard_map/while/body/eval_jaxpr/ijp,cep->icje/dot_general | solution.py:64
  131.8 8.4 %copy.65 = bf16[16,32,64,32]{3,2,1,0:T(8,128)(2,1)} copy(bf16[16,32,64,32]{2,3,1,0:T(8,128)(2,1)} %convert_bitcast_fusion.3) | data formatting | bytes 4194304 | tf_op jit(solution)/shard_map/while/body/eval_jaxpr/convert_element_type | solution.py:67
  140.3 11.1 %reshape.115 = bf16[512,2048]{1,0:T(8,128)(2,1)S(1)} reshape(bf16[16,32,64,32]{3,2,1,0:T(8,128)(2,1)} %copy.65) | data formatting | bytes 4194304 | tf_op jit(solution)/shard_map/while/body/eval_jaxpr/reshape | solution.py:67
  154.1 8.1 %reshape.114 = bf16[16,32,64,32]{3,2,1,0:T(8,128)(2,1)} reshape(bf16[512,2048]{1,0:T(8,128)(2,1)S(1)} %convolution_convert_fusion.2) | data formatting | bytes 4194304 | tf_op jit(solution)/shard_map/while/body/eval_jaxpr/reshape | solution.py:47
  162.2 6.0 %fusion.69 = bf16[4,16,64,128]{3,2,1,0:T(8,128)(2,1)} fusion(bf16[4,16,64,128]{3,2,1,0:T(8,128)(2,1)} %get-tuple-element.270, s32[]{:T(128)} %get-tuple-element.267, bf16[16,32,64,32]{3,2,1,0:T(8,128)(2,1)} %reshape.114, bf16[32,32,128]{2,1,0:T(8,128)(2,1)S(1)} %get-tuple-element.292, f32[16,64]{1,0:T(8,128)S(1)} %multiply_maximum_fusion.2), kind=kOutput, calls=%fused_computation.9.clone.1 | convolution fusion | flops 268697600 | bytes 8917504 | tf_op jit(solution)/shard_map/while/body/eval_jaxpr/icje,cep->ijp/dot_general | solution.py:53
  177.6 8.4 %copy.65 = bf16[16,32,64,32]{3,2,1,0:T(8,128)(2,1)} copy(bf16[16,32,64,32]{2,3,1,0:T(8,128)(2,1)} %convert_bitcast_fusion.3) | data formatting | bytes 4194304 | tf_op jit(solution)/shard_map/while/body/eval_jaxpr/convert_element_type | solution.py:67
  186.0 11.1 %reshape.115 = bf16[512,2048]{1,0:T(8,128)(2,1)S(1)} reshape(bf16[16,32,64,32]{3,2,1,0:T(8,128)(2,1)} %copy.65) | data formatting | bytes 4194304 | tf_op jit(solution)/shard_map/while/body/eval_jaxpr/reshape | solution.py:67
  199.8 8.1 %reshape.114 = bf16[16,32,64,32]{3,2,1,0:T(8,128)(2,1)} reshape(bf16[512,2048]{1,0:T(8,128)(2,1)S(1)} %convolution_convert_fusion.2) | data formatting | bytes 4194304 | tf_op jit(solution)/shard_map/while/body/eval_jaxpr/reshape | solution.py:47
  207.9 6.0 %fusion.69 = bf16[4,16,64,128]{3,2,1,0:T(8,128)(2,1)} fusion(bf16[4,16,64,128]{3,2,1,0:T(8,128)(2,1)} %get-tuple-element.270, s32[]{:T(128)} %get-tuple-element.267, bf16[16,32,64,32]{3,2,1,0:T(8,128)(2,1)} %reshape.114, bf16[32,32,128]{2,1,0:T(8,128)(2,1)S(1)} %get-tuple-element.292, f32[16,64]{1,0:T(8,128)S(1)} %multiply_maximum_fusion.2), kind=kOutput, calls=%fused_computation.9.clone.1 | convolution fusion | flops 268697600 | bytes 8917504 | tf_op jit(solution)/shard_map/while/body/eval_jaxpr/icje,cep->ijp/dot_general | solution.py:53
  225.0 18.2 %reduce-scatter.4.cloned.1.call-done = bf16[16,2048]{1,0:T(8,128)(2,1)} async-done(((bf16[64,2048]{1,0:T(8,128)(2,1)}), bf16[16,2048]{1,0:T(8,128)(2,1)}) %reduce-scatter.4.cloned.1.call-update) | async-done | bytes 65552 | tf_op jit(solution)/shard_map/reduce_scatter | solution.py:101
  243.2 20.9 %reduce-scatter.6.cloned.1.call-done = bf16[16,2048]{1,0:T(8,128)(2,1)} async-done(((bf16[64,2048]{1,0:T(8,128)(2,1)}), bf16[16,2048]{1,0:T(8,128)(2,1)}) %reduce-scatter.6.cloned.1.call-update) | async-done | bytes 65552 | tf_op jit(solution)/shard_map/reduce_scatter | solution.py:104
  265.8 58.2 %reduce-scatter.8.cloned.1.call-done = f32[64,128]{1,0:T(8,128)} async-done(((f32[1024,128]{1,0:T(8,128)}), f32[64,128]{1,0:T(8,128)}) %reduce-scatter.8.cloned.1.call-update) | async-done | bytes 32784 | tf_op jit(solution)/shard_map/reduce_scatter | solution.py:115
  (84 shorter events, 54.2 us)
Async XLA Ops:
  7.2 28.0 %copy-start.1 = (bf16[1024,128]{1,0:T(8,128)(2,1)S(1)}, bf16[1024,128]{1,0:T(8,128)(2,1)}, u32[]{:S(2)}) copy-start(bf16[1024,128]{1,0:T(8,128)(2,1)} %param.12) | copy-start | bytes 786436
  7.2 236.1 %reduce-scatter.4.cloned.1.call-start = ((), (), s32[]{:S(2)}) async-start(), calls=%async_computation.3 | async-start | bytes 327680 | tf_op jit(solution)/shard_map/reduce_scatter | solution.py:101
  70.7 6.0 %copy-start = (bf16[16,32,64,32]{3,2,1,0:T(8,128)(2,1)S(1)}, bf16[16,32,64,32]{3,2,1,0:T(8,128)(2,1)}, u32[]{:S(2)}) copy-start(bf16[16,32,64,32]{3,2,1,0:T(8,128)(2,1)} %reshape.114) | copy-start | bytes 6291460 | tf_op jit(solution)/shard_map/while
  70.7 6.0 %copy-start.2 = (f32[32,32,128]{2,1,0:T(8,128)S(1)}, f32[32,32,128]{2,1,0:T(8,128)}, u32[]{:S(2)}) copy-start(f32[32,32,128]{2,1,0:T(8,128)} %get-tuple-element.268) | copy-start | bytes 1572868 | tf_op jit(solution)/shard_map/while
  80.3 0.8 copy-start.3
  116.4 6.0 %copy-start = (bf16[16,32,64,32]{3,2,1,0:T(8,128)(2,1)S(1)}, bf16[16,32,64,32]{3,2,1,0:T(8,128)(2,1)}, u32[]{:S(2)}) copy-start(bf16[16,32,64,32]{3,2,1,0:T(8,128)(2,1)} %reshape.114) | copy-start | bytes 6291460 | tf_op jit(solution)/shard_map/while
  116.4 6.0 %copy-start.2 = (f32[32,32,128]{2,1,0:T(8,128)S(1)}, f32[32,32,128]{2,1,0:T(8,128)}, u32[]{:S(2)}) copy-start(f32[32,32,128]{2,1,0:T(8,128)} %get-tuple-element.268) | copy-start | bytes 1572868 | tf_op jit(solution)/shard_map/while
  126.0 0.8 copy-start.3
  162.2 6.0 %copy-start = (bf16[16,32,64,32]{3,2,1,0:T(8,128)(2,1)S(1)}, bf16[16,32,64,32]{3,2,1,0:T(8,128)(2,1)}, u32[]{:S(2)}) copy-start(bf16[16,32,64,32]{3,2,1,0:T(8,128)(2,1)} %reshape.114) | copy-start | bytes 6291460 | tf_op jit(solution)/shard_map/while
  162.2 6.0 %copy-start.2 = (f32[32,32,128]{2,1,0:T(8,128)S(1)}, f32[32,32,128]{2,1,0:T(8,128)}, u32[]{:S(2)}) copy-start(f32[32,32,128]{2,1,0:T(8,128)} %get-tuple-element.268) | copy-start | bytes 1572868 | tf_op jit(solution)/shard_map/while
  171.8 0.8 copy-start.3
  207.9 6.0 %copy-start = (bf16[16,32,64,32]{3,2,1,0:T(8,128)(2,1)S(1)}, bf16[16,32,64,32]{3,2,1,0:T(8,128)(2,1)}, u32[]{:S(2)}) copy-start(bf16[16,32,64,32]{3,2,1,0:T(8,128)(2,1)} %reshape.114) | copy-start | bytes 6291460 | tf_op jit(solution)/shard_map/while
  207.9 6.0 %copy-start.2 = (f32[32,32,128]{2,1,0:T(8,128)S(1)}, f32[32,32,128]{2,1,0:T(8,128)}, u32[]{:S(2)}) copy-start(f32[32,32,128]{2,1,0:T(8,128)} %get-tuple-element.268) | copy-start | bytes 1572868 | tf_op jit(solution)/shard_map/while
  217.5 0.8 copy-start.3
  221.9 42.3 %reduce-scatter.6.cloned.1.call-start = ((), (), s32[]{:S(2)}) async-start(), calls=%async_computation.4 | async-start | bytes 327680 | tf_op jit(solution)/shard_map/reduce_scatter | solution.py:104
  224.2 99.8 %reduce-scatter.8.cloned.1.call-start = ((), (), s32[]{:S(2)}) async-start(), calls=%async_computation.5 | async-start | bytes 557056 | tf_op jit(solution)/shard_map/reduce_scatter | solution.py:115
Sparse Core Ops, SparseCore 0:
  222.0 21.2 reduce-scatter.3
  245.8 18.2 reduce-scatter.5
  268.3 55.6 reduce-scatter.7
where the time goes:
time: 332 us; the launch traced here: 331 us
  local copies, waits for them, and re-layouts  123 us (37%)
  waiting for transfers between devices  98 us (30%)
  matrix products  66.1 us (20%)
  blocking collectives  21.8 us (7%)
  between operations  13.9 us (4%)
  other arithmetic  7.35 us (2%)
    reduce_scatter x1, waiting for transfers between devices, shards(): lax.psum_scatter(grad_w, ('row', 'col'), scatter_dimension=0, tiled=True)  58.2 us
    reshape x4, local copies, waits for them, and re-layouts, backward_part(): inner_grad.astype(jnp.bfloat16).reshape(wide_block, j_rows * channels)  44.4 us
    convert_element_type x4, local copies, waits for them, and re-layouts, backward_part(): inner_grad.astype(jnp.bfloat16).reshape(wide_block, j_rows * channels)  33.8 us
    reshape x4, local copies, waits for them, and re-layouts, outer_of(): products.astype(jnp.bfloat16)  32.3 us
    dot_general x4, matrix products, forward_part(): jnp.einsum('icje,cep->ijp', outer_block, weight_cube, preferred_element_t...  23.9 us
    reduce_scatter x1, waiting for transfers between devices, shards(): lax.psum_scatter(right_rows_out.astype(jnp.bfloat16), 'row', scatter_dime...  20.9 us
    reduce_scatter x1, waiting for transfers between devices, shards(): lax.psum_scatter(left_rows_out.astype(jnp.bfloat16), 'col', scatter_dimen...  18.2 us
    dot_general x4, matrix products, backward_part(): jnp.einsum('ijp,cep->icje', scaled, weight_cube, preferred_element_type=j...  17.1 us
  transfers between devices with their start and end apart: 3, of which 3 were waited for; matrix products, arithmetic and copies ran while one was open for 1% of the time, Pallas kernels for 0%

commit v1 on v0

v1 whole, which is shorter than its diff:
```python
import functools

import jax
import jax.numpy as jnp
from jax import lax
from jax.experimental import pallas as pl
from jax.experimental.pallas import tpu as pltpu
from jax.sharding import PartitionSpec as P

LANES = 128
VMEM_BYTES = 48 * 1024 * 1024
NT = (((1,), (1,)), ((), ()))
F32 = jnp.float32
BF16 = jnp.bfloat16


def params():
    return pltpu.CompilerParams(
        dimension_semantics=("arbitrary",), vmem_limit_bytes=VMEM_BYTES
    )


def cost(flops, nbytes):
    return pl.CostEstimate(flops=int(flops), bytes_accessed=int(nbytes), transcendentals=0)


def spread_rows(mask_ref, first, count, out_ref):
    def body(r, carry):
        value = mask_ref[first + r].astype(F32)
        out_ref[pl.ds(r, 1), :] = jnp.full((1, LANES), value, F32)
        return carry

    lax.fori_loop(0, count, body, 0, unroll=8)


def inner_kernel(dims, res_ref, seq_ref, cot_ref, w_ref, scaled_ref, z_ref, inv_ref, wp_ref, w32):
    chans, groups, blocks, i_rows, j_rows, step_rows, sequences = dims
    step = pl.program_id(0)

    @pl.when(step == 0)
    def _():
        w32[...] = w_ref[...].astype(F32)
        for e in range(chans):
            wp_ref[e * chans : (e + 1) * chans, :] = w32[
                pl.ds(e, chans, stride=chans), :
            ].astype(BF16)
        spread_rows(res_ref, lax.axis_index("col") * j_rows, j_rows, inv_ref)
        valid = lax.fori_loop(
            0, sequences, lambda s, total: total + seq_ref[s], jnp.int32(0), unroll=8
        ).astype(F32)
        inv_ref[...] = 1.0 / jnp.maximum(valid * inv_ref[...], 1.0)

    first = lax.axis_index("row") * i_rows + step * step_rows
    for i in range(step_rows):
        kept = res_ref[first + i] > 0
        inverse = jnp.where(kept, inv_ref[...], 1.0)
        scaled_ref[i] = (cot_ref[i].astype(F32) * inverse).astype(BF16)
    scaled = scaled_ref[...].reshape(step_rows * j_rows, LANES)
    for pair in range(0, blocks, 2):
        width = 2 * LANES
        part = lax.dot_general(
            scaled, wp_ref[pair * LANES : pair * LANES + width, :], NT, preferred_element_type=F32
        ).astype(BF16)
        for k in range(2):
            for i in range(step_rows):
                z_ref[
                    (pair + k) * j_rows : (pair + k + 1) * j_rows, i * LANES : (i + 1) * LANES
                ] = part[i * j_rows : (i + 1) * j_rows, k * LANES : (k + 1) * LANES]


def lane_group(shape, chans):
    return lax.broadcasted_iota(jnp.int32, shape, 1) // chans


def outer_kernel(dims, n_row, n_col, *refs):
    chans, groups, blocks, i_rows, j_rows, step_rows, sequences = dims
    tiles = sequences * chans // LANES
    depth = groups * sequences
    width = sequences * chans
    j_pad = -(-j_rows // LANES) * LANES
    res_ref, keep_ref, scaled_ref = refs[:3]
    left_refs = refs[3 : 3 + n_col]
    right_refs = refs[3 + n_col : 3 + n_col + n_row]
    y_ref, diag_ref, rbt_ref = refs[3 + n_col + n_row : 6 + n_col + n_row]
    gw_refs = refs[6 + n_col + n_row : 6 + n_col + 2 * n_row]
    flat, turned, keep_rows, lsplit, rbig, expand, gwt, gwr = refs[6 + n_col + 2 * n_row :]
    step = pl.program_id(0)
    row, col = lax.axis_index("row"), lax.axis_index("col")

    @pl.when(step == 0)
    def _():
        piece = right_refs[0].shape[0]
        for k in range(n_row):
            owner = lax.rem(row - k + n_row, n_row)
            flat[pl.ds(pl.multiple_of(owner * piece, 8), piece), :] = right_refs[k][...].astype(F32)
        if j_rows < j_pad:
            flat[j_rows:j_pad, :] = jnp.zeros((j_pad - j_rows, width), F32)
            keep_rows[j_rows:j_pad, :] = jnp.zeros((j_pad - j_rows, LANES), F32)
        spread_rows(res_ref, col * j_rows, j_rows, keep_rows)
        for t in range(tiles):
            lanes = slice(t * LANES, (t + 1) * LANES)
            masked = flat[0:j_pad, lanes] * keep_rows[0:j_pad, :] * keep_ref[:, lanes]
            turned[lanes, :] = masked.T
        for a in range(blocks):
            parts = [
                turned[pl.ds(lo * chans + groups * a + b, tiles, stride=LANES), :]
                for b in range(groups)
                for lo in range(groups)
            ]
            block = jnp.concatenate(parts, axis=0)
            rbig[a * j_rows : (a + 1) * j_rows, :] = block.T[:j_rows].astype(BF16)
        rbt_ref[...] = rbig[...].T
        piece = left_refs[0].shape[0]
        for k in range(n_col):
            owner = lax.rem(col - k + n_col, n_col)
            flat[pl.ds(pl.multiple_of(owner * piece, 8), piece), :] = left_refs[k][...].astype(F32)
        spread_rows(res_ref, row * i_rows, i_rows, keep_rows)
        for t in range(tiles):
            lanes = slice(t * LANES, (t + 1) * LANES)
            masked = flat[0:i_rows, lanes] * keep_rows[0:i_rows, :] * keep_ref[:, lanes]
            lsplit[pl.ds(t, i_rows, stride=tiles), :] = masked
        shape = (LANES, groups * LANES)
        source = lax.broadcasted_iota(jnp.int32, shape, 0)
        target = lax.broadcasted_iota(jnp.int32, shape, 1)
        same = (source // chans == target // LANES) & (source % chans == target % chans)
        expand[...] = same.astype(F32).astype(BF16)
        gwt[...] = jnp.zeros_like(gwt)

    rows = step_rows * tiles
    spread = jnp.dot(
        lsplit[pl.ds(pl.multiple_of(step * rows, rows), rows), :].astype(BF16),
        expand[...],
        preferred_element_type=F32,
    ).astype(BF16)
    group = lane_group((tiles, LANES), chans)
    for b in range(groups):
        chosen = (group == b).astype(F32).astype(BF16)
        for lo in range(groups):
            at = b * sequences + lo * tiles
            for i in range(step_rows):
                diag_ref[at : at + tiles, i * LANES : (i + 1) * LANES] = (
                    spread[i * tiles : (i + 1) * tiles, lo * LANES : (lo + 1) * LANES] * chosen
                )
    for pair in range(0, step_rows, 2):
        part = jnp.dot(
            rbig[...], diag_ref[:, pair * LANES : (pair + 2) * LANES], preferred_element_type=F32
        ).astype(BF16)
        for k in range(2):
            for a in range(blocks):
                y_ref[pair + k, :, a * LANES : (a + 1) * LANES] = part[
                    a * j_rows : (a + 1) * j_rows, k * LANES : (k + 1) * LANES
                ]
    pairs = step_rows * j_rows
    scaled_t = scaled_ref[...].reshape(pairs, LANES).T
    y_flat = y_ref[...].reshape(pairs, blocks * LANES)
    gwt[...] += jnp.dot(scaled_t, y_flat, preferred_element_type=F32)

    @pl.when(step == pl.num_programs(0) - 1)
    def _():
        per_tile = LANES // chans
        for k in range(blocks):
            turned_tile = gwt[:, k * LANES : (k + 1) * LANES].T
            for q in range(per_tile):
                gwr[pl.ds(k * per_tile + q, chans, stride=chans), :] = turned_tile[
                    q * chans : (q + 1) * chans
                ]
        owned = chans * chans // n_row
        for k in range(n_row):
            owner = lax.rem(row + k, n_row)
            gw_refs[k][...] = gwr[pl.ds(pl.multiple_of(owner * owned, 8), owned), :].astype(BF16)


def grads_kernel(dims, n_row, n_col, *refs):
    chans, groups, blocks, i_rows, j_rows, step_rows, sequences = dims
    tiles = sequences * chans // LANES
    depth = groups * sequences
    j_pad = -(-j_rows // LANES) * LANES
    z_ref, diag_ref, rbt_ref = refs[:3]
    gl_refs = refs[3 : 3 + n_col]
    gr_refs = refs[3 + n_col : 3 + n_col + n_row]
    gl_all, acc, turned, gr_all = refs[3 + n_col + n_row :]
    step = pl.program_id(0)

    @pl.when(step == 0)
    def _():
        acc[...] = jnp.zeros_like(acc)

    span = blocks * j_rows
    acc[0:span, :] += lax.dot_general(z_ref[...], diag_ref[...], NT, preferred_element_type=F32)
    group = lane_group((sequences, LANES), chans)
    group_t = lane_group((tiles, LANES), chans)
    for pair in range(0, step_rows, 2):
        part = jnp.dot(
            rbt_ref[...], z_ref[:, pair * LANES : (pair + 2) * LANES], preferred_element_type=F32
        )
        for k in range(2):
            mine = part[:, k * LANES : (k + 1) * LANES]
            total = mine[0:sequences]
            for b in range(1, groups):
                total = jnp.where(group == b, mine[b * sequences : (b + 1) * sequences], total)
            shift = LANES // 2
            while shift >= chans:
                total = total + pltpu.roll(total, shift, axis=1)
                shift //= 2
            merged = total[0:tiles]
            for lo in range(1, groups):
                merged = jnp.where(group_t == lo, total[lo * tiles : (lo + 1) * tiles], merged)
            at = (step * step_rows + pair + k) * tiles
            gl_all[pl.ds(pl.multiple_of(at, tiles), tiles), :] = merged.astype(BF16)

    @pl.when(step == pl.num_programs(0) - 1)
    def _():
        row, col = lax.axis_index("row"), lax.axis_index("col")
        owned = i_rows * tiles // n_col
        for k in range(n_col):
            owner = lax.rem(col + k, n_col)
            gl_refs[k][...] = gl_all[pl.ds(pl.multiple_of(owner * owned, 16), owned), :]
        for a in range(blocks):
            flipped = acc[a * j_rows : a * j_rows + j_pad, :].T
            for b in range(groups):
                for lo in range(groups):
                    at = b * sequences + lo * tiles
                    turned[pl.ds(lo * chans + groups * a + b, tiles, stride=LANES), :] = flipped[
                        at : at + tiles
                    ]
        for t in range(tiles):
            lanes = slice(t * LANES, (t + 1) * LANES)
            gr_all[:, lanes] = turned[lanes, :].T[:j_rows]
        owned = j_rows // n_row
        for k in range(n_row):
            owner = lax.rem(row + k, n_row)
            gr_refs[k][...] = gr_all[pl.ds(pl.multiple_of(owner * owned, 8), owned), :].astype(BF16)


def pair_kernel(dims, res_ref, y_ref, wp_ref, inv_ref, out_ref):
    chans, groups, blocks, i_rows, j_rows, step_rows, sequences = dims
    pairs = step_rows * j_rows
    projected = jnp.dot(
        y_ref[...].reshape(pairs, blocks * LANES), wp_ref[...], preferred_element_type=F32
    )
    first = lax.axis_index("row") * i_rows + pl.program_id(0) * step_rows
    for i in range(step_rows):
        kept = res_ref[first + i] > 0
        inverse = jnp.where(kept, inv_ref[...], 1.0)
        out_ref[i] = (projected[i * j_rows : (i + 1) * j_rows] * inverse).astype(BF16)


def total_of(refs):
    total = refs[0][...].astype(F32)
    for ref in refs[1:]:
        total = total + ref[...].astype(F32)
    return total


def weight_kernel(n_row, n_col, *refs):
    ins, outs, whole = refs[:n_row], refs[n_row : n_row + n_col], refs[n_row + n_col]
    whole[...] = total_of(ins)
    owned = whole.shape[0] // n_col
    col = lax.axis_index("col")
    for k in range(n_col):
        owner = lax.rem(col + k, n_col)
        outs[k][...] = whole[pl.ds(pl.multiple_of(owner * owned, 8), owned), :].astype(BF16)


def final_kernel(dims, n_row, n_col, *refs):
    chans, groups, blocks, i_rows, j_rows, step_rows, sequences = dims
    tiles = sequences * chans // LANES
    res_ref, keep_ref = refs[:2]
    gl_in = refs[2 : 2 + n_col]
    gr_in = refs[2 + n_col : 2 + n_col + n_row]
    gw_in = refs[2 + n_col + n_row : 2 + 2 * n_col + n_row]
    gl_out, gr_out, gw_out, whole, left_rows, right_rows = refs[2 + 2 * n_col + n_row :]
    row, col = lax.axis_index("row"), lax.axis_index("col")
    gw_out[...] = total_of(gw_in)
    whole[...] = total_of(gl_in)
    own_left, own_right = gl_out.shape[0], gr_out.shape[0]
    spread_rows(res_ref, (row * n_col + col) * own_left, own_left, left_rows)
    spread_rows(res_ref, (col * n_row + row) * own_right, own_right, right_rows)
    right = total_of(gr_in)
    for t in range(tiles):
        lanes = slice(t * LANES, (t + 1) * LANES)
        keep = keep_ref[:, lanes]
        gl_out[:, lanes] = whole[pl.ds(t, own_left, stride=tiles), :] * (left_rows[...] * keep)
        gr_out[:, lanes] = right[:, lanes] * (right_rows[...] * keep)


def exchange(pieces, axis):
    n = len(pieces)
    came = [pieces[0]]
    for k in range(1, n):
        came.append(lax.ppermute(pieces[k], axis, [(s, (s + k) % n) for s in range(n)]))
    return came


def smem():
    return pl.BlockSpec(memory_space=pltpu.SMEM)


def whole_spec(shape):
    return pl.BlockSpec(shape, lambda *_: (0,) * len(shape))


def shards(left_act, right_act, row_mask, res_mask, out_weight, cotangent):
    n_col = lax.axis_size("col")
    n_row = lax.axis_size("row")
    i_rows, j_rows, pair_width = cotangent.shape
    sequences = row_mask.shape[0]
    width = left_act.shape[1]
    chans = width // sequences
    groups = LANES // chans
    blocks = chans // groups
    tiles = width // LANES
    depth = groups * sequences
    inner = chans * chans
    step_rows = 8
    steps = i_rows // step_rows
    dims = (chans, groups, blocks, i_rows, j_rows, step_rows, sequences)
    j_pad = -(-j_rows // LANES) * LANES
    pad = max(j_pad, i_rows)
    span = blocks * j_rows
    own_left, own_right = left_act.shape[0], right_act.shape[0]
    struct = jax.ShapeDtypeStruct
    macs = i_rows * j_rows * inner * pair_width

    lefts = exchange([left_act] * n_col, "col")
    rights = exchange([right_act] * n_row, "row")
    keep = jnp.repeat(row_mask.astype(F32), chans)[None, :]

    pair_block = pl.BlockSpec((step_rows, j_rows, pair_width), lambda g: (g, 0, 0))
    z_block = pl.BlockSpec((span, step_rows * LANES), lambda g: (0, g))
    diag_block = pl.BlockSpec((depth, step_rows * LANES), lambda g: (0, g))
    y_block = pl.BlockSpec((step_rows, j_rows, inner), lambda g: (g, 0, 0))

    scaled, z, inverse, weight = pl.pallas_call(
        functools.partial(inner_kernel, dims),
        grid=(steps,),
        in_specs=[smem(), smem(), pair_block, whole_spec(out_weight.shape)],
        out_specs=[
            pair_block,
            z_block,
            whole_spec((j_rows, LANES)),
            whole_spec(out_weight.shape),
        ],
        out_shape=[
            struct(cotangent.shape, BF16),
            struct((span, i_rows * LANES), BF16),
            struct((j_rows, LANES), F32),
            struct(out_weight.shape, BF16),
        ],
        scratch_shapes=[pltpu.VMEM(out_weight.shape, F32)],
        compiler_params=params(),
        cost_estimate=cost(2 * macs, 12 * 2**20),
        name="inner",
    )(res_mask, row_mask, cotangent, out_weight)

    owned_w = inner // n_row
    outs = pl.pallas_call(
        functools.partial(outer_kernel, dims, n_row, n_col),
        grid=(steps,),
        in_specs=[smem(), whole_spec((1, width)), pair_block]
        + [whole_spec(left_act.shape)] * n_col
        + [whole_spec(right_act.shape)] * n_row,
        out_specs=[y_block, diag_block, whole_spec((depth, span))]
        + [whole_spec((owned_w, pair_width))] * n_row,
        out_shape=[
            struct((i_rows, j_rows, inner), BF16),
            struct((depth, i_rows * LANES), BF16),
            struct((depth, span), BF16),
        ]
        + [struct((owned_w, pair_width), BF16)] * n_row,
        scratch_shapes=[
            pltpu.VMEM((pad, width), F32),
            pltpu.VMEM((width, j_pad), F32),
            pltpu.VMEM((pad, LANES), F32),
            pltpu.VMEM((i_rows * tiles, LANES), F32),
            pltpu.VMEM((span, depth), BF16),
            pltpu.VMEM((LANES, groups * LANES), BF16),
            pltpu.VMEM((pair_width, inner), F32),
            pltpu.VMEM((inner, pair_width), F32),
        ],
        compiler_params=params(),
        cost_estimate=cost(4 * macs, 16 * 2**20),
        name="outer",
    )(res_mask, keep, scaled, *lefts, *rights)
    y, diag, right_turned = outs[:3]
    weight_parts = exchange(outs[3:], "row")

    outs = pl.pallas_call(
        functools.partial(grads_kernel, dims, n_row, n_col),
        grid=(steps,),
        in_specs=[z_block, diag_block, whole_spec((depth, span))],
        out_specs=[whole_spec((i_rows * tiles // n_col, LANES))] * n_col
        + [whole_spec((j_rows // n_row, width))] * n_row,
        out_shape=[struct((i_rows * tiles // n_col, LANES), BF16)] * n_col
        + [struct((j_rows // n_row, width), BF16)] * n_row,
        scratch_shapes=[
            pltpu.VMEM((i_rows * tiles, LANES), BF16),
            pltpu.VMEM((span + j_pad, depth), F32),
            pltpu.VMEM((width, j_pad), F32),
            pltpu.VMEM((j_rows, width), F32),
        ],
        compiler_params=params(),
        cost_estimate=cost(4 * macs, 16 * 2**20),
        name="grads",
    )(z, diag, right_turned)
    left_parts = exchange(outs[:n_col], "col")
    right_parts = exchange(outs[n_col:], "row")

    weight_cut = pl.pallas_call(
        functools.partial(weight_kernel, n_row, n_col),
        out_shape=[struct((owned_w // n_col, pair_width), BF16)] * n_col,
        scratch_shapes=[pltpu.VMEM((owned_w, pair_width), F32)],
        name="weight_sum",
    )(*weight_parts)
    weight_parts = exchange(weight_cut, "col")

    pair_out = pl.pallas_call(
        functools.partial(pair_kernel, dims),
        grid=(steps,),
        in_specs=[
            smem(),
            y_block,
            whole_spec(out_weight.shape),
            whole_spec((j_rows, LANES)),
        ],
        out_specs=pair_block,
        out_shape=struct(cotangent.shape, BF16),
        compiler_params=params(),
        cost_estimate=cost(2 * macs, 12 * 2**20),
        name="pair",
    )(res_mask, y, weight, inverse)

    grad_left, grad_right, grad_weight = pl.pallas_call(
        functools.partial(final_kernel, dims, n_row, n_col),
        in_specs=[smem()] + [pl.BlockSpec(memory_space=pltpu.VMEM)] * (1 + 2 * n_col + n_row),
        out_shape=[
            struct((own_left, width), F32),
            struct((own_right, width), F32),
            struct((owned_w // n_col, pair_width), F32),
        ],
        scratch_shapes=[
            pltpu.VMEM((own_left * tiles, LANES), F32),
            pltpu.VMEM((own_left, LANES), F32),
            pltpu.VMEM((own_right, LANES), F32),
        ],
        name="final_sums",
    )(res_mask, keep, *left_parts, *right_parts, *weight_parts)
    return (pair_out, grad_left, grad_right, grad_weight)


def solution(mesh):
    placed = (
        P(("grp", "row", "col"), None),
        P(("grp", "col", "row"), None),
        P("grp"),
        P("grp"),
        P(),
        P(("grp", "row"), "col", None),
    )
    return jax.shard_map(
        shards,
        mesh=mesh,
        in_specs=placed,
        out_specs=(
            P(("grp", "row"), "col", None),
            P(("grp", "row", "col"), None),
            P(("grp", "col", "row"), None),
            P(("grp", "row", "col"), None),
        ),
        check_vma=False,
    )
```

time: 332 us -> 79.5 us (0.24)
  local copies, waits for them, and re-layouts: 123 us -> 10 us
  waiting for transfers between devices: 98 us -> 0.05 us
  matrix products: 66.1 us -> 0 us
  Pallas kernels: 0 us -> 42.2 us
  starting transfers between devices: 0.12 us -> 25 us
  blocking collectives: 21.8 us -> 0 us
  between operations: 13.9 us -> 0.85 us
  other arithmetic: 7.35 us -> 0.66 us
    reduce_scatter x3 -> x0, waiting for transfers between devices: 97.3 us -> none  [the longest x1 58.2 us: shards(): lax.psum_scatter(grad_w, ('row', 'col'), scatter_dimension=0, tiled=True)]
    reshape x10 -> x0, local copies, waits for them, and re-layouts: 77.6 us -> none  [the longest x4 44.4 us: backward_part(): inner_grad.astype(jnp.bfloat16).reshape(wide_block, j_rows * channels)]
    dot_general x24 -> x0, matrix products: 66.1 us -> none  [the longest x4 23.9 us: forward_part(): jnp.einsum('icje,cep->ijp', outer_block, weight_cube, preferred_element_t...]
    pallas_call x0 -> x6, Pallas kernels: none -> 42.2 us  [the longest x1 12.1 us: shards(): pl.pallas_call(functools.partial(outer_kernel, dims, n_row, n_col), grid=...]
    convert_element_type x8 -> x0, local copies, waits for them, and re-layouts: 38.1 us -> none  [the longest x4 33.8 us: backward_part(): inner_grad.astype(jnp.bfloat16).reshape(wide_block, j_rows * channels)]
    ppermute x0 -> x18, starting transfers between devices: none -> 25 us  [exchange(): lax.ppermute(pieces[k], axis, [(s, (s + k) % n) for s in range(n)])]
    all_gather x2 -> x0, blocking collectives: 21.8 us -> none  [the longest x1 15.8 us: shards(): left_all = lax.all_gather(left_act, 'col', axis=0, tiled=True)]
    unnamed x4 -> x48, local copies, waits for them, and re-layouts: 0.4 us -> 9.86 us
  transfers between devices with their start and end apart: 3 -> 18, of which waited for: 3 -> 0; matrix products, arithmetic and copies ran while one was open for 1% -> 1% of each run, Pallas kernels for 0% -> 36%
where the time goes in v1:
time: 79.5 us; the launch traced here: 78.7 us
  Pallas kernels  42.2 us (53%)
  starting transfers between devices  25 us (31%)
  local copies, waits for them, and re-layouts  10 us (13%)
  between operations  0.85 us (1%)
    ppermute x18, starting transfers between devices, exchange(): lax.ppermute(pieces[k], axis, [(s, (s + k) % n) for s in range(n)])  25 us
    pallas_call x1, Pallas kernels, shards(): pl.pallas_call(functools.partial(outer_kernel, dims, n_row, n_col), grid=...  12.1 us
    pallas_call x1, Pallas kernels, shards(): pl.pallas_call(functools.partial(grads_kernel, dims, n_row, n_col), grid=...  10.6 us
    unnamed x48, local copies, waits for them, and re-layouts  9.86 us
    pallas_call x1, Pallas kernels, shards(): pl.pallas_call(functools.partial(pair_kernel, dims), grid=(steps,), in_sp...  8.34 us
    pallas_call x1, Pallas kernels, shards(): pl.pallas_call(functools.partial(inner_kernel, dims), grid=(steps,), in_s...  7.66 us
    pallas_call x1, Pallas kernels, shards(): pl.pallas_call(functools.partial(final_kernel, dims, n_row, n_col), in_sp...  1.98 us
    pallas_call x1, Pallas kernels, shards(): pl.pallas_call(functools.partial(weight_kernel, n_row, n_col), out_shape=...  1.59 us
  transfers between devices with their start and end apart: 18, of which 0 were waited for; matrix products, arithmetic and copies ran while one was open for 1% of the time, Pallas kernels for 36%

profile of v1, /device:TPU:0, one launch (start us, length us, event | category | flops | bytes accessed | tf_op | source)
XLA Modules:
  0.0 78.7 jit_solution(2375903672531116225)
XLA Ops:
  0.6 4.1 %collective-permute-start.1 = (bf16[16,2048]{1,0:T(8,128)(2,1)}, bf16[16,2048]{1,0:T(8,128)(2,1)S(1)}, u32[]{:S(2)}, u32[]{:S(2)}) collective-permute-start(bf16[16,2048]{1,0:T(8,128)(2,1)} %refs_3_.1), channel_id=1, source_target_pairs={{0,2},{1,3},{2,0},{3,1},{4,6},{5,7},{6,4},{7,5},{8,10},{9,11},{10,... | collective-permute-start | bytes 196616 | tf_op jit(solution)/shard_map/ppermute | solution.py:291
  4.7 1.6 %collective-permute-start = (bf16[16,2048]{1,0:T(8,128)(2,1)}, bf16[16,2048]{1,0:T(8,128)(2,1)S(1)}, u32[]{:S(2)}, u32[]{:S(2)}) collective-permute-start(bf16[16,2048]{1,0:T(8,128)(2,1)} %refs_3_.1), channel_id=1, source_target_pairs={{0,1},{1,2},{2,3},{3,0},{4,5},{5,6},{6,7},{7,4},{8,9},{9,10},{10,1... | collective-permute-start | bytes 196616 | tf_op jit(solution)/shard_map/ppermute | solution.py:291
  6.3 2.2 %collective-permute-start.2 = (bf16[16,2048]{1,0:T(8,128)(2,1)}, bf16[16,2048]{1,0:T(8,128)(2,1)S(1)}, u32[]{:S(2)}, u32[]{:S(2)}) collective-permute-start(bf16[16,2048]{1,0:T(8,128)(2,1)} %refs_3_.1), channel_id=1, source_target_pairs={{0,3},{1,0},{2,1},{3,2},{4,7},{5,4},{6,5},{7,6},{8,11},{9,8},{10,9... | collective-permute-start | bytes 196616 | tf_op jit(solution)/shard_map/ppermute | solution.py:291
  8.6 1.5 %collective-permute-start.4 = (bf16[16,2048]{1,0:T(8,128)(2,1)}, bf16[16,2048]{1,0:T(8,128)(2,1)S(1)}, u32[]{:S(2)}, u32[]{:S(2)}) collective-permute-start(bf16[16,2048]{1,0:T(8,128)(2,1)} %refs_7_.1), channel_id=1, source_target_pairs={{0,8},{4,12},{8,0},{12,4},{1,9},{5,13},{9,1},{13,5},{2,10},{6,14},... | collective-permute-start | bytes 196616 | tf_op jit(solution)/shard_map/ppermute | solution.py:291
  10.9 1.8 %collective-permute-start.5 = (bf16[16,2048]{1,0:T(8,128)(2,1)}, bf16[16,2048]{1,0:T(8,128)(2,1)S(1)}, u32[]{:S(2)}, u32[]{:S(2)}) collective-permute-start(bf16[16,2048]{1,0:T(8,128)(2,1)} %refs_7_.1), channel_id=1, source_target_pairs={{0,12},{4,0},{8,4},{12,8},{1,13},{5,1},{9,5},{13,9},{2,14},{6,2},{... | collective-permute-start | bytes 196616 | tf_op jit(solution)/shard_map/ppermute | solution.py:291
  12.7 0.7 copy-done.5
  13.4 1.2 %copy-done.7 = bf16[64,64,128]{2,1,0:T(8,128)(2,1)S(1)} copy-done((bf16[64,64,128]{2,1,0:T(8,128)(2,1)S(1)}, bf16[64,64,128]{2,1,0:T(8,128)(2,1)}, u32[]{:S(2)}) %copy-start.7) | copy-done | bytes 1048600
  14.6 0.9 %copy-done.8 = bf16[1024,128]{1,0:T(8,128)(2,1)S(1)} copy-done((bf16[1024,128]{1,0:T(8,128)(2,1)S(1)}, bf16[1024,128]{1,0:T(8,128)(2,1)}, u32[]{:S(2)}) %copy-start.8) | copy-done | bytes 262168
  16.2 7.7 %inner.1 = (bf16[64,64,128]{2,1,0:T(8,128)(2,1)S(1)}, bf16[512,8192]{1,0:T(8,128)(2,1)}, f32[64,128]{1,0:T(8,128)S(1)}, bf16[1024,128]{1,0:T(8,128)(2,1)S(1)}) custom-call(s32[256]{0:T(256)S(1)} %copy-done.5, s32[64]{0:T(128)S(1)} %copy-done.11, bf16[64,64,128]{2,1,0:T(8,128)(2,1)S(1)} %copy-done.7, bf16[1024,128]{1,0:T(8,128)(2,1)S(1)} %copy-done.8), custom_call_target="tpu_custom_call" | custom-call | flops 1073741824 | bytes 12582912 | tf_op jit(solution)/shard_map/inner/pallas_call | solution.py:334
  23.9 0.8 %copy-done.9 = bf16[16,2048]{1,0:T(8,128)(2,1)S(1)} copy-done((bf16[16,2048]{1,0:T(8,128)(2,1)S(1)}, bf16[16,2048]{1,0:T(8,128)(2,1)}, u32[]{:S(2)}) %copy-start.9) | copy-done | bytes 65560
  24.7 0.8 %copy-done.10 = bf16[16,2048]{1,0:T(8,128)(2,1)S(1)} copy-done((bf16[16,2048]{1,0:T(8,128)(2,1)S(1)}, bf16[16,2048]{1,0:T(8,128)(2,1)}, u32[]{:S(2)}) %copy-start.10) | copy-done | bytes 65560
  25.6 12.1 %outer.1 = (bf16[64,64,1024]{2,1,0:T(8,128)(2,1)}, bf16[256,8192]{1,0:T(8,128)(2,1)}, bf16[256,512]{1,0:T(8,128)(2,1)S(1)}, bf16[256,128]{1,0:T(8,128)(2,1)S(1)}...) custom-call(s32[256]{0:T(256)S(1)} %copy-done.5, ...), custom_call_target="tpu_custom_call" | custom-call | flops 2147483648 | bytes 16777216 | tf_op jit(solution)/shard_map/outer/pallas_call | solution.py:357
  38.8 1.4 %collective-permute-start.14 = (bf16[256,128]{1,0:T(8,128)(2,1)S(1)}, bf16[256,128]{1,0:T(8,128)(2,1)S(1)}, u32[]{:S(2)}, u32[]{:S(2)}) collective-permute-start(bf16[256,128]{1,0:T(8,128)(2,1)S(1)} %get-tuple-element.48), channel_id=1, source_target_pairs={{0,12},{4,0},{8,4},{12,8},{1,13},{5,1},{9,5},{13,9},{2,14},{6,2},{... | collective-permute-start | bytes 196616 | tf_op jit(solution)/shard_map/ppermute | solution.py:291
  40.3 2.2 %copy-done = bf16[256,8192]{1,0:T(8,128)(2,1)S(1)} copy-done((bf16[256,8192]{1,0:T(8,128)(2,1)S(1)}, bf16[256,8192]{1,0:T(8,128)(2,1)}, u32[]{:S(2)}) %copy-start) | copy-done | bytes 4194328
  42.4 10.6 %grads.1 = (bf16[256,128]{1,0:T(8,128)(2,1)S(1)}, bf16[256,128]{1,0:T(8,128)(2,1)S(1)}, bf16[256,128]{1,0:T(8,128)(2,1)S(1)}, bf16[256,128]{1,0:T(8,128)(2,1)S(1...) custom-call(bf16[512,8192]{1,0:T(8,128)(2,1)} %get-tuple-element.34., ...), custom_call_target="tpu_custom_call" | custom-call | flops 2147483648 | bytes 16777216 | tf_op jit(solution)/shard_map/grads/pallas_call | solution.py:388
  54.3 1.3 %collective-permute-start.7 = (bf16[256,128]{1,0:T(8,128)(2,1)S(1)}, bf16[256,128]{1,0:T(8,128)(2,1)S(1)}, u32[]{:S(2)}, u32[]{:S(2)}) collective-permute-start(bf16[256,128]{1,0:T(8,128)(2,1)S(1)} %get-tuple-element.39), channel_id=1, source_target_pairs={{0,2},{1,3},{2,0},{3,1},{4,6},{5,7},{6,4},{7,5},{8,10},{9,11},{10,... | collective-permute-start | bytes 196616 | tf_op jit(solution)/shard_map/ppermute | solution.py:291
  55.6 2.6 %collective-permute-start.8 = (bf16[256,128]{1,0:T(8,128)(2,1)S(1)}, bf16[256,128]{1,0:T(8,128)(2,1)S(1)}, u32[]{:S(2)}, u32[]{:S(2)}) collective-permute-start(bf16[256,128]{1,0:T(8,128)(2,1)S(1)} %get-tuple-element.40), channel_id=1, source_target_pairs={{0,3},{1,0},{2,1},{3,2},{4,7},{5,4},{6,5},{7,6},{8,11},{9,8},{10,9... | collective-permute-start | bytes 196616 | tf_op jit(solution)/shard_map/ppermute | solution.py:291
  58.2 1.6 %collective-permute-start.10 = (bf16[16,2048]{1,0:T(8,128)(2,1)S(1)}, bf16[16,2048]{1,0:T(8,128)(2,1)S(1)}, u32[]{:S(2)}, u32[]{:S(2)}) collective-permute-start(bf16[16,2048]{1,0:T(8,128)(2,1)S(1)} %get-tuple-element.43), channel_id=1, source_target_pairs={{0,8},{4,12},{8,0},{12,4},{1,9},{5,13},{9,1},{13,5},{2,10},{6,14},... | collective-permute-start | bytes 196616 | tf_op jit(solution)/shard_map/ppermute | solution.py:291
  59.8 1.6 %weight_sum.1 = (bf16[64,128]{1,0:T(8,128)(2,1)}, bf16[64,128]{1,0:T(8,128)(2,1)}, bf16[64,128]{1,0:T(8,128)(2,1)}, bf16[64,128]{1,0:T(8,128)(2,1)}) custom-call(bf16[256,128]{1,0:T(8,128)(2,1)} %copy-done.3, bf16[256,128]{1,0:T(8,128)(2,1)} %copy-done.18, bf16[256,128]{1,0:T(8,128)(2,1)} %copy-done.19, bf16[256,128]{1,0:T(8,128)(2,1)} %copy-done.20), custom_call_target="tpu_custom_call" | custom-call | tf_op jit(solution)/shard_map/weight_sum/pallas_call | solution.py:409
  61.4 1.4 %collective-permute-start.11 = (bf16[16,2048]{1,0:T(8,128)(2,1)S(1)}, bf16[16,2048]{1,0:T(8,128)(2,1)S(1)}, u32[]{:S(2)}, u32[]{:S(2)}) collective-permute-start(bf16[16,2048]{1,0:T(8,128)(2,1)S(1)} %get-tuple-element.44), channel_id=1, source_target_pairs={{0,12},{4,0},{8,4},{12,8},{1,13},{5,1},{9,5},{13,9},{2,14},{6,2},{... | collective-permute-start | bytes 196616 | tf_op jit(solution)/shard_map/ppermute | solution.py:291
  63.4 1.6 %collective-permute-start.16 = (bf16[64,128]{1,0:T(8,128)(2,1)}, bf16[64,128]{1,0:T(8,128)(2,1)S(1)}, u32[]{:S(2)}, u32[]{:S(2)}) collective-permute-start(bf16[64,128]{1,0:T(8,128)(2,1)} %get-tuple-element.51), channel_id=1, source_target_pairs={{0,2},{1,3},{2,0},{3,1},{4,6},{5,7},{6,4},{7,5},{8,10},{9,11},{10,... | collective-permute-start | bytes 49160 | tf_op jit(solution)/shard_map/ppermute | solution.py:291
  65.0 2.7 %collective-permute-start.17 = (bf16[64,128]{1,0:T(8,128)(2,1)}, bf16[64,128]{1,0:T(8,128)(2,1)S(1)}, u32[]{:S(2)}, u32[]{:S(2)}) collective-permute-start(bf16[64,128]{1,0:T(8,128)(2,1)} %get-tuple-element.52), channel_id=1, source_target_pairs={{0,3},{1,0},{2,1},{3,2},{4,7},{5,4},{6,5},{7,6},{8,11},{9,8},{10,9... | collective-permute-start | bytes 49160 | tf_op jit(solution)/shard_map/ppermute | solution.py:291
  67.7 8.3 %pair.1 = bf16[64,64,128]{2,1,0:T(8,128)(2,1)} custom-call(s32[256]{0:T(256)S(1)} %copy-done.6, bf16[64,64,1024]{2,1,0:T(8,128)(2,1)} %get-tuple-element.31.y_ref, bf16[1024,128]{1,0:T(8,128)(2,1)S(1)} %get-tuple-element.32.wp_ref, f32[64,128]{1,0:T(8,128)S(1)} %get-tuple-element.33.inv_ref), custom_call_target="tpu_custom_call" | custom-call | flops 1073741824 | bytes 12582912 | tf_op jit(solution)/shard_map/pair/pallas_call | solution.py:417
  76.8 2.0 %final_sums.1 = (f32[16,2048]{1,0:T(8,128)}, f32[16,2048]{1,0:T(8,128)}, f32[64,128]{1,0:T(8,128)}) custom-call(s32[256]{0:T(256)} %refs_0_.3, f32[1,2048]{1,0:T(1,128)} %copy-done.4, bf16[256,128]{1,0:T(8,128)(2,1)} %copy-done.1, bf16[256,128]{1,0:T(8,128)(2,1)} %copy-done.12, bf16[256,128]{1,0:T(8,128)(2,1)} %copy-done.13, bf16[256,128]{1,0:T(8,128)(2,1)} %copy-done.14, ...), custom_call_target="tpu_custom_call" | custom-call | tf_op jit(solution)/shard_map/final_sums/pallas_call | solution.py:433
  (69 shorter events, 5.2 us)
Async XLA Ops:
  0.6 10.3 %collective-permute-start.1 = (bf16[16,2048]{1,0:T(8,128)(2,1)}, bf16[16,2048]{1,0:T(8,128)(2,1)S(1)}, u32[]{:S(2)}, u32[]{:S(2)}) collective-permute-start(bf16[16,2048]{1,0:T(8,128)(2,1)} %refs_3_.1), channel_id=1, source_target_pairs={{0,2},{1,3},{2,0},{3,1},{4,6},{5,7},{6,4},{7,5},{8,10},{9,11},{10,... | collective-permute-start | bytes 196616 | tf_op jit(solution)/shard_map/ppermute | solution.py:291
  4.7 19.1 %collective-permute-start = (bf16[16,2048]{1,0:T(8,128)(2,1)}, bf16[16,2048]{1,0:T(8,128)(2,1)S(1)}, u32[]{:S(2)}, u32[]{:S(2)}) collective-permute-start(bf16[16,2048]{1,0:T(8,128)(2,1)} %refs_3_.1), channel_id=1, source_target_pairs={{0,1},{1,2},{2,3},{3,0},{4,5},{5,6},{6,7},{7,4},{8,9},{9,10},{10,1... | collective-permute-start | bytes 196616 | tf_op jit(solution)/shard_map/ppermute | solution.py:291
  6.3 17.6 %collective-permute-start.2 = (bf16[16,2048]{1,0:T(8,128)(2,1)}, bf16[16,2048]{1,0:T(8,128)(2,1)S(1)}, u32[]{:S(2)}, u32[]{:S(2)}) collective-permute-start(bf16[16,2048]{1,0:T(8,128)(2,1)} %refs_3_.1), channel_id=1, source_target_pairs={{0,3},{1,0},{2,1},{3,2},{4,7},{5,4},{6,5},{7,6},{8,11},{9,8},{10,9... | collective-permute-start | bytes 196616 | tf_op jit(solution)/shard_map/ppermute | solution.py:291
  8.6 15.3 %collective-permute-start.4 = (bf16[16,2048]{1,0:T(8,128)(2,1)}, bf16[16,2048]{1,0:T(8,128)(2,1)S(1)}, u32[]{:S(2)}, u32[]{:S(2)}) collective-permute-start(bf16[16,2048]{1,0:T(8,128)(2,1)} %refs_7_.1), channel_id=1, source_target_pairs={{0,8},{4,12},{8,0},{12,4},{1,9},{5,13},{9,1},{13,5},{2,10},{6,14},... | collective-permute-start | bytes 196616 | tf_op jit(solution)/shard_map/ppermute | solution.py:291
  10.0 13.8 %collective-permute-start.3 = (bf16[16,2048]{1,0:T(8,128)(2,1)}, bf16[16,2048]{1,0:T(8,128)(2,1)S(1)}, u32[]{:S(2)}, u32[]{:S(2)}) collective-permute-start(bf16[16,2048]{1,0:T(8,128)(2,1)} %refs_7_.1), channel_id=1, source_target_pairs={{0,4},{4,8},{8,12},{12,0},{1,5},{5,9},{9,13},{13,1},{2,6},{6,10},{... | collective-permute-start | bytes 196616 | tf_op jit(solution)/shard_map/ppermute | solution.py:291
  10.9 42.2 %copy-start.4 = (f32[1,2048]{1,0:T(1,128)}, f32[1,2048]{1,0:T(1,128)S(1)}, u32[]{:S(2)}) copy-start(f32[1,2048]{1,0:T(1,128)S(1)} %broadcast_in_dim_reshape.3.refs_1_) | copy-start | bytes 24580
  10.9 13.0 %collective-permute-start.5 = (bf16[16,2048]{1,0:T(8,128)(2,1)}, bf16[16,2048]{1,0:T(8,128)(2,1)S(1)}, u32[]{:S(2)}, u32[]{:S(2)}) collective-permute-start(bf16[16,2048]{1,0:T(8,128)(2,1)} %refs_7_.1), channel_id=1, source_target_pairs={{0,12},{4,0},{8,4},{12,8},{1,13},{5,1},{9,5},{13,9},{2,14},{6,2},{... | collective-permute-start | bytes 196616 | tf_op jit(solution)/shard_map/ppermute | solution.py:291
  38.3 29.5 %copy-start.6 = (s32[256]{0:T(256)S(1)}, s32[256]{0:T(256)}, u32[]{:S(2)}) copy-start(s32[256]{0:T(256)} %refs_0_.3) | copy-start | bytes 3076
  38.3 17.3 %collective-permute-start.12 = (bf16[256,128]{1,0:T(8,128)(2,1)S(1)}, bf16[256,128]{1,0:T(8,128)(2,1)S(1)}, u32[]{:S(2)}, u32[]{:S(2)}) collective-permute-start(bf16[256,128]{1,0:T(8,128)(2,1)S(1)} %get-tuple-element.46), channel_id=1, source_target_pairs={{0,4},{4,8},{8,12},{12,0},{1,5},{5,9},{9,13},{13,1},{2,6},{6,10},{... | collective-permute-start | bytes 196616 | tf_op jit(solution)/shard_map/ppermute | solution.py:291
  38.3 19.9 %collective-permute-start.13 = (bf16[256,128]{1,0:T(8,128)(2,1)S(1)}, bf16[256,128]{1,0:T(8,128)(2,1)S(1)}, u32[]{:S(2)}, u32[]{:S(2)}) collective-permute-start(bf16[256,128]{1,0:T(8,128)(2,1)S(1)} %get-tuple-element.47), channel_id=1, source_target_pairs={{0,8},{4,12},{8,0},{12,4},{1,9},{5,13},{9,1},{13,5},{2,10},{6,14},... | collective-permute-start | bytes 196616 | tf_op jit(solution)/shard_map/ppermute | solution.py:291
  38.8 19.4 %collective-permute-start.14 = (bf16[256,128]{1,0:T(8,128)(2,1)S(1)}, bf16[256,128]{1,0:T(8,128)(2,1)S(1)}, u32[]{:S(2)}, u32[]{:S(2)}) collective-permute-start(bf16[256,128]{1,0:T(8,128)(2,1)S(1)} %get-tuple-element.48), channel_id=1, source_target_pairs={{0,12},{4,0},{8,4},{12,8},{1,13},{5,1},{9,5},{13,9},{2,14},{6,2},{... | collective-permute-start | bytes 196616 | tf_op jit(solution)/shard_map/ppermute | solution.py:291
  54.3 7.1 %collective-permute-start.6 = (bf16[256,128]{1,0:T(8,128)(2,1)S(1)}, bf16[256,128]{1,0:T(8,128)(2,1)S(1)}, u32[]{:S(2)}, u32[]{:S(2)}) collective-permute-start(bf16[256,128]{1,0:T(8,128)(2,1)S(1)} %get-tuple-element.38), channel_id=1, source_target_pairs={{0,1},{1,2},{2,3},{3,0},{4,5},{5,6},{6,7},{7,4},{8,9},{9,10},{10,1... | collective-permute-start | bytes 196616 | tf_op jit(solution)/shard_map/ppermute | solution.py:291
  54.3 8.5 %collective-permute-start.7 = (bf16[256,128]{1,0:T(8,128)(2,1)S(1)}, bf16[256,128]{1,0:T(8,128)(2,1)S(1)}, u32[]{:S(2)}, u32[]{:S(2)}) collective-permute-start(bf16[256,128]{1,0:T(8,128)(2,1)S(1)} %get-tuple-element.39), channel_id=1, source_target_pairs={{0,2},{1,3},{2,0},{3,1},{4,6},{5,7},{6,4},{7,5},{8,10},{9,11},{10,... | collective-permute-start | bytes 196616 | tf_op jit(solution)/shard_map/ppermute | solution.py:291
  55.6 7.8 %collective-permute-start.8 = (bf16[256,128]{1,0:T(8,128)(2,1)S(1)}, bf16[256,128]{1,0:T(8,128)(2,1)S(1)}, u32[]{:S(2)}, u32[]{:S(2)}) collective-permute-start(bf16[256,128]{1,0:T(8,128)(2,1)S(1)} %get-tuple-element.40), channel_id=1, source_target_pairs={{0,3},{1,0},{2,1},{3,2},{4,7},{5,4},{6,5},{7,6},{8,11},{9,8},{10,9... | collective-permute-start | bytes 196616 | tf_op jit(solution)/shard_map/ppermute | solution.py:291
  58.2 6.8 %collective-permute-start.9 = (bf16[16,2048]{1,0:T(8,128)(2,1)S(1)}, bf16[16,2048]{1,0:T(8,128)(2,1)S(1)}, u32[]{:S(2)}, u32[]{:S(2)}) collective-permute-start(bf16[16,2048]{1,0:T(8,128)(2,1)S(1)} %get-tuple-element.42), channel_id=1, source_target_pairs={{0,4},{4,8},{8,12},{12,0},{1,5},{5,9},{9,13},{13,1},{2,6},{6,10},{... | collective-permute-start | bytes 196616 | tf_op jit(solution)/shard_map/ppermute | solution.py:291
  58.2 17.9 %collective-permute-start.10 = (bf16[16,2048]{1,0:T(8,128)(2,1)S(1)}, bf16[16,2048]{1,0:T(8,128)(2,1)S(1)}, u32[]{:S(2)}, u32[]{:S(2)}) collective-permute-start(bf16[16,2048]{1,0:T(8,128)(2,1)S(1)} %get-tuple-element.43), channel_id=1, source_target_pairs={{0,8},{4,12},{8,0},{12,4},{1,9},{5,13},{9,1},{13,5},{2,10},{6,14},... | collective-permute-start | bytes 196616 | tf_op jit(solution)/shard_map/ppermute | solution.py:291
  61.4 14.8 %copy-start.12 = (bf16[256,128]{1,0:T(8,128)(2,1)}, bf16[256,128]{1,0:T(8,128)(2,1)S(1)}, u32[]{:S(2)}) copy-start(bf16[256,128]{1,0:T(8,128)(2,1)S(1)} %collective-permute-done.6.refs_3_) | copy-start | bytes 196612
  61.4 14.7 %collective-permute-start.11 = (bf16[16,2048]{1,0:T(8,128)(2,1)S(1)}, bf16[16,2048]{1,0:T(8,128)(2,1)S(1)}, u32[]{:S(2)}, u32[]{:S(2)}) collective-permute-start(bf16[16,2048]{1,0:T(8,128)(2,1)S(1)} %get-tuple-element.44), channel_id=1, source_target_pairs={{0,12},{4,0},{8,4},{12,8},{1,13},{5,1},{9,5},{13,9},{2,14},{6,2},{... | collective-permute-start | bytes 196616 | tf_op jit(solution)/shard_map/ppermute | solution.py:291
  62.8 13.4 %copy-start.13 = (bf16[256,128]{1,0:T(8,128)(2,1)}, bf16[256,128]{1,0:T(8,128)(2,1)S(1)}, u32[]{:S(2)}) copy-start(bf16[256,128]{1,0:T(8,128)(2,1)S(1)} %collective-permute-done.7.refs_4_) | copy-start | bytes 196612
  62.8 13.3 %collective-permute-start.15 = (bf16[64,128]{1,0:T(8,128)(2,1)}, bf16[64,128]{1,0:T(8,128)(2,1)S(1)}, u32[]{:S(2)}, u32[]{:S(2)}) collective-permute-start(bf16[64,128]{1,0:T(8,128)(2,1)} %get-tuple-element.50), channel_id=1, source_target_pairs={{0,1},{1,2},{2,3},{3,0},{4,5},{5,6},{6,7},{7,4},{8,9},{9,10},{10,1... | collective-permute-start | bytes 49160 | tf_op jit(solution)/shard_map/ppermute | solution.py:291
  63.4 12.8 %copy-start.14 = (bf16[256,128]{1,0:T(8,128)(2,1)}, bf16[256,128]{1,0:T(8,128)(2,1)S(1)}, u32[]{:S(2)}) copy-start(bf16[256,128]{1,0:T(8,128)(2,1)S(1)} %collective-permute-done.8.refs_5_) | copy-start | bytes 196612
  63.4 12.7 %collective-permute-start.16 = (bf16[64,128]{1,0:T(8,128)(2,1)}, bf16[64,128]{1,0:T(8,128)(2,1)S(1)}, u32[]{:S(2)}, u32[]{:S(2)}) collective-permute-start(bf16[64,128]{1,0:T(8,128)(2,1)} %get-tuple-element.51), channel_id=1, source_target_pairs={{0,2},{1,3},{2,0},{3,1},{4,6},{5,7},{6,4},{7,5},{8,10},{9,11},{10,... | collective-permute-start | bytes 49160 | tf_op jit(solution)/shard_map/ppermute | solution.py:291
  65.0 11.2 %copy-start.15 = (bf16[16,2048]{1,0:T(8,128)(2,1)}, bf16[16,2048]{1,0:T(8,128)(2,1)S(1)}, u32[]{:S(2)}) copy-start(bf16[16,2048]{1,0:T(8,128)(2,1)S(1)} %collective-permute-done.9.refs_7_) | copy-start | bytes 196612
  65.0 11.1 %collective-permute-start.17 = (bf16[64,128]{1,0:T(8,128)(2,1)}, bf16[64,128]{1,0:T(8,128)(2,1)S(1)}, u32[]{:S(2)}, u32[]{:S(2)}) collective-permute-start(bf16[64,128]{1,0:T(8,128)(2,1)} %get-tuple-element.52), channel_id=1, source_target_pairs={{0,3},{1,0},{2,1},{3,2},{4,7},{5,4},{6,5},{7,6},{8,11},{9,8},{10,9... | collective-permute-start | bytes 49160 | tf_op jit(solution)/shard_map/ppermute | solution.py:291
  (18 other events, 19.8 us)

commit v2 on v1

v2 whole, which is shorter than its diff:
```python
import functools

import jax
import jax.numpy as jnp
from jax import lax
from jax.experimental import pallas as pl
from jax.experimental.pallas import tpu as pltpu
from jax.sharding import PartitionSpec as P

LANES = 128
VMEM_BYTES = 60 * 1024 * 1024
NT = (((1,), (1,)), ((), ()))
F32 = jnp.float32
BF16 = jnp.bfloat16


def params():
    return pltpu.CompilerParams(
        dimension_semantics=("arbitrary",), vmem_limit_bytes=VMEM_BYTES
    )


def cost(flops, nbytes):
    return pl.CostEstimate(flops=int(flops), bytes_accessed=int(nbytes), transcendentals=0)


def spread_rows(mask_ref, first, count, out_ref):
    def body(r, carry):
        value = mask_ref[first + r].astype(F32)
        out_ref[pl.ds(r, 1), :] = jnp.full((1, LANES), value, F32)
        return carry

    lax.fori_loop(0, count, body, 0, unroll=8)


def inner_kernel(dims, res_ref, seq_ref, cot_ref, w_ref, scaled_ref, z_ref, inv_ref, wp_ref, w32):
    chans, groups, blocks, i_rows, j_rows, step_rows, sequences = dims
    step = pl.program_id(0)

    @pl.when(step == 0)
    def _():
        w32[...] = w_ref[...].astype(F32)
        for e in range(chans):
            wp_ref[e * chans : (e + 1) * chans, :] = w32[
                pl.ds(e, chans, stride=chans), :
            ].astype(BF16)
        spread_rows(res_ref, lax.axis_index("col") * j_rows, j_rows, inv_ref)
        valid = lax.fori_loop(
            0, sequences, lambda s, total: total + seq_ref[s], jnp.int32(0), unroll=8
        ).astype(F32)
        inv_ref[...] = 1.0 / jnp.maximum(valid * inv_ref[...], 1.0)

    first = lax.axis_index("row") * i_rows + step * step_rows
    for i in range(step_rows):
        kept = res_ref[first + i] > 0
        inverse = jnp.where(kept, inv_ref[...], 1.0)
        scaled_ref[i] = (cot_ref[i].astype(F32) * inverse).astype(BF16)
    scaled = scaled_ref[...].reshape(step_rows * j_rows, LANES)
    part = lax.dot_general(scaled, wp_ref[...], NT, preferred_element_type=F32).astype(BF16)
    for a in range(blocks):
        for i in range(step_rows):
            z_ref[a * j_rows : (a + 1) * j_rows, i * LANES : (i + 1) * LANES] = part[
                i * j_rows : (i + 1) * j_rows, a * LANES : (a + 1) * LANES
            ]


def lane_group(shape, chans):
    return lax.broadcasted_iota(jnp.int32, shape, 1) // chans


def outer_kernel(dims, n_row, *refs):
    chans, groups, blocks, i_rows, j_rows, step_rows, sequences = dims
    tiles = sequences * chans // LANES
    depth = groups * sequences
    width = sequences * chans
    j_pad = -(-j_rows // LANES) * LANES
    res_ref, keep_ref, scaled_ref, z_ref, left_ref, right_ref = refs[:6]
    y_ref, rbt_ref, send_ref = refs[6:9]
    keep_rows, turned, lsplit, rbig, expand, diag, gwt, gwr, acc, gr_all = refs[9:]
    step = pl.program_id(0)
    row, col = lax.axis_index("row"), lax.axis_index("col")

    @pl.when(step == 0)
    def _():
        if j_rows < j_pad:
            keep_rows[j_rows:j_pad, :] = jnp.zeros((j_pad - j_rows, LANES), F32)
        spread_rows(res_ref, col * j_rows, j_rows, keep_rows)
        for t in range(tiles):
            lanes = slice(t * LANES, (t + 1) * LANES)
            masked = right_ref[:, lanes].astype(F32) * keep_rows[0:j_rows, :] * keep_ref[:, lanes]
            if j_rows < j_pad:
                masked = jnp.concatenate([masked, jnp.zeros((j_pad - j_rows, LANES), F32)], axis=0)
            turned[lanes, :] = masked.T
        for a in range(blocks):
            parts = [
                turned[pl.ds(lo * chans + groups * a + b, tiles, stride=LANES), :]
                for b in range(groups)
                for lo in range(groups)
            ]
            block = jnp.concatenate(parts, axis=0)
            rbig[a * j_rows : (a + 1) * j_rows, :] = block.T[:j_rows].astype(BF16)
        rbt_ref[...] = rbig[...].T
        spread_rows(res_ref, row * i_rows, i_rows, keep_rows)
        for t in range(tiles):
            lanes = slice(t * LANES, (t + 1) * LANES)
            masked = left_ref[:, lanes].astype(F32) * keep_rows[0:i_rows, :] * keep_ref[:, lanes]
            lsplit[pl.ds(t, i_rows, stride=tiles), :] = masked
        shape = (LANES, groups * LANES)
        source = lax.broadcasted_iota(jnp.int32, shape, 0)
        target = lax.broadcasted_iota(jnp.int32, shape, 1)
        same = (source // chans == target // LANES) & (source % chans == target % chans)
        expand[...] = same.astype(F32).astype(BF16)
        gwt[...] = jnp.zeros_like(gwt)
        acc[...] = jnp.zeros_like(acc)

    rows = step_rows * tiles
    spread = jnp.dot(
        lsplit[pl.ds(pl.multiple_of(step * rows, rows), rows), :].astype(BF16),
        expand[...],
        preferred_element_type=F32,
    ).astype(BF16)
    group = lane_group((tiles, LANES), chans)
    for b in range(groups):
        chosen = (group == b).astype(F32).astype(BF16)
        for lo in range(groups):
            at = b * sequences + lo * tiles
            for i in range(step_rows):
                diag[at : at + tiles, i * LANES : (i + 1) * LANES] = (
                    spread[i * tiles : (i + 1) * tiles, lo * LANES : (lo + 1) * LANES] * chosen
                )
    part = jnp.dot(rbig[...], diag[...], preferred_element_type=F32).astype(BF16)
    for i in range(step_rows):
        for a in range(blocks):
            y_ref[i, :, a * LANES : (a + 1) * LANES] = part[
                a * j_rows : (a + 1) * j_rows, i * LANES : (i + 1) * LANES
            ]
    acc[...] += lax.dot_general(diag[...], z_ref[...], NT, preferred_element_type=F32)
    pairs = step_rows * j_rows
    scaled_t = scaled_ref[...].reshape(pairs, LANES).T
    y_flat = y_ref[...].reshape(pairs, blocks * LANES)
    gwt[...] += jnp.dot(scaled_t, y_flat, preferred_element_type=F32)

    @pl.when(step == pl.num_programs(0) - 1)
    def _():
        for k in range(blocks):
            turned_tile = gwt[:, k * LANES : (k + 1) * LANES].T
            for q in range(groups):
                gwr[pl.ds(k * groups + q, chans, stride=chans), :] = turned_tile[
                    q * chans : (q + 1) * chans
                ]
        for a in range(blocks):
            at, shift = divmod(a * j_rows, LANES)
            mine = acc[:, at * LANES : at * LANES + j_pad]
            if shift:
                mine = pltpu.roll(mine, LANES - shift, axis=1)
            for b in range(groups):
                for lo in range(groups):
                    first = b * sequences + lo * tiles
                    turned[pl.ds(lo * chans + groups * a + b, tiles, stride=LANES), :] = mine[
                        first : first + tiles
                    ]
        for t in range(tiles):
            lanes = slice(t * LANES, (t + 1) * LANES)
            gr_all[pl.ds(t, j_rows, stride=tiles), :] = turned[lanes, :].T[:j_rows]
        right_owned = j_rows * tiles // n_row
        weight_owned = chans * chans // n_row
        for k in range(n_row):
            send_ref[k, :right_owned, :] = gr_all[
                k * right_owned : (k + 1) * right_owned, :
            ].astype(BF16)
            send_ref[k, right_owned:, :] = gwr[k * weight_owned : (k + 1) * weight_owned, :].astype(
                BF16
            )


def left_kernel(dims, n_row, n_col, *refs):
    chans, groups, blocks, i_rows, j_rows, step_rows, sequences = dims
    tiles = sequences * chans // LANES
    res_ref, keep_ref, z_ref, rbt_ref, came_ref = refs[:5]
    send_ref, gr_out, gl_all, whole, keep_rows = refs[5:]
    step = pl.program_id(0)

    group = lane_group((sequences, LANES), chans)
    group_t = lane_group((tiles, LANES), chans)
    part = jnp.dot(rbt_ref[...], z_ref[...], preferred_element_type=F32)
    for i in range(step_rows):
        mine = part[:, i * LANES : (i + 1) * LANES]
        total = mine[0:sequences]
        for b in range(1, groups):
            total = jnp.where(group == b, mine[b * sequences : (b + 1) * sequences], total)
        shift = LANES // 2
        while shift >= chans:
            total = total + pltpu.roll(total, shift, axis=1)
            shift //= 2
        merged = total[0:tiles]
        for lo in range(1, groups):
            merged = jnp.where(group_t == lo, total[lo * tiles : (lo + 1) * tiles], merged)
        at = (step * step_rows + i) * tiles
        gl_all[pl.ds(pl.multiple_of(at, tiles), tiles), :] = merged.astype(BF16)

    @pl.when(step == pl.num_programs(0) - 1)
    def _():
        row, col = lax.axis_index("row"), lax.axis_index("col")
        left_owned = i_rows * tiles // n_col
        right_owned = j_rows * tiles // n_row
        whole[...] = sum_of(came_ref, n_row)
        weight_owned = (whole.shape[0] - right_owned) // n_col
        for k in range(n_col):
            send_ref[k, :left_owned, :] = gl_all[k * left_owned : (k + 1) * left_owned, :]
            at = right_owned + k * weight_owned
            send_ref[k, left_owned:, :] = whole[at : at + weight_owned, :].astype(BF16)
        own = gr_out.shape[0]
        spread_rows(res_ref, (col * n_row + row) * own, own, keep_rows)
        write_rows(whole, keep_rows, keep_ref, gr_out, tiles)


def sum_of(came_ref, count):
    total = came_ref[0].astype(F32)
    for k in range(1, count):
        total = total + came_ref[k].astype(F32)
    return total


def write_rows(whole, keep_rows, keep_ref, out_ref, tiles):
    own = out_ref.shape[0]
    for t in range(tiles):
        lanes = slice(t * LANES, (t + 1) * LANES)
        out_ref[:, lanes] = whole[pl.ds(t, own, stride=tiles), :] * (
            keep_rows[...] * keep_ref[:, lanes]
        )


def pair_kernel(dims, n_row, n_col, *refs):
    chans, groups, blocks, i_rows, j_rows, step_rows, sequences = dims
    tiles = sequences * chans // LANES
    res_ref, keep_ref, y_ref, wp_ref, inv_ref, came_ref = refs[:6]
    out_ref, gl_out, gw_out, wpt, whole, keep_rows = refs[6:]
    step = pl.program_id(0)

    @pl.when(step == 0)
    def _():
        wpt[...] = wp_ref[...].T

    pairs = step_rows * j_rows
    projected = lax.dot_general(
        wpt[...], y_ref[...].reshape(pairs, blocks * LANES), NT, preferred_element_type=F32
    ).T
    first = lax.axis_index("row") * i_rows + step * step_rows
    for i in range(step_rows):
        kept = res_ref[first + i] > 0
        inverse = jnp.where(kept, inv_ref[...], 1.0)
        out_ref[i] = (projected[i * j_rows : (i + 1) * j_rows] * inverse).astype(BF16)

    @pl.when(step == pl.num_programs(0) - 1)
    def _():
        row, col = lax.axis_index("row"), lax.axis_index("col")
        own = gl_out.shape[0]
        whole[...] = sum_of(came_ref, n_col)
        gw_out[...] = whole[own * tiles :, :]
        spread_rows(res_ref, (row * n_col + col) * own, own, keep_rows)
        write_rows(whole, keep_rows, keep_ref, gl_out, tiles)


def exchange(array, axis):
    return lax.all_to_all(array, axis, split_axis=0, concat_axis=0, tiled=True)


def smem():
    return pl.BlockSpec(memory_space=pltpu.SMEM)


def whole_spec(shape):
    return pl.BlockSpec(shape, lambda *_: (0,) * len(shape))


def shards(left_act, right_act, row_mask, res_mask, out_weight, cotangent):
    n_col = lax.axis_size("col")
    n_row = lax.axis_size("row")
    i_rows, j_rows, pair_width = cotangent.shape
    sequences = row_mask.shape[0]
    width = left_act.shape[1]
    chans = width // sequences
    groups = LANES // chans
    blocks = chans // groups
    tiles = width // LANES
    depth = groups * sequences
    inner = chans * chans
    step_rows = 8
    steps = i_rows // step_rows
    dims = (chans, groups, blocks, i_rows, j_rows, step_rows, sequences)
    j_pad = -(-j_rows // LANES) * LANES
    pad = max(j_pad, i_rows)
    span = blocks * j_rows
    own_left, own_right = left_act.shape[0], right_act.shape[0]
    struct = jax.ShapeDtypeStruct
    macs = i_rows * j_rows * inner * pair_width

    left = exchange(jnp.tile(left_act, (n_col, 1)), "col")
    right = exchange(jnp.tile(right_act, (n_row, 1)), "row")
    keep = jnp.repeat(row_mask.astype(F32), chans)[None, :]

    pair_block = pl.BlockSpec((step_rows, j_rows, pair_width), lambda g: (g, 0, 0))
    z_block = pl.BlockSpec((span, step_rows * LANES), lambda g: (0, g))
    y_block = pl.BlockSpec((step_rows, j_rows, inner), lambda g: (g, 0, 0))

    scaled, z, inverse, weight = pl.pallas_call(
        functools.partial(inner_kernel, dims),
        grid=(steps,),
        in_specs=[smem(), smem(), pair_block, whole_spec(out_weight.shape)],
        out_specs=[
            pair_block,
            z_block,
            whole_spec((j_rows, LANES)),
            whole_spec(out_weight.shape),
        ],
        out_shape=[
            struct(cotangent.shape, BF16),
            struct((span, i_rows * LANES), BF16),
            struct((j_rows, LANES), F32),
            struct(out_weight.shape, BF16),
        ],
        scratch_shapes=[pltpu.VMEM(out_weight.shape, F32)],
        compiler_params=params(),
        cost_estimate=cost(2 * macs, 12 * 2**20),
        name="inner",
    )(res_mask, row_mask, cotangent, out_weight)

    row_piece = own_right * tiles + inner // n_row
    y, right_turned, row_send = pl.pallas_call(
        functools.partial(outer_kernel, dims, n_row),
        grid=(steps,),
        in_specs=[
            smem(),
            whole_spec((1, width)),
            pair_block,
            z_block,
            whole_spec((i_rows, width)),
            whole_spec((j_rows, width)),
        ],
        out_specs=[
            y_block,
            whole_spec((depth, span)),
            whole_spec((n_row, row_piece, LANES)),
        ],
        out_shape=[
            struct((i_rows, j_rows, inner), BF16),
            struct((depth, span), BF16),
            struct((n_row, row_piece, LANES), BF16),
        ],
        scratch_shapes=[
            pltpu.VMEM((pad, LANES), F32),
            pltpu.VMEM((width, j_pad), F32),
            pltpu.VMEM((i_rows * tiles, LANES), F32),
            pltpu.VMEM((span, depth), BF16),
            pltpu.VMEM((LANES, groups * LANES), BF16),
            pltpu.VMEM((depth, step_rows * LANES), BF16),
            pltpu.VMEM((pair_width, inner), F32),
            pltpu.VMEM((inner, pair_width), F32),
            pltpu.VMEM((depth, span), F32),
            pltpu.VMEM((j_rows * tiles, LANES), F32),
        ],
        compiler_params=params(),
        cost_estimate=cost(6 * macs, 16 * 2**20),
        name="outer",
    )(res_mask, keep, scaled, z, left, right)
    row_came = exchange(row_send, "row")

    col_piece = own_left * tiles + inner // n_row // n_col
    col_send, grad_right = pl.pallas_call(
        functools.partial(left_kernel, dims, n_row, n_col),
        grid=(steps,),
        in_specs=[
            smem(),
            whole_spec((1, width)),
            z_block,
            whole_spec((depth, span)),
            whole_spec((n_row, row_piece, LANES)),
        ],
        out_specs=[
            whole_spec((n_col, col_piece, LANES)),
            whole_spec((own_right, width)),
        ],
        out_shape=[
            struct((n_col, col_piece, LANES), BF16),
            struct((own_right, width), F32),
        ],
        scratch_shapes=[
            pltpu.VMEM((i_rows * tiles, LANES), BF16),
            pltpu.VMEM((row_piece, LANES), F32),
            pltpu.VMEM((own_right, LANES), F32),
        ],
        compiler_params=params(),
        cost_estimate=cost(2 * macs, 8 * 2**20),
        name="left",
    )(res_mask, keep, z, right_turned, row_came)
    col_came = exchange(col_send, "col")

    pair_out, grad_left, grad_weight = pl.pallas_call(
        functools.partial(pair_kernel, dims, n_row, n_col),
        grid=(steps,),
        in_specs=[
            smem(),
            whole_spec((1, width)),
            y_block,
            whole_spec(out_weight.shape),
            whole_spec((j_rows, LANES)),
            whole_spec((n_col, col_piece, LANES)),
        ],
        out_specs=[
            pair_block,
            whole_spec((own_left, width)),
            whole_spec((inner // n_row // n_col, pair_width)),
        ],
        out_shape=[
            struct(cotangent.shape, BF16),
            struct((own_left, width), F32),
            struct((inner // n_row // n_col, pair_width), F32),
        ],
        scratch_shapes=[
            pltpu.VMEM((pair_width, inner), BF16),
            pltpu.VMEM((col_piece, LANES), F32),
            pltpu.VMEM((own_left, LANES), F32),
        ],
        compiler_params=params(),
        cost_estimate=cost(2 * macs, 12 * 2**20),
        name="pair",
    )(res_mask, keep, y, weight, inverse, col_came)
    return (pair_out, grad_left, grad_right, grad_weight)


def solution(mesh):
    placed = (
        P(("grp", "row", "col"), None),
        P(("grp", "col", "row"), None),
        P("grp"),
        P("grp"),
        P(),
        P(("grp", "row"), "col", None),
    )
    return jax.shard_map(
        shards,
        mesh=mesh,
        in_specs=placed,
        out_specs=(
            P(("grp", "row"), "col", None),
            P(("grp", "row", "col"), None),
            P(("grp", "col", "row"), None),
            P(("grp", "row", "col"), None),
        ),
        check_vma=False,
    )
```

time: 79.5 us -> 94.2 us (1.18)
  blocking collectives: 0 us -> 38.3 us
  starting transfers between devices: 25 us -> 5.27 us
  local copies, waits for them, and re-layouts: 10 us -> 3.86 us
  Pallas kernels: 42.2 us -> 44.2 us
    all_to_all x0 -> x3, blocking collectives: none -> 38.3 us  [exchange(): return lax.all_to_all(array, axis, split_axis=0, concat_axis=0, tiled=True)]
    ppermute x18 -> x0, starting transfers between devices: 25 us -> none  [exchange(): lax.ppermute(pieces[k], axis, [(s, (s + k) % n) for s in range(n)])]
    unnamed x48 -> x2, local copies, waits for them, and re-layouts: 9.86 us -> 0.69 us
    all_to_all x0 -> x1, starting transfers between devices: none -> 5.27 us  [exchange(): return lax.all_to_all(array, axis, split_axis=0, concat_axis=0, tiled=True)]
    another operation x0 -> x2, local copies, waits for them, and re-layouts: none -> 2.41 us  [the longest x1 1.55 us: shards(): left = exchange(jnp.tile(left_act, (n_col, 1)), 'col')]
    pallas_call x1, Pallas kernels: 7.66 us -> 8.78 us  [shards(): pl.pallas_call(functools.partial(inner_kernel, dims), grid=(steps,), in_s...]
    pallas_call x5 -> x3, Pallas kernels: 34.5 us -> 35.4 us  [the longest x1 16.6 us: shards(): pl.pallas_call(functools.partial(outer_kernel, dims, n_row), grid=(steps,...]
  transfers between devices with their start and end apart: 18 -> 1, of which waited for: 0 -> 0; matrix products, arithmetic and copies ran while one was open for 1% -> 2% of each run, Pallas kernels for 36% -> 9%
where the time goes in v2:
time: 94.2 us; the launch traced here: 93 us
  Pallas kernels  44.2 us (47%)
  blocking collectives  38.3 us (41%)
  starting transfers between devices  5.27 us (6%)
  local copies, waits for them, and re-layouts  3.86 us (4%)
    all_to_all x3, blocking collectives, exchange(): return lax.all_to_all(array, axis, split_axis=0, concat_axis=0, tiled=True)  38.3 us
    pallas_call x1, Pallas kernels, shards(): pl.pallas_call(functools.partial(outer_kernel, dims, n_row), grid=(steps,...  16.6 us
    pallas_call x1, Pallas kernels, shards(): pl.pallas_call(functools.partial(pair_kernel, dims, n_row, n_col), grid=(...  9.47 us
    pallas_call x1, Pallas kernels, shards(): pl.pallas_call(functools.partial(left_kernel, dims, n_row, n_col), grid=(...  9.37 us
    pallas_call x1, Pallas kernels, shards(): pl.pallas_call(functools.partial(inner_kernel, dims), grid=(steps,), in_s...  8.78 us
    all_to_all x1, starting transfers between devices, exchange(): return lax.all_to_all(array, axis, split_axis=0, concat_axis=0, tiled=True)  5.27 us
  transfers between devices with their start and end apart: 1, of which 0 were waited for; matrix products, arithmetic and copies ran while one was open for 2% of the time, Pallas kernels for 9%

profile of v2, /device:TPU:0, one launch (start us, length us, event | category | flops | bytes accessed | tf_op | source)
XLA Modules:
  0.0 93.0 jit_solution(8417557342226594844)
XLA Ops:
  0.6 0.9 tile.5
  1.5 10.2 %all_to_all.26 = bf16[4,16,2048]{2,1,0:T(8,128)(2,1)} all-to-all(bf16[4,16,2048]{2,1,0:T(8,128)(2,1)S(1)} %tile.5), channel_id=1, replica_groups=mesh['grp'=2,'row'=4,'col'=4] {'row'}, dimensions={0} | all-to-all | bytes 524288 | tf_op jit(solution)/shard_map/all_to_all | solution.py:265
  11.6 1.6 %tile.4 = bf16[4,16,2048]{2,1,0:T(8,128)(2,1)} broadcast(bf16[16,2048]{1,0:T(8,128)(2,1)} %param.6), dimensions={1,2} | broadcast | bytes 327680 | tf_op jit(solution)/shard_map/tile | solution.py:298
  13.2 5.3 %all-to-all-start = ((bf16[4,16,2048]{2,1,0:T(8,128)(2,1)}), bf16[4,16,2048]{2,1,0:T(8,128)(2,1)S(1)}, u32[]{:S(2)}, u32[]{:S(2)}) async-start(bf16[4,16,2048]{2,1,0:T(8,128)(2,1)} %tile.4), calls=%async_computation | async-start | bytes 524288 | tf_op jit(solution)/shard_map/all_to_all | solution.py:265
  18.5 0.7 convert_element_type.3
  19.1 0.1 broadcast_in_dim.3
  19.2 0.7 broadcast_in_dim_reshape.3.refs_1_
  19.9 8.8 %inner.1 = (bf16[64,64,128]{2,1,0:T(8,128)(2,1)}, bf16[512,8192]{1,0:T(8,128)(2,1)}, f32[64,128]{1,0:T(8,128)}, bf16[1024,128]{1,0:T(8,128)(2,1)}) custom-call(s32[256]{0:T(256)} %refs_0_.5, s32[64]{0:T(128)} %seq_ref.1, bf16[64,64,128]{2,1,0:T(8,128)(2,1)} %cot_ref.1, bf16[1024,128]{1,0:T(8,128)(2,1)} %w_ref.1), custom_call_target="tpu_custom_call" | custom-call | flops 1073741824 | bytes 12582912 | tf_op jit(solution)/shard_map/inner/pallas_call | solution.py:306
  28.7 0.0 all-to-all-done
  28.7 0.0 copy-start
  28.7 0.7 copy-done
  29.4 16.6 %outer.1 = (bf16[64,64,1024]{2,1,0:T(8,128)(2,1)}, bf16[256,512]{1,0:T(8,128)(2,1)}, bf16[4,512,128]{2,1,0:T(8,128)(2,1)}) custom-call(s32[256]{0:T(256)} %refs_0_.5, f32[1,2048]{1,0:T(1,128)} %broadcast_in_dim_reshape.3.refs_1_, bf16[64,64,128]{2,1,0:T(8,128)(2,1)} %get-tuple-element.16.refs_2_, bf16[512,8192]{1,0:T(8,128)(2,1)} %get-tuple-element.17.refs_3_.refs_2_, ...), custom_call_target="tpu_custom_call" | custom-call | flops 3221225472 | bytes 16777216 | tf_op jit(solution)/shard_map/outer/pallas_call | solution.py:329
  46.0 13.0 %all_to_all.27.refs_4_ = bf16[4,512,128]{2,1,0:T(8,128)(2,1)} all-to-all(bf16[4,512,128]{2,1,0:T(8,128)(2,1)} %get-tuple-element.22), channel_id=1, replica_groups=mesh['grp'=2,'row'=4,'col'=4] {'row'}, dimensions={0} | all-to-all | bytes 1048576 | tf_op jit(solution)/shard_map/all_to_all | solution.py:265
  59.0 9.4 %left.1 = (bf16[4,320,128]{2,1,0:T(8,128)(2,1)}, f32[16,2048]{1,0:T(8,128)}) custom-call(s32[256]{0:T(256)} %refs_0_.5, f32[1,2048]{1,0:T(1,128)} %broadcast_in_dim_reshape.3.refs_1_, bf16[512,8192]{1,0:T(8,128)(2,1)} %get-tuple-element.17.refs_3_.refs_2_, bf16[256,512]{1,0:T(8,128)(2,1)} %get-tuple-element.21.refs_3_, bf16[4,512,128]{2,1,0:T(8,128)(2,1)} %all_to_all.27.refs_4_), custom_call_target="tpu_custom_call" | custom-call | flops 1073741824 | bytes 8388608 | tf_op jit(solution)/shard_map/left/pallas_call | solution.py:369
  68.4 15.1 %all_to_all.28.refs_5_ = bf16[4,320,128]{2,1,0:T(8,128)(2,1)} all-to-all(bf16[4,320,128]{2,1,0:T(8,128)(2,1)} %get-tuple-element.23), channel_id=1, replica_groups=mesh['grp'=2,'row'=4,'col'=4] {'col'}, dimensions={0} | all-to-all | bytes 655360 | tf_op jit(solution)/shard_map/all_to_all | solution.py:265
  83.5 9.5 %pair.1 = (bf16[64,64,128]{2,1,0:T(8,128)(2,1)}, f32[16,2048]{1,0:T(8,128)}, f32[64,128]{1,0:T(8,128)}) custom-call(s32[256]{0:T(256)} %refs_0_.5, f32[1,2048]{1,0:T(1,128)} %broadcast_in_dim_reshape.3.refs_1_, bf16[64,64,1024]{2,1,0:T(8,128)(2,1)} %get-tuple-element.18.refs_2_, bf16[1024,128]{1,0:T(8,128)(2,1)} %get-tuple-element.19.refs_3_, ...), custom_call_target="tpu_custom_call" | custom-call | flops 1073741824 | bytes 12582912 | tf_op jit(solution)/shard_map/pair/pallas_call | solution.py:398
Async XLA Ops:
  13.2 15.5 %all-to-all-start = ((bf16[4,16,2048]{2,1,0:T(8,128)(2,1)}), bf16[4,16,2048]{2,1,0:T(8,128)(2,1)S(1)}, u32[]{:S(2)}, u32[]{:S(2)}) async-start(bf16[4,16,2048]{2,1,0:T(8,128)(2,1)} %tile.4), calls=%async_computation | async-start | bytes 524288 | tf_op jit(solution)/shard_map/all_to_all | solution.py:265
  28.7 0.7 copy-start

commit v3 on v0

v3 whole, which is shorter than its diff:
```python
import functools

import jax
import jax.numpy as jnp
from jax import lax
from jax.experimental import pallas as pl
from jax.experimental.pallas import tpu as pltpu
from jax.sharding import PartitionSpec as P

LANES = 128
NT = (((1,), (1,)), ((), ()))
F32 = jnp.float32
BF16 = jnp.bfloat16


def params(mib):
    return pltpu.CompilerParams(vmem_limit_bytes=mib * 2**20)


def cost(flops, nbytes):
    return pl.CostEstimate(flops=int(flops), bytes_accessed=int(nbytes), transcendentals=0)


def spread_rows(mask_ref, first, count, out_ref):
    def body(r, carry):
        value = mask_ref[first + r].astype(F32)
        out_ref[pl.ds(r, 1), :] = jnp.full((1, LANES), value, F32)
        return carry

    lax.fori_loop(0, count, body, 0, unroll=8)


def lane_group(shape, chans):
    return lax.broadcasted_iota(jnp.int32, shape, 1) // chans


def inner_kernel(dims, *refs):
    chans, groups, blocks, i_rows, j_rows, step_rows, sequences = dims
    tiles = sequences * chans // LANES
    res_ref, seq_ref, cot_ref, w_hbm, left_hbm, right_hbm = refs[:6]
    scaled_ref, z_ref, inv_ref, wp_ref, keep_ref, ri_ref, rj_ref, left_ref, right_ref = refs[6:15]
    w_ref, w32, cot, sems, more_sems = refs[15:]
    steps = i_rows // step_rows

    def fetch(step):
        rows = pl.ds(step * step_rows, step_rows)
        return pltpu.make_async_copy(cot_ref.at[rows], cot.at[rows], sems.at[step])

    more = [
        pltpu.make_async_copy(w_hbm, w_ref, more_sems.at[0]),
        pltpu.make_async_copy(left_hbm, left_ref, more_sems.at[1]),
        pltpu.make_async_copy(right_hbm, right_ref, more_sems.at[2]),
    ]
    more[0].start()
    for step in range(steps):
        fetch(step).start()
    more[1].start()
    more[2].start()
    spread_rows(res_ref, lax.axis_index("row") * i_rows, i_rows, ri_ref)
    spread_rows(res_ref, lax.axis_index("col") * j_rows, j_rows, rj_ref)
    group = lane_group((1, LANES), chans)
    valid = jnp.int32(0)
    for t in range(tiles):
        kept = jnp.zeros((1, LANES), F32)
        for lo in range(groups):
            value = seq_ref[t * groups + lo]
            valid = valid + value
            kept = jnp.where(group == lo, value.astype(F32), kept)
        keep_ref[:, t * LANES : (t + 1) * LANES] = kept
    inv_ref[...] = 1.0 / jnp.maximum(valid.astype(F32) * rj_ref[...], 1.0)
    more[0].wait()
    w32[...] = w_ref[...].astype(F32)
    for e in range(chans):
        wp_ref[e * chans : (e + 1) * chans, :] = w32[pl.ds(e, chans, stride=chans), :].astype(BF16)

    def body(step, carry):
        fetch(step).wait()
        for i in range(step_rows):
            at = step * step_rows + i
            inverse = jnp.where(ri_ref[pl.ds(at, 1), :] > 0, inv_ref[...], 1.0)
            scaled_ref[at] = (cot[at].astype(F32) * inverse).astype(BF16)
        scaled = scaled_ref[pl.ds(step * step_rows, step_rows)].reshape(step_rows * j_rows, LANES)
        for pair in range(0, blocks, 2):
            part = lax.dot_general(
                scaled,
                wp_ref[pair * LANES : (pair + 2) * LANES, :],
                NT,
                preferred_element_type=F32,
            ).astype(BF16)
            for k in range(2):
                a = pair + k
                for i in range(step_rows):
                    z_ref[
                        step, a * j_rows : (a + 1) * j_rows, i * LANES : (i + 1) * LANES
                    ] = part[i * j_rows : (i + 1) * j_rows, k * LANES : (k + 1) * LANES]
        return carry

    lax.fori_loop(0, steps, body, 0)
    more[1].wait()
    more[2].wait()


def outer_kernel(dims, n_row, n_col, *refs):
    chans, groups, blocks, i_rows, j_rows, step_rows, sequences = dims
    tiles = sequences * chans // LANES
    width = sequences * chans
    j_pad = -(-j_rows // LANES) * LANES
    ri_ref, rj_ref, keep_ref, scaled_ref, z_ref = refs[:5]
    left_refs = refs[5 : 5 + n_col]
    right_refs = refs[5 + n_col : 5 + n_col + n_row]
    y_ref, rbt_ref = refs[5 + n_col + n_row : 7 + n_col + n_row]
    send_refs = refs[7 + n_col + n_row : 7 + n_col + 2 * n_row]
    flat, turned, lsplit, rbig, expand, diag, gwt, gwr, acc, gr_all = refs[
        7 + n_col + 2 * n_row :
    ]
    row, col = lax.axis_index("row"), lax.axis_index("col")

    piece = right_refs[0].shape[0]
    for k in range(n_row):
        owner = lax.rem(row - k + n_row, n_row)
        flat[pl.ds(pl.multiple_of(owner * piece, 8), piece), :] = right_refs[k][...].astype(F32)
    for t in range(tiles):
        lanes = slice(t * LANES, (t + 1) * LANES)
        masked = flat[0:j_rows, lanes] * rj_ref[...] * keep_ref[:, lanes]
        if j_rows < j_pad:
            masked = jnp.concatenate([masked, jnp.zeros((j_pad - j_rows, LANES), F32)], axis=0)
        turned[lanes, :] = masked.T
    for a in range(blocks):
        parts = [
            turned[pl.ds(lo * chans + groups * a + b, tiles, stride=LANES), :]
            for b in range(groups)
            for lo in range(groups)
        ]
        block = jnp.concatenate(parts, axis=0)
        rbig[a * j_rows : (a + 1) * j_rows, :] = block.T[:j_rows].astype(BF16)
    rbt_ref[...] = rbig[...].T
    piece = left_refs[0].shape[0]
    for k in range(n_col):
        owner = lax.rem(col - k + n_col, n_col)
        flat[pl.ds(pl.multiple_of(owner * piece, 8), piece), :] = left_refs[k][...].astype(F32)
    for t in range(tiles):
        lanes = slice(t * LANES, (t + 1) * LANES)
        masked = flat[0:i_rows, lanes] * ri_ref[...] * keep_ref[:, lanes]
        lsplit[pl.ds(t, i_rows, stride=tiles), :] = masked
    shape = (LANES, groups * LANES)
    source = lax.broadcasted_iota(jnp.int32, shape, 0)
    target = lax.broadcasted_iota(jnp.int32, shape, 1)
    same = (source // chans == target // LANES) & (source % chans == target % chans)
    expand[...] = same.astype(F32).astype(BF16)
    gwt[...] = jnp.zeros_like(gwt)
    acc[...] = jnp.zeros_like(acc)
    rows = step_rows * tiles
    pairs = step_rows * j_rows
    group = lane_group((tiles, LANES), chans)

    def body(step, carry):
        spread = jnp.dot(
            lsplit[pl.ds(pl.multiple_of(step * rows, rows), rows), :].astype(BF16),
            expand[...],
            preferred_element_type=F32,
        ).astype(BF16)
        for b in range(groups):
            chosen = (group == b).astype(F32).astype(BF16)
            for lo in range(groups):
                at = b * sequences + lo * tiles
                for i in range(step_rows):
                    diag[at : at + tiles, i * LANES : (i + 1) * LANES] = (
                        spread[i * tiles : (i + 1) * tiles, lo * LANES : (lo + 1) * LANES] * chosen
                    )
        for pair in range(0, step_rows, 2):
            part = jnp.dot(
                rbig[...], diag[:, pair * LANES : (pair + 2) * LANES], preferred_element_type=F32
            ).astype(BF16)
            for k in range(2):
                for a in range(blocks):
                    y_ref[step * step_rows + pair + k, :, a * LANES : (a + 1) * LANES] = part[
                        a * j_rows : (a + 1) * j_rows, k * LANES : (k + 1) * LANES
                    ]
        acc[...] += lax.dot_general(diag[...], z_ref[step], NT, preferred_element_type=F32)
        block = pl.ds(step * step_rows, step_rows)
        scaled_t = scaled_ref[block].reshape(pairs, LANES).T
        y_flat = y_ref[block].reshape(pairs, blocks * LANES)
        gwt[...] += jnp.dot(scaled_t, y_flat, preferred_element_type=F32)
        return carry

    lax.fori_loop(0, i_rows // step_rows, body, 0)
    for k in range(blocks):
        turned_tile = gwt[:, k * LANES : (k + 1) * LANES].T
        for q in range(groups):
            gwr[pl.ds(k * groups + q, chans, stride=chans), :] = turned_tile[
                q * chans : (q + 1) * chans
            ]
    for a in range(blocks):
        at, shift = divmod(a * j_rows, LANES)
        mine = acc[:, at * LANES : at * LANES + j_pad]
        if shift:
            mine = pltpu.roll(mine, LANES - shift, axis=1)
        for b in range(groups):
            for lo in range(groups):
                first = b * sequences + lo * tiles
                turned[pl.ds(lo * chans + groups * a + b, tiles, stride=LANES), :] = mine[
                    first : first + tiles
                ]
    for t in range(tiles):
        lanes = slice(t * LANES, (t + 1) * LANES)
        gr_all[pl.ds(t, j_rows, stride=tiles), :] = turned[lanes, :].T[:j_rows]
    right_owned = j_rows * tiles // n_row
    weight_owned = chans * chans // n_row
    for k in range(n_row):
        owner = lax.rem(row + k, n_row)
        at = pl.multiple_of(owner * right_owned, right_owned)
        send_refs[k][:right_owned, :] = gr_all[pl.ds(at, right_owned), :].astype(BF16)
        at = pl.multiple_of(owner * weight_owned, weight_owned)
        send_refs[k][right_owned:, :] = gwr[pl.ds(at, weight_owned), :].astype(BF16)


def left_kernel(dims, z_ref, rbt_ref, gl_all):
    chans, groups, blocks, i_rows, j_rows, step_rows, sequences = dims
    tiles = sequences * chans // LANES
    group = lane_group((sequences, LANES), chans)
    group_t = lane_group((tiles, LANES), chans)

    def body(step, carry):
        for pair in range(0, step_rows, 2):
            part = jnp.dot(
                rbt_ref[...],
                z_ref[step, :, pair * LANES : (pair + 2) * LANES],
                preferred_element_type=F32,
            )
            for k in range(2):
                mine = part[:, k * LANES : (k + 1) * LANES]
                total = mine[0:sequences]
                for b in range(1, groups):
                    total = jnp.where(group == b, mine[b * sequences : (b + 1) * sequences], total)
                shift = LANES // 2
                while shift >= chans:
                    total = total + pltpu.roll(total, shift, axis=1)
                    shift //= 2
                merged = total[0:tiles]
                for lo in range(1, groups):
                    merged = jnp.where(group_t == lo, total[lo * tiles : (lo + 1) * tiles], merged)
                at = (step * step_rows + pair + k) * tiles
                gl_all[pl.ds(pl.multiple_of(at, tiles), tiles), :] = merged.astype(BF16)
        return carry

    lax.fori_loop(0, i_rows // step_rows, body, 0)


def sum_of(refs):
    total = refs[0][...].astype(F32)
    for ref in refs[1:]:
        total = total + ref[...].astype(F32)
    return total


def write_rows(whole, rows, keep_ref, out_ref, tiles):
    own = out_ref.shape[0]
    for t in range(tiles):
        lanes = slice(t * LANES, (t + 1) * LANES)
        out_ref[:, lanes] = whole[pl.ds(t, own, stride=tiles), :] * (
            rows * keep_ref[:, lanes]
        )


def middle_kernel(dims, n_row, n_col, *refs):
    chans, groups, blocks, i_rows, j_rows, step_rows, sequences = dims
    tiles = sequences * chans // LANES
    rj_ref, keep_ref, gl_ref = refs[:3]
    came = refs[3 : 3 + n_row]
    gr_out = refs[3 + n_row]
    send_refs = refs[4 + n_row : 4 + n_row + n_col]
    whole = refs[4 + n_row + n_col]
    row, col = lax.axis_index("row"), lax.axis_index("col")
    whole[...] = sum_of(came)
    left_owned = i_rows * tiles // n_col
    right_owned = j_rows * tiles // n_row
    weight_owned = (whole.shape[0] - right_owned) // n_col
    for k in range(n_col):
        owner = lax.rem(col + k, n_col)
        at = pl.multiple_of(owner * left_owned, left_owned)
        send_refs[k][:left_owned, :] = gl_ref[pl.ds(at, left_owned), :]
        at = pl.multiple_of(right_owned + owner * weight_owned, 8)
        send_refs[k][left_owned:, :] = whole[pl.ds(at, weight_owned), :].astype(BF16)
    own = gr_out.shape[0]
    rows = rj_ref[pl.ds(pl.multiple_of(row * own, 8), own), :]
    write_rows(whole, rows, keep_ref, gr_out, tiles)


def pair_kernel(dims, ri_ref, y_ref, wp_ref, inv_ref, out_ref, staged, sems):
    chans, groups, blocks, i_rows, j_rows, step_rows, sequences = dims
    pairs = step_rows * j_rows
    steps = i_rows // step_rows

    def store(step):
        rows = pl.ds(step * step_rows, step_rows)
        return pltpu.make_async_copy(staged.at[rows], out_ref.at[rows], sems.at[step])

    def body(step, carry):
        y_flat = y_ref[pl.ds(step * step_rows, step_rows)].reshape(pairs, blocks * LANES)
        projected = jnp.dot(y_flat, wp_ref[...], preferred_element_type=F32)
        for i in range(step_rows):
            at = step * step_rows + i
            inverse = jnp.where(ri_ref[pl.ds(at, 1), :] > 0, inv_ref[...], 1.0)
            staged[at] = (projected[i * j_rows : (i + 1) * j_rows] * inverse).astype(BF16)
        store(step).start()
        return carry

    lax.fori_loop(0, steps, body, 0)
    for step in range(steps):
        store(step).wait()


def final_kernel(dims, n_row, n_col, *refs):
    chans, groups, blocks, i_rows, j_rows, step_rows, sequences = dims
    tiles = sequences * chans // LANES
    ri_ref, keep_ref = refs[:2]
    came = refs[2 : 2 + n_col]
    gl_out, gw_out, whole = refs[2 + n_col :]
    own = gl_out.shape[0]
    whole[...] = sum_of(came)
    gw_out[...] = whole[own * tiles :, :]
    first = pl.multiple_of(lax.axis_index("col") * own, 8)
    write_rows(whole, ri_ref[pl.ds(first, own), :], keep_ref, gl_out, tiles)


def exchange(pieces, axis):
    n = len(pieces)
    came = [pieces[0]]
    for k in range(1, n):
        came.append(lax.ppermute(pieces[k], axis, [(s, (s + k) % n) for s in range(n)]))
    return came


def smem():
    return pl.BlockSpec(memory_space=pltpu.SMEM)


def vmem(count=1):
    return [pl.BlockSpec(memory_space=pltpu.VMEM)] * count


def hbm():
    return pl.BlockSpec(memory_space=pl.ANY)


def in_hbm(array):
    return pltpu.with_memory_space_constraint(array, pltpu.HBM)


def shards(left_act, right_act, row_mask, res_mask, out_weight, cotangent):
    n_col = lax.axis_size("col")
    n_row = lax.axis_size("row")
    i_rows, j_rows, pair_width = cotangent.shape
    sequences = row_mask.shape[0]
    width = left_act.shape[1]
    chans = width // sequences
    groups = LANES // chans
    blocks = chans // groups
    tiles = width // LANES
    depth = groups * sequences
    inner = chans * chans
    step_rows = 8
    steps = i_rows // step_rows
    dims = (chans, groups, blocks, i_rows, j_rows, step_rows, sequences)
    j_pad = -(-j_rows // LANES) * LANES
    span = blocks * j_rows
    own_left, own_right = left_act.shape[0], right_act.shape[0]
    macs = i_rows * j_rows * inner * pair_width

    lefts = exchange([left_act] * n_col, "col")
    rights = exchange([right_act] * n_row, "row")

    scaled, z, inverse, weight, keep, i_keep, j_keep, lefts[0], rights[0] = pl.pallas_call(
        functools.partial(inner_kernel, dims),
        in_specs=[smem(), smem()] + [hbm()] * 4,
        out_specs=vmem(9),
        out_shape=[
            pltpu.VMEM(cotangent.shape, BF16),
            pltpu.VMEM((steps, span, step_rows * LANES), BF16),
            pltpu.VMEM((j_rows, LANES), F32),
            pltpu.VMEM(out_weight.shape, BF16),
            pltpu.VMEM((1, width), F32),
            pltpu.VMEM((i_rows, LANES), F32),
            pltpu.VMEM((j_rows, LANES), F32),
            pltpu.VMEM(left_act.shape, BF16),
            pltpu.VMEM(right_act.shape, BF16),
        ],
        scratch_shapes=[
            pltpu.VMEM(out_weight.shape, BF16),
            pltpu.VMEM(out_weight.shape, F32),
            pltpu.VMEM(cotangent.shape, BF16),
            pltpu.SemaphoreType.DMA((steps,)),
            pltpu.SemaphoreType.DMA((3,)),
        ],
        compiler_params=params(16),
        cost_estimate=cost(2 * macs, 12 * 2**20),
        name="inner",
    )(*map(in_hbm, (res_mask, row_mask, cotangent, out_weight, left_act, right_act)))

    row_piece = own_right * tiles + inner // n_row
    outs = pl.pallas_call(
        functools.partial(outer_kernel, dims, n_row, n_col),
        in_specs=vmem(5 + n_col + n_row),
        out_specs=vmem(2 + n_row),
        out_shape=[
            pltpu.VMEM((i_rows, j_rows, inner), BF16),
            pltpu.VMEM((depth, span), BF16),
        ]
        + [pltpu.VMEM((row_piece, LANES), BF16)] * n_row,
        scratch_shapes=[
            pltpu.VMEM((max(i_rows, j_rows), width), F32),
            pltpu.VMEM((width, j_pad), F32),
            pltpu.VMEM((i_rows * tiles, LANES), F32),
            pltpu.VMEM((span, depth), BF16),
            pltpu.VMEM((LANES, groups * LANES), BF16),
            pltpu.VMEM((depth, step_rows * LANES), BF16),
            pltpu.VMEM((pair_width, inner), F32),
            pltpu.VMEM((inner, pair_width), F32),
            pltpu.VMEM((depth, span), F32),
            pltpu.VMEM((j_rows * tiles, LANES), F32),
        ],
        compiler_params=params(24),
        cost_estimate=cost(6 * macs, 16 * 2**20),
        name="outer",
    )(i_keep, j_keep, keep, scaled, z, *lefts, *rights)
    y, right_turned = outs[:2]
    row_came = exchange(outs[2:], "row")

    left_all = pl.pallas_call(
        functools.partial(left_kernel, dims),
        in_specs=vmem(2),
        out_specs=vmem()[0],
        out_shape=pltpu.VMEM((i_rows * tiles, LANES), BF16),
        compiler_params=params(8),
        cost_estimate=cost(2 * macs, 8 * 2**20),
        name="left",
    )(z, right_turned)

    col_piece = own_left * tiles + inner // n_row // n_col
    outs = pl.pallas_call(
        functools.partial(middle_kernel, dims, n_row, n_col),
        in_specs=vmem(3 + n_row),
        out_specs=vmem(1 + n_col),
        out_shape=[jax.ShapeDtypeStruct((own_right, width), F32)]
        + [pltpu.VMEM((col_piece, LANES), BF16)] * n_col,
        scratch_shapes=[
            pltpu.VMEM((row_piece, LANES), F32),
        ],
        compiler_params=params(4),
        cost_estimate=cost(0, 2**20),
        name="middle",
    )(j_keep, keep, left_all, *row_came)
    grad_right = outs[0]
    col_came = exchange(outs[1:], "col")

    pair_out = pl.pallas_call(
        functools.partial(pair_kernel, dims),
        in_specs=vmem(4),
        out_specs=hbm(),
        out_shape=jax.ShapeDtypeStruct(cotangent.shape, BF16),
        scratch_shapes=[
            pltpu.VMEM(cotangent.shape, BF16),
            pltpu.SemaphoreType.DMA((steps,)),
        ],
        compiler_params=params(16),
        cost_estimate=cost(2 * macs, 12 * 2**20),
        name="pair",
    )(i_keep, y, weight, inverse)

    grad_left, grad_weight = pl.pallas_call(
        functools.partial(final_kernel, dims, n_row, n_col),
        in_specs=vmem(2 + n_col),
        out_specs=vmem(2),
        out_shape=[
            jax.ShapeDtypeStruct((own_left, width), F32),
            jax.ShapeDtypeStruct((inner // n_row // n_col, pair_width), F32),
        ],
        scratch_shapes=[
            pltpu.VMEM((col_piece, LANES), F32),
        ],
        compiler_params=params(4),
        cost_estimate=cost(0, 2**20),
        name="final_sums",
    )(i_keep, keep, *col_came)
    return (pair_out, grad_left, grad_right, grad_weight)


def solution(mesh):
    placed = (
        P(("grp", "row", "col"), None),
        P(("grp", "col", "row"), None),
        P("grp"),
        P("grp"),
        P(),
        P(("grp", "row"), "col", None),
    )
    return jax.shard_map(
        shards,
        mesh=mesh,
        in_specs=placed,
        out_specs=(
            P(("grp", "row"), "col", None),
            P(("grp", "row", "col"), None),
            P(("grp", "col", "row"), None),
            P(("grp", "row", "col"), None),
        ),
        check_vma=False,
    )
```

time: 332 us -> 47.7 us (0.14)
  local copies, waits for them, and re-layouts: 123 us -> 0 us
  waiting for transfers between devices: 98 us -> 1.51 us
  matrix products: 66.1 us -> 0 us
  Pallas kernels: 0 us -> 29 us
  blocking collectives: 21.8 us -> 0 us
  starting transfers between devices: 0.12 us -> 16.3 us
  between operations: 13.9 us -> 0.75 us
  other arithmetic: 7.35 us -> 0 us
    reduce_scatter x3 -> x0, waiting for transfers between devices: 97.3 us -> none  [the longest x1 58.2 us: shards(): lax.psum_scatter(grad_w, ('row', 'col'), scatter_dimension=0, tiled=True)]
    reshape x10 -> x0, local copies, waits for them, and re-layouts: 77.6 us -> none  [the longest x4 44.4 us: backward_part(): inner_grad.astype(jnp.bfloat16).reshape(wide_block, j_rows * channels)]
    dot_general x24 -> x0, matrix products: 66.1 us -> none  [the longest x4 23.9 us: forward_part(): jnp.einsum('icje,cep->ijp', outer_block, weight_cube, preferred_element_t...]
    convert_element_type x8 -> x0, local copies, waits for them, and re-layouts: 38.1 us -> none  [the longest x4 33.8 us: backward_part(): inner_grad.astype(jnp.bfloat16).reshape(wide_block, j_rows * channels)]
    pallas_call x0 -> x6, Pallas kernels: none -> 29 us  [the longest x1 11.9 us: shards(): pl.pallas_call(functools.partial(outer_kernel, dims, n_row, n_col), in_sp...]
    all_gather x2 -> x0, blocking collectives: 21.8 us -> none  [the longest x1 15.8 us: shards(): left_all = lax.all_gather(left_act, 'col', axis=0, tiled=True)]
    ppermute x0 -> x12, starting transfers between devices: none -> 16.3 us  [exchange(): lax.ppermute(pieces[k], axis, [(s, (s + k) % n) for s in range(n)])]
    while x26 -> x0, local copies, waits for them, and re-layouts: 4.75 us -> none
  transfers between devices with their start and end apart: 3 -> 12, of which waited for: 3 -> 1; matrix products, arithmetic and copies ran while one was open for 1% -> 0% of each run, Pallas kernels for 0% -> 33%
where the time goes in v3:
time: 47.7 us; the launch traced here: 47.5 us
  Pallas kernels  29 us (61%)
  starting transfers between devices  16.3 us (34%)
  waiting for transfers between devices  1.51 us (3%)
  between operations  0.75 us (2%)
    ppermute x12, starting transfers between devices, exchange(): lax.ppermute(pieces[k], axis, [(s, (s + k) % n) for s in range(n)])  16.3 us
    pallas_call x1, Pallas kernels, shards(): pl.pallas_call(functools.partial(outer_kernel, dims, n_row, n_col), in_sp...  11.9 us
    pallas_call x1, Pallas kernels, shards(): pl.pallas_call(functools.partial(inner_kernel, dims), in_specs=[smem(), s...  6.41 us
    pallas_call x1, Pallas kernels, shards(): pl.pallas_call(functools.partial(left_kernel, dims), in_specs=vmem(2), ou...  4.78 us
    pallas_call x1, Pallas kernels, shards(): pl.pallas_call(functools.partial(pair_kernel, dims), in_specs=vmem(4), ou...  4.27 us
    ppermute x12, waiting for transfers between devices, exchange(): lax.ppermute(pieces[k], axis, [(s, (s + k) % n) for s in range(n)])  1.51 us
  transfers between devices with their start and end apart: 12, of which 1 were waited for; matrix products, arithmetic and copies ran while one was open for 0% of the time, Pallas kernels for 33%

profile of v3, /device:TPU:0, one launch (start us, length us, event | category | flops | bytes accessed | tf_op | source)
XLA Modules:
  0.0 47.5 jit_solution(12828073734903847491)
XLA Ops:
  0.6 3.1 %collective-permute-start = (bf16[16,2048]{1,0:T(8,128)(2,1)}, bf16[16,2048]{1,0:T(8,128)(2,1)S(1)}, u32[]{:S(2)}, u32[]{:S(2)}) collective-permute-start(bf16[16,2048]{1,0:T(8,128)(2,1)} %refs_4_.1), channel_id=1, source_target_pairs={{0,1},{1,2},{2,3},{3,0},{4,5},{5,6},{6,7},{7,4},{8,9},{9,10},{10,1... | collective-permute-start | bytes 196616 | tf_op jit(solution)/shard_map/ppermute | solution.py:330
  3.7 2.1 %collective-permute-start.2 = (bf16[16,2048]{1,0:T(8,128)(2,1)}, bf16[16,2048]{1,0:T(8,128)(2,1)S(1)}, u32[]{:S(2)}, u32[]{:S(2)}) collective-permute-start(bf16[16,2048]{1,0:T(8,128)(2,1)} %refs_4_.1), channel_id=1, source_target_pairs={{0,3},{1,0},{2,1},{3,2},{4,7},{5,4},{6,5},{7,6},{8,11},{9,8},{10,9... | collective-permute-start | bytes 196616 | tf_op jit(solution)/shard_map/ppermute | solution.py:330
  5.8 0.9 %collective-permute-start.1 = (bf16[16,2048]{1,0:T(8,128)(2,1)}, bf16[16,2048]{1,0:T(8,128)(2,1)S(1)}, u32[]{:S(2)}, u32[]{:S(2)}) collective-permute-start(bf16[16,2048]{1,0:T(8,128)(2,1)} %refs_4_.1), channel_id=1, source_target_pairs={{0,2},{1,3},{2,0},{3,1},{4,6},{5,7},{6,4},{7,5},{8,10},{9,11},{10,... | collective-permute-start | bytes 196616 | tf_op jit(solution)/shard_map/ppermute | solution.py:330
  6.8 1.7 %collective-permute-start.5 = (bf16[16,2048]{1,0:T(8,128)(2,1)}, bf16[16,2048]{1,0:T(8,128)(2,1)S(1)}, u32[]{:S(2)}, u32[]{:S(2)}) collective-permute-start(bf16[16,2048]{1,0:T(8,128)(2,1)} %refs_5_.1), channel_id=1, source_target_pairs={{0,12},{4,0},{8,4},{12,8},{1,13},{5,1},{9,5},{13,9},{2,14},{6,2},{... | collective-permute-start | bytes 196616 | tf_op jit(solution)/shard_map/ppermute | solution.py:330
  8.5 1.8 %collective-permute-start.4 = (bf16[16,2048]{1,0:T(8,128)(2,1)}, bf16[16,2048]{1,0:T(8,128)(2,1)S(1)}, u32[]{:S(2)}, u32[]{:S(2)}) collective-permute-start(bf16[16,2048]{1,0:T(8,128)(2,1)} %refs_5_.1), channel_id=1, source_target_pairs={{0,8},{4,12},{8,0},{12,4},{1,9},{5,13},{9,1},{13,5},{2,10},{6,14},... | collective-permute-start | bytes 196616 | tf_op jit(solution)/shard_map/ppermute | solution.py:330
  10.3 6.4 %inner.1 = (bf16[64,64,128]{2,1,0:T(8,128)(2,1)S(1)}, bf16[8,512,1024]{2,1,0:T(8,128)(2,1)S(1)}, f32[64,128]{1,0:T(8,128)S(1)}, bf16[1024,128]{1,0:T(8,128)(2,1)...) custom-call(s32[256]{0:T(256)} %refs_0_.1, ...), custom_call_target="tpu_custom_call" | custom-call | flops 1073741824 | bytes 12582912 | tf_op jit(solution)/shard_map/inner/pallas_call | solution.py:373
  16.7 0.0 collective-permute-done.1.refs_7_
  16.7 0.0 collective-permute-done.3.refs_10_
  16.8 0.0 collective-permute-done.4.refs_11_
  16.8 11.9 %outer.1 = (bf16[64,64,1024]{2,1,0:T(8,128)(2,1)S(1)}, bf16[256,512]{1,0:T(8,128)(2,1)S(1)}, bf16[512,128]{1,0:T(8,128)(2,1)S(1)}, bf16[512,128]{1,0:T(8,128)(2,...) custom-call(f32[64,128]{1,0:T(8,128)S(1)} %get-tuple-element.26.refs_0_.ri_ref, ...), custom_call_target="tpu_custom_call" | custom-call | flops 3221225472 | bytes 16777216 | tf_op jit(solution)/shard_map/outer/pallas_call | solution.py:401
  28.7 0.1 collective-permute-start.6
  28.8 0.3 collective-permute-start.7
  29.1 1.5 %collective-permute-start.8 = (bf16[512,128]{1,0:T(8,128)(2,1)S(1)}, bf16[512,128]{1,0:T(8,128)(2,1)S(1)}, u32[]{:S(2)}, u32[]{:S(2)}) collective-permute-start(bf16[512,128]{1,0:T(8,128)(2,1)S(1)} %get-tuple-element.40), channel_id=1, source_target_pairs={{0,12},{4,0},{8,4},{12,8},{1,13},{5,1},{9,5},{13,9},{2,14},{6,2},{... | collective-permute-start | bytes 393224 | tf_op jit(solution)/shard_map/ppermute | solution.py:330
  30.6 4.8 %left.1.refs_2_ = bf16[1024,128]{1,0:T(8,128)(2,1)S(1)} custom-call(bf16[8,512,1024]{2,1,0:T(8,128)(2,1)S(1)} %get-tuple-element.30.refs_4_.z_ref, bf16[256,512]{1,0:T(8,128)(2,1)S(1)} %get-tuple-element.36.rbt_ref), custom_call_target="tpu_custom_call" | custom-call | flops 1073741824 | bytes 8388608 | tf_op jit(solution)/shard_map/left/pallas_call | solution.py:429
  35.3 0.0 collective-permute-done.6.refs_4_
  35.4 0.0 collective-permute-done.8.refs_6_
  35.4 0.8 %middle.1 = (f32[16,2048]{1,0:T(8,128)}, bf16[320,128]{1,0:T(8,128)(2,1)S(1)}, bf16[320,128]{1,0:T(8,128)(2,1)S(1)}, bf16[320,128]{1,0:T(8,128)(2,1)S(1)}, bf16[320,128]{1,0:T(8,128)(2,1)S(1)}) custom-call(f32[64,128]{1,0:T(8,128)S(1)} %get-tuple-element.27.refs_1_.refs_0_, f32[1,2048]{1,0:T(1,128)S(1)} %get-tuple-element.28.refs_2_.refs_1_, ...), custom_call_target="tpu_custom_call" | custom-call | bytes 1048576 | tf_op jit(solution)/shard_map/middle/pallas_call | solution.py:440
  36.2 1.5 %collective-permute-start.9 = (bf16[320,128]{1,0:T(8,128)(2,1)S(1)}, bf16[320,128]{1,0:T(8,128)(2,1)S(1)}, u32[]{:S(2)}, u32[]{:S(2)}) collective-permute-start(bf16[320,128]{1,0:T(8,128)(2,1)S(1)} %get-tuple-element.42), channel_id=1, source_target_pairs={{0,1},{1,2},{2,3},{3,0},{4,5},{5,6},{6,7},{7,4},{8,9},{9,10},{10,1... | collective-permute-start | bytes 245768 | tf_op jit(solution)/shard_map/ppermute | solution.py:330
  37.7 0.7 %collective-permute-start.10 = (bf16[320,128]{1,0:T(8,128)(2,1)S(1)}, bf16[320,128]{1,0:T(8,128)(2,1)S(1)}, u32[]{:S(2)}, u32[]{:S(2)}) collective-permute-start(bf16[320,128]{1,0:T(8,128)(2,1)S(1)} %get-tuple-element.43), channel_id=1, source_target_pairs={{0,2},{1,3},{2,0},{3,1},{4,6},{5,7},{6,4},{7,5},{8,10},{9,11},{10,... | collective-permute-start | bytes 245768 | tf_op jit(solution)/shard_map/ppermute | solution.py:330
  38.4 2.6 %collective-permute-start.11 = (bf16[320,128]{1,0:T(8,128)(2,1)S(1)}, bf16[320,128]{1,0:T(8,128)(2,1)S(1)}, u32[]{:S(2)}, u32[]{:S(2)}) collective-permute-start(bf16[320,128]{1,0:T(8,128)(2,1)S(1)} %get-tuple-element.44), channel_id=1, source_target_pairs={{0,3},{1,0},{2,1},{3,2},{4,7},{5,4},{6,5},{7,6},{8,11},{9,8},{10,9... | collective-permute-start | bytes 245768 | tf_op jit(solution)/shard_map/ppermute | solution.py:330
  41.0 4.3 %pair.1 = bf16[64,64,128]{2,1,0:T(8,128)(2,1)} custom-call(f32[64,128]{1,0:T(8,128)S(1)} %get-tuple-element.26.refs_0_.ri_ref, bf16[64,64,1024]{2,1,0:T(8,128)(2,1)S(1)} %get-tuple-element.33.y_ref, bf16[1024,128]{1,0:T(8,128)(2,1)S(1)} %get-tuple-element.34.wp_ref, f32[64,128]{1,0:T(8,128)S(1)} %get-tuple-element.35.inv_ref), custom_call_target="tpu_custom_call" | custom-call | flops 1073741824 | bytes 12582912 | tf_op jit(solution)/shard_map/pair/pallas_call | solution.py:456
  45.3 0.0 collective-permute-done.9.refs_3_
  45.3 1.5 %collective-permute-done.10.refs_4_ = bf16[320,128]{1,0:T(8,128)(2,1)S(1)} collective-permute-done((bf16[320,128]{1,0:T(8,128)(2,1)S(1)}, bf16[320,128]{1,0:T(8,128)(2,1)S(1)}, u32[]{:S(2)}, u32[]{:S(2)}) %collective-permute-start.10) | collective-permute-done | bytes 81952 | tf_op jit(solution)/shard_map/ppermute | solution.py:330
  46.8 0.8 %final_sums.1 = (f32[16,2048]{1,0:T(8,128)}, f32[64,128]{1,0:T(8,128)}) custom-call(f32[64,128]{1,0:T(8,128)S(1)} %get-tuple-element.26.refs_0_.ri_ref, f32[1,2048]{1,0:T(1,128)S(1)} %get-tuple-element.28.refs_2_.refs_1_, bf16[320,128]{1,0:T(8,128)(2,1)S(1)} %get-tuple-element.41.refs_2_, bf16[320,128]{1,0:T(8,128)(2,1)S(1)} %collective-permute-done.9.refs_3_, ...), custom_call_target="tpu_custom_call" | custom-call | bytes 1048576 | tf_op jit(solution)/shard_map/final_sums/pallas_call | solution.py:470
  (6 shorter events, 0.0 us)
Async XLA Ops:
  0.6 7.9 %collective-permute-start = (bf16[16,2048]{1,0:T(8,128)(2,1)}, bf16[16,2048]{1,0:T(8,128)(2,1)S(1)}, u32[]{:S(2)}, u32[]{:S(2)}) collective-permute-start(bf16[16,2048]{1,0:T(8,128)(2,1)} %refs_4_.1), channel_id=1, source_target_pairs={{0,1},{1,2},{2,3},{3,0},{4,5},{5,6},{6,7},{7,4},{8,9},{9,10},{10,1... | collective-permute-start | bytes 196616 | tf_op jit(solution)/shard_map/ppermute | solution.py:330
  3.7 13.0 %collective-permute-start.2 = (bf16[16,2048]{1,0:T(8,128)(2,1)}, bf16[16,2048]{1,0:T(8,128)(2,1)S(1)}, u32[]{:S(2)}, u32[]{:S(2)}) collective-permute-start(bf16[16,2048]{1,0:T(8,128)(2,1)} %refs_4_.1), channel_id=1, source_target_pairs={{0,3},{1,0},{2,1},{3,2},{4,7},{5,4},{6,5},{7,6},{8,11},{9,8},{10,9... | collective-permute-start | bytes 196616 | tf_op jit(solution)/shard_map/ppermute | solution.py:330
  5.8 10.9 %collective-permute-start.1 = (bf16[16,2048]{1,0:T(8,128)(2,1)}, bf16[16,2048]{1,0:T(8,128)(2,1)S(1)}, u32[]{:S(2)}, u32[]{:S(2)}) collective-permute-start(bf16[16,2048]{1,0:T(8,128)(2,1)} %refs_4_.1), channel_id=1, source_target_pairs={{0,2},{1,3},{2,0},{3,1},{4,6},{5,7},{6,4},{7,5},{8,10},{9,11},{10,... | collective-permute-start | bytes 196616 | tf_op jit(solution)/shard_map/ppermute | solution.py:330
  6.7 10.0 %collective-permute-start.3 = (bf16[16,2048]{1,0:T(8,128)(2,1)}, bf16[16,2048]{1,0:T(8,128)(2,1)S(1)}, u32[]{:S(2)}, u32[]{:S(2)}) collective-permute-start(bf16[16,2048]{1,0:T(8,128)(2,1)} %refs_5_.1), channel_id=1, source_target_pairs={{0,4},{4,8},{8,12},{12,0},{1,5},{5,9},{9,13},{13,1},{2,6},{6,10},{... | collective-permute-start | bytes 196616 | tf_op jit(solution)/shard_map/ppermute | solution.py:330
  6.8 10.0 %collective-permute-start.5 = (bf16[16,2048]{1,0:T(8,128)(2,1)}, bf16[16,2048]{1,0:T(8,128)(2,1)S(1)}, u32[]{:S(2)}, u32[]{:S(2)}) collective-permute-start(bf16[16,2048]{1,0:T(8,128)(2,1)} %refs_5_.1), channel_id=1, source_target_pairs={{0,12},{4,0},{8,4},{12,8},{1,13},{5,1},{9,5},{13,9},{2,14},{6,2},{... | collective-permute-start | bytes 196616 | tf_op jit(solution)/shard_map/ppermute | solution.py:330
  8.5 8.3 %collective-permute-start.4 = (bf16[16,2048]{1,0:T(8,128)(2,1)}, bf16[16,2048]{1,0:T(8,128)(2,1)S(1)}, u32[]{:S(2)}, u32[]{:S(2)}) collective-permute-start(bf16[16,2048]{1,0:T(8,128)(2,1)} %refs_5_.1), channel_id=1, source_target_pairs={{0,8},{4,12},{8,0},{12,4},{1,9},{5,13},{9,1},{13,5},{2,10},{6,14},... | collective-permute-start | bytes 196616 | tf_op jit(solution)/shard_map/ppermute | solution.py:330
  28.7 6.6 %collective-permute-start.6 = (bf16[512,128]{1,0:T(8,128)(2,1)S(1)}, bf16[512,128]{1,0:T(8,128)(2,1)S(1)}, u32[]{:S(2)}, u32[]{:S(2)}) collective-permute-start(bf16[512,128]{1,0:T(8,128)(2,1)S(1)} %get-tuple-element.38), channel_id=1, source_target_pairs={{0,4},{4,8},{8,12},{12,0},{1,5},{5,9},{9,13},{13,1},{2,6},{6,10},{... | collective-permute-start | bytes 393224 | tf_op jit(solution)/shard_map/ppermute | solution.py:330
  28.8 6.6 %collective-permute-start.7 = (bf16[512,128]{1,0:T(8,128)(2,1)S(1)}, bf16[512,128]{1,0:T(8,128)(2,1)S(1)}, u32[]{:S(2)}, u32[]{:S(2)}) collective-permute-start(bf16[512,128]{1,0:T(8,128)(2,1)S(1)} %get-tuple-element.39), channel_id=1, source_target_pairs={{0,8},{4,12},{8,0},{12,4},{1,9},{5,13},{9,1},{13,5},{2,10},{6,14},... | collective-permute-start | bytes 393224 | tf_op jit(solution)/shard_map/ppermute | solution.py:330
  29.1 6.3 %collective-permute-start.8 = (bf16[512,128]{1,0:T(8,128)(2,1)S(1)}, bf16[512,128]{1,0:T(8,128)(2,1)S(1)}, u32[]{:S(2)}, u32[]{:S(2)}) collective-permute-start(bf16[512,128]{1,0:T(8,128)(2,1)S(1)} %get-tuple-element.40), channel_id=1, source_target_pairs={{0,12},{4,0},{8,4},{12,8},{1,13},{5,1},{9,5},{13,9},{2,14},{6,2},{... | collective-permute-start | bytes 393224 | tf_op jit(solution)/shard_map/ppermute | solution.py:330
  36.2 9.1 %collective-permute-start.9 = (bf16[320,128]{1,0:T(8,128)(2,1)S(1)}, bf16[320,128]{1,0:T(8,128)(2,1)S(1)}, u32[]{:S(2)}, u32[]{:S(2)}) collective-permute-start(bf16[320,128]{1,0:T(8,128)(2,1)S(1)} %get-tuple-element.42), channel_id=1, source_target_pairs={{0,1},{1,2},{2,3},{3,0},{4,5},{5,6},{6,7},{7,4},{8,9},{9,10},{10,1... | collective-permute-start | bytes 245768 | tf_op jit(solution)/shard_map/ppermute | solution.py:330
  37.7 9.1 %collective-permute-start.10 = (bf16[320,128]{1,0:T(8,128)(2,1)S(1)}, bf16[320,128]{1,0:T(8,128)(2,1)S(1)}, u32[]{:S(2)}, u32[]{:S(2)}) collective-permute-start(bf16[320,128]{1,0:T(8,128)(2,1)S(1)} %get-tuple-element.43), channel_id=1, source_target_pairs={{0,2},{1,3},{2,0},{3,1},{4,6},{5,7},{6,4},{7,5},{8,10},{9,11},{10,... | collective-permute-start | bytes 245768 | tf_op jit(solution)/shard_map/ppermute | solution.py:330
  38.4 8.4 %collective-permute-start.11 = (bf16[320,128]{1,0:T(8,128)(2,1)S(1)}, bf16[320,128]{1,0:T(8,128)(2,1)S(1)}, u32[]{:S(2)}, u32[]{:S(2)}) collective-permute-start(bf16[320,128]{1,0:T(8,128)(2,1)S(1)} %get-tuple-element.44), channel_id=1, source_target_pairs={{0,3},{1,0},{2,1},{3,2},{4,7},{5,4},{6,5},{7,6},{8,11},{9,8},{10,9... | collective-permute-start | bytes 245768 | tf_op jit(solution)/shard_map/ppermute | solution.py:330

commit v4 on v3

--- a/solution.py
+++ b/solution.py
@@ -28,6 +28,14 @@
         return carry
 
     lax.fori_loop(0, count, body, 0, unroll=8)
+
+
+def send_to(index, k, n):
+    return index ^ k if n & (n - 1) == 0 else (index + k) % n
+
+
+def came_from(index, k, n):
+    return index ^ k if n & (n - 1) == 0 else (index + n - k) % n
 
 
 def lane_group(shape, chans):
@@ -95,7 +103,7 @@
                     ] = part[i * j_rows : (i + 1) * j_rows, k * LANES : (k + 1) * LANES]
         return carry
 
-    lax.fori_loop(0, steps, body, 0)
+    lax.fori_loop(0, steps, body, 0, unroll=True)
     more[1].wait()
     more[2].wait()
 
@@ -117,7 +125,7 @@
 
     piece = right_refs[0].shape[0]
     for k in range(n_row):
-        owner = lax.rem(row - k + n_row, n_row)
+        owner = came_from(row, k, n_row)
         flat[pl.ds(pl.multiple_of(owner * piece, 8), piece), :] = right_refs[k][...].astype(F32)
     for t in range(tiles):
         lanes = slice(t * LANES, (t + 1) * LANES)
@@ -136,7 +144,7 @@
     rbt_ref[...] = rbig[...].T
     piece = left_refs[0].shape[0]
     for k in range(n_col):
-        owner = lax.rem(col - k + n_col, n_col)
+        owner = came_from(col, k, n_col)
         flat[pl.ds(pl.multiple_of(owner * piece, 8), piece), :] = left_refs[k][...].astype(F32)
     for t in range(tiles):
         lanes = slice(t * LANES, (t + 1) * LANES)
@@ -183,7 +191,7 @@
         gwt[...] += jnp.dot(scaled_t, y_flat, preferred_element_type=F32)
         return carry
 
-    lax.fori_loop(0, i_rows // step_rows, body, 0)
+    lax.fori_loop(0, i_rows // step_rows, body, 0, unroll=True)
     for k in range(blocks):
         turned_tile = gwt[:, k * LANES : (k + 1) * LANES].T
         for q in range(groups):
@@ -207,7 +215,7 @@
     right_owned = j_rows * tiles // n_row
     weight_owned = chans * chans // n_row
     for k in range(n_row):
-        owner = lax.rem(row + k, n_row)
+        owner = send_to(row, k, n_row)
         at = pl.multiple_of(owner * right_owned, right_owned)
         send_refs[k][:right_owned, :] = gr_all[pl.ds(at, right_owned), :].astype(BF16)
         at = pl.multiple_of(owner * weight_owned, weight_owned)
@@ -243,7 +251,7 @@
                 gl_all[pl.ds(pl.multiple_of(at, tiles), tiles), :] = merged.astype(BF16)
         return carry
 
-    lax.fori_loop(0, i_rows // step_rows, body, 0)
+    lax.fori_loop(0, i_rows // step_rows, body, 0, unroll=True)
 
 
 def sum_of(refs):
@@ -276,7 +284,7 @@
     right_owned = j_rows * tiles // n_row
     weight_owned = (whole.shape[0] - right_owned) // n_col
     for k in range(n_col):
-        owner = lax.rem(col + k, n_col)
+        owner = send_to(col, k, n_col)
         at = pl.multiple_of(owner * left_owned, left_owned)
         send_refs[k][:left_owned, :] = gl_ref[pl.ds(at, left_owned), :]
         at = pl.multiple_of(right_owned + owner * weight_owned, 8)
@@ -305,7 +313,7 @@
         store(step).start()
         return carry
 
-    lax.fori_loop(0, steps, body, 0)
+    lax.fori_loop(0, steps, body, 0, unroll=True)
     for step in range(steps):
         store(step).wait()
 
@@ -327,7 +335,7 @@
     n = len(pieces)
     came = [pieces[0]]
     for k in range(1, n):
-        came.append(lax.ppermute(pieces[k], axis, [(s, (s + k) % n) for s in range(n)]))
+        came.append(lax.ppermute(pieces[k], axis, [(s, send_to(s, k, n)) for s in range(n)]))
     return came
 
 

time: 47.7 us -> 46.5 us (0.975)
  waiting for transfers between devices: 1.51 us -> 7.49 us
  Pallas kernels: 29 us -> 23.9 us
  starting transfers between devices: 16.3 us -> 14.1 us
    ppermute x12, waiting for transfers between devices: 1.51 us -> 7.49 us  [exchange(): lax.ppermute(pieces[k], axis, [(s, send_to(s, k, n)) for s in range(n)])]
    ppermute x12, starting transfers between devices: 16.3 us -> 14.1 us  [exchange(): lax.ppermute(pieces[k], axis, [(s, send_to(s, k, n)) for s in range(n)])]
    pallas_call x1, Pallas kernels: 4.78 us -> 2.71 us  [shards(): pl.pallas_call(functools.partial(left_kernel, dims), in_specs=vmem(2), ou...]
    pallas_call x1, Pallas kernels: 11.9 us -> 10.1 us  [shards(): pl.pallas_call(functools.partial(outer_kernel, dims, n_row, n_col), in_sp...]
    pallas_call x1, Pallas kernels: 4.27 us -> 3.12 us  [shards(): pl.pallas_call(functools.partial(pair_kernel, dims), in_specs=vmem(4), ou...]
  transfers between devices with their start and end apart: 12 -> 12, of which waited for: 1 -> 3; matrix products, arithmetic and copies ran while one was open for 0% -> 0% of each run, Pallas kernels for 33% -> 27%
where the time goes in v4:
time: 46.5 us; the launch traced here: 46.3 us
  Pallas kernels  23.9 us (51%)
  starting transfers between devices  14.1 us (30%)
  waiting for transfers between devices  7.49 us (16%)
  between operations  0.74 us (2%)
    ppermute x12, starting transfers between devices, exchange(): lax.ppermute(pieces[k], axis, [(s, send_to(s, k, n)) for s in range(n)])  14.1 us
    pallas_call x1, Pallas kernels, shards(): pl.pallas_call(functools.partial(outer_kernel, dims, n_row, n_col), in_sp...  10.1 us
    ppermute x12, waiting for transfers between devices, exchange(): lax.ppermute(pieces[k], axis, [(s, send_to(s, k, n)) for s in range(n)])  7.49 us
    pallas_call x1, Pallas kernels, shards(): pl.pallas_call(functools.partial(inner_kernel, dims), in_specs=[smem(), s...  6.45 us
    pallas_call x1, Pallas kernels, shards(): pl.pallas_call(functools.partial(pair_kernel, dims), in_specs=vmem(4), ou...  3.12 us
    pallas_call x1, Pallas kernels, shards(): pl.pallas_call(functools.partial(left_kernel, dims), in_specs=vmem(2), ou...  2.71 us
  transfers between devices with their start and end apart: 12, of which 3 were waited for; matrix products, arithmetic and copies ran while one was open for 0% of the time, Pallas kernels for 27%

profile of v4, /device:TPU:0, one launch (start us, length us, event | category | flops | bytes accessed | tf_op | source)
XLA Modules:
  0.0 46.3 jit_solution(367192883727415861)
XLA Ops:
  0.6 3.1 %collective-permute-start = (bf16[16,2048]{1,0:T(8,128)(2,1)}, bf16[16,2048]{1,0:T(8,128)(2,1)S(1)}, u32[]{:S(2)}, u32[]{:S(2)}) collective-permute-start(bf16[16,2048]{1,0:T(8,128)(2,1)} %refs_4_.1), channel_id=1, source_target_pairs={{0,1},{1,0},{2,3},{3,2},{4,5},{5,4},{6,7},{7,6},{8,9},{9,8},{10,11... | collective-permute-start | bytes 196616 | tf_op jit(solution)/shard_map/ppermute | solution.py:338
  3.7 2.5 %collective-permute-start.2 = (bf16[16,2048]{1,0:T(8,128)(2,1)}, bf16[16,2048]{1,0:T(8,128)(2,1)S(1)}, u32[]{:S(2)}, u32[]{:S(2)}) collective-permute-start(bf16[16,2048]{1,0:T(8,128)(2,1)} %refs_4_.1), channel_id=1, source_target_pairs={{0,3},{1,2},{2,1},{3,0},{4,7},{5,6},{6,5},{7,4},{8,11},{9,10},{10,... | collective-permute-start | bytes 196616 | tf_op jit(solution)/shard_map/ppermute | solution.py:338
  6.2 0.1 collective-permute-start.1
  6.3 1.6 %collective-permute-start.5 = (bf16[16,2048]{1,0:T(8,128)(2,1)}, bf16[16,2048]{1,0:T(8,128)(2,1)S(1)}, u32[]{:S(2)}, u32[]{:S(2)}) collective-permute-start(bf16[16,2048]{1,0:T(8,128)(2,1)} %refs_5_.1), channel_id=1, source_target_pairs={{0,12},{4,8},{8,4},{12,0},{1,13},{5,9},{9,5},{13,1},{2,14},{6,10},... | collective-permute-start | bytes 196616 | tf_op jit(solution)/shard_map/ppermute | solution.py:338
  7.9 0.5 %collective-permute-start.4 = (bf16[16,2048]{1,0:T(8,128)(2,1)}, bf16[16,2048]{1,0:T(8,128)(2,1)S(1)}, u32[]{:S(2)}, u32[]{:S(2)}) collective-permute-start(bf16[16,2048]{1,0:T(8,128)(2,1)} %refs_5_.1), channel_id=1, source_target_pairs={{0,8},{4,12},{8,0},{12,4},{1,9},{5,13},{9,1},{13,5},{2,10},{6,14},... | collective-permute-start | bytes 196616 | tf_op jit(solution)/shard_map/ppermute | solution.py:338
  8.5 6.5 %inner.1 = (bf16[64,64,128]{2,1,0:T(8,128)(2,1)S(1)}, bf16[8,512,1024]{2,1,0:T(8,128)(2,1)S(1)}, f32[64,128]{1,0:T(8,128)S(1)}, bf16[1024,128]{1,0:T(8,128)(2,1)...) custom-call(s32[256]{0:T(256)} %refs_0_.1, ...), custom_call_target="tpu_custom_call" | custom-call | flops 1073741824 | bytes 12582912 | tf_op jit(solution)/shard_map/inner/pallas_call | solution.py:381
  14.9 0.0 collective-permute-done.1.refs_7_
  14.9 0.0 collective-permute-done.3.refs_10_
  15.0 0.0 collective-permute-done.4.refs_11_
  15.0 10.1 %outer.1 = (bf16[64,64,1024]{2,1,0:T(8,128)(2,1)S(1)}, bf16[256,512]{1,0:T(8,128)(2,1)S(1)}, bf16[512,128]{1,0:T(8,128)(2,1)S(1)}, bf16[512,128]{1,0:T(8,128)(2,...) custom-call(f32[64,128]{1,0:T(8,128)S(1)} %get-tuple-element.26.refs_0_.ri_ref, ...), custom_call_target="tpu_custom_call" | custom-call | flops 3221225472 | bytes 16777216 | tf_op jit(solution)/shard_map/outer/pallas_call | solution.py:409
  25.1 0.1 collective-permute-start.6
  25.1 1.6 %collective-permute-start.7 = (bf16[512,128]{1,0:T(8,128)(2,1)S(1)}, bf16[512,128]{1,0:T(8,128)(2,1)S(1)}, u32[]{:S(2)}, u32[]{:S(2)}) collective-permute-start(bf16[512,128]{1,0:T(8,128)(2,1)S(1)} %get-tuple-element.39), channel_id=1, source_target_pairs={{0,8},{4,12},{8,0},{12,4},{1,9},{5,13},{9,1},{13,5},{2,10},{6,14},... | collective-permute-start | bytes 393224 | tf_op jit(solution)/shard_map/ppermute | solution.py:338
  26.7 0.3 collective-permute-start.8
  27.0 2.7 %left.1.refs_2_ = bf16[1024,128]{1,0:T(8,128)(2,1)S(1)} custom-call(bf16[8,512,1024]{2,1,0:T(8,128)(2,1)S(1)} %get-tuple-element.30.refs_4_.z_ref, bf16[256,512]{1,0:T(8,128)(2,1)S(1)} %get-tuple-element.36.rbt_ref), custom_call_target="tpu_custom_call" | custom-call | flops 1073741824 | bytes 8388608 | tf_op jit(solution)/shard_map/left/pallas_call | solution.py:437
  29.7 1.8 %collective-permute-done.7.refs_5_ = bf16[512,128]{1,0:T(8,128)(2,1)S(1)} collective-permute-done((bf16[512,128]{1,0:T(8,128)(2,1)S(1)}, bf16[512,128]{1,0:T(8,128)(2,1)S(1)}, u32[]{:S(2)}, u32[]{:S(2)}) %collective-permute-start.7) | collective-permute-done | bytes 131104 | tf_op jit(solution)/shard_map/ppermute | solution.py:338
  31.5 1.9 %collective-permute-done.8.refs_6_ = bf16[512,128]{1,0:T(8,128)(2,1)S(1)} collective-permute-done((bf16[512,128]{1,0:T(8,128)(2,1)S(1)}, bf16[512,128]{1,0:T(8,128)(2,1)S(1)}, u32[]{:S(2)}, u32[]{:S(2)}) %collective-permute-start.8) | collective-permute-done | bytes 131104 | tf_op jit(solution)/shard_map/ppermute | solution.py:338
  33.4 0.8 %middle.1 = (f32[16,2048]{1,0:T(8,128)}, bf16[320,128]{1,0:T(8,128)(2,1)S(1)}, bf16[320,128]{1,0:T(8,128)(2,1)S(1)}, bf16[320,128]{1,0:T(8,128)(2,1)S(1)}, bf16[320,128]{1,0:T(8,128)(2,1)S(1)}) custom-call(f32[64,128]{1,0:T(8,128)S(1)} %get-tuple-element.27.refs_1_.refs_0_, f32[1,2048]{1,0:T(1,128)S(1)} %get-tuple-element.28.refs_2_.refs_1_, ...), custom_call_target="tpu_custom_call" | custom-call | bytes 1048576 | tf_op jit(solution)/shard_map/middle/pallas_call | solution.py:448
  34.2 1.8 %collective-permute-start.9 = (bf16[320,128]{1,0:T(8,128)(2,1)S(1)}, bf16[320,128]{1,0:T(8,128)(2,1)S(1)}, u32[]{:S(2)}, u32[]{:S(2)}) collective-permute-start(bf16[320,128]{1,0:T(8,128)(2,1)S(1)} %get-tuple-element.42), channel_id=1, source_target_pairs={{0,1},{1,0},{2,3},{3,2},{4,5},{5,4},{6,7},{7,6},{8,9},{9,8},{10,11... | collective-permute-start | bytes 245768 | tf_op jit(solution)/shard_map/ppermute | solution.py:338
  36.0 2.0 %collective-permute-start.10 = (bf16[320,128]{1,0:T(8,128)(2,1)S(1)}, bf16[320,128]{1,0:T(8,128)(2,1)S(1)}, u32[]{:S(2)}, u32[]{:S(2)}) collective-permute-start(bf16[320,128]{1,0:T(8,128)(2,1)S(1)} %get-tuple-element.43), channel_id=1, source_target_pairs={{0,2},{1,3},{2,0},{3,1},{4,6},{5,7},{6,4},{7,5},{8,10},{9,11},{10,... | collective-permute-start | bytes 245768 | tf_op jit(solution)/shard_map/ppermute | solution.py:338
  38.0 0.6 %collective-permute-start.11 = (bf16[320,128]{1,0:T(8,128)(2,1)S(1)}, bf16[320,128]{1,0:T(8,128)(2,1)S(1)}, u32[]{:S(2)}, u32[]{:S(2)}) collective-permute-start(bf16[320,128]{1,0:T(8,128)(2,1)S(1)} %get-tuple-element.44), channel_id=1, source_target_pairs={{0,3},{1,2},{2,1},{3,0},{4,7},{5,6},{6,5},{7,4},{8,11},{9,10},{10,... | collective-permute-start | bytes 245768 | tf_op jit(solution)/shard_map/ppermute | solution.py:338
  38.6 3.1 %pair.1 = bf16[64,64,128]{2,1,0:T(8,128)(2,1)} custom-call(f32[64,128]{1,0:T(8,128)S(1)} %get-tuple-element.26.refs_0_.ri_ref, bf16[64,64,1024]{2,1,0:T(8,128)(2,1)S(1)} %get-tuple-element.33.y_ref, bf16[1024,128]{1,0:T(8,128)(2,1)S(1)} %get-tuple-element.34.wp_ref, f32[64,128]{1,0:T(8,128)S(1)} %get-tuple-element.35.inv_ref), custom_call_target="tpu_custom_call" | custom-call | flops 1073741824 | bytes 12582912 | tf_op jit(solution)/shard_map/pair/pallas_call | solution.py:464
  41.7 0.0 collective-permute-done.9.refs_3_
  41.7 3.8 %collective-permute-done.10.refs_4_ = bf16[320,128]{1,0:T(8,128)(2,1)S(1)} collective-permute-done((bf16[320,128]{1,0:T(8,128)(2,1)S(1)}, bf16[320,128]{1,0:T(8,128)(2,1)S(1)}, u32[]{:S(2)}, u32[]{:S(2)}) %collective-permute-start.10) | collective-permute-done | bytes 81952 | tf_op jit(solution)/shard_map/ppermute | solution.py:338
  45.5 0.8 %final_sums.1 = (f32[16,2048]{1,0:T(8,128)}, f32[64,128]{1,0:T(8,128)}) custom-call(f32[64,128]{1,0:T(8,128)S(1)} %get-tuple-element.26.refs_0_.ri_ref, f32[1,2048]{1,0:T(1,128)S(1)} %get-tuple-element.28.refs_2_.refs_1_, bf16[320,128]{1,0:T(8,128)(2,1)S(1)} %get-tuple-element.41.refs_2_, bf16[320,128]{1,0:T(8,128)(2,1)S(1)} %collective-permute-done.9.refs_3_, ...), custom_call_target="tpu_custom_call" | custom-call | bytes 1048576 | tf_op jit(solution)/shard_map/final_sums/pallas_call | solution.py:478
  (6 shorter events, 0.0 us)
Async XLA Ops:
  0.6 7.3 %collective-permute-start = (bf16[16,2048]{1,0:T(8,128)(2,1)}, bf16[16,2048]{1,0:T(8,128)(2,1)S(1)}, u32[]{:S(2)}, u32[]{:S(2)}) collective-permute-start(bf16[16,2048]{1,0:T(8,128)(2,1)} %refs_4_.1), channel_id=1, source_target_pairs={{0,1},{1,0},{2,3},{3,2},{4,5},{5,4},{6,7},{7,6},{8,9},{9,8},{10,11... | collective-permute-start | bytes 196616 | tf_op jit(solution)/shard_map/ppermute | solution.py:338
  3.7 11.2 %collective-permute-start.2 = (bf16[16,2048]{1,0:T(8,128)(2,1)}, bf16[16,2048]{1,0:T(8,128)(2,1)S(1)}, u32[]{:S(2)}, u32[]{:S(2)}) collective-permute-start(bf16[16,2048]{1,0:T(8,128)(2,1)} %refs_4_.1), channel_id=1, source_target_pairs={{0,3},{1,2},{2,1},{3,0},{4,7},{5,6},{6,5},{7,4},{8,11},{9,10},{10,... | collective-permute-start | bytes 196616 | tf_op jit(solution)/shard_map/ppermute | solution.py:338
  6.2 8.7 %collective-permute-start.1 = (bf16[16,2048]{1,0:T(8,128)(2,1)}, bf16[16,2048]{1,0:T(8,128)(2,1)S(1)}, u32[]{:S(2)}, u32[]{:S(2)}) collective-permute-start(bf16[16,2048]{1,0:T(8,128)(2,1)} %refs_4_.1), channel_id=1, source_target_pairs={{0,2},{1,3},{2,0},{3,1},{4,6},{5,7},{6,4},{7,5},{8,10},{9,11},{10,... | collective-permute-start | bytes 196616 | tf_op jit(solution)/shard_map/ppermute | solution.py:338
  6.3 8.6 %collective-permute-start.3 = (bf16[16,2048]{1,0:T(8,128)(2,1)}, bf16[16,2048]{1,0:T(8,128)(2,1)S(1)}, u32[]{:S(2)}, u32[]{:S(2)}) collective-permute-start(bf16[16,2048]{1,0:T(8,128)(2,1)} %refs_5_.1), channel_id=1, source_target_pairs={{0,4},{4,0},{8,12},{12,8},{1,5},{5,1},{9,13},{13,9},{2,6},{6,2},{1... | collective-permute-start | bytes 196616 | tf_op jit(solution)/shard_map/ppermute | solution.py:338
  6.3 8.6 %collective-permute-start.5 = (bf16[16,2048]{1,0:T(8,128)(2,1)}, bf16[16,2048]{1,0:T(8,128)(2,1)S(1)}, u32[]{:S(2)}, u32[]{:S(2)}) collective-permute-start(bf16[16,2048]{1,0:T(8,128)(2,1)} %refs_5_.1), channel_id=1, source_target_pairs={{0,12},{4,8},{8,4},{12,0},{1,13},{5,9},{9,5},{13,1},{2,14},{6,10},... | collective-permute-start | bytes 196616 | tf_op jit(solution)/shard_map/ppermute | solution.py:338
  7.9 7.0 %collective-permute-start.4 = (bf16[16,2048]{1,0:T(8,128)(2,1)}, bf16[16,2048]{1,0:T(8,128)(2,1)S(1)}, u32[]{:S(2)}, u32[]{:S(2)}) collective-permute-start(bf16[16,2048]{1,0:T(8,128)(2,1)} %refs_5_.1), channel_id=1, source_target_pairs={{0,8},{4,12},{8,0},{12,4},{1,9},{5,13},{9,1},{13,5},{2,10},{6,14},... | collective-permute-start | bytes 196616 | tf_op jit(solution)/shard_map/ppermute | solution.py:338
  25.1 4.7 %collective-permute-start.6 = (bf16[512,128]{1,0:T(8,128)(2,1)S(1)}, bf16[512,128]{1,0:T(8,128)(2,1)S(1)}, u32[]{:S(2)}, u32[]{:S(2)}) collective-permute-start(bf16[512,128]{1,0:T(8,128)(2,1)S(1)} %get-tuple-element.38), channel_id=1, source_target_pairs={{0,4},{4,0},{8,12},{12,8},{1,5},{5,1},{9,13},{13,9},{2,6},{6,2},{1... | collective-permute-start | bytes 393224 | tf_op jit(solution)/shard_map/ppermute | solution.py:338
  25.1 6.4 %collective-permute-start.7 = (bf16[512,128]{1,0:T(8,128)(2,1)S(1)}, bf16[512,128]{1,0:T(8,128)(2,1)S(1)}, u32[]{:S(2)}, u32[]{:S(2)}) collective-permute-start(bf16[512,128]{1,0:T(8,128)(2,1)S(1)} %get-tuple-element.39), channel_id=1, source_target_pairs={{0,8},{4,12},{8,0},{12,4},{1,9},{5,13},{9,1},{13,5},{2,10},{6,14},... | collective-permute-start | bytes 393224 | tf_op jit(solution)/shard_map/ppermute | solution.py:338
  26.7 6.7 %collective-permute-start.8 = (bf16[512,128]{1,0:T(8,128)(2,1)S(1)}, bf16[512,128]{1,0:T(8,128)(2,1)S(1)}, u32[]{:S(2)}, u32[]{:S(2)}) collective-permute-start(bf16[512,128]{1,0:T(8,128)(2,1)S(1)} %get-tuple-element.40), channel_id=1, source_target_pairs={{0,12},{4,8},{8,4},{12,0},{1,13},{5,9},{9,5},{13,1},{2,14},{6,10},... | collective-permute-start | bytes 393224 | tf_op jit(solution)/shard_map/ppermute | solution.py:338
  34.2 7.5 %collective-permute-start.9 = (bf16[320,128]{1,0:T(8,128)(2,1)S(1)}, bf16[320,128]{1,0:T(8,128)(2,1)S(1)}, u32[]{:S(2)}, u32[]{:S(2)}) collective-permute-start(bf16[320,128]{1,0:T(8,128)(2,1)S(1)} %get-tuple-element.42), channel_id=1, source_target_pairs={{0,1},{1,0},{2,3},{3,2},{4,5},{5,4},{6,7},{7,6},{8,9},{9,8},{10,11... | collective-permute-start | bytes 245768 | tf_op jit(solution)/shard_map/ppermute | solution.py:338
  36.0 9.5 %collective-permute-start.10 = (bf16[320,128]{1,0:T(8,128)(2,1)S(1)}, bf16[320,128]{1,0:T(8,128)(2,1)S(1)}, u32[]{:S(2)}, u32[]{:S(2)}) collective-permute-start(bf16[320,128]{1,0:T(8,128)(2,1)S(1)} %get-tuple-element.43), channel_id=1, source_target_pairs={{0,2},{1,3},{2,0},{3,1},{4,6},{5,7},{6,4},{7,5},{8,10},{9,11},{10,... | collective-permute-start | bytes 245768 | tf_op jit(solution)/shard_map/ppermute | solution.py:338
  38.0 7.5 %collective-permute-start.11 = (bf16[320,128]{1,0:T(8,128)(2,1)S(1)}, bf16[320,128]{1,0:T(8,128)(2,1)S(1)}, u32[]{:S(2)}, u32[]{:S(2)}) collective-permute-start(bf16[320,128]{1,0:T(8,128)(2,1)S(1)} %get-tuple-element.44), channel_id=1, source_target_pairs={{0,3},{1,2},{2,1},{3,0},{4,7},{5,6},{6,5},{7,4},{8,11},{9,10},{10,... | collective-permute-start | bytes 245768 | tf_op jit(solution)/shard_map/ppermute | solution.py:338

commit v5 on v4

--- a/solution.py
+++ b/solution.py
@@ -21,15 +21,6 @@
     return pl.CostEstimate(flops=int(flops), bytes_accessed=int(nbytes), transcendentals=0)
 
 
-def spread_rows(mask_ref, first, count, out_ref):
-    def body(r, carry):
-        value = mask_ref[first + r].astype(F32)
-        out_ref[pl.ds(r, 1), :] = jnp.full((1, LANES), value, F32)
-        return carry
-
-    lax.fori_loop(0, count, body, 0, unroll=8)
-
-
 def send_to(index, k, n):
     return index ^ k if n & (n - 1) == 0 else (index + k) % n
 
@@ -42,52 +33,74 @@
     return lax.broadcasted_iota(jnp.int32, shape, 1) // chans
 
 
-def inner_kernel(dims, *refs):
+def mask_rows(res_ref, first, count):
+    shape = (count, res_ref.shape[1])
+    row = lax.broadcasted_iota(jnp.int32, shape, 0) + first
+    here = lax.broadcasted_iota(jnp.int32, shape, 1) == row
+    chosen = jnp.where(here, res_ref[...].astype(F32), 0.0)
+    return jnp.broadcast_to(jnp.sum(chosen, axis=1, keepdims=True), (count, LANES))
+
+
+def scale_kernel(dims, *refs):
     chans, groups, blocks, i_rows, j_rows, step_rows, sequences = dims
     tiles = sequences * chans // LANES
-    res_ref, seq_ref, cot_ref, w_hbm, left_hbm, right_hbm = refs[:6]
-    scaled_ref, z_ref, inv_ref, wp_ref, keep_ref, ri_ref, rj_ref, left_ref, right_ref = refs[6:15]
-    w_ref, w32, cot, sems, more_sems = refs[15:]
+    res_hbm, seq_hbm, cot_ref, w_hbm, left_hbm, right_hbm = refs[:6]
+    scaled_ref, inv_ref, wp_ref, keep_ref, ri_ref, rj_ref, left_ref, right_ref = refs[6:14]
+    res_ref, seq_ref, w_ref, w32, cot, sems, more_sems = refs[14:]
     steps = i_rows // step_rows
 
     def fetch(step):
         rows = pl.ds(step * step_rows, step_rows)
         return pltpu.make_async_copy(cot_ref.at[rows], cot.at[rows], sems.at[step])
 
+    pairs = [
+        (res_hbm, res_ref),
+        (seq_hbm, seq_ref),
+        (w_hbm, w_ref),
+        (left_hbm, left_ref),
+        (right_hbm, right_ref),
+    ]
     more = [
-        pltpu.make_async_copy(w_hbm, w_ref, more_sems.at[0]),
-        pltpu.make_async_copy(left_hbm, left_ref, more_sems.at[1]),
-        pltpu.make_async_copy(right_hbm, right_ref, more_sems.at[2]),
+        pltpu.make_async_copy(source, to, more_sems.at[k]) for k, (source, to) in enumerate(pairs)
     ]
-    more[0].start()
+    for copy in more[:3]:
+        copy.start()
     for step in range(steps):
         fetch(step).start()
-    more[1].start()
-    more[2].start()
-    spread_rows(res_ref, lax.axis_index("row") * i_rows, i_rows, ri_ref)
-    spread_rows(res_ref, lax.axis_index("col") * j_rows, j_rows, rj_ref)
-    group = lane_group((1, LANES), chans)
-    valid = jnp.int32(0)
-    for t in range(tiles):
-        kept = jnp.zeros((1, LANES), F32)
-        for lo in range(groups):
-            value = seq_ref[t * groups + lo]
-            valid = valid + value
-            kept = jnp.where(group == lo, value.astype(F32), kept)
-        keep_ref[:, t * LANES : (t + 1) * LANES] = kept
-    inv_ref[...] = 1.0 / jnp.maximum(valid.astype(F32) * rj_ref[...], 1.0)
+    for copy in more[3:]:
+        copy.start()
+    shape = (sequences, tiles * LANES)
+    own = lax.broadcasted_iota(jnp.int32, shape, 1) // chans
+    repeat = (own == lax.broadcasted_iota(jnp.int32, shape, 0)).astype(F32).astype(BF16)
     more[0].wait()
+    ri_ref[...] = mask_rows(res_ref, lax.axis_index("row") * i_rows, i_rows)
+    rj_ref[...] = mask_rows(res_ref, lax.axis_index("col") * j_rows, j_rows)
+    more[1].wait()
+    seq = seq_ref[...].astype(F32)
+    keep_ref[...] = jnp.dot(
+        jnp.broadcast_to(seq, (8, sequences)).astype(BF16), repeat, preferred_element_type=F32
+    )[0:1]
+    valid = jnp.sum(seq, axis=1, keepdims=True)
+    inv_ref[...] = 1.0 / jnp.maximum(valid * rj_ref[...], 1.0)
+    more[2].wait()
     w32[...] = w_ref[...].astype(F32)
     for e in range(chans):
         wp_ref[e * chans : (e + 1) * chans, :] = w32[pl.ds(e, chans, stride=chans), :].astype(BF16)
-
-    def body(step, carry):
+    for step in range(steps):
         fetch(step).wait()
         for i in range(step_rows):
             at = step * step_rows + i
-            inverse = jnp.where(ri_ref[pl.ds(at, 1), :] > 0, inv_ref[...], 1.0)
+            inverse = jnp.where(ri_ref[at : at + 1, :] > 0, inv_ref[...], 1.0)
             scaled_ref[at] = (cot[at].astype(F32) * inverse).astype(BF16)
-        scaled = scaled_ref[pl.ds(step * step_rows, step_rows)].reshape(step_rows * j_rows, LANES)
+    more[3].wait()
+    more[4].wait()
+
+
+def inner_kernel(dims, after_left, after_right, scaled_ref, wp_ref, z_ref):
+    chans, groups, blocks, i_rows, j_rows, step_rows, sequences = dims
+    for step in range(i_rows // step_rows):
+        rows = slice(step * step_rows, (step + 1) * step_rows)
+        scaled = scaled_ref[rows].reshape(step_rows * j_rows, LANES)
         for pair in range(0, blocks, 2):
             part = lax.dot_general(
                 scaled,
@@ -101,11 +114,6 @@
                     z_ref[
                         step, a * j_rows : (a + 1) * j_rows, i * LANES : (i + 1) * LANES
                     ] = part[i * j_rows : (i + 1) * j_rows, k * LANES : (k + 1) * LANES]
-        return carry
-
-    lax.fori_loop(0, steps, body, 0, unroll=True)
-    more[1].wait()
-    more[2].wait()
 
 
 def outer_kernel(dims, n_row, n_col, *refs):
@@ -113,14 +121,12 @@
     tiles = sequences * chans // LANES
     width = sequences * chans
     j_pad = -(-j_rows // LANES) * LANES
-    ri_ref, rj_ref, keep_ref, scaled_ref, z_ref = refs[:5]
-    left_refs = refs[5 : 5 + n_col]
-    right_refs = refs[5 + n_col : 5 + n_col + n_row]
-    y_ref, rbt_ref = refs[5 + n_col + n_row : 7 + n_col + n_row]
+    ri_ref, rj_ref, keep_ref, scaled_ref = refs[:4]
+    left_refs = refs[4 : 4 + n_col]
+    right_refs = refs[4 + n_col : 4 + n_col + n_row]
+    y_ref, rbt_ref, diag_ref = refs[4 + n_col + n_row : 7 + n_col + n_row]
     send_refs = refs[7 + n_col + n_row : 7 + n_col + 2 * n_row]
-    flat, turned, lsplit, rbig, expand, diag, gwt, gwr, acc, gr_all = refs[
-        7 + n_col + 2 * n_row :
-    ]
+    flat, turned, lsplit, rbig, expand, gwt, gwr = refs[7 + n_col + 2 * n_row :]
     row, col = lax.axis_index("row"), lax.axis_index("col")
 
     piece = right_refs[0].shape[0]
@@ -156,7 +162,6 @@
     same = (source // chans == target // LANES) & (source % chans == target % chans)
     expand[...] = same.astype(F32).astype(BF16)
     gwt[...] = jnp.zeros_like(gwt)
-    acc[...] = jnp.zeros_like(acc)
     rows = step_rows * tiles
     pairs = step_rows * j_rows
     group = lane_group((tiles, LANES), chans)
@@ -172,19 +177,20 @@
             for lo in range(groups):
                 at = b * sequences + lo * tiles
                 for i in range(step_rows):
-                    diag[at : at + tiles, i * LANES : (i + 1) * LANES] = (
+                    diag_ref[step, at : at + tiles, i * LANES : (i + 1) * LANES] = (
                         spread[i * tiles : (i + 1) * tiles, lo * LANES : (lo + 1) * LANES] * chosen
                     )
         for pair in range(0, step_rows, 2):
             part = jnp.dot(
-                rbig[...], diag[:, pair * LANES : (pair + 2) * LANES], preferred_element_type=F32
+                rbig[...],
+                diag_ref[step, :, pair * LANES : (pair + 2) * LANES],
+                preferred_element_type=F32,
             ).astype(BF16)
             for k in range(2):
                 for a in range(blocks):
                     y_ref[step * step_rows + pair + k, :, a * LANES : (a + 1) * LANES] = part[
                         a * j_rows : (a + 1) * j_rows, k * LANES : (k + 1) * LANES
                     ]
-        acc[...] += lax.dot_general(diag[...], z_ref[step], NT, preferred_element_type=F32)
         block = pl.ds(step * step_rows, step_rows)
         scaled_t = scaled_ref[block].reshape(pairs, LANES).T
         y_flat = y_ref[block].reshape(pairs, blocks * LANES)
@@ -198,6 +204,25 @@
             gwr[pl.ds(k * groups + q, chans, stride=chans), :] = turned_tile[
                 q * chans : (q + 1) * chans
             ]
+    owned = chans * chans // n_row
+    for k in range(n_row):
+        at = pl.multiple_of(send_to(row, k, n_row) * owned, owned)
+        send_refs[k][...] = gwr[pl.ds(at, owned), :].astype(BF16)
+
+
+def right_kernel(dims, n_row, *refs):
+    chans, groups, blocks, i_rows, j_rows, step_rows, sequences = dims
+    tiles = sequences * chans // LANES
+    j_pad = -(-j_rows // LANES) * LANES
+    after, z_ref, diag_ref = refs[:3]
+    send_refs = refs[3 : 3 + n_row]
+    acc, turned, gr_all = refs[3 + n_row :]
+    for step in range(i_rows // step_rows):
+        part = lax.dot_general(diag_ref[step], z_ref[step], NT, preferred_element_type=F32)
+        if step:
+            acc[...] += part
+        else:
+            acc[...] = part
     for a in range(blocks):
         at, shift = divmod(a * j_rows, LANES)
         mine = acc[:, at * LANES : at * LANES + j_pad]
@@ -212,14 +237,11 @@
     for t in range(tiles):
         lanes = slice(t * LANES, (t + 1) * LANES)
         gr_all[pl.ds(t, j_rows, stride=tiles), :] = turned[lanes, :].T[:j_rows]
-    right_owned = j_rows * tiles // n_row
-    weight_owned = chans * chans // n_row
+    row = lax.axis_index("row")
+    owned = j_rows * tiles // n_row
     for k in range(n_row):
-        owner = send_to(row, k, n_row)
-        at = pl.multiple_of(owner * right_owned, right_owned)
-        send_refs[k][:right_owned, :] = gr_all[pl.ds(at, right_owned), :].astype(BF16)
-        at = pl.multiple_of(owner * weight_owned, weight_owned)
-        send_refs[k][right_owned:, :] = gwr[pl.ds(at, weight_owned), :].astype(BF16)
+        at = pl.multiple_of(send_to(row, k, n_row) * owned, owned)
+        send_refs[k][...] = gr_all[pl.ds(at, owned), :].astype(BF16)
 
 
 def left_kernel(dims, z_ref, rbt_ref, gl_all):
@@ -271,30 +293,21 @@
 
 
 def middle_kernel(dims, n_row, n_col, *refs):
-    chans, groups, blocks, i_rows, j_rows, step_rows, sequences = dims
-    tiles = sequences * chans // LANES
-    rj_ref, keep_ref, gl_ref = refs[:3]
-    came = refs[3 : 3 + n_row]
-    gr_out = refs[3 + n_row]
-    send_refs = refs[4 + n_row : 4 + n_row + n_col]
-    whole = refs[4 + n_row + n_col]
-    row, col = lax.axis_index("row"), lax.axis_index("col")
+    gl_ref, came = refs[0], refs[1 : 1 + n_row]
+    send_refs, whole = refs[1 + n_row : 1 + n_row + n_col], refs[1 + n_row + n_col]
+    col = lax.axis_index("col")
     whole[...] = sum_of(came)
-    left_owned = i_rows * tiles // n_col
-    right_owned = j_rows * tiles // n_row
-    weight_owned = (whole.shape[0] - right_owned) // n_col
+    left_owned = gl_ref.shape[0] // n_col
+    weight_owned = whole.shape[0] // n_col
     for k in range(n_col):
         owner = send_to(col, k, n_col)
         at = pl.multiple_of(owner * left_owned, left_owned)
         send_refs[k][:left_owned, :] = gl_ref[pl.ds(at, left_owned), :]
-        at = pl.multiple_of(right_owned + owner * weight_owned, 8)
+        at = pl.multiple_of(owner * weight_owned, 8)
         send_refs[k][left_owned:, :] = whole[pl.ds(at, weight_owned), :].astype(BF16)
-    own = gr_out.shape[0]
-    rows = rj_ref[pl.ds(pl.multiple_of(row * own, 8), own), :]
-    write_rows(whole, rows, keep_ref, gr_out, tiles)
-
-
-def pair_kernel(dims, ri_ref, y_ref, wp_ref, inv_ref, out_ref, staged, sems):
+
+
+def pair_kernel(dims, after, ri_ref, y_ref, wp_ref, inv_ref, out_ref, staged, sems):
     chans, groups, blocks, i_rows, j_rows, step_rows, sequences = dims
     pairs = step_rows * j_rows
     steps = i_rows // step_rows
@@ -321,11 +334,15 @@
 def final_kernel(dims, n_row, n_col, *refs):
     chans, groups, blocks, i_rows, j_rows, step_rows, sequences = dims
     tiles = sequences * chans // LANES
-    ri_ref, keep_ref = refs[:2]
-    came = refs[2 : 2 + n_col]
-    gl_out, gw_out, whole = refs[2 + n_col :]
+    ri_ref, rj_ref, keep_ref = refs[:3]
+    row_came, col_came = refs[3 : 3 + n_row], refs[3 + n_row : 3 + n_row + n_col]
+    gl_out, gr_out, gw_out, whole, right = refs[3 + n_col + n_row :]
+    right[...] = sum_of(row_came)
+    own = gr_out.shape[0]
+    first = pl.multiple_of(lax.axis_index("row") * own, 8)
+    write_rows(right, rj_ref[pl.ds(first, own), :], keep_ref, gr_out, tiles)
+    whole[...] = sum_of(col_came)
     own = gl_out.shape[0]
-    whole[...] = sum_of(came)
     gw_out[...] = whole[own * tiles :, :]
     first = pl.multiple_of(lax.axis_index("col") * own, 8)
     write_rows(whole, ri_ref[pl.ds(first, own), :], keep_ref, gl_out, tiles)
@@ -339,8 +356,16 @@
     return came
 
 
-def smem():
-    return pl.BlockSpec(memory_space=pltpu.SMEM)
+def gather(block, axis, n):
+    if n & (n - 1):
+        return exchange([block] * n, axis)
+    held = {0: block}
+    bit = n // 2
+    while bit:
+        flips = [(s, s ^ bit) for s in range(n)]
+        held |= {k ^ bit: lax.ppermute(held[k], axis, flips) for k in sorted(held)}
+        bit //= 2
+    return [held[k] for k in range(n)]
 
 
 def vmem(count=1):
@@ -375,16 +400,16 @@
     own_left, own_right = left_act.shape[0], right_act.shape[0]
     macs = i_rows * j_rows * inner * pair_width
 
-    lefts = exchange([left_act] * n_col, "col")
-    rights = exchange([right_act] * n_row, "row")
-
-    scaled, z, inverse, weight, keep, i_keep, j_keep, lefts[0], rights[0] = pl.pallas_call(
-        functools.partial(inner_kernel, dims),
-        in_specs=[smem(), smem()] + [hbm()] * 4,
-        out_specs=vmem(9),
+    lefts = gather(left_act, "col", n_col)
+    rights = gather(right_act, "row", n_row)
+
+    mask_row = (res_mask.reshape(1, -1), row_mask.reshape(1, -1))
+    scaled, inverse, weight, keep, i_keep, j_keep, lefts[0], rights[0] = pl.pallas_call(
+        functools.partial(scale_kernel, dims),
+        in_specs=[hbm()] * 6,
+        out_specs=vmem(8),
         out_shape=[
             pltpu.VMEM(cotangent.shape, BF16),
-            pltpu.VMEM((steps, span, step_rows * LANES), BF16),
             pltpu.VMEM((j_rows, LANES), F32),
             pltpu.VMEM(out_weight.shape, BF16),
             pltpu.VMEM((1, width), F32),
@@ -394,45 +419,55 @@
             pltpu.VMEM(right_act.shape, BF16),
         ],
         scratch_shapes=[
+            pltpu.VMEM((1, res_mask.shape[0]), jnp.int32),
+            pltpu.VMEM((1, sequences), jnp.int32),
             pltpu.VMEM(out_weight.shape, BF16),
             pltpu.VMEM(out_weight.shape, F32),
             pltpu.VMEM(cotangent.shape, BF16),
             pltpu.SemaphoreType.DMA((steps,)),
-            pltpu.SemaphoreType.DMA((3,)),
-        ],
-        compiler_params=params(16),
+            pltpu.SemaphoreType.DMA((5,)),
+        ],
+        compiler_params=params(12),
+        cost_estimate=cost(macs, 6 * 2**20),
+        name="scale",
+    )(*map(in_hbm, (*mask_row, cotangent, out_weight, left_act, right_act)))
+
+    z = pl.pallas_call(
+        functools.partial(inner_kernel, dims),
+        in_specs=[hbm()] * 2 + vmem(2),
+        out_specs=vmem()[0],
+        out_shape=pltpu.VMEM((steps, span, step_rows * LANES), BF16),
+        compiler_params=params(12),
         cost_estimate=cost(2 * macs, 12 * 2**20),
         name="inner",
-    )(*map(in_hbm, (res_mask, row_mask, cotangent, out_weight, left_act, right_act)))
-
-    row_piece = own_right * tiles + inner // n_row
+    )(lefts[n_col // 2], rights[n_row // 2], scaled, weight)
+
+    owned_w = inner // n_row
     outs = pl.pallas_call(
         functools.partial(outer_kernel, dims, n_row, n_col),
-        in_specs=vmem(5 + n_col + n_row),
-        out_specs=vmem(2 + n_row),
+        in_specs=vmem(4 + n_col + n_row),
+        out_specs=vmem(3 + n_row),
         out_shape=[
             pltpu.VMEM((i_rows, j_rows, inner), BF16),
             pltpu.VMEM((depth, span), BF16),
+            pltpu.VMEM((steps, depth, step_rows * LANES), BF16),
         ]
-        + [pltpu.VMEM((row_piece, LANES), BF16)] * n_row,
+        + [pltpu.VMEM((owned_w, LANES), BF16)] * n_row,
         scratch_shapes=[
             pltpu.VMEM((max(i_rows, j_rows), width), F32),
             pltpu.VMEM((width, j_pad), F32),
             pltpu.VMEM((i_rows * tiles, LANES), F32),
             pltpu.VMEM((span, depth), BF16),
             pltpu.VMEM((LANES, groups * LANES), BF16),
-            pltpu.VMEM((depth, step_rows * LANES), BF16),
             pltpu.VMEM((pair_width, inner), F32),
             pltpu.VMEM((inner, pair_width), F32),
-            pltpu.VMEM((depth, span), F32),
-            pltpu.VMEM((j_rows * tiles, LANES), F32),
-        ],
-        compiler_params=params(24),
-        cost_estimate=cost(6 * macs, 16 * 2**20),
+        ],
+        compiler_params=params(18),
+        cost_estimate=cost(4 * macs, 16 * 2**20),
         name="outer",
-    )(i_keep, j_keep, keep, scaled, z, *lefts, *rights)
-    y, right_turned = outs[:2]
-    row_came = exchange(outs[2:], "row")
+    )(i_keep, j_keep, keep, scaled, *lefts, *rights)
+    y, right_turned, diag = outs[:3]
+    weight_came = exchange(outs[3:], "row")
 
     left_all = pl.pallas_call(
         functools.partial(left_kernel, dims),
@@ -444,26 +479,38 @@
         name="left",
     )(z, right_turned)
 
-    col_piece = own_left * tiles + inner // n_row // n_col
+    col_piece = own_left * tiles + owned_w // n_col
     outs = pl.pallas_call(
         functools.partial(middle_kernel, dims, n_row, n_col),
-        in_specs=vmem(3 + n_row),
-        out_specs=vmem(1 + n_col),
-        out_shape=[jax.ShapeDtypeStruct((own_right, width), F32)]
-        + [pltpu.VMEM((col_piece, LANES), BF16)] * n_col,
-        scratch_shapes=[
-            pltpu.VMEM((row_piece, LANES), F32),
-        ],
+        in_specs=vmem(1 + n_row),
+        out_specs=vmem(n_col),
+        out_shape=[pltpu.VMEM((col_piece, LANES), BF16)] * n_col,
+        scratch_shapes=[pltpu.VMEM((owned_w, LANES), F32)],
         compiler_params=params(4),
         cost_estimate=cost(0, 2**20),
         name="middle",
-    )(j_keep, keep, left_all, *row_came)
-    grad_right = outs[0]
-    col_came = exchange(outs[1:], "col")
+    )(left_all, *weight_came)
+    col_came = exchange(outs, "col")
+
+    outs = pl.pallas_call(
+        functools.partial(right_kernel, dims, n_row),
+        in_specs=[hbm()] + vmem(2),
+        out_specs=vmem(n_row),
+        out_shape=[pltpu.VMEM((own_right * tiles, LANES), BF16)] * n_row,
+        scratch_shapes=[
+            pltpu.VMEM((depth, span), F32),
+            pltpu.VMEM((width, j_pad), F32),
+            pltpu.VMEM((j_rows * tiles, LANES), F32),
+        ],
+        compiler_params=params(18),
+        cost_estimate=cost(2 * macs, 8 * 2**20),
+        name="right",
+    )(outs[0], z, diag)
+    row_came = exchange(outs, "row")
 
     pair_out = pl.pallas_call(
         functools.partial(pair_kernel, dims),
-        in_specs=vmem(4),
+        in_specs=[hbm()] + vmem(4),
         out_specs=hbm(),
         out_shape=jax.ShapeDtypeStruct(cotangent.shape, BF16),
         scratch_shapes=[
@@ -473,23 +520,25 @@
         compiler_params=params(16),
         cost_estimate=cost(2 * macs, 12 * 2**20),
         name="pair",
-    )(i_keep, y, weight, inverse)
-
-    grad_left, grad_weight = pl.pallas_call(
+    )(outs[0], i_keep, y, weight, inverse)
+
+    grad_left, grad_right, grad_weight = pl.pallas_call(
         functools.partial(final_kernel, dims, n_row, n_col),
-        in_specs=vmem(2 + n_col),
-        out_specs=vmem(2),
+        in_specs=vmem(3 + n_col + n_row),
+        out_specs=vmem(3),
         out_shape=[
             jax.ShapeDtypeStruct((own_left, width), F32),
-            jax.ShapeDtypeStruct((inner // n_row // n_col, pair_width), F32),
+            jax.ShapeDtypeStruct((own_right, width), F32),
+            jax.ShapeDtypeStruct((owned_w // n_col, pair_width), F32),
         ],
         scratch_shapes=[
             pltpu.VMEM((col_piece, LANES), F32),
+            pltpu.VMEM((own_right * tiles, LANES), F32),
         ],
         compiler_params=params(4),
         cost_estimate=cost(0, 2**20),
         name="final_sums",
-    )(i_keep, keep, *col_came)
+    )(i_keep, j_keep, keep, *row_came, *col_came)
     return (pair_out, grad_left, grad_right, grad_weight)
 
 

time: 46.5 us -> 44.2 us (0.951)
  waiting for transfers between devices: 7.49 us -> 4.54 us
  starting transfers between devices: 14.1 us -> 16.3 us
  Pallas kernels: 23.9 us -> 22.5 us
    ppermute x0 -> x6, starting transfers between devices: none -> 7.91 us  [gather(): held |= {k ^ bit: lax.ppermute(held[k], axis, flips) for k in sorted(held)}]
    ppermute x12 -> x9, starting transfers between devices: 14.1 us -> 8.36 us  [exchange(): lax.ppermute(pieces[k], axis, [(s, send_to(s, k, n)) for s in range(n)])]
    ppermute x12 -> x9, waiting for transfers between devices: 7.49 us -> 3.6 us  [exchange(): lax.ppermute(pieces[k], axis, [(s, send_to(s, k, n)) for s in range(n)])]
    pallas_call x1, Pallas kernels: 10.1 us -> 7.48 us  [shards(): pl.pallas_call(functools.partial(outer_kernel, dims, n_row, n_col), in_sp...]
    pallas_call x2 -> x4, Pallas kernels: 9.57 us -> 11.6 us  [the longest x1 3.61 us: shards(): pl.pallas_call(functools.partial(right_kernel, dims, n_row), in_specs=[hb...]
    ppermute x0 -> x6, waiting for transfers between devices: none -> 0.94 us  [gather(): held |= {k ^ bit: lax.ppermute(held[k], axis, flips) for k in sorted(held)}]
    pallas_call x1, Pallas kernels: 0.8 us -> 0.05 us  [shards(): pl.pallas_call(functools.partial(middle_kernel, dims, n_row, n_col), in_s...]
  transfers between devices with their start and end apart: 12 -> 15, of which waited for: 3 -> 5; matrix products, arithmetic and copies ran while one was open for 0% -> 0% of each run, Pallas kernels for 27% -> 24%
where the time goes in v5:
time: 44.2 us; the launch traced here: 44.1 us
  Pallas kernels  22.5 us (51%)
  starting transfers between devices  16.3 us (37%)
  waiting for transfers between devices  4.54 us (10%)
  between operations  0.76 us (2%)
    ppermute x9, starting transfers between devices, exchange(): lax.ppermute(pieces[k], axis, [(s, send_to(s, k, n)) for s in range(n)])  8.36 us
    ppermute x6, starting transfers between devices, gather(): held |= {k ^ bit: lax.ppermute(held[k], axis, flips) for k in sorted(held)}  7.91 us
    pallas_call x1, Pallas kernels, shards(): pl.pallas_call(functools.partial(outer_kernel, dims, n_row, n_col), in_sp...  7.48 us
    pallas_call x1, Pallas kernels, shards(): pl.pallas_call(functools.partial(right_kernel, dims, n_row), in_specs=[hb...  3.61 us
    ppermute x9, waiting for transfers between devices, exchange(): lax.ppermute(pieces[k], axis, [(s, send_to(s, k, n)) for s in range(n)])  3.6 us
    pallas_call x1, Pallas kernels, shards(): pl.pallas_call(functools.partial(pair_kernel, dims), in_specs=[hbm()] + v...  3.12 us
    pallas_call x1, Pallas kernels, shards(): pl.pallas_call(functools.partial(inner_kernel, dims), in_specs=[hbm()] *...  2.87 us
    pallas_call x1, Pallas kernels, shards(): pl.pallas_call(functools.partial(left_kernel, dims), in_specs=vmem(2), ou...  2.51 us
  transfers between devices with their start and end apart: 15, of which 5 were waited for; matrix products, arithmetic and copies ran while one was open for 0% of the time, Pallas kernels for 24%

profile of v5, /device:TPU:0, one launch (start us, length us, event | category | flops | bytes accessed | tf_op | source)
XLA Modules:
  0.0 44.1 jit_solution(15678670448582736276)
XLA Ops:
  0.6 4.1 %collective-permute-start = (bf16[16,2048]{1,0:T(8,128)(2,1)}, bf16[16,2048]{1,0:T(8,128)(2,1)S(1)}, u32[]{:S(2)}, u32[]{:S(2)}) collective-permute-start(bf16[16,2048]{1,0:T(8,128)(2,1)} %refs_4_.1), channel_id=1, source_target_pairs={{0,2},{1,3},{2,0},{3,1},{4,6},{5,7},{6,4},{7,5},{8,10},{9,11},{10,... | collective-permute-start | bytes 196616 | tf_op jit(solution)/shard_map/ppermute | solution.py:366
  4.7 1.5 %collective-permute-start.1 = (bf16[16,2048]{1,0:T(8,128)(2,1)}, bf16[16,2048]{1,0:T(8,128)(2,1)S(1)}, u32[]{:S(2)}, u32[]{:S(2)}) collective-permute-start(bf16[16,2048]{1,0:T(8,128)(2,1)} %refs_5_.1), channel_id=1, source_target_pairs={{0,8},{4,12},{8,0},{12,4},{1,9},{5,13},{9,1},{13,5},{2,10},{6,14},... | collective-permute-start | bytes 196616 | tf_op jit(solution)/shard_map/ppermute | solution.py:366
  6.2 1.6 %collective-permute-start.2 = (bf16[16,2048]{1,0:T(8,128)(2,1)}, bf16[16,2048]{1,0:T(8,128)(2,1)S(1)}, u32[]{:S(2)}, u32[]{:S(2)}) collective-permute-start(bf16[16,2048]{1,0:T(8,128)(2,1)} %refs_4_.1), channel_id=1, source_target_pairs={{0,1},{1,0},{2,3},{3,2},{4,5},{5,4},{6,7},{7,6},{8,9},{9,8},{10,11... | collective-permute-start | bytes 196616 | tf_op jit(solution)/shard_map/ppermute | solution.py:366
  7.8 2.0 %scale.1 = (bf16[64,64,128]{2,1,0:T(8,128)(2,1)S(1)}, f32[64,128]{1,0:T(8,128)S(1)}, bf16[1024,128]{1,0:T(8,128)(2,1)S(1)}, f32[1,2048]{1,0:T(1,128)S(1)}, f32[6...) custom-call(s32[1,256]{1,0:T(1,128)} %bitcast.2, ...), custom_call_target="tpu_custom_call" | custom-call | flops 536870912 | bytes 6291456 | tf_op jit(solution)/shard_map/scale/pallas_call | solution.py:407
  9.9 0.5 %collective-permute-start.3 = (bf16[16,2048]{1,0:T(8,128)(2,1)S(1)}, bf16[16,2048]{1,0:T(8,128)(2,1)S(1)}, u32[]{:S(2)}, u32[]{:S(2)}) collective-permute-start(bf16[16,2048]{1,0:T(8,128)(2,1)S(1)} %collective-permute-done.after_left.refs_6_), channel_id=1, source_target_pairs={{0,1},{1,0},{2,3},{3,2},{4,5},{5,4},{6,7},{7,6},{8,9},{9,8},{10,11... | collective-permute-start | bytes 196616 | tf_op jit(solution)/shard_map/ppermute | solution.py:366
  10.4 0.2 collective-permute-start.5
  10.6 2.9 %inner.1.z_ref.refs_1_ = bf16[8,512,1024]{2,1,0:T(8,128)(2,1)S(1)} custom-call(bf16[16,2048]{1,0:T(8,128)(2,1)S(1)} %collective-permute-done.after_left.refs_6_, bf16[16,2048]{1,0:T(8,128)(2,1)S(1)} %collective-permute-done.1.after_right.refs_10_, bf16[64,64,128]{2,1,0:T(8,128)(2,1)S(1)} %get-tuple-element.30.scaled_ref.refs_3_, ...), custom_call_target="tpu_custom_call" | custom-call | flops 1073741824 | bytes 12582912 | tf_op jit(solution)/shard_map/inner/pallas_call | solution.py:435
  13.5 0.9 %collective-permute-done.3.refs_7_ = bf16[16,2048]{1,0:T(8,128)(2,1)S(1)} collective-permute-done((bf16[16,2048]{1,0:T(8,128)(2,1)S(1)}, bf16[16,2048]{1,0:T(8,128)(2,1)S(1)}, u32[]{:S(2)}, u32[]{:S(2)}) %collective-permute-start.3) | collective-permute-done | bytes 65568 | tf_op jit(solution)/shard_map/ppermute | solution.py:366
  14.4 7.5 %outer.1 = (bf16[64,64,1024]{2,1,0:T(8,128)(2,1)S(1)}, bf16[256,512]{1,0:T(8,128)(2,1)S(1)}, bf16[8,256,1024]{2,1,0:T(8,128)(2,1)S(1)}, bf16[256,128]{1,0:T(8,12...) custom-call(f32[64,128]{1,0:T(8,128)S(1)} %get-tuple-element.32.refs_0_.ri_ref, ...), custom_call_target="tpu_custom_call" | custom-call | flops 2147483648 | bytes 16777216 | tf_op jit(solution)/shard_map/outer/pallas_call | solution.py:446
  22.0 0.6 %collective-permute-start.7 = (bf16[256,128]{1,0:T(8,128)(2,1)S(1)}, bf16[256,128]{1,0:T(8,128)(2,1)S(1)}, u32[]{:S(2)}, u32[]{:S(2)}) collective-permute-start(bf16[256,128]{1,0:T(8,128)(2,1)S(1)} %get-tuple-element.40), channel_id=1, source_target_pairs={{0,8},{4,12},{8,0},{12,4},{1,9},{5,13},{9,1},{13,5},{2,10},{6,14},... | collective-permute-start | bytes 196616 | tf_op jit(solution)/shard_map/ppermute | solution.py:355
  22.6 1.3 %collective-permute-start.8 = (bf16[256,128]{1,0:T(8,128)(2,1)S(1)}, bf16[256,128]{1,0:T(8,128)(2,1)S(1)}, u32[]{:S(2)}, u32[]{:S(2)}) collective-permute-start(bf16[256,128]{1,0:T(8,128)(2,1)S(1)} %get-tuple-element.41), channel_id=1, source_target_pairs={{0,12},{4,8},{8,4},{12,0},{1,13},{5,9},{9,5},{13,1},{2,14},{6,10},... | collective-permute-start | bytes 196616 | tf_op jit(solution)/shard_map/ppermute | solution.py:355
  23.9 2.5 %left.1.refs_0_ = bf16[1024,128]{1,0:T(8,128)(2,1)S(1)} custom-call(bf16[8,512,1024]{2,1,0:T(8,128)(2,1)S(1)} %inner.1.z_ref.refs_1_, bf16[256,512]{1,0:T(8,128)(2,1)S(1)} %get-tuple-element.37.rbt_ref), custom_call_target="tpu_custom_call" | custom-call | flops 1073741824 | bytes 8388608 | tf_op jit(solution)/shard_map/left/pallas_call | solution.py:472
  26.4 0.6 %collective-permute-done.7.refs_3_ = bf16[256,128]{1,0:T(8,128)(2,1)S(1)} collective-permute-done((bf16[256,128]{1,0:T(8,128)(2,1)S(1)}, bf16[256,128]{1,0:T(8,128)(2,1)S(1)}, u32[]{:S(2)}, u32[]{:S(2)}) %collective-permute-start.7) | collective-permute-done | bytes 65568 | tf_op jit(solution)/shard_map/ppermute | solution.py:355
  27.0 0.5 %collective-permute-done.8.refs_4_ = bf16[256,128]{1,0:T(8,128)(2,1)S(1)} collective-permute-done((bf16[256,128]{1,0:T(8,128)(2,1)S(1)}, bf16[256,128]{1,0:T(8,128)(2,1)S(1)}, u32[]{:S(2)}, u32[]{:S(2)}) %collective-permute-start.8) | collective-permute-done | bytes 65568 | tf_op jit(solution)/shard_map/ppermute | solution.py:355
  27.5 3.6 %right.1 = (bf16[256,128]{1,0:T(8,128)(2,1)S(1)}, bf16[256,128]{1,0:T(8,128)(2,1)S(1)}, bf16[256,128]{1,0:T(8,128)(2,1)S(1)}, bf16[256,128]{1,0:T(8,128)(2,1)S(1)}) custom-call(bf16[320,128]{1,0:T(8,128)(2,1)S(1)} %get-tuple-element.42.refs_0_.refs_7_, bf16[8,512,1024]{2,1,0:T(8,128)(2,1)S(1)} %inner.1.z_ref.refs_1_, ...), custom_call_target="tpu_custom_call" | custom-call | flops 1073741824 | bytes 8388608 | tf_op jit(solution)/shard_map/right/pallas_call | solution.py:495
  31.1 0.7 %collective-permute-start.10 = (bf16[256,128]{1,0:T(8,128)(2,1)S(1)}, bf16[256,128]{1,0:T(8,128)(2,1)S(1)}, u32[]{:S(2)}, u32[]{:S(2)}) collective-permute-start(bf16[256,128]{1,0:T(8,128)(2,1)S(1)} %get-tuple-element.48), channel_id=1, source_target_pairs={{0,8},{4,12},{8,0},{12,4},{1,9},{5,13},{9,1},{13,5},{2,10},{6,14},... | collective-permute-start | bytes 196616 | tf_op jit(solution)/shard_map/ppermute | solution.py:355
  31.9 0.9 %collective-permute-start.11 = (bf16[256,128]{1,0:T(8,128)(2,1)S(1)}, bf16[256,128]{1,0:T(8,128)(2,1)S(1)}, u32[]{:S(2)}, u32[]{:S(2)}) collective-permute-start(bf16[256,128]{1,0:T(8,128)(2,1)S(1)} %get-tuple-element.49), channel_id=1, source_target_pairs={{0,12},{4,8},{8,4},{12,0},{1,13},{5,9},{9,5},{13,1},{2,14},{6,10},... | collective-permute-start | bytes 196616 | tf_op jit(solution)/shard_map/ppermute | solution.py:355
  32.8 0.5 %collective-permute-start.9 = (bf16[256,128]{1,0:T(8,128)(2,1)S(1)}, bf16[256,128]{1,0:T(8,128)(2,1)S(1)}, u32[]{:S(2)}, u32[]{:S(2)}) collective-permute-start(bf16[256,128]{1,0:T(8,128)(2,1)S(1)} %get-tuple-element.47), channel_id=1, source_target_pairs={{0,4},{4,0},{8,12},{12,8},{1,5},{5,1},{9,13},{13,9},{2,6},{6,2},{1... | collective-permute-start | bytes 196616 | tf_op jit(solution)/shard_map/ppermute | solution.py:355
  33.4 0.4 collective-permute-start.12
  33.8 2.1 %collective-permute-start.13 = (bf16[320,128]{1,0:T(8,128)(2,1)S(1)}, bf16[320,128]{1,0:T(8,128)(2,1)S(1)}, u32[]{:S(2)}, u32[]{:S(2)}) collective-permute-start(bf16[320,128]{1,0:T(8,128)(2,1)S(1)} %get-tuple-element.51), channel_id=1, source_target_pairs={{0,2},{1,3},{2,0},{3,1},{4,6},{5,7},{6,4},{7,5},{8,10},{9,11},{10,... | collective-permute-start | bytes 245768 | tf_op jit(solution)/shard_map/ppermute | solution.py:355
  36.1 1.7 %collective-permute-start.14 = (bf16[320,128]{1,0:T(8,128)(2,1)S(1)}, bf16[320,128]{1,0:T(8,128)(2,1)S(1)}, u32[]{:S(2)}, u32[]{:S(2)}) collective-permute-start(bf16[320,128]{1,0:T(8,128)(2,1)S(1)} %get-tuple-element.52), channel_id=1, source_target_pairs={{0,3},{1,2},{2,1},{3,0},{4,7},{5,6},{6,5},{7,4},{8,11},{9,10},{10,... | collective-permute-start | bytes 245768 | tf_op jit(solution)/shard_map/ppermute | solution.py:355
  37.7 3.1 %pair.1 = bf16[64,64,128]{2,1,0:T(8,128)(2,1)} custom-call(bf16[256,128]{1,0:T(8,128)(2,1)S(1)} %get-tuple-element.44.after.refs_3_, f32[64,128]{1,0:T(8,128)S(1)} %get-tuple-element.32.refs_0_.ri_ref, bf16[64,64,1024]{2,1,0:T(8,128)(2,1)S(1)} %get-tuple-element.45.y_ref, bf16[1024,128]{1,0:T(8,128)(2,1)S(1)} %get-tuple-element.31.wp_ref, ...), custom_call_target="tpu_custom_call" | custom-call | flops 1073741824 | bytes 12582912 | tf_op jit(solution)/shard_map/pair/pallas_call | solution.py:511
  40.9 2.3 %collective-permute-done.13.refs_9_ = bf16[320,128]{1,0:T(8,128)(2,1)S(1)} collective-permute-done((bf16[320,128]{1,0:T(8,128)(2,1)S(1)}, bf16[320,128]{1,0:T(8,128)(2,1)S(1)}, u32[]{:S(2)}, u32[]{:S(2)}) %collective-permute-start.13) | collective-permute-done | bytes 81952 | tf_op jit(solution)/shard_map/ppermute | solution.py:355
  43.2 0.8 %final_sums.1 = (f32[16,2048]{1,0:T(8,128)}, f32[16,2048]{1,0:T(8,128)}, f32[64,128]{1,0:T(8,128)}) custom-call(f32[64,128]{1,0:T(8,128)S(1)} %get-tuple-element.32.refs_0_.ri_ref, f32[64,128]{1,0:T(8,128)S(1)} %get-tuple-element.33.refs_1_, f32[1,2048]{1,0:T(1,128)S(1)} %get-tuple-element.34.refs_2_, bf16[256,128]{1,0:T(8,128)(2,1)S(1)} %get-tuple-element.44.after.refs_3_, ...), custom_call_target="tpu_custom_call" | custom-call | bytes 1048576 | tf_op jit(solution)/shard_map/final_sums/pallas_call | solution.py:525
  (14 shorter events, 0.3 us)
Async XLA Ops:
  0.6 9.2 %collective-permute-start = (bf16[16,2048]{1,0:T(8,128)(2,1)}, bf16[16,2048]{1,0:T(8,128)(2,1)S(1)}, u32[]{:S(2)}, u32[]{:S(2)}) collective-permute-start(bf16[16,2048]{1,0:T(8,128)(2,1)} %refs_4_.1), channel_id=1, source_target_pairs={{0,2},{1,3},{2,0},{3,1},{4,6},{5,7},{6,4},{7,5},{8,10},{9,11},{10,... | collective-permute-start | bytes 196616 | tf_op jit(solution)/shard_map/ppermute | solution.py:366
  4.7 5.7 %collective-permute-start.1 = (bf16[16,2048]{1,0:T(8,128)(2,1)}, bf16[16,2048]{1,0:T(8,128)(2,1)S(1)}, u32[]{:S(2)}, u32[]{:S(2)}) collective-permute-start(bf16[16,2048]{1,0:T(8,128)(2,1)} %refs_5_.1), channel_id=1, source_target_pairs={{0,8},{4,12},{8,0},{12,4},{1,9},{5,13},{9,1},{13,5},{2,10},{6,14},... | collective-permute-start | bytes 196616 | tf_op jit(solution)/shard_map/ppermute | solution.py:366
  6.2 7.3 %collective-permute-start.2 = (bf16[16,2048]{1,0:T(8,128)(2,1)}, bf16[16,2048]{1,0:T(8,128)(2,1)S(1)}, u32[]{:S(2)}, u32[]{:S(2)}) collective-permute-start(bf16[16,2048]{1,0:T(8,128)(2,1)} %refs_4_.1), channel_id=1, source_target_pairs={{0,1},{1,0},{2,3},{3,2},{4,5},{5,4},{6,7},{7,6},{8,9},{9,8},{10,11... | collective-permute-start | bytes 196616 | tf_op jit(solution)/shard_map/ppermute | solution.py:366
  7.8 5.7 %collective-permute-start.4 = (bf16[16,2048]{1,0:T(8,128)(2,1)}, bf16[16,2048]{1,0:T(8,128)(2,1)S(1)}, u32[]{:S(2)}, u32[]{:S(2)}) collective-permute-start(bf16[16,2048]{1,0:T(8,128)(2,1)} %refs_5_.1), channel_id=1, source_target_pairs={{0,4},{4,0},{8,12},{12,8},{1,5},{5,1},{9,13},{13,9},{2,6},{6,2},{1... | collective-permute-start | bytes 196616 | tf_op jit(solution)/shard_map/ppermute | solution.py:366
  9.9 4.6 %collective-permute-start.3 = (bf16[16,2048]{1,0:T(8,128)(2,1)S(1)}, bf16[16,2048]{1,0:T(8,128)(2,1)S(1)}, u32[]{:S(2)}, u32[]{:S(2)}) collective-permute-start(bf16[16,2048]{1,0:T(8,128)(2,1)S(1)} %collective-permute-done.after_left.refs_6_), channel_id=1, source_target_pairs={{0,1},{1,0},{2,3},{3,2},{4,5},{5,4},{6,7},{7,6},{8,9},{9,8},{10,11... | collective-permute-start | bytes 196616 | tf_op jit(solution)/shard_map/ppermute | solution.py:366
  10.4 4.1 %collective-permute-start.5 = (bf16[16,2048]{1,0:T(8,128)(2,1)S(1)}, bf16[16,2048]{1,0:T(8,128)(2,1)S(1)}, u32[]{:S(2)}, u32[]{:S(2)}) collective-permute-start(bf16[16,2048]{1,0:T(8,128)(2,1)S(1)} %collective-permute-done.1.after_right.refs_10_), channel_id=1, source_target_pairs={{0,4},{4,0},{8,12},{12,8},{1,5},{5,1},{9,13},{13,9},{2,6},{6,2},{1... | collective-permute-start | bytes 196616 | tf_op jit(solution)/shard_map/ppermute | solution.py:366
  21.9 4.5 %collective-permute-start.6 = (bf16[256,128]{1,0:T(8,128)(2,1)S(1)}, bf16[256,128]{1,0:T(8,128)(2,1)S(1)}, u32[]{:S(2)}, u32[]{:S(2)}) collective-permute-start(bf16[256,128]{1,0:T(8,128)(2,1)S(1)} %get-tuple-element.39), channel_id=1, source_target_pairs={{0,4},{4,0},{8,12},{12,8},{1,5},{5,1},{9,13},{13,9},{2,6},{6,2},{1... | collective-permute-start | bytes 196616 | tf_op jit(solution)/shard_map/ppermute | solution.py:355
  22.0 5.0 %collective-permute-start.7 = (bf16[256,128]{1,0:T(8,128)(2,1)S(1)}, bf16[256,128]{1,0:T(8,128)(2,1)S(1)}, u32[]{:S(2)}, u32[]{:S(2)}) collective-permute-start(bf16[256,128]{1,0:T(8,128)(2,1)S(1)} %get-tuple-element.40), channel_id=1, source_target_pairs={{0,8},{4,12},{8,0},{12,4},{1,9},{5,13},{9,1},{13,5},{2,10},{6,14},... | collective-permute-start | bytes 196616 | tf_op jit(solution)/shard_map/ppermute | solution.py:355
  22.6 4.9 %collective-permute-start.8 = (bf16[256,128]{1,0:T(8,128)(2,1)S(1)}, bf16[256,128]{1,0:T(8,128)(2,1)S(1)}, u32[]{:S(2)}, u32[]{:S(2)}) collective-permute-start(bf16[256,128]{1,0:T(8,128)(2,1)S(1)} %get-tuple-element.41), channel_id=1, source_target_pairs={{0,12},{4,8},{8,4},{12,0},{1,13},{5,9},{9,5},{13,1},{2,14},{6,10},... | collective-permute-start | bytes 196616 | tf_op jit(solution)/shard_map/ppermute | solution.py:355
  31.1 4.9 %collective-permute-start.10 = (bf16[256,128]{1,0:T(8,128)(2,1)S(1)}, bf16[256,128]{1,0:T(8,128)(2,1)S(1)}, u32[]{:S(2)}, u32[]{:S(2)}) collective-permute-start(bf16[256,128]{1,0:T(8,128)(2,1)S(1)} %get-tuple-element.48), channel_id=1, source_target_pairs={{0,8},{4,12},{8,0},{12,4},{1,9},{5,13},{9,1},{13,5},{2,10},{6,14},... | collective-permute-start | bytes 196616 | tf_op jit(solution)/shard_map/ppermute | solution.py:355
  31.9 9.0 %collective-permute-start.11 = (bf16[256,128]{1,0:T(8,128)(2,1)S(1)}, bf16[256,128]{1,0:T(8,128)(2,1)S(1)}, u32[]{:S(2)}, u32[]{:S(2)}) collective-permute-start(bf16[256,128]{1,0:T(8,128)(2,1)S(1)} %get-tuple-element.49), channel_id=1, source_target_pairs={{0,12},{4,8},{8,4},{12,0},{1,13},{5,9},{9,5},{13,1},{2,14},{6,10},... | collective-permute-start | bytes 196616 | tf_op jit(solution)/shard_map/ppermute | solution.py:355
  32.8 8.0 %collective-permute-start.9 = (bf16[256,128]{1,0:T(8,128)(2,1)S(1)}, bf16[256,128]{1,0:T(8,128)(2,1)S(1)}, u32[]{:S(2)}, u32[]{:S(2)}) collective-permute-start(bf16[256,128]{1,0:T(8,128)(2,1)S(1)} %get-tuple-element.47), channel_id=1, source_target_pairs={{0,4},{4,0},{8,12},{12,8},{1,5},{5,1},{9,13},{13,9},{2,6},{6,2},{1... | collective-permute-start | bytes 196616 | tf_op jit(solution)/shard_map/ppermute | solution.py:355
  33.4 7.5 %collective-permute-start.12 = (bf16[320,128]{1,0:T(8,128)(2,1)S(1)}, bf16[320,128]{1,0:T(8,128)(2,1)S(1)}, u32[]{:S(2)}, u32[]{:S(2)}) collective-permute-start(bf16[320,128]{1,0:T(8,128)(2,1)S(1)} %get-tuple-element.50), channel_id=1, source_target_pairs={{0,1},{1,0},{2,3},{3,2},{4,5},{5,4},{6,7},{7,6},{8,9},{9,8},{10,11... | collective-permute-start | bytes 245768 | tf_op jit(solution)/shard_map/ppermute | solution.py:355
  33.8 9.5 %collective-permute-start.13 = (bf16[320,128]{1,0:T(8,128)(2,1)S(1)}, bf16[320,128]{1,0:T(8,128)(2,1)S(1)}, u32[]{:S(2)}, u32[]{:S(2)}) collective-permute-start(bf16[320,128]{1,0:T(8,128)(2,1)S(1)} %get-tuple-element.51), channel_id=1, source_target_pairs={{0,2},{1,3},{2,0},{3,1},{4,6},{5,7},{6,4},{7,5},{8,10},{9,11},{10,... | collective-permute-start | bytes 245768 | tf_op jit(solution)/shard_map/ppermute | solution.py:355
  36.1 7.2 %collective-permute-start.14 = (bf16[320,128]{1,0:T(8,128)(2,1)S(1)}, bf16[320,128]{1,0:T(8,128)(2,1)S(1)}, u32[]{:S(2)}, u32[]{:S(2)}) collective-permute-start(bf16[320,128]{1,0:T(8,128)(2,1)S(1)} %get-tuple-element.52), channel_id=1, source_target_pairs={{0,3},{1,2},{2,1},{3,0},{4,7},{5,6},{6,5},{7,4},{8,11},{9,10},{10,... | collective-permute-start | bytes 245768 | tf_op jit(solution)/shard_map/ppermute | solution.py:355

commit v6 on v5

v6 whole, which is shorter than its diff:
```python
import functools

import jax
import jax.numpy as jnp
from jax import lax
from jax.experimental import pallas as pl
from jax.experimental.pallas import tpu as pltpu
from jax.sharding import PartitionSpec as P

LANES = 128
NT = (((1,), (1,)), ((), ()))
F32 = jnp.float32
BF16 = jnp.bfloat16


def params(mib):
    return pltpu.CompilerParams(vmem_limit_bytes=mib * 2**20)


def cost(flops, nbytes):
    return pl.CostEstimate(flops=int(flops), bytes_accessed=int(nbytes), transcendentals=0)


def cut(source, index, n, keep_ref, send_ref):
    rows = source.shape[0] // n
    for k in range(n):
        at = pl.multiple_of((index ^ k) * rows, rows)
        into = send_ref if k % 2 else keep_ref
        into[k // 2] = source[pl.ds(at, rows), :].astype(into.dtype)


def place(buffers, index, n, flat):
    for buffer, owners in zip(buffers, owners_of(n)):
        rows = buffer.shape[1]
        for k, owner in enumerate(owners):
            at = pl.multiple_of((index ^ owner) * rows, 8)
            flat[pl.ds(at, rows), :] = buffer[k].astype(F32)


def lane_group(shape, chans):
    return lax.broadcasted_iota(jnp.int32, shape, 1) // chans


def mask_rows(res_ref, first, count):
    shape = (count, res_ref.shape[1])
    row = lax.broadcasted_iota(jnp.int32, shape, 0) + first
    here = lax.broadcasted_iota(jnp.int32, shape, 1) == row
    chosen = jnp.where(here, res_ref[...].astype(F32), 0.0)
    return jnp.broadcast_to(jnp.sum(chosen, axis=1, keepdims=True), (count, LANES))


def scale_kernel(dims, *refs):
    chans, groups, blocks, i_rows, j_rows, step_rows, sequences = dims
    tiles = sequences * chans // LANES
    res_hbm, seq_hbm, cot_ref, w_hbm, left_hbm, right_hbm = refs[:6]
    scaled_ref, inv_ref, wp_ref, keep_ref, ri_ref, rj_ref, left_ref, right_ref = refs[6:14]
    res_ref, seq_ref, w_ref, w32, cot, sems, more_sems = refs[14:]
    steps = i_rows // step_rows

    def fetch(step):
        rows = pl.ds(step * step_rows, step_rows)
        return pltpu.make_async_copy(cot_ref.at[rows], cot.at[rows], sems.at[step])

    pairs = [
        (res_hbm, res_ref),
        (seq_hbm, seq_ref),
        (w_hbm, w_ref),
        (left_hbm, left_ref.at[0]),
        (right_hbm, right_ref.at[0]),
    ]
    more = [
        pltpu.make_async_copy(source, to, more_sems.at[k]) for k, (source, to) in enumerate(pairs)
    ]
    for copy in more[:3]:
        copy.start()
    for step in range(steps):
        fetch(step).start()
    for copy in more[3:]:
        copy.start()
    shape = (sequences, tiles * LANES)
    own = lax.broadcasted_iota(jnp.int32, shape, 1) // chans
    repeat = (own == lax.broadcasted_iota(jnp.int32, shape, 0)).astype(F32).astype(BF16)
    more[0].wait()
    ri_ref[...] = mask_rows(res_ref, lax.axis_index("row") * i_rows, i_rows)
    rj_ref[...] = mask_rows(res_ref, lax.axis_index("col") * j_rows, j_rows)
    more[1].wait()
    seq = seq_ref[...].astype(F32)
    keep_ref[...] = jnp.dot(
        jnp.broadcast_to(seq, (8, sequences)).astype(BF16), repeat, preferred_element_type=F32
    )[0:1]
    valid = jnp.sum(seq, axis=1, keepdims=True)
    inv_ref[...] = 1.0 / jnp.maximum(valid * rj_ref[...], 1.0)
    more[2].wait()
    w32[...] = w_ref[...].astype(F32)
    for e in range(chans):
        wp_ref[e * chans : (e + 1) * chans, :] = w32[pl.ds(e, chans, stride=chans), :].astype(BF16)
    for step in range(steps):
        fetch(step).wait()
        for i in range(step_rows):
            at = step * step_rows + i
            inverse = jnp.where(ri_ref[at : at + 1, :] > 0, inv_ref[...], 1.0)
            scaled_ref[at] = (cot[at].astype(F32) * inverse).astype(BF16)
    more[3].wait()
    more[4].wait()


def inner_kernel(dims, after, scaled_ref, wp_ref, z_ref):
    chans, groups, blocks, i_rows, j_rows, step_rows, sequences = dims
    for step in range(i_rows // step_rows):
        rows = slice(step * step_rows, (step + 1) * step_rows)
        scaled = scaled_ref[rows].reshape(step_rows * j_rows, LANES)
        for pair in range(0, blocks, 2):
            part = lax.dot_general(
                scaled,
                wp_ref[pair * LANES : (pair + 2) * LANES, :],
                NT,
                preferred_element_type=F32,
            ).astype(BF16)
            for k in range(2):
                a = pair + k
                for i in range(step_rows):
                    z_ref[
                        step, a * j_rows : (a + 1) * j_rows, i * LANES : (i + 1) * LANES
                    ] = part[i * j_rows : (i + 1) * j_rows, k * LANES : (k + 1) * LANES]


def outer_kernel(dims, n_row, n_col, *refs):
    chans, groups, blocks, i_rows, j_rows, step_rows, sequences = dims
    tiles = sequences * chans // LANES
    ri_ref, keep_ref, scaled_ref, rbig, left_held, left_came = refs[:6]
    y_ref, diag_ref, keep_out, send_out = refs[6:10]
    flat, lsplit, expand, gwt, gwr = refs[10:]
    place((left_held, left_came), lax.axis_index("col"), n_col, flat)
    for t in range(tiles):
        lanes = slice(t * LANES, (t + 1) * LANES)
        masked = flat[0:i_rows, lanes] * ri_ref[...] * keep_ref[:, lanes]
        lsplit[pl.ds(t, i_rows, stride=tiles), :] = masked
    shape = (LANES, groups * LANES)
    source = lax.broadcasted_iota(jnp.int32, shape, 0)
    target = lax.broadcasted_iota(jnp.int32, shape, 1)
    same = (source // chans == target // LANES) & (source % chans == target % chans)
    expand[...] = same.astype(F32).astype(BF16)
    gwt[...] = jnp.zeros_like(gwt)
    rows = step_rows * tiles
    pairs = step_rows * j_rows
    group = lane_group((tiles, LANES), chans)

    def body(step, carry):
        spread = jnp.dot(
            lsplit[pl.ds(pl.multiple_of(step * rows, rows), rows), :].astype(BF16),
            expand[...],
            preferred_element_type=F32,
        ).astype(BF16)
        for b in range(groups):
            chosen = (group == b).astype(F32).astype(BF16)
            for lo in range(groups):
                at = b * sequences + lo * tiles
                for i in range(step_rows):
                    diag_ref[step, at : at + tiles, i * LANES : (i + 1) * LANES] = (
                        spread[i * tiles : (i + 1) * tiles, lo * LANES : (lo + 1) * LANES] * chosen
                    )
        for pair in range(0, step_rows, 2):
            part = jnp.dot(
                rbig[...],
                diag_ref[step, :, pair * LANES : (pair + 2) * LANES],
                preferred_element_type=F32,
            ).astype(BF16)
            for k in range(2):
                for a in range(blocks):
                    y_ref[step * step_rows + pair + k, :, a * LANES : (a + 1) * LANES] = part[
                        a * j_rows : (a + 1) * j_rows, k * LANES : (k + 1) * LANES
                    ]
        block = pl.ds(step * step_rows, step_rows)
        scaled_t = scaled_ref[block].reshape(pairs, LANES).T
        y_flat = y_ref[block].reshape(pairs, blocks * LANES)
        gwt[...] += jnp.dot(scaled_t, y_flat, preferred_element_type=F32)
        return carry

    lax.fori_loop(0, i_rows // step_rows, body, 0, unroll=True)
    for k in range(blocks):
        turned_tile = gwt[:, k * LANES : (k + 1) * LANES].T
        for q in range(groups):
            gwr[pl.ds(k * groups + q, chans, stride=chans), :] = turned_tile[
                q * chans : (q + 1) * chans
            ]
    cut(gwr, lax.axis_index("row"), n_row, keep_out, send_out)


def right_kernel(dims, n_row, *refs):
    chans, groups, blocks, i_rows, j_rows, step_rows, sequences = dims
    tiles = sequences * chans // LANES
    j_pad = -(-j_rows // LANES) * LANES
    after, z_ref, diag_ref = refs[:3]
    keep_out, send_out, acc, turned, gr_all = refs[3:]
    for step in range(i_rows // step_rows):
        part = lax.dot_general(diag_ref[step], z_ref[step], NT, preferred_element_type=F32)
        if step:
            acc[...] += part
        else:
            acc[...] = part
    for a in range(blocks):
        at, shift = divmod(a * j_rows, LANES)
        mine = acc[:, at * LANES : at * LANES + j_pad]
        if shift:
            mine = pltpu.roll(mine, LANES - shift, axis=1)
        for b in range(groups):
            for lo in range(groups):
                first = b * sequences + lo * tiles
                turned[pl.ds(lo * chans + groups * a + b, tiles, stride=LANES), :] = mine[
                    first : first + tiles
                ]
    for t in range(tiles):
        lanes = slice(t * LANES, (t + 1) * LANES)
        gr_all[pl.ds(t, j_rows, stride=tiles), :] = turned[lanes, :].T[:j_rows]
    cut(gr_all, lax.axis_index("row"), n_row, keep_out, send_out)


def left_kernel(dims, n_row, n_col, *refs):
    chans, groups, blocks, i_rows, j_rows, step_rows, sequences = dims
    tiles = sequences * chans // LANES
    j_pad = -(-j_rows // LANES) * LANES
    after, rj_ref, keep_ref, z_ref, right_held, right_came = refs[:6]
    rbig, keep_out, send_out = refs[6:9]
    flat, turned, rbt, gl_all = refs[9:]
    place((right_held, right_came), lax.axis_index("row"), n_row, flat)
    for t in range(tiles):
        lanes = slice(t * LANES, (t + 1) * LANES)
        masked = flat[0:j_rows, lanes] * rj_ref[...] * keep_ref[:, lanes]
        if j_rows < j_pad:
            masked = jnp.concatenate([masked, jnp.zeros((j_pad - j_rows, LANES), F32)], axis=0)
        turned[lanes, :] = masked.T
    for a in range(blocks):
        parts = [
            turned[pl.ds(lo * chans + groups * a + b, tiles, stride=LANES), :]
            for b in range(groups)
            for lo in range(groups)
        ]
        block = jnp.concatenate(parts, axis=0)
        rbig[a * j_rows : (a + 1) * j_rows, :] = block.T[:j_rows].astype(BF16)
    rbt[...] = rbig[...].T
    group = lane_group((sequences, LANES), chans)
    group_t = lane_group((tiles, LANES), chans)

    def body(step, carry):
        for pair in range(0, step_rows, 2):
            part = jnp.dot(
                rbt[...],
                z_ref[step, :, pair * LANES : (pair + 2) * LANES],
                preferred_element_type=F32,
            )
            for k in range(2):
                mine = part[:, k * LANES : (k + 1) * LANES]
                total = mine[0:sequences]
                for b in range(1, groups):
                    total = jnp.where(group == b, mine[b * sequences : (b + 1) * sequences], total)
                shift = LANES // 2
                while shift >= chans:
                    total = total + pltpu.roll(total, shift, axis=1)
                    shift //= 2
                merged = total[0:tiles]
                for lo in range(1, groups):
                    merged = jnp.where(group_t == lo, total[lo * tiles : (lo + 1) * tiles], merged)
                at = (step * step_rows + pair + k) * tiles
                gl_all[pl.ds(pl.multiple_of(at, tiles), tiles), :] = merged
        return carry

    lax.fori_loop(0, i_rows // step_rows, body, 0, unroll=True)
    cut(gl_all, lax.axis_index("col"), n_col, keep_out, send_out)


def total_of(keep_ref, came_ref, k=0):
    return keep_ref[k].astype(F32) + came_ref[k].astype(F32)


def join_kernel(after, held_ref, came_ref, out_ref):
    count = held_ref.shape[0]
    for k in range(count):
        out_ref[k] = held_ref[k]
        out_ref[count + k] = came_ref[k]


def fold_kernel(after, held_ref, came_ref, keep_out, send_out):
    for k in range(held_ref.shape[0]):
        into = send_out if k % 2 else keep_out
        into[k // 2] = total_of(held_ref, came_ref, k).astype(into.dtype)


def turn_kernel(n_col, after, held_ref, came_ref, keep_out, send_out, whole):
    whole[...] = total_of(held_ref, came_ref)
    cut(whole, lax.axis_index("col"), n_col, keep_out, send_out)


def write_rows(whole, rows, keep_ref, out_ref, tiles):
    own = out_ref.shape[0]
    for t in range(tiles):
        lanes = slice(t * LANES, (t + 1) * LANES)
        out_ref[:, lanes] = whole[pl.ds(t, own, stride=tiles), :] * (
            rows * keep_ref[:, lanes]
        )


def pair_kernel(dims, first, last, *refs):
    chans, groups, blocks, i_rows, j_rows, step_rows, sequences = dims
    ri_ref, y_ref, wp_ref, inv_ref = refs[1:5]
    out_ref, mark_ref, staged, sems = refs[-4:]
    pairs = step_rows * j_rows

    def store(step):
        rows = pl.ds(step * step_rows, step_rows)
        return pltpu.make_async_copy(
            staged.at[pl.ds((step - first) * step_rows, step_rows)],
            out_ref.at[rows],
            sems.at[step - first],
        )

    for step in range(first, last):
        y_flat = y_ref[step * step_rows : (step + 1) * step_rows].reshape(pairs, blocks * LANES)
        projected = jnp.dot(y_flat, wp_ref[...], preferred_element_type=F32)
        for i in range(step_rows):
            at = step * step_rows + i
            inverse = jnp.where(ri_ref[at : at + 1, :] > 0, inv_ref[...], 1.0)
            staged[at - first * step_rows] = (
                projected[i * j_rows : (i + 1) * j_rows] * inverse
            ).astype(BF16)
        store(step).start()
    mark_ref[...] = jnp.zeros_like(mark_ref)
    for step in range(first, last):
        store(step).wait()


def final_kernel(dims, after, ri_ref, rj_ref, keep_ref, *refs):
    chans, groups, blocks, i_rows, j_rows, step_rows, sequences = dims
    tiles = sequences * chans // LANES
    left, right, weight = refs[0:2], refs[2:4], refs[4:6]
    gl_out, gr_out, gw_out, whole = refs[6:]
    for refs_in, out, rows_ref, axis in (
        (left, gl_out, ri_ref, "col"),
        (right, gr_out, rj_ref, "row"),
    ):
        own = out.shape[0]
        whole[0 : own * tiles, :] = total_of(*refs_in)
        first = pl.multiple_of(lax.axis_index(axis) * own, 8)
        write_rows(whole, rows_ref[pl.ds(first, own), :], keep_ref, out, tiles)
    gw_out[...] = total_of(*weight)


def swap(array, axis, n, bit):
    return lax.ppermute(array, axis, [(s, s ^ bit) for s in range(n)])


def owners_of(n):
    held, bit = [0], n // 2
    while bit > 1:
        held, bit = held + [k ^ bit for k in held], bit // 2
    return held, [k ^ 1 for k in held]


def gather(block, own, axis, n, after):
    held, sent, bit = own, block[None], n // 2
    while bit > 1:
        came = swap(sent, axis, n, bit)
        shape = (2 * held.shape[0],) + held.shape[1:]
        held = small_call(join_kernel, [pltpu.VMEM(shape, BF16)], "join")(after, held, came)[0]
        sent, bit = held, bit // 2
    return held, swap(sent, axis, n, 1)


def reduce(keep, send, axis, n, after):
    bit = 1
    while True:
        came = swap(send, axis, n, bit)
        bit *= 2
        if bit >= n:
            return keep, came
        half = (keep.shape[0] // 2,) + keep.shape[1:]
        outs = [pltpu.VMEM(half, F32), pltpu.VMEM(half, BF16)]
        keep, send = small_call(fold_kernel, outs, "fold")(after, keep, came)


def small_call(body, outs, name, scratch=()):
    def call(after, *operands):
        return pl.pallas_call(
            body,
            in_specs=[hbm()] + vmem(len(operands)),
            out_specs=vmem(len(outs)),
            out_shape=outs,
            scratch_shapes=list(scratch),
            compiler_params=params(4),
            cost_estimate=cost(1000, 1000),
            name=name,
        )(after, *operands)

    return call


def halves(rows, n):
    return [pltpu.VMEM((n // 2, rows // n, LANES), BF16)] * 2


def vmem(count=1):
    return [pl.BlockSpec(memory_space=pltpu.VMEM)] * count


def hbm():
    return pl.BlockSpec(memory_space=pl.ANY)


def in_hbm(array):
    return pltpu.with_memory_space_constraint(array, pltpu.HBM)


def shards(left_act, right_act, row_mask, res_mask, out_weight, cotangent):
    n_col = lax.axis_size("col")
    n_row = lax.axis_size("row")
    i_rows, j_rows, pair_width = cotangent.shape
    sequences = row_mask.shape[0]
    width = left_act.shape[1]
    chans = width // sequences
    groups = LANES // chans
    blocks = chans // groups
    tiles = width // LANES
    depth = groups * sequences
    inner = chans * chans
    step_rows = 8
    steps = i_rows // step_rows
    dims = (chans, groups, blocks, i_rows, j_rows, step_rows, sequences)
    j_pad = -(-j_rows // LANES) * LANES
    span = blocks * j_rows
    own_left, own_right = left_act.shape[0], right_act.shape[0]
    macs = i_rows * j_rows * inner * pair_width

    mask_row = (res_mask.reshape(1, -1), row_mask.reshape(1, -1))
    scaled, inverse, weight, keep, i_keep, j_keep, own_l, own_r = pl.pallas_call(
        functools.partial(scale_kernel, dims),
        in_specs=[hbm()] * 6,
        out_specs=vmem(8),
        out_shape=[
            pltpu.VMEM(cotangent.shape, BF16),
            pltpu.VMEM((j_rows, LANES), F32),
            pltpu.VMEM(out_weight.shape, BF16),
            pltpu.VMEM((1, width), F32),
            pltpu.VMEM((i_rows, LANES), F32),
            pltpu.VMEM((j_rows, LANES), F32),
            pltpu.VMEM((1,) + left_act.shape, BF16),
            pltpu.VMEM((1,) + right_act.shape, BF16),
        ],
        scratch_shapes=[
            pltpu.VMEM((1, res_mask.shape[0]), jnp.int32),
            pltpu.VMEM((1, sequences), jnp.int32),
            pltpu.VMEM(out_weight.shape, BF16),
            pltpu.VMEM(out_weight.shape, F32),
            pltpu.VMEM(cotangent.shape, BF16),
            pltpu.SemaphoreType.DMA((steps,)),
            pltpu.SemaphoreType.DMA((5,)),
        ],
        compiler_params=params(12),
        cost_estimate=cost(macs, 6 * 2**20),
        name="scale",
    )(*map(in_hbm, (*mask_row, cotangent, out_weight, left_act, right_act)))

    lefts = gather(left_act, own_l, "col", n_col, own_l)
    rights = gather(right_act, own_r, "row", n_row, lefts[0])

    z = pl.pallas_call(
        functools.partial(inner_kernel, dims),
        in_specs=[hbm()] + vmem(2),
        out_specs=vmem()[0],
        out_shape=pltpu.VMEM((steps, span, step_rows * LANES), BF16),
        compiler_params=params(12),
        cost_estimate=cost(macs, 2**20),
        name="inner",
    )(rights[0], scaled, weight)

    rbig, *gl_cut = pl.pallas_call(
        functools.partial(left_kernel, dims, n_row, n_col),
        in_specs=[hbm()] + vmem(5),
        out_specs=vmem(3),
        out_shape=[pltpu.VMEM((span, depth), BF16)] + halves(i_rows * tiles, n_col),
        scratch_shapes=[
            pltpu.VMEM((j_rows, width), F32),
            pltpu.VMEM((width, j_pad), F32),
            pltpu.VMEM((depth, span), BF16),
            pltpu.VMEM((i_rows * tiles, LANES), F32),
        ],
        compiler_params=params(16),
        cost_estimate=cost(macs, 2**20),
        name="left",
    )(z, j_keep, keep, z, *rights)

    y, diag, *gw_cut = pl.pallas_call(
        functools.partial(outer_kernel, dims, n_row, n_col),
        in_specs=vmem(6),
        out_specs=vmem(4),
        out_shape=[
            pltpu.VMEM((i_rows, j_rows, inner), BF16),
            pltpu.VMEM((steps, depth, step_rows * LANES), BF16),
        ]
        + halves(inner, n_row),
        scratch_shapes=[
            pltpu.VMEM((i_rows, width), F32),
            pltpu.VMEM((i_rows * tiles, LANES), F32),
            pltpu.VMEM((LANES, groups * LANES), BF16),
            pltpu.VMEM((pair_width, inner), F32),
            pltpu.VMEM((inner, pair_width), F32),
        ],
        compiler_params=params(16),
        cost_estimate=cost(2 * macs, 2**20),
        name="outer",
    )(i_keep, keep, scaled, rbig, *lefts)
    gl_last = reduce(*gl_cut, "col", n_col, gw_cut[0])

    gr_cut = pl.pallas_call(
        functools.partial(right_kernel, dims, n_row),
        in_specs=[hbm()] + vmem(2),
        out_specs=vmem(2),
        out_shape=halves(j_rows * tiles, n_row),
        scratch_shapes=[
            pltpu.VMEM((depth, span), F32),
            pltpu.VMEM((width, j_pad), F32),
            pltpu.VMEM((j_rows * tiles, LANES), F32),
        ],
        compiler_params=params(18),
        cost_estimate=cost(macs, 2**20),
        name="right",
    )(gl_last[0], z, diag)
    gw_row = reduce(*gw_cut, "row", n_row, gr_cut[0])

    def pair_part(first, last, so_far, after):
        done = [] if so_far is None else [so_far]
        return pl.pallas_call(
            functools.partial(pair_kernel, dims, first, last),
            in_specs=[hbm()] + vmem(4) + [hbm()] * len(done),
            out_specs=[hbm()] + vmem(),
            out_shape=[jax.ShapeDtypeStruct(cotangent.shape, BF16), pltpu.VMEM((8, LANES), F32)],
            scratch_shapes=[
                pltpu.VMEM(((last - first) * step_rows, j_rows, pair_width), BF16),
                pltpu.SemaphoreType.DMA((last - first,)),
            ],
            input_output_aliases={5: 0} if done else {},
            compiler_params=params(12),
            cost_estimate=cost(macs // 2, 2**20),
            name="pair",
        )(after, i_keep, y, weight, inverse, *done)

    ends = (3 * steps // 8, 6 * steps // 8, steps)
    pair_out, mark = pair_part(0, ends[0], None, gw_row[0])
    gr_last = reduce(*gr_cut, "row", n_row, mark)
    gw_cut = small_call(
        functools.partial(turn_kernel, n_col),
        halves(inner // n_row, n_col),
        "turn",
        [pltpu.VMEM((inner // n_row, pair_width), F32)],
    )(mark, *gw_row)
    pair_out, mark = pair_part(ends[0], ends[1], pair_out, gw_cut[0])
    gw_last = reduce(*gw_cut, "col", n_col, mark)
    pair_out, mark = pair_part(ends[1], ends[2], pair_out, gw_last[0])

    grad_left, grad_right, grad_weight = pl.pallas_call(
        functools.partial(final_kernel, dims),
        in_specs=[hbm()] + vmem(9),
        out_specs=vmem(3),
        out_shape=[
            jax.ShapeDtypeStruct((own_left, width), F32),
            jax.ShapeDtypeStruct((own_right, width), F32),
            jax.ShapeDtypeStruct((inner // n_row // n_col, pair_width), F32),
        ],
        scratch_shapes=[pltpu.VMEM((max(own_left, own_right) * tiles, LANES), F32)],
        compiler_params=params(4),
        cost_estimate=cost(1000, 1000),
        name="final_sums",
    )(mark, i_keep, j_keep, keep, *gl_last, *gr_last, *gw_last)
    return (pair_out, grad_left, grad_right, grad_weight)


def solution(mesh):
    placed = (
        P(("grp", "row", "col"), None),
        P(("grp", "col", "row"), None),
        P("grp"),
        P("grp"),
        P(),
        P(("grp", "row"), "col", None),
    )
    return jax.shard_map(
        shards,
        mesh=mesh,
        in_specs=placed,
        out_specs=(
            P(("grp", "row"), "col", None),
            P(("grp", "row", "col"), None),
            P(("grp", "col", "row"), None),
            P(("grp", "row", "col"), None),
        ),
        check_vma=False,
    )
```

time: 44.2 us -> 43.9 us (level)
  Pallas kernels: 22.5 us -> 24.5 us
  waiting for transfers between devices: 4.54 us -> 2.8 us
  starting transfers between devices: 16.3 us -> 15.6 us
    pallas_call x5 -> x13, Pallas kernels: 9.37 us -> 12.2 us  [the longest x3 4.84 us: pair_part(): pl.pallas_call(functools.partial(pair_kernel, dims, first, last), in_spec...]
    ppermute x15 -> x12, waiting for transfers between devices: 4.54 us -> 2.8 us  [swap(): return lax.ppermute(array, axis, [(s, s ^ bit) for s in range(n)])]
    pallas_call x1, Pallas kernels: 7.48 us -> 6.64 us  [shards(): pl.pallas_call(functools.partial(outer_kernel, dims, n_row, n_col), in_sp...]
    ppermute x15 -> x12, starting transfers between devices: 16.3 us -> 15.6 us  [swap(): return lax.ppermute(array, axis, [(s, s ^ bit) for s in range(n)])]
  transfers between devices with their start and end apart: 15 -> 12, of which waited for: 5 -> 4; matrix products, arithmetic and copies ran while one was open for 0% -> 0% of each run, Pallas kernels for 24% -> 54%
where the time goes in v6:
time: 43.9 us; the launch traced here: 43.8 us
  Pallas kernels  24.5 us (56%)
  starting transfers between devices  15.6 us (36%)
  waiting for transfers between devices  2.8 us (6%)
  between operations  0.78 us (2%)
    ppermute x12, starting transfers between devices, swap(): return lax.ppermute(array, axis, [(s, s ^ bit) for s in range(n)])  15.6 us
    pallas_call x1, Pallas kernels, shards(): pl.pallas_call(functools.partial(outer_kernel, dims, n_row, n_col), in_sp...  6.64 us
    pallas_call x3, Pallas kernels, pair_part(): pl.pallas_call(functools.partial(pair_kernel, dims, first, last), in_spec...  4.84 us
    pallas_call x1, Pallas kernels, shards(): pl.pallas_call(functools.partial(right_kernel, dims, n_row), in_specs=[hb...  3.61 us
    pallas_call x1, Pallas kernels, shards(): pl.pallas_call(functools.partial(left_kernel, dims, n_row, n_col), in_spe...  3.55 us
    pallas_call x1, Pallas kernels, shards(): pl.pallas_call(functools.partial(inner_kernel, dims), in_specs=[hbm()] +...  2.86 us
    ppermute x12, waiting for transfers between devices, swap(): return lax.ppermute(array, axis, [(s, s ^ bit) for s in range(n)])  2.8 us
    pallas_call x1, Pallas kernels, shards(): pl.pallas_call(functools.partial(scale_kernel, dims), in_specs=[hbm()] *...  2.05 us
  transfers between devices with their start and end apart: 12, of which 4 were waited for; matrix products, arithmetic and copies ran while one was open for 0% of the time, Pallas kernels for 54%

profile of v6, /device:TPU:0, one launch (start us, length us, event | category | flops | bytes accessed | tf_op | source)
XLA Modules:
  0.0 43.8 jit_solution(984350330261123258)
XLA Ops:
  0.6 4.1 %collective-permute-start = (bf16[1,16,2048]{2,1,0:T(8,128)(2,1)}, bf16[1,16,2048]{2,1,0:T(8,128)(2,1)S(1)}, u32[]{:S(2)}, u32[]{:S(2)}) collective-permute-start(bf16[1,16,2048]{2,1,0:T(8,128)(2,1)} %bitcast.4), channel_id=1, source_target_pairs={{0,2},{1,3},{2,0},{3,1},{4,6},{5,7},{6,4},{7,5},{8,10},{9,11},{10,... | collective-permute-start | bytes 196616 | tf_op jit(solution)/shard_map/ppermute | solution.py:348
  4.7 1.5 %collective-permute-start.1 = (bf16[1,16,2048]{2,1,0:T(8,128)(2,1)}, bf16[1,16,2048]{2,1,0:T(8,128)(2,1)S(1)}, u32[]{:S(2)}, u32[]{:S(2)}) collective-permute-start(bf16[1,16,2048]{2,1,0:T(8,128)(2,1)} %bitcast.5), channel_id=1, source_target_pairs={{0,8},{4,12},{8,0},{12,4},{1,9},{5,13},{9,1},{13,5},{2,10},{6,14},... | collective-permute-start | bytes 196616 | tf_op jit(solution)/shard_map/ppermute | solution.py:348
  6.2 2.1 %scale.1 = (bf16[64,64,128]{2,1,0:T(8,128)(2,1)S(1)}, f32[64,128]{1,0:T(8,128)S(1)}, bf16[1024,128]{1,0:T(8,128)(2,1)S(1)}, f32[1,2048]{1,0:T(1,128)S(1)}, f32[6...) custom-call(s32[1,256]{1,0:T(1,128)} %bitcast.6, ...), custom_call_target="tpu_custom_call" | custom-call | flops 536870912 | bytes 6291456 | tf_op jit(solution)/shard_map/scale/pallas_call | solution.py:433
  8.3 0.3 collective-permute-done.came_ref
  8.6 0.6 %collective-permute-done.1.came_ref = bf16[1,16,2048]{2,1,0:T(8,128)(2,1)S(1)} collective-permute-done((bf16[1,16,2048]{2,1,0:T(8,128)(2,1)}, bf16[1,16,2048]{2,1,0:T(8,128)(2,1)S(1)}, u32[]{:S(2)}, u32[]{:S(2)}) %collective-permute-start.1) | collective-permute-done | bytes 65568 | tf_op jit(solution)/shard_map/ppermute | solution.py:348
  9.2 0.1 collective-permute-start.2
  9.3 1.6 %collective-permute-start.3 = (bf16[2,16,2048]{2,1,0:T(8,128)(2,1)S(1)}, bf16[2,16,2048]{2,1,0:T(8,128)(2,1)S(1)}, u32[]{:S(2)}, u32[]{:S(2)}) collective-permute-start(bf16[2,16,2048]{2,1,0:T(8,128)(2,1)S(1)} %join.2.after.refs_4_), channel_id=1, source_target_pairs={{0,1},{1,0},{2,3},{3,2},{4,5},{5,4},{6,7},{7,6},{8,9},{9,8},{10,11... | collective-permute-start | bytes 393224 | tf_op jit(solution)/shard_map/ppermute | solution.py:348
  10.9 2.9 %inner.1.refs_0_.refs_3_.refs_1_ = bf16[8,512,1024]{2,1,0:T(8,128)(2,1)S(1)} custom-call(bf16[2,16,2048]{2,1,0:T(8,128)(2,1)S(1)} %join.3.after.refs_4_, bf16[64,64,128]{2,1,0:T(8,128)(2,1)S(1)} %get-tuple-element.42.scaled_ref.refs_2_, bf16[1024,128]{1,0:T(8,128)(2,1)S(1)} %get-tuple-element.45.wp_ref.refs_3_), custom_call_target="tpu_custom_call" | custom-call | flops 536870912 | bytes 1048576 | tf_op jit(solution)/shard_map/inner/pallas_call | solution.py:464
  13.8 3.5 %left.1 = (bf16[512,256]{1,0:T(8,128)(2,1)S(1)}, bf16[2,256,128]{2,1,0:T(8,128)(2,1)S(1)}, bf16[2,256,128]{2,1,0:T(8,128)(2,1)S(1)}) custom-call(bf16[8,512,1024]{2,1,0:T(8,128)(2,1)S(1)} %inner.1.refs_0_.refs_3_.refs_1_, f32[64,128]{1,0:T(8,128)S(1)} %get-tuple-element.46.refs_1_.rj_ref, f32[1,2048]{1,0:T(1,128)S(1)} %get-tuple-element.41.refs_2_.refs_1_.keep_ref, ...), custom_call_target="tpu_custom_call" | custom-call | flops 536870912 | bytes 1048576 | tf_op jit(solution)/shard_map/left/pallas_call | solution.py:474
  17.4 0.5 %collective-permute-start.4 = (bf16[2,256,128]{2,1,0:T(8,128)(2,1)S(1)}, bf16[2,256,128]{2,1,0:T(8,128)(2,1)S(1)}, u32[]{:S(2)}, u32[]{:S(2)}) collective-permute-start(bf16[2,256,128]{2,1,0:T(8,128)(2,1)S(1)} %get-tuple-element.50), channel_id=1, source_target_pairs={{0,1},{1,0},{2,3},{3,2},{4,5},{5,4},{6,7},{7,6},{8,9},{9,8},{10,11... | collective-permute-start | bytes 393224 | tf_op jit(solution)/shard_map/ppermute | solution.py:348
  17.9 6.6 %outer.1 = (bf16[64,64,1024]{2,1,0:T(8,128)(2,1)S(1)}, bf16[8,256,1024]{2,1,0:T(8,128)(2,1)S(1)}, bf16[2,256,128]{2,1,0:T(8,128)(2,1)S(1)}, bf16[2,256,128]{2,1,0:T(8,128)(2,1)S(1)}) custom-call(f32[64,128]{1,0:T(8,128)S(1)} %get-tuple-element.40.refs_0_.refs_1_.ri_ref, f32[1,2048]{1,0:T(1,128)S(1)} %get-tuple-element.41.refs_2_.refs_1_.keep_ref, ...), custom_call_target="tpu_custom_call" | custom-call | flops 1073741824 | bytes 1048576 | tf_op jit(solution)/shard_map/outer/pallas_call | solution.py:490
  24.7 3.6 %right.1 = (bf16[2,256,128]{2,1,0:T(8,128)(2,1)S(1)}, bf16[2,256,128]{2,1,0:T(8,128)(2,1)S(1)}) custom-call(f32[1,256,128]{2,1,0:T(8,128)S(1)} %get-tuple-element.51.refs_0_, bf16[8,512,1024]{2,1,0:T(8,128)(2,1)S(1)} %inner.1.refs_0_.refs_3_.refs_1_, bf16[8,256,1024]{2,1,0:T(8,128)(2,1)S(1)} %get-tuple-element.52.refs_2_), custom_call_target="tpu_custom_call" | custom-call | flops 536870912 | bytes 1048576 | tf_op jit(solution)/shard_map/right/pallas_call | solution.py:512
  28.3 0.5 %collective-permute-start.9 = (bf16[2,256,128]{2,1,0:T(8,128)(2,1)S(1)}, bf16[2,256,128]{2,1,0:T(8,128)(2,1)S(1)}, u32[]{:S(2)}, u32[]{:S(2)}) collective-permute-start(bf16[2,256,128]{2,1,0:T(8,128)(2,1)S(1)} %get-tuple-element.69), channel_id=1, source_target_pairs={{0,4},{4,0},{8,12},{12,8},{1,5},{5,1},{9,13},{13,9},{2,6},{6,2},{1... | collective-permute-start | bytes 393224 | tf_op jit(solution)/shard_map/ppermute | solution.py:348
  28.9 1.6 %collective-permute-start.6 = (bf16[1,256,128]{2,1,0:T(8,128)(2,1)S(1)}, bf16[1,256,128]{2,1,0:T(8,128)(2,1)S(1)}, u32[]{:S(2)}, u32[]{:S(2)}) collective-permute-start(bf16[1,256,128]{2,1,0:T(8,128)(2,1)S(1)} %get-tuple-element.59), channel_id=1, source_target_pairs={{0,8},{4,12},{8,0},{12,4},{1,9},{5,13},{9,1},{13,5},{2,10},{6,14},... | collective-permute-start | bytes 196616 | tf_op jit(solution)/shard_map/ppermute | solution.py:348
  30.4 1.4 %collective-permute-start.8 = (bf16[1,256,128]{2,1,0:T(8,128)(2,1)S(1)}, bf16[1,256,128]{2,1,0:T(8,128)(2,1)S(1)}, u32[]{:S(2)}, u32[]{:S(2)}) collective-permute-start(bf16[1,256,128]{2,1,0:T(8,128)(2,1)S(1)} %get-tuple-element.68), channel_id=1, source_target_pairs={{0,2},{1,3},{2,0},{3,1},{4,6},{5,7},{6,4},{7,5},{8,10},{9,11},{10,... | collective-permute-start | bytes 196616 | tf_op jit(solution)/shard_map/ppermute | solution.py:348
  31.8 1.7 %pair.3 = (bf16[64,64,128]{2,1,0:T(8,128)(2,1)}, f32[8,128]{1,0:T(8,128)S(1)}) custom-call(f32[1,256,128]{2,1,0:T(8,128)S(1)} %get-tuple-element.55.refs_0_.held_ref, f32[64,128]{1,0:T(8,128)S(1)} %get-tuple-element.40.refs_0_.refs_1_.ri_ref, bf16[64,64,1024]{2,1,0:T(8,128)(2,1)S(1)} %get-tuple-element.56.refs_2_, ...), custom_call_target="tpu_custom_call" | custom-call | flops 268435456 | bytes 1048576 | tf_op jit(solution)/shard_map/pair/pallas_call | solution.py:530
  33.6 0.6 %collective-permute-start.10 = (bf16[1,256,128]{2,1,0:T(8,128)(2,1)S(1)}, bf16[1,256,128]{2,1,0:T(8,128)(2,1)S(1)}, u32[]{:S(2)}, u32[]{:S(2)}) collective-permute-start(bf16[1,256,128]{2,1,0:T(8,128)(2,1)S(1)} %get-tuple-element.71), channel_id=1, source_target_pairs={{0,8},{4,12},{8,0},{12,4},{1,9},{5,13},{9,1},{13,5},{2,10},{6,14},... | collective-permute-start | bytes 196616 | tf_op jit(solution)/shard_map/ppermute | solution.py:348
  34.2 2.0 %collective-permute-start.7 = (bf16[2,64,128]{2,1,0:T(8,128)(2,1)S(1)}, bf16[2,64,128]{2,1,0:T(8,128)(2,1)S(1)}, u32[]{:S(2)}, u32[]{:S(2)}) collective-permute-start(bf16[2,64,128]{2,1,0:T(8,128)(2,1)S(1)} %get-tuple-element.63), channel_id=1, source_target_pairs={{0,1},{1,0},{2,3},{3,2},{4,5},{5,4},{6,7},{7,6},{8,9},{9,8},{10,11... | collective-permute-start | bytes 98312 | tf_op jit(solution)/shard_map/ppermute | solution.py:348
  36.3 1.7 %pair.4 = (bf16[64,64,128]{2,1,0:T(8,128)(2,1)}, f32[8,128]{1,0:T(8,128)S(1)}) custom-call(bf16[2,64,128]{2,1,0:T(8,128)(2,1)S(1)} %get-tuple-element.60.refs_0_.held_ref, f32[64,128]{1,0:T(8,128)S(1)} %get-tuple-element.40.refs_0_.refs_1_.ri_ref, bf16[64,64,1024]{2,1,0:T(8,128)(2,1)S(1)} %get-tuple-element.56.refs_2_, ...), custom_call_target="tpu_custom_call", output_to_operand_aliasing={{0}: (5, {})} | custom-call | flops 268435456 | bytes 1048576 | tf_op jit(solution)/shard_map/pair/pallas_call | solution.py:530
  38.0 0.2 collective-permute-done.7.came_ref
  38.2 1.6 %collective-permute-start.11 = (bf16[1,64,128]{2,1,0:T(8,128)(2,1)S(1)}, bf16[1,64,128]{2,1,0:T(8,128)(2,1)S(1)}, u32[]{:S(2)}, u32[]{:S(2)}) collective-permute-start(bf16[1,64,128]{2,1,0:T(8,128)(2,1)S(1)} %get-tuple-element.72), channel_id=1, source_target_pairs={{0,2},{1,3},{2,0},{3,1},{4,6},{5,7},{6,4},{7,5},{8,10},{9,11},{10,... | collective-permute-start | bytes 49160 | tf_op jit(solution)/shard_map/ppermute | solution.py:348
  39.8 1.4 %pair.5 = (bf16[64,64,128]{2,1,0:T(8,128)(2,1)}, f32[8,128]{1,0:T(8,128)S(1)}) custom-call(f32[1,64,128]{2,1,0:T(8,128)S(1)} %get-tuple-element.64.refs_0_.refs_4_, f32[64,128]{1,0:T(8,128)S(1)} %get-tuple-element.40.refs_0_.refs_1_.ri_ref, bf16[64,64,1024]{2,1,0:T(8,128)(2,1)S(1)} %get-tuple-element.56.refs_2_, ...), custom_call_target="tpu_custom_call", output_to_operand_aliasing={{0}: (5, {})} | custom-call | flops 268435456 | bytes 1048576 | tf_op jit(solution)/shard_map/pair/pallas_call | solution.py:530
  41.3 1.6 %collective-permute-done.11.refs_5_ = bf16[1,64,128]{2,1,0:T(8,128)(2,1)S(1)} collective-permute-done((bf16[1,64,128]{2,1,0:T(8,128)(2,1)S(1)}, bf16[1,64,128]{2,1,0:T(8,128)(2,1)S(1)}, u32[]{:S(2)}, u32[]{:S(2)}) %collective-permute-start.11) | collective-permute-done | bytes 16416 | tf_op jit(solution)/shard_map/ppermute | solution.py:348
  42.9 0.8 %final_sums.1 = (f32[16,2048]{1,0:T(8,128)}, f32[16,2048]{1,0:T(8,128)}, f32[64,128]{1,0:T(8,128)}) custom-call(f32[8,128]{1,0:T(8,128)S(1)} %get-tuple-element.67.after, f32[64,128]{1,0:T(8,128)S(1)} %get-tuple-element.40.refs_0_.refs_1_.ri_ref, f32[64,128]{1,0:T(8,128)S(1)} %get-tuple-element.46.refs_1_.rj_ref, ...), custom_call_target="tpu_custom_call" | custom-call | flops 1000 | bytes 1000 | tf_op jit(solution)/shard_map/final_sums/pallas_call | solution.py:558
  (16 shorter events, 0.2 us)
Async XLA Ops:
  0.6 8.0 %collective-permute-start = (bf16[1,16,2048]{2,1,0:T(8,128)(2,1)}, bf16[1,16,2048]{2,1,0:T(8,128)(2,1)S(1)}, u32[]{:S(2)}, u32[]{:S(2)}) collective-permute-start(bf16[1,16,2048]{2,1,0:T(8,128)(2,1)} %bitcast.4), channel_id=1, source_target_pairs={{0,2},{1,3},{2,0},{3,1},{4,6},{5,7},{6,4},{7,5},{8,10},{9,11},{10,... | collective-permute-start | bytes 196616 | tf_op jit(solution)/shard_map/ppermute | solution.py:348
  4.7 4.5 %collective-permute-start.1 = (bf16[1,16,2048]{2,1,0:T(8,128)(2,1)}, bf16[1,16,2048]{2,1,0:T(8,128)(2,1)S(1)}, u32[]{:S(2)}, u32[]{:S(2)}) collective-permute-start(bf16[1,16,2048]{2,1,0:T(8,128)(2,1)} %bitcast.5), channel_id=1, source_target_pairs={{0,8},{4,12},{8,0},{12,4},{1,9},{5,13},{9,1},{13,5},{2,10},{6,14},... | collective-permute-start | bytes 196616 | tf_op jit(solution)/shard_map/ppermute | solution.py:348
  9.2 4.6 %collective-permute-start.2 = (bf16[2,16,2048]{2,1,0:T(8,128)(2,1)S(1)}, bf16[2,16,2048]{2,1,0:T(8,128)(2,1)S(1)}, u32[]{:S(2)}, u32[]{:S(2)}) collective-permute-start(bf16[2,16,2048]{2,1,0:T(8,128)(2,1)S(1)} %join.3.after.refs_4_), channel_id=1, source_target_pairs={{0,4},{4,0},{8,12},{12,8},{1,5},{5,1},{9,13},{13,9},{2,6},{6,2},{1... | collective-permute-start | bytes 393224 | tf_op jit(solution)/shard_map/ppermute | solution.py:348
  9.3 8.6 %collective-permute-start.3 = (bf16[2,16,2048]{2,1,0:T(8,128)(2,1)S(1)}, bf16[2,16,2048]{2,1,0:T(8,128)(2,1)S(1)}, u32[]{:S(2)}, u32[]{:S(2)}) collective-permute-start(bf16[2,16,2048]{2,1,0:T(8,128)(2,1)S(1)} %join.2.after.refs_4_), channel_id=1, source_target_pairs={{0,1},{1,0},{2,3},{3,2},{4,5},{5,4},{6,7},{7,6},{8,9},{9,8},{10,11... | collective-permute-start | bytes 393224 | tf_op jit(solution)/shard_map/ppermute | solution.py:348
  17.4 7.2 %collective-permute-start.4 = (bf16[2,256,128]{2,1,0:T(8,128)(2,1)S(1)}, bf16[2,256,128]{2,1,0:T(8,128)(2,1)S(1)}, u32[]{:S(2)}, u32[]{:S(2)}) collective-permute-start(bf16[2,256,128]{2,1,0:T(8,128)(2,1)S(1)} %get-tuple-element.50), channel_id=1, source_target_pairs={{0,1},{1,0},{2,3},{3,2},{4,5},{5,4},{6,7},{7,6},{8,9},{9,8},{10,11... | collective-permute-start | bytes 393224 | tf_op jit(solution)/shard_map/ppermute | solution.py:348
  24.5 4.3 %collective-permute-start.5 = (bf16[2,256,128]{2,1,0:T(8,128)(2,1)S(1)}, bf16[2,256,128]{2,1,0:T(8,128)(2,1)S(1)}, u32[]{:S(2)}, u32[]{:S(2)}) collective-permute-start(bf16[2,256,128]{2,1,0:T(8,128)(2,1)S(1)} %get-tuple-element.54), channel_id=1, source_target_pairs={{0,4},{4,0},{8,12},{12,8},{1,5},{5,1},{9,13},{13,9},{2,6},{6,2},{1... | collective-permute-start | bytes 393224 | tf_op jit(solution)/shard_map/ppermute | solution.py:348
  28.3 5.2 %collective-permute-start.9 = (bf16[2,256,128]{2,1,0:T(8,128)(2,1)S(1)}, bf16[2,256,128]{2,1,0:T(8,128)(2,1)S(1)}, u32[]{:S(2)}, u32[]{:S(2)}) collective-permute-start(bf16[2,256,128]{2,1,0:T(8,128)(2,1)S(1)} %get-tuple-element.69), channel_id=1, source_target_pairs={{0,4},{4,0},{8,12},{12,8},{1,5},{5,1},{9,13},{13,9},{2,6},{6,2},{1... | collective-permute-start | bytes 393224 | tf_op jit(solution)/shard_map/ppermute | solution.py:348
  28.9 5.3 %collective-permute-start.6 = (bf16[1,256,128]{2,1,0:T(8,128)(2,1)S(1)}, bf16[1,256,128]{2,1,0:T(8,128)(2,1)S(1)}, u32[]{:S(2)}, u32[]{:S(2)}) collective-permute-start(bf16[1,256,128]{2,1,0:T(8,128)(2,1)S(1)} %get-tuple-element.59), channel_id=1, source_target_pairs={{0,8},{4,12},{8,0},{12,4},{1,9},{5,13},{9,1},{13,5},{2,10},{6,14},... | collective-permute-start | bytes 196616 | tf_op jit(solution)/shard_map/ppermute | solution.py:348
  30.4 10.8 %collective-permute-start.8 = (bf16[1,256,128]{2,1,0:T(8,128)(2,1)S(1)}, bf16[1,256,128]{2,1,0:T(8,128)(2,1)S(1)}, u32[]{:S(2)}, u32[]{:S(2)}) collective-permute-start(bf16[1,256,128]{2,1,0:T(8,128)(2,1)S(1)} %get-tuple-element.68), channel_id=1, source_target_pairs={{0,2},{1,3},{2,0},{3,1},{4,6},{5,7},{6,4},{7,5},{8,10},{9,11},{10,... | collective-permute-start | bytes 196616 | tf_op jit(solution)/shard_map/ppermute | solution.py:348
  33.6 9.3 %collective-permute-start.10 = (bf16[1,256,128]{2,1,0:T(8,128)(2,1)S(1)}, bf16[1,256,128]{2,1,0:T(8,128)(2,1)S(1)}, u32[]{:S(2)}, u32[]{:S(2)}) collective-permute-start(bf16[1,256,128]{2,1,0:T(8,128)(2,1)S(1)} %get-tuple-element.71), channel_id=1, source_target_pairs={{0,8},{4,12},{8,0},{12,4},{1,9},{5,13},{9,1},{13,5},{2,10},{6,14},... | collective-permute-start | bytes 196616 | tf_op jit(solution)/shard_map/ppermute | solution.py:348
  34.2 4.0 %collective-permute-start.7 = (bf16[2,64,128]{2,1,0:T(8,128)(2,1)S(1)}, bf16[2,64,128]{2,1,0:T(8,128)(2,1)S(1)}, u32[]{:S(2)}, u32[]{:S(2)}) collective-permute-start(bf16[2,64,128]{2,1,0:T(8,128)(2,1)S(1)} %get-tuple-element.63), channel_id=1, source_target_pairs={{0,1},{1,0},{2,3},{3,2},{4,5},{5,4},{6,7},{7,6},{8,9},{9,8},{10,11... | collective-permute-start | bytes 98312 | tf_op jit(solution)/shard_map/ppermute | solution.py:348
  38.2 4.7 %collective-permute-start.11 = (bf16[1,64,128]{2,1,0:T(8,128)(2,1)S(1)}, bf16[1,64,128]{2,1,0:T(8,128)(2,1)S(1)}, u32[]{:S(2)}, u32[]{:S(2)}) collective-permute-start(bf16[1,64,128]{2,1,0:T(8,128)(2,1)S(1)} %get-tuple-element.72), channel_id=1, source_target_pairs={{0,2},{1,3},{2,0},{3,1},{4,6},{5,7},{6,4},{7,5},{8,10},{9,11},{10,... | collective-permute-start | bytes 49160 | tf_op jit(solution)/shard_map/ppermute | solution.py:348

commit v7 on v6

--- a/solution.py
+++ b/solution.py
@@ -186,18 +186,25 @@
     cut(gwr, lax.axis_index("row"), n_row, keep_out, send_out)
 
 
+def right_sum(first, last, z_ref, diag_ref, acc, so_far=None):
+    for step in range(first, last):
+        part = lax.dot_general(diag_ref[step], z_ref[step], NT, preferred_element_type=F32)
+        acc[...] = part if so_far is None else so_far[...] + part
+        so_far = acc
+
+
+def right_first_kernel(steps, after, z_ref, diag_ref, acc):
+    right_sum(0, steps // 2, z_ref, diag_ref, acc)
+
+
 def right_kernel(dims, n_row, *refs):
     chans, groups, blocks, i_rows, j_rows, step_rows, sequences = dims
     tiles = sequences * chans // LANES
     j_pad = -(-j_rows // LANES) * LANES
-    after, z_ref, diag_ref = refs[:3]
-    keep_out, send_out, acc, turned, gr_all = refs[3:]
-    for step in range(i_rows // step_rows):
-        part = lax.dot_general(diag_ref[step], z_ref[step], NT, preferred_element_type=F32)
-        if step:
-            acc[...] += part
-        else:
-            acc[...] = part
+    after, z_ref, diag_ref, acc_first = refs[:4]
+    keep_out, send_out, acc, turned, gr_all = refs[4:]
+    steps = i_rows // step_rows
+    right_sum(steps // 2, steps, z_ref, diag_ref, acc, acc_first)
     for a in range(blocks):
         at, shift = divmod(a * j_rows, LANES)
         mine = acc[:, at * LANES : at * LANES + j_pad]
@@ -299,33 +306,42 @@
         )
 
 
-def pair_kernel(dims, first, last, *refs):
+def pair_rows(dims, step, ri_ref, y_ref, wp_ref, inv_ref, out_ref, at):
     chans, groups, blocks, i_rows, j_rows, step_rows, sequences = dims
-    ri_ref, y_ref, wp_ref, inv_ref = refs[1:5]
-    out_ref, mark_ref, staged, sems = refs[-4:]
     pairs = step_rows * j_rows
-
-    def store(step):
-        rows = pl.ds(step * step_rows, step_rows)
-        return pltpu.make_async_copy(
-            staged.at[pl.ds((step - first) * step_rows, step_rows)],
-            out_ref.at[rows],
-            sems.at[step - first],
+    y_flat = y_ref[step * step_rows : (step + 1) * step_rows].reshape(pairs, blocks * LANES)
+    projected = jnp.dot(y_flat, wp_ref[...], preferred_element_type=F32)
+    for i in range(step_rows):
+        row = step * step_rows + i
+        inverse = jnp.where(ri_ref[row : row + 1, :] > 0, inv_ref[...], 1.0)
+        out_ref[at + i] = (projected[i * j_rows : (i + 1) * j_rows] * inverse).astype(BF16)
+
+
+def pair_first_kernel(dims, steps, after, ri_ref, y_ref, wp_ref, inv_ref, out_ref):
+    for step in range(steps):
+        pair_rows(dims, step, ri_ref, y_ref, wp_ref, inv_ref, out_ref, step * dims[5])
+
+
+def pair_kernel(dims, *refs):
+    i_rows, j_rows, step_rows = dims[3:6]
+    after_left, after_right, ri_ref, y_ref, wp_ref, inv_ref, early = refs[:7]
+    out_ref, staged, sems = refs[7:]
+    begin = early.shape[0]
+    copies = [pltpu.make_async_copy(early, out_ref.at[pl.ds(0, begin)], sems.at[0])]
+    copies[0].start()
+    for step in range(begin // step_rows, i_rows // step_rows):
+        at = step * step_rows - begin
+        pair_rows(dims, step, ri_ref, y_ref, wp_ref, inv_ref, staged, at)
+        copies.append(
+            pltpu.make_async_copy(
+                staged.at[pl.ds(at, step_rows)],
+                out_ref.at[pl.ds(begin + at, step_rows)],
+                sems.at[len(copies)],
+            )
         )
-
-    for step in range(first, last):
-        y_flat = y_ref[step * step_rows : (step + 1) * step_rows].reshape(pairs, blocks * LANES)
-        projected = jnp.dot(y_flat, wp_ref[...], preferred_element_type=F32)
-        for i in range(step_rows):
-            at = step * step_rows + i
-            inverse = jnp.where(ri_ref[at : at + 1, :] > 0, inv_ref[...], 1.0)
-            staged[at - first * step_rows] = (
-                projected[i * j_rows : (i + 1) * j_rows] * inverse
-            ).astype(BF16)
-        store(step).start()
-    mark_ref[...] = jnp.zeros_like(mark_ref)
-    for step in range(first, last):
-        store(step).wait()
+        copies[-1].start()
+    for copy in copies:
+        copy.wait()
 
 
 def final_kernel(dims, after, ri_ref, rj_ref, keep_ref, *refs):
@@ -454,7 +470,7 @@
             pltpu.SemaphoreType.DMA((5,)),
         ],
         compiler_params=params(12),
-        cost_estimate=cost(macs, 6 * 2**20),
+        cost_estimate=cost(16 * macs, 2**20),
         name="scale",
     )(*map(in_hbm, (*mask_row, cotangent, out_weight, left_act, right_act)))
 
@@ -467,7 +483,7 @@
         out_specs=vmem()[0],
         out_shape=pltpu.VMEM((steps, span, step_rows * LANES), BF16),
         compiler_params=params(12),
-        cost_estimate=cost(macs, 2**20),
+        cost_estimate=cost(16 * macs, 2**20),
         name="inner",
     )(rights[0], scaled, weight)
 
@@ -483,7 +499,7 @@
             pltpu.VMEM((i_rows * tiles, LANES), F32),
         ],
         compiler_params=params(16),
-        cost_estimate=cost(macs, 2**20),
+        cost_estimate=cost(16 * macs, 2**20),
         name="left",
     )(z, j_keep, keep, z, *rights)
 
@@ -504,14 +520,24 @@
             pltpu.VMEM((inner, pair_width), F32),
         ],
         compiler_params=params(16),
-        cost_estimate=cost(2 * macs, 2**20),
+        cost_estimate=cost(16 * macs, 2**20),
         name="outer",
     )(i_keep, keep, scaled, rbig, *lefts)
     gl_last = reduce(*gl_cut, "col", n_col, gw_cut[0])
 
+    acc = pl.pallas_call(
+        functools.partial(right_first_kernel, steps),
+        in_specs=[hbm()] + vmem(2),
+        out_specs=vmem()[0],
+        out_shape=pltpu.VMEM((depth, span), F32),
+        compiler_params=params(12),
+        cost_estimate=cost(16 * macs, 2**20),
+        name="right_first",
+    )(gl_last[0], z, diag)
+    gw_row = reduce(*gw_cut, "row", n_row, acc)
     gr_cut = pl.pallas_call(
         functools.partial(right_kernel, dims, n_row),
-        in_specs=[hbm()] + vmem(2),
+        in_specs=[hbm()] + vmem(3),
         out_specs=vmem(2),
         out_shape=halves(j_rows * tiles, n_row),
         scratch_shapes=[
@@ -520,40 +546,41 @@
             pltpu.VMEM((j_rows * tiles, LANES), F32),
         ],
         compiler_params=params(18),
-        cost_estimate=cost(macs, 2**20),
+        cost_estimate=cost(16 * macs, 2**20),
         name="right",
-    )(gl_last[0], z, diag)
-    gw_row = reduce(*gw_cut, "row", n_row, gr_cut[0])
-
-    def pair_part(first, last, so_far, after):
-        done = [] if so_far is None else [so_far]
-        return pl.pallas_call(
-            functools.partial(pair_kernel, dims, first, last),
-            in_specs=[hbm()] + vmem(4) + [hbm()] * len(done),
-            out_specs=[hbm()] + vmem(),
-            out_shape=[jax.ShapeDtypeStruct(cotangent.shape, BF16), pltpu.VMEM((8, LANES), F32)],
-            scratch_shapes=[
-                pltpu.VMEM(((last - first) * step_rows, j_rows, pair_width), BF16),
-                pltpu.SemaphoreType.DMA((last - first,)),
-            ],
-            input_output_aliases={5: 0} if done else {},
-            compiler_params=params(12),
-            cost_estimate=cost(macs // 2, 2**20),
-            name="pair",
-        )(after, i_keep, y, weight, inverse, *done)
-
-    ends = (3 * steps // 8, 6 * steps // 8, steps)
-    pair_out, mark = pair_part(0, ends[0], None, gw_row[0])
-    gr_last = reduce(*gr_cut, "row", n_row, mark)
+    )(gw_row[0], z, diag, acc)
     gw_cut = small_call(
         functools.partial(turn_kernel, n_col),
         halves(inner // n_row, n_col),
         "turn",
         [pltpu.VMEM((inner // n_row, pair_width), F32)],
-    )(mark, *gw_row)
-    pair_out, mark = pair_part(ends[0], ends[1], pair_out, gw_cut[0])
-    gw_last = reduce(*gw_cut, "col", n_col, mark)
-    pair_out, mark = pair_part(ends[1], ends[2], pair_out, gw_last[0])
+    )(gr_cut[0], *gw_row)
+
+    half = steps // 2
+    early = pl.pallas_call(
+        functools.partial(pair_first_kernel, dims, half),
+        in_specs=[hbm()] + vmem(4),
+        out_specs=vmem()[0],
+        out_shape=pltpu.VMEM((half * step_rows, j_rows, pair_width), BF16),
+        compiler_params=params(12),
+        cost_estimate=cost(16 * macs, 2**20),
+        name="pair_first",
+    )(gw_cut[0], i_keep, y, weight, inverse)
+    gw_last = reduce(*gw_cut, "col", n_col, early)
+    gr_last = reduce(*gr_cut, "row", n_row, gw_last[0])
+    pair_out = pl.pallas_call(
+        functools.partial(pair_kernel, dims),
+        in_specs=[hbm()] * 2 + vmem(5),
+        out_specs=hbm(),
+        out_shape=jax.ShapeDtypeStruct(cotangent.shape, BF16),
+        scratch_shapes=[
+            pltpu.VMEM((i_rows - half * step_rows, j_rows, pair_width), BF16),
+            pltpu.SemaphoreType.DMA((1 + steps - half,)),
+        ],
+        compiler_params=params(12),
+        cost_estimate=cost(16 * macs, 2**20),
+        name="pair",
+    )(gl_last[1], gr_last[0], i_keep, y, weight, inverse, early)
 
     grad_left, grad_right, grad_weight = pl.pallas_call(
         functools.partial(final_kernel, dims),
@@ -568,7 +595,7 @@
         compiler_params=params(4),
         cost_estimate=cost(1000, 1000),
         name="final_sums",
-    )(mark, i_keep, j_keep, keep, *gl_last, *gr_last, *gw_last)
+    )(in_hbm(pair_out), i_keep, j_keep, keep, *gl_last, *gr_last, *gw_last)
     return (pair_out, grad_left, grad_right, grad_weight)
 
 

time: 43.9 us -> 43.4 us (0.989)
  waiting for transfers between devices: 2.8 us -> 5.11 us
  starting transfers between devices: 15.6 us -> 14.2 us
  Pallas kernels: 24.5 us -> 23.2 us
    ppermute x12, waiting for transfers between devices: 2.8 us -> 5.11 us  [swap(): return lax.ppermute(array, axis, [(s, s ^ bit) for s in range(n)])]
    ppermute x12, starting transfers between devices: 15.6 us -> 14.2 us  [swap(): return lax.ppermute(array, axis, [(s, s ^ bit) for s in range(n)])]
    pallas_call x1, Pallas kernels: 3.61 us -> 2.33 us  [shards(): pl.pallas_call(functools.partial(right_kernel, dims, n_row), in_specs=[hb...]
  transfers between devices with their start and end apart: 12 -> 12, of which waited for: 4 -> 4; matrix products, arithmetic and copies ran while one was open for 0% -> 0% of each run, Pallas kernels for 54% -> 52%
where the time goes in v7:
time: 43.4 us; the launch traced here: 43.3 us
  Pallas kernels  23.2 us (53%)
  starting transfers between devices  14.2 us (33%)
  waiting for transfers between devices  5.11 us (12%)
  between operations  0.76 us (2%)
    ppermute x12, starting transfers between devices, swap(): return lax.ppermute(array, axis, [(s, s ^ bit) for s in range(n)])  14.2 us
    pallas_call x1, Pallas kernels, shards(): pl.pallas_call(functools.partial(outer_kernel, dims, n_row, n_col), in_sp...  6.63 us
    ppermute x12, waiting for transfers between devices, swap(): return lax.ppermute(array, axis, [(s, s ^ bit) for s in range(n)])  5.11 us
    pallas_call x1, Pallas kernels, shards(): pl.pallas_call(functools.partial(left_kernel, dims, n_row, n_col), in_spe...  3.63 us
    pallas_call x1, Pallas kernels, shards(): pl.pallas_call(functools.partial(inner_kernel, dims), in_specs=[hbm()] +...  2.87 us
    pallas_call x1, Pallas kernels, shards(): pl.pallas_call(functools.partial(right_kernel, dims, n_row), in_specs=[hb...  2.33 us
    pallas_call x1, Pallas kernels, shards(): pl.pallas_call(functools.partial(scale_kernel, dims), in_specs=[hbm()] *...  2.03 us
    pallas_call x1, Pallas kernels, shards(): pl.pallas_call(functools.partial(pair_kernel, dims), in_specs=[hbm()] * 2...  2 us
  transfers between devices with their start and end apart: 12, of which 4 were waited for; matrix products, arithmetic and copies ran while one was open for 0% of the time, Pallas kernels for 52%

profile of v7, /device:TPU:0, one launch (start us, length us, event | category | flops | bytes accessed | tf_op | source)
XLA Modules:
  0.0 43.3 jit_solution(8482629708879025167)
XLA Ops:
  0.6 3.0 %collective-permute-start.1 = (bf16[1,16,2048]{2,1,0:T(8,128)(2,1)}, bf16[1,16,2048]{2,1,0:T(8,128)(2,1)S(1)}, u32[]{:S(2)}, u32[]{:S(2)}) collective-permute-start(bf16[1,16,2048]{2,1,0:T(8,128)(2,1)} %bitcast.5), channel_id=1, source_target_pairs={{0,8},{4,12},{8,0},{12,4},{1,9},{5,13},{9,1},{13,5},{2,10},{6,14},... | collective-permute-start | bytes 196616 | tf_op jit(solution)/shard_map/ppermute | solution.py:364
  3.6 2.6 %collective-permute-start = (bf16[1,16,2048]{2,1,0:T(8,128)(2,1)}, bf16[1,16,2048]{2,1,0:T(8,128)(2,1)S(1)}, u32[]{:S(2)}, u32[]{:S(2)}) collective-permute-start(bf16[1,16,2048]{2,1,0:T(8,128)(2,1)} %bitcast.4), channel_id=1, source_target_pairs={{0,2},{1,3},{2,0},{3,1},{4,6},{5,7},{6,4},{7,5},{8,10},{9,11},{10,... | collective-permute-start | bytes 196616 | tf_op jit(solution)/shard_map/ppermute | solution.py:364
  6.2 2.0 %scale.1 = (bf16[64,64,128]{2,1,0:T(8,128)(2,1)S(1)}, f32[64,128]{1,0:T(8,128)S(1)}, bf16[1024,128]{1,0:T(8,128)(2,1)S(1)}, f32[1,2048]{1,0:T(1,128)S(1)}, f32[6...) custom-call(s32[1,256]{1,0:T(1,128)} %bitcast.6, ...), custom_call_target="tpu_custom_call" | custom-call | flops 8589934592 | bytes 1048576 | tf_op jit(solution)/shard_map/scale/pallas_call | solution.py:449
  8.3 1.0 %collective-permute-done.came_ref = bf16[1,16,2048]{2,1,0:T(8,128)(2,1)S(1)} collective-permute-done((bf16[1,16,2048]{2,1,0:T(8,128)(2,1)}, bf16[1,16,2048]{2,1,0:T(8,128)(2,1)S(1)}, u32[]{:S(2)}, u32[]{:S(2)}) %collective-permute-start) | collective-permute-done | bytes 65568 | tf_op jit(solution)/shard_map/ppermute | solution.py:364
  9.3 1.3 %collective-permute-start.3 = (bf16[2,16,2048]{2,1,0:T(8,128)(2,1)S(1)}, bf16[2,16,2048]{2,1,0:T(8,128)(2,1)S(1)}, u32[]{:S(2)}, u32[]{:S(2)}) collective-permute-start(bf16[2,16,2048]{2,1,0:T(8,128)(2,1)S(1)} %join.2.after.refs_4_), channel_id=1, source_target_pairs={{0,1},{1,0},{2,3},{3,2},{4,5},{5,4},{6,7},{7,6},{8,9},{9,8},{10,11... | collective-permute-start | bytes 393224 | tf_op jit(solution)/shard_map/ppermute | solution.py:364
  10.7 0.1 collective-permute-start.2
  10.8 2.9 %inner.1.refs_0_.refs_3_.z_ref.refs_1_ = bf16[8,512,1024]{2,1,0:T(8,128)(2,1)S(1)} custom-call(bf16[2,16,2048]{2,1,0:T(8,128)(2,1)S(1)} %join.3.after.refs_4_, bf16[64,64,128]{2,1,0:T(8,128)(2,1)S(1)} %get-tuple-element.36.scaled_ref.refs_2_, bf16[1024,128]{1,0:T(8,128)(2,1)S(1)} %get-tuple-element.39.wp_ref.refs_4_), custom_call_target="tpu_custom_call" | custom-call | flops 8589934592 | bytes 1048576 | tf_op jit(solution)/shard_map/inner/pallas_call | solution.py:480
  13.6 3.6 %left.1 = (bf16[512,256]{1,0:T(8,128)(2,1)S(1)}, bf16[2,256,128]{2,1,0:T(8,128)(2,1)S(1)}, bf16[2,256,128]{2,1,0:T(8,128)(2,1)S(1)}) custom-call(bf16[8,512,1024]{2,1,0:T(8,128)(2,1)S(1)} %inner.1.refs_0_.refs_3_.z_ref.refs_1_, f32[64,128]{1,0:T(8,128)S(1)} %get-tuple-element.40.refs_1_.rj_ref, f32[1,2048]{1,0:T(1,128)S(1)} %get-tuple-element.35.refs_2_.refs_1_.keep_ref, ...), custom_call_target="tpu_custom_call" | custom-call | flops 8589934592 | bytes 1048576 | tf_op jit(solution)/shard_map/left/pallas_call | solution.py:490
  17.3 0.8 %collective-permute-start.4 = (bf16[2,256,128]{2,1,0:T(8,128)(2,1)S(1)}, bf16[2,256,128]{2,1,0:T(8,128)(2,1)S(1)}, u32[]{:S(2)}, u32[]{:S(2)}) collective-permute-start(bf16[2,256,128]{2,1,0:T(8,128)(2,1)S(1)} %get-tuple-element.44), channel_id=1, source_target_pairs={{0,1},{1,0},{2,3},{3,2},{4,5},{5,4},{6,7},{7,6},{8,9},{9,8},{10,11... | collective-permute-start | bytes 393224 | tf_op jit(solution)/shard_map/ppermute | solution.py:364
  18.1 6.6 %outer.1 = (bf16[64,64,1024]{2,1,0:T(8,128)(2,1)S(1)}, bf16[8,256,1024]{2,1,0:T(8,128)(2,1)S(1)}, bf16[2,256,128]{2,1,0:T(8,128)(2,1)S(1)}, bf16[2,256,128]{2,1,0:T(8,128)(2,1)S(1)}) custom-call(f32[64,128]{1,0:T(8,128)S(1)} %get-tuple-element.34.refs_0_.ri_ref.refs_2_, f32[1,2048]{1,0:T(1,128)S(1)} %get-tuple-element.35.refs_2_.refs_1_.keep_ref, ...), custom_call_target="tpu_custom_call" | custom-call | flops 8589934592 | bytes 1048576 | tf_op jit(solution)/shard_map/outer/pallas_call | solution.py:506
  24.7 0.3 collective-permute-start.6
  25.1 2.8 %collective-permute-start.5 = (bf16[1,256,128]{2,1,0:T(8,128)(2,1)S(1)}, bf16[1,256,128]{2,1,0:T(8,128)(2,1)S(1)}, u32[]{:S(2)}, u32[]{:S(2)}) collective-permute-start(bf16[1,256,128]{2,1,0:T(8,128)(2,1)S(1)} %get-tuple-element.45), channel_id=1, source_target_pairs={{0,2},{1,3},{2,0},{3,1},{4,6},{5,7},{6,4},{7,5},{8,10},{9,11},{10,... | collective-permute-start | bytes 196616 | tf_op jit(solution)/shard_map/ppermute | solution.py:364
  27.8 1.5 %right_first.1.after.refs_3_ = f32[256,512]{1,0:T(8,128)S(1)} custom-call(f32[1,256,128]{2,1,0:T(8,128)S(1)} %get-tuple-element.46.after.refs_0_, bf16[8,512,1024]{2,1,0:T(8,128)(2,1)S(1)} %inner.1.refs_0_.refs_3_.z_ref.refs_1_, bf16[8,256,1024]{2,1,0:T(8,128)(2,1)S(1)} %get-tuple-element.47.diag_ref.refs_2_), custom_call_target="tpu_custom_call" | custom-call | flops 8589934592 | bytes 1048576 | tf_op jit(solution)/shard_map/right_first/pallas_call | solution.py:528
  29.4 0.6 %collective-permute-start.7 = (bf16[1,256,128]{2,1,0:T(8,128)(2,1)S(1)}, bf16[1,256,128]{2,1,0:T(8,128)(2,1)S(1)}, u32[]{:S(2)}, u32[]{:S(2)}) collective-permute-start(bf16[1,256,128]{2,1,0:T(8,128)(2,1)S(1)} %get-tuple-element.51), channel_id=1, source_target_pairs={{0,8},{4,12},{8,0},{12,4},{1,9},{5,13},{9,1},{13,5},{2,10},{6,14},... | collective-permute-start | bytes 196616 | tf_op jit(solution)/shard_map/ppermute | solution.py:364
  30.0 2.3 %right.1 = (bf16[2,256,128]{2,1,0:T(8,128)(2,1)S(1)}, bf16[2,256,128]{2,1,0:T(8,128)(2,1)S(1)}) custom-call(f32[1,256,128]{2,1,0:T(8,128)S(1)} %get-tuple-element.49.refs_0_.held_ref, bf16[8,512,1024]{2,1,0:T(8,128)(2,1)S(1)} %inner.1.refs_0_.refs_3_.z_ref.refs_1_, bf16[8,256,1024]{2,1,0:T(8,128)(2,1)S(1)} %get-tuple-element.47.diag_ref.refs_2_, ...), custom_call_target="tpu_custom_call" | custom-call | flops 8589934592 | bytes 1048576 | tf_op jit(solution)/shard_map/right/pallas_call | solution.py:538
  32.4 1.3 %collective-permute-done.7.came_ref = bf16[1,256,128]{2,1,0:T(8,128)(2,1)S(1)} collective-permute-done((bf16[1,256,128]{2,1,0:T(8,128)(2,1)S(1)}, bf16[1,256,128]{2,1,0:T(8,128)(2,1)S(1)}, u32[]{:S(2)}, u32[]{:S(2)}) %collective-permute-start.7) | collective-permute-done | bytes 65568 | tf_op jit(solution)/shard_map/ppermute | solution.py:364
  33.7 1.8 %collective-permute-start.8 = (bf16[2,64,128]{2,1,0:T(8,128)(2,1)S(1)}, bf16[2,64,128]{2,1,0:T(8,128)(2,1)S(1)}, u32[]{:S(2)}, u32[]{:S(2)}) collective-permute-start(bf16[2,64,128]{2,1,0:T(8,128)(2,1)S(1)} %get-tuple-element.55), channel_id=1, source_target_pairs={{0,1},{1,0},{2,3},{3,2},{4,5},{5,4},{6,7},{7,6},{8,9},{9,8},{10,11... | collective-permute-start | bytes 98312 | tf_op jit(solution)/shard_map/ppermute | solution.py:364
  35.5 1.2 %pair_first.1.after.refs_6_ = bf16[32,64,128]{2,1,0:T(8,128)(2,1)S(1)} custom-call(bf16[2,64,128]{2,1,0:T(8,128)(2,1)S(1)} %get-tuple-element.52.after.held_ref, f32[64,128]{1,0:T(8,128)S(1)} %get-tuple-element.34.refs_0_.ri_ref.refs_2_, bf16[64,64,1024]{2,1,0:T(8,128)(2,1)S(1)} %get-tuple-element.53.y_ref.refs_3_, ...), custom_call_target="tpu_custom_call" | custom-call | flops 8589934592 | bytes 1048576 | tf_op jit(solution)/shard_map/pair_first/pallas_call | solution.py:560
  36.8 0.9 %collective-permute-done.8.came_ref = bf16[2,64,128]{2,1,0:T(8,128)(2,1)S(1)} collective-permute-done((bf16[2,64,128]{2,1,0:T(8,128)(2,1)S(1)}, bf16[2,64,128]{2,1,0:T(8,128)(2,1)S(1)}, u32[]{:S(2)}, u32[]{:S(2)}) %collective-permute-start.8) | collective-permute-done | bytes 32800 | tf_op jit(solution)/shard_map/ppermute | solution.py:364
  37.7 0.3 collective-permute-start.11
  38.0 0.6 %collective-permute-start.10 = (bf16[1,256,128]{2,1,0:T(8,128)(2,1)S(1)}, bf16[1,256,128]{2,1,0:T(8,128)(2,1)S(1)}, u32[]{:S(2)}, u32[]{:S(2)}) collective-permute-start(bf16[1,256,128]{2,1,0:T(8,128)(2,1)S(1)} %get-tuple-element.59), channel_id=1, source_target_pairs={{0,8},{4,12},{8,0},{12,4},{1,9},{5,13},{9,1},{13,5},{2,10},{6,14},... | collective-permute-start | bytes 196616 | tf_op jit(solution)/shard_map/ppermute | solution.py:364
  38.6 2.0 %pair.1.after = bf16[64,64,128]{2,1,0:T(8,128)(2,1)} custom-call(bf16[1,256,128]{2,1,0:T(8,128)(2,1)S(1)} %collective-permute-done.5.refs_0_.refs_1_, f32[1,256,128]{2,1,0:T(8,128)S(1)} %get-tuple-element.58.refs_1_.refs_2_, f32[64,128]{1,0:T(8,128)S(1)} %get-tuple-element.34.refs_0_.ri_ref.refs_2_, ...), custom_call_target="tpu_custom_call" | custom-call | flops 8589934592 | bytes 1048576 | tf_op jit(solution)/shard_map/pair/pallas_call | solution.py:571
  40.6 1.8 %collective-permute-done.11.refs_5_ = bf16[1,64,128]{2,1,0:T(8,128)(2,1)S(1)} collective-permute-done((bf16[1,64,128]{2,1,0:T(8,128)(2,1)S(1)}, bf16[1,64,128]{2,1,0:T(8,128)(2,1)S(1)}, u32[]{:S(2)}, u32[]{:S(2)}) %collective-permute-start.11) | collective-permute-done | bytes 16416 | tf_op jit(solution)/shard_map/ppermute | solution.py:364
  42.4 0.8 %final_sums.1 = (f32[16,2048]{1,0:T(8,128)}, f32[16,2048]{1,0:T(8,128)}, f32[64,128]{1,0:T(8,128)}) custom-call(bf16[64,64,128]{2,1,0:T(8,128)(2,1)} %pair.1.after, f32[64,128]{1,0:T(8,128)S(1)} %get-tuple-element.34.refs_0_.ri_ref.refs_2_, f32[64,128]{1,0:T(8,128)S(1)} %get-tuple-element.40.refs_1_.rj_ref, ...), custom_call_target="tpu_custom_call" | custom-call | flops 1000 | bytes 1000 | tf_op jit(solution)/shard_map/final_sums/pallas_call | solution.py:585
  (16 shorter events, 0.2 us)
Async XLA Ops:
  0.6 10.0 %collective-permute-start.1 = (bf16[1,16,2048]{2,1,0:T(8,128)(2,1)}, bf16[1,16,2048]{2,1,0:T(8,128)(2,1)S(1)}, u32[]{:S(2)}, u32[]{:S(2)}) collective-permute-start(bf16[1,16,2048]{2,1,0:T(8,128)(2,1)} %bitcast.5), channel_id=1, source_target_pairs={{0,8},{4,12},{8,0},{12,4},{1,9},{5,13},{9,1},{13,5},{2,10},{6,14},... | collective-permute-start | bytes 196616 | tf_op jit(solution)/shard_map/ppermute | solution.py:364
  3.6 5.7 %collective-permute-start = (bf16[1,16,2048]{2,1,0:T(8,128)(2,1)}, bf16[1,16,2048]{2,1,0:T(8,128)(2,1)S(1)}, u32[]{:S(2)}, u32[]{:S(2)}) collective-permute-start(bf16[1,16,2048]{2,1,0:T(8,128)(2,1)} %bitcast.4), channel_id=1, source_target_pairs={{0,2},{1,3},{2,0},{3,1},{4,6},{5,7},{6,4},{7,5},{8,10},{9,11},{10,... | collective-permute-start | bytes 196616 | tf_op jit(solution)/shard_map/ppermute | solution.py:364
  9.3 8.8 %collective-permute-start.3 = (bf16[2,16,2048]{2,1,0:T(8,128)(2,1)S(1)}, bf16[2,16,2048]{2,1,0:T(8,128)(2,1)S(1)}, u32[]{:S(2)}, u32[]{:S(2)}) collective-permute-start(bf16[2,16,2048]{2,1,0:T(8,128)(2,1)S(1)} %join.2.after.refs_4_), channel_id=1, source_target_pairs={{0,1},{1,0},{2,3},{3,2},{4,5},{5,4},{6,7},{7,6},{8,9},{9,8},{10,11... | collective-permute-start | bytes 393224 | tf_op jit(solution)/shard_map/ppermute | solution.py:364
  10.7 3.0 %collective-permute-start.2 = (bf16[2,16,2048]{2,1,0:T(8,128)(2,1)S(1)}, bf16[2,16,2048]{2,1,0:T(8,128)(2,1)S(1)}, u32[]{:S(2)}, u32[]{:S(2)}) collective-permute-start(bf16[2,16,2048]{2,1,0:T(8,128)(2,1)S(1)} %join.3.after.refs_4_), channel_id=1, source_target_pairs={{0,4},{4,0},{8,12},{12,8},{1,5},{5,1},{9,13},{13,9},{2,6},{6,2},{1... | collective-permute-start | bytes 393224 | tf_op jit(solution)/shard_map/ppermute | solution.py:364
  17.3 7.7 %collective-permute-start.4 = (bf16[2,256,128]{2,1,0:T(8,128)(2,1)S(1)}, bf16[2,256,128]{2,1,0:T(8,128)(2,1)S(1)}, u32[]{:S(2)}, u32[]{:S(2)}) collective-permute-start(bf16[2,256,128]{2,1,0:T(8,128)(2,1)S(1)} %get-tuple-element.44), channel_id=1, source_target_pairs={{0,1},{1,0},{2,3},{3,2},{4,5},{5,4},{6,7},{7,6},{8,9},{9,8},{10,11... | collective-permute-start | bytes 393224 | tf_op jit(solution)/shard_map/ppermute | solution.py:364
  24.7 4.6 %collective-permute-start.6 = (bf16[2,256,128]{2,1,0:T(8,128)(2,1)S(1)}, bf16[2,256,128]{2,1,0:T(8,128)(2,1)S(1)}, u32[]{:S(2)}, u32[]{:S(2)}) collective-permute-start(bf16[2,256,128]{2,1,0:T(8,128)(2,1)S(1)} %get-tuple-element.48), channel_id=1, source_target_pairs={{0,4},{4,0},{8,12},{12,8},{1,5},{5,1},{9,13},{13,9},{2,6},{6,2},{1... | collective-permute-start | bytes 393224 | tf_op jit(solution)/shard_map/ppermute | solution.py:364
  25.1 13.6 %collective-permute-start.5 = (bf16[1,256,128]{2,1,0:T(8,128)(2,1)S(1)}, bf16[1,256,128]{2,1,0:T(8,128)(2,1)S(1)}, u32[]{:S(2)}, u32[]{:S(2)}) collective-permute-start(bf16[1,256,128]{2,1,0:T(8,128)(2,1)S(1)} %get-tuple-element.45), channel_id=1, source_target_pairs={{0,2},{1,3},{2,0},{3,1},{4,6},{5,7},{6,4},{7,5},{8,10},{9,11},{10,... | collective-permute-start | bytes 196616 | tf_op jit(solution)/shard_map/ppermute | solution.py:364
  29.4 4.3 %collective-permute-start.7 = (bf16[1,256,128]{2,1,0:T(8,128)(2,1)S(1)}, bf16[1,256,128]{2,1,0:T(8,128)(2,1)S(1)}, u32[]{:S(2)}, u32[]{:S(2)}) collective-permute-start(bf16[1,256,128]{2,1,0:T(8,128)(2,1)S(1)} %get-tuple-element.51), channel_id=1, source_target_pairs={{0,8},{4,12},{8,0},{12,4},{1,9},{5,13},{9,1},{13,5},{2,10},{6,14},... | collective-permute-start | bytes 196616 | tf_op jit(solution)/shard_map/ppermute | solution.py:364
  32.3 5.7 %collective-permute-start.9 = (bf16[2,256,128]{2,1,0:T(8,128)(2,1)S(1)}, bf16[2,256,128]{2,1,0:T(8,128)(2,1)S(1)}, u32[]{:S(2)}, u32[]{:S(2)}) collective-permute-start(bf16[2,256,128]{2,1,0:T(8,128)(2,1)S(1)} %get-tuple-element.57), channel_id=1, source_target_pairs={{0,4},{4,0},{8,12},{12,8},{1,5},{5,1},{9,13},{13,9},{2,6},{6,2},{1... | collective-permute-start | bytes 393224 | tf_op jit(solution)/shard_map/ppermute | solution.py:364
  33.7 4.0 %collective-permute-start.8 = (bf16[2,64,128]{2,1,0:T(8,128)(2,1)S(1)}, bf16[2,64,128]{2,1,0:T(8,128)(2,1)S(1)}, u32[]{:S(2)}, u32[]{:S(2)}) collective-permute-start(bf16[2,64,128]{2,1,0:T(8,128)(2,1)S(1)} %get-tuple-element.55), channel_id=1, source_target_pairs={{0,1},{1,0},{2,3},{3,2},{4,5},{5,4},{6,7},{7,6},{8,9},{9,8},{10,11... | collective-permute-start | bytes 98312 | tf_op jit(solution)/shard_map/ppermute | solution.py:364
  37.7 4.7 %collective-permute-start.11 = (bf16[1,64,128]{2,1,0:T(8,128)(2,1)S(1)}, bf16[1,64,128]{2,1,0:T(8,128)(2,1)S(1)}, u32[]{:S(2)}, u32[]{:S(2)}) collective-permute-start(bf16[1,64,128]{2,1,0:T(8,128)(2,1)S(1)} %get-tuple-element.60), channel_id=1, source_target_pairs={{0,2},{1,3},{2,0},{3,1},{4,6},{5,7},{6,4},{7,5},{8,10},{9,11},{10,... | collective-permute-start | bytes 49160 | tf_op jit(solution)/shard_map/ppermute | solution.py:364
  38.0 4.4 %collective-permute-start.10 = (bf16[1,256,128]{2,1,0:T(8,128)(2,1)S(1)}, bf16[1,256,128]{2,1,0:T(8,128)(2,1)S(1)}, u32[]{:S(2)}, u32[]{:S(2)}) collective-permute-start(bf16[1,256,128]{2,1,0:T(8,128)(2,1)S(1)} %get-tuple-element.59), channel_id=1, source_target_pairs={{0,8},{4,12},{8,0},{12,4},{1,9},{5,13},{9,1},{13,5},{2,10},{6,14},... | collective-permute-start | bytes 196616 | tf_op jit(solution)/shard_map/ppermute | solution.py:364

commit v8 on v7

--- a/solution.py
+++ b/solution.py
@@ -53,8 +53,8 @@
     chans, groups, blocks, i_rows, j_rows, step_rows, sequences = dims
     tiles = sequences * chans // LANES
     res_hbm, seq_hbm, cot_ref, w_hbm, left_hbm, right_hbm = refs[:6]
-    scaled_ref, inv_ref, wp_ref, keep_ref, ri_ref, rj_ref, left_ref, right_ref = refs[6:14]
-    res_ref, seq_ref, w_ref, w32, cot, sems, more_sems = refs[14:]
+    scaled_ref, inv_ref, wp_ref, keep_ref, ri_ref, rj_ref, left_ref, right_ref, z_ref = refs[6:15]
+    res_ref, seq_ref, w_ref, w32, cot, sems, more_sems = refs[15:]
     steps = i_rows // step_rows
 
     def fetch(step):
@@ -100,28 +100,42 @@
             at = step * step_rows + i
             inverse = jnp.where(ri_ref[at : at + 1, :] > 0, inv_ref[...], 1.0)
             scaled_ref[at] = (cot[at].astype(F32) * inverse).astype(BF16)
+        if step < z_ref.shape[0]:
+            rows = slice(step * step_rows, (step + 1) * step_rows)
+            inner_rows(dims, scaled_ref[rows], wp_ref, z_ref, step)
     more[3].wait()
     more[4].wait()
 
 
-def inner_kernel(dims, after, scaled_ref, wp_ref, z_ref):
-    chans, groups, blocks, i_rows, j_rows, step_rows, sequences = dims
-    for step in range(i_rows // step_rows):
-        rows = slice(step * step_rows, (step + 1) * step_rows)
-        scaled = scaled_ref[rows].reshape(step_rows * j_rows, LANES)
-        for pair in range(0, blocks, 2):
-            part = lax.dot_general(
-                scaled,
-                wp_ref[pair * LANES : (pair + 2) * LANES, :],
-                NT,
-                preferred_element_type=F32,
-            ).astype(BF16)
-            for k in range(2):
-                a = pair + k
-                for i in range(step_rows):
-                    z_ref[
-                        step, a * j_rows : (a + 1) * j_rows, i * LANES : (i + 1) * LANES
-                    ] = part[i * j_rows : (i + 1) * j_rows, k * LANES : (k + 1) * LANES]
+def inner_rows(dims, scaled, wp_ref, z_ref, at):
+    chans, groups, blocks, i_rows, j_rows, step_rows, sequences = dims
+    for pair in range(0, blocks, 2):
+        part = lax.dot_general(
+            scaled.reshape(step_rows * j_rows, LANES),
+            wp_ref[pair * LANES : (pair + 2) * LANES, :],
+            NT,
+            preferred_element_type=F32,
+        ).astype(BF16)
+        for k in range(2):
+            a = pair + k
+            for i in range(step_rows):
+                z_ref[at, a * j_rows : (a + 1) * j_rows, i * LANES : (i + 1) * LANES] = part[
+                    i * j_rows : (i + 1) * j_rows, k * LANES : (k + 1) * LANES
+                ]
+
+
+def inner_kernel(dims, first, after, scaled_ref, wp_ref, z_ref):
+    step_rows = dims[5]
+    for at in range(z_ref.shape[0]):
+        rows = slice((first + at) * step_rows, (first + at + 1) * step_rows)
+        inner_rows(dims, scaled_ref[rows], wp_ref, z_ref, at)
+
+
+def at_step(refs, step):
+    for ref in refs:
+        if step < ref.shape[0]:
+            return ref.at[step]
+        step -= ref.shape[0]
 
 
 def outer_kernel(dims, n_row, n_col, *refs):
@@ -140,14 +154,13 @@
     target = lax.broadcasted_iota(jnp.int32, shape, 1)
     same = (source // chans == target // LANES) & (source % chans == target % chans)
     expand[...] = same.astype(F32).astype(BF16)
-    gwt[...] = jnp.zeros_like(gwt)
     rows = step_rows * tiles
     pairs = step_rows * j_rows
     group = lane_group((tiles, LANES), chans)
 
-    def body(step, carry):
+    for step in range(i_rows // step_rows):
         spread = jnp.dot(
-            lsplit[pl.ds(pl.multiple_of(step * rows, rows), rows), :].astype(BF16),
+            lsplit[step * rows : (step + 1) * rows, :].astype(BF16),
             expand[...],
             preferred_element_type=F32,
         ).astype(BF16)
@@ -170,13 +183,11 @@
                     y_ref[step * step_rows + pair + k, :, a * LANES : (a + 1) * LANES] = part[
                         a * j_rows : (a + 1) * j_rows, k * LANES : (k + 1) * LANES
                     ]
-        block = pl.ds(step * step_rows, step_rows)
+        block = slice(step * step_rows, (step + 1) * step_rows)
         scaled_t = scaled_ref[block].reshape(pairs, LANES).T
         y_flat = y_ref[block].reshape(pairs, blocks * LANES)
-        gwt[...] += jnp.dot(scaled_t, y_flat, preferred_element_type=F32)
-        return carry
-
-    lax.fori_loop(0, i_rows // step_rows, body, 0, unroll=True)
+        part = jnp.dot(scaled_t, y_flat, preferred_element_type=F32)
+        gwt[...] = gwt[...] + part if step else part
     for k in range(blocks):
         turned_tile = gwt[:, k * LANES : (k + 1) * LANES].T
         for q in range(groups):
@@ -186,25 +197,16 @@
     cut(gwr, lax.axis_index("row"), n_row, keep_out, send_out)
 
 
-def right_sum(first, last, z_ref, diag_ref, acc, so_far=None):
-    for step in range(first, last):
-        part = lax.dot_general(diag_ref[step], z_ref[step], NT, preferred_element_type=F32)
-        acc[...] = part if so_far is None else so_far[...] + part
-        so_far = acc
-
-
-def right_first_kernel(steps, after, z_ref, diag_ref, acc):
-    right_sum(0, steps // 2, z_ref, diag_ref, acc)
-
-
-def right_kernel(dims, n_row, *refs):
+def right_kernel(dims, n_row, after, diag_ref, *refs):
     chans, groups, blocks, i_rows, j_rows, step_rows, sequences = dims
     tiles = sequences * chans // LANES
     j_pad = -(-j_rows // LANES) * LANES
-    after, z_ref, diag_ref, acc_first = refs[:4]
-    keep_out, send_out, acc, turned, gr_all = refs[4:]
-    steps = i_rows // step_rows
-    right_sum(steps // 2, steps, z_ref, diag_ref, acc, acc_first)
+    z_refs, (keep_out, send_out, acc, turned, gr_all) = refs[:-5], refs[-5:]
+    for step in range(i_rows // step_rows):
+        part = lax.dot_general(
+            diag_ref[step], at_step(z_refs, step)[...], NT, preferred_element_type=F32
+        )
+        acc[...] = acc[...] + part if step else part
     for a in range(blocks):
         at, shift = divmod(a * j_rows, LANES)
         mine = acc[:, at * LANES : at * LANES + j_pad]
@@ -222,13 +224,11 @@
     cut(gr_all, lax.axis_index("row"), n_row, keep_out, send_out)
 
 
-def left_kernel(dims, n_row, n_col, *refs):
+def right_rows_kernel(dims, n_row, after, rj_ref, keep_ref, right_held, right_came, *refs):
     chans, groups, blocks, i_rows, j_rows, step_rows, sequences = dims
     tiles = sequences * chans // LANES
     j_pad = -(-j_rows // LANES) * LANES
-    after, rj_ref, keep_ref, z_ref, right_held, right_came = refs[:6]
-    rbig, keep_out, send_out = refs[6:9]
-    flat, turned, rbt, gl_all = refs[9:]
+    rbig, rbt_ref, flat, turned = refs
     place((right_held, right_came), lax.axis_index("row"), n_row, flat)
     for t in range(tiles):
         lanes = slice(t * LANES, (t + 1) * LANES)
@@ -244,15 +244,22 @@
         ]
         block = jnp.concatenate(parts, axis=0)
         rbig[a * j_rows : (a + 1) * j_rows, :] = block.T[:j_rows].astype(BF16)
-    rbt[...] = rbig[...].T
+    rbt_ref[...] = rbig[...].T
+
+
+def left_kernel(dims, n_col, after, rbt_ref, *refs):
+    chans, groups, blocks, i_rows, j_rows, step_rows, sequences = dims
+    tiles = sequences * chans // LANES
+    z_refs, (keep_out, send_out, gl_all) = refs[:-3], refs[-3:]
     group = lane_group((sequences, LANES), chans)
     group_t = lane_group((tiles, LANES), chans)
 
-    def body(step, carry):
+    for step in range(i_rows // step_rows):
+        z_ref = at_step(z_refs, step)
         for pair in range(0, step_rows, 2):
             part = jnp.dot(
-                rbt[...],
-                z_ref[step, :, pair * LANES : (pair + 2) * LANES],
+                rbt_ref[...],
+                z_ref[:, pair * LANES : (pair + 2) * LANES],
                 preferred_element_type=F32,
             )
             for k in range(2):
@@ -268,10 +275,7 @@
                 for lo in range(1, groups):
                     merged = jnp.where(group_t == lo, total[lo * tiles : (lo + 1) * tiles], merged)
                 at = (step * step_rows + pair + k) * tiles
-                gl_all[pl.ds(pl.multiple_of(at, tiles), tiles), :] = merged
-        return carry
-
-    lax.fori_loop(0, i_rows // step_rows, body, 0, unroll=True)
+                gl_all[at : at + tiles, :] = merged
     cut(gl_all, lax.axis_index("col"), n_col, keep_out, send_out)
 
 
@@ -437,8 +441,9 @@
     tiles = width // LANES
     depth = groups * sequences
     inner = chans * chans
-    step_rows = 8
+    step_rows = 16
     steps = i_rows // step_rows
+    early_steps = steps // 4
     dims = (chans, groups, blocks, i_rows, j_rows, step_rows, sequences)
     j_pad = -(-j_rows // LANES) * LANES
     span = blocks * j_rows
@@ -446,10 +451,10 @@
     macs = i_rows * j_rows * inner * pair_width
 
     mask_row = (res_mask.reshape(1, -1), row_mask.reshape(1, -1))
-    scaled, inverse, weight, keep, i_keep, j_keep, own_l, own_r = pl.pallas_call(
+    scaled, inverse, weight, keep, i_keep, j_keep, own_l, own_r, z_first = pl.pallas_call(
         functools.partial(scale_kernel, dims),
         in_specs=[hbm()] * 6,
-        out_specs=vmem(8),
+        out_specs=vmem(9),
         out_shape=[
             pltpu.VMEM(cotangent.shape, BF16),
             pltpu.VMEM((j_rows, LANES), F32),
@@ -459,6 +464,7 @@
             pltpu.VMEM((j_rows, LANES), F32),
             pltpu.VMEM((1,) + left_act.shape, BF16),
             pltpu.VMEM((1,) + right_act.shape, BF16),
+            pltpu.VMEM((early_steps, span, step_rows * LANES), BF16),
         ],
         scratch_shapes=[
             pltpu.VMEM((1, res_mask.shape[0]), jnp.int32),
@@ -469,7 +475,7 @@
             pltpu.SemaphoreType.DMA((steps,)),
             pltpu.SemaphoreType.DMA((5,)),
         ],
-        compiler_params=params(12),
+        compiler_params=params(16),
         cost_estimate=cost(16 * macs, 2**20),
         name="scale",
     )(*map(in_hbm, (*mask_row, cotangent, out_weight, left_act, right_act)))
@@ -477,31 +483,27 @@
     lefts = gather(left_act, own_l, "col", n_col, own_l)
     rights = gather(right_act, own_r, "row", n_row, lefts[0])
 
-    z = pl.pallas_call(
-        functools.partial(inner_kernel, dims),
+    z_last = pl.pallas_call(
+        functools.partial(inner_kernel, dims, early_steps),
         in_specs=[hbm()] + vmem(2),
         out_specs=vmem()[0],
-        out_shape=pltpu.VMEM((steps, span, step_rows * LANES), BF16),
-        compiler_params=params(12),
+        out_shape=pltpu.VMEM((steps - early_steps, span, step_rows * LANES), BF16),
+        compiler_params=params(16),
         cost_estimate=cost(16 * macs, 2**20),
         name="inner",
     )(rights[0], scaled, weight)
-
-    rbig, *gl_cut = pl.pallas_call(
-        functools.partial(left_kernel, dims, n_row, n_col),
-        in_specs=[hbm()] + vmem(5),
-        out_specs=vmem(3),
-        out_shape=[pltpu.VMEM((span, depth), BF16)] + halves(i_rows * tiles, n_col),
-        scratch_shapes=[
-            pltpu.VMEM((j_rows, width), F32),
-            pltpu.VMEM((width, j_pad), F32),
-            pltpu.VMEM((depth, span), BF16),
-            pltpu.VMEM((i_rows * tiles, LANES), F32),
-        ],
-        compiler_params=params(16),
-        cost_estimate=cost(16 * macs, 2**20),
-        name="left",
-    )(z, j_keep, keep, z, *rights)
+    z = (z_first, z_last)
+
+    rbig, right_turned = pl.pallas_call(
+        functools.partial(right_rows_kernel, dims, n_row),
+        in_specs=[hbm()] + vmem(4),
+        out_specs=vmem(2),
+        out_shape=[pltpu.VMEM((span, depth), BF16), pltpu.VMEM((depth, span), BF16)],
+        scratch_shapes=[pltpu.VMEM((j_rows, width), F32), pltpu.VMEM((width, j_pad), F32)],
+        compiler_params=params(12),
+        cost_estimate=cost(16 * macs, 2**20),
+        name="right_rows",
+    )(z_last, j_keep, keep, *rights)
 
     y, diag, *gw_cut = pl.pallas_call(
         functools.partial(outer_kernel, dims, n_row, n_col),
@@ -523,21 +525,22 @@
         cost_estimate=cost(16 * macs, 2**20),
         name="outer",
     )(i_keep, keep, scaled, rbig, *lefts)
-    gl_last = reduce(*gl_cut, "col", n_col, gw_cut[0])
-
-    acc = pl.pallas_call(
-        functools.partial(right_first_kernel, steps),
-        in_specs=[hbm()] + vmem(2),
-        out_specs=vmem()[0],
-        out_shape=pltpu.VMEM((depth, span), F32),
-        compiler_params=params(12),
-        cost_estimate=cost(16 * macs, 2**20),
-        name="right_first",
-    )(gl_last[0], z, diag)
-    gw_row = reduce(*gw_cut, "row", n_row, acc)
+
+    gl_cut = pl.pallas_call(
+        functools.partial(left_kernel, dims, n_col),
+        in_specs=[hbm()] + vmem(1 + len(z)),
+        out_specs=vmem(2),
+        out_shape=halves(i_rows * tiles, n_col),
+        scratch_shapes=[pltpu.VMEM((i_rows * tiles, LANES), F32)],
+        compiler_params=params(16),
+        cost_estimate=cost(16 * macs, 2**20),
+        name="left",
+    )(gw_cut[0], right_turned, *z)
+    gw_row = reduce(*gw_cut, "row", n_row, gl_cut[0])
+
     gr_cut = pl.pallas_call(
         functools.partial(right_kernel, dims, n_row),
-        in_specs=[hbm()] + vmem(3),
+        in_specs=[hbm()] + vmem(1 + len(z)),
         out_specs=vmem(2),
         out_shape=halves(j_rows * tiles, n_row),
         scratch_shapes=[
@@ -545,16 +548,17 @@
             pltpu.VMEM((width, j_pad), F32),
             pltpu.VMEM((j_rows * tiles, LANES), F32),
         ],
-        compiler_params=params(18),
+        compiler_params=params(20),
         cost_estimate=cost(16 * macs, 2**20),
         name="right",
-    )(gw_row[0], z, diag, acc)
+    )(gw_row[0], diag, *z)
     gw_cut = small_call(
         functools.partial(turn_kernel, n_col),
         halves(inner // n_row, n_col),
         "turn",
         [pltpu.VMEM((inner // n_row, pair_width), F32)],
     )(gr_cut[0], *gw_row)
+    gl_last = reduce(*gl_cut, "col", n_col, gw_cut[0])
 
     half = steps // 2
     early = pl.pallas_call(
@@ -565,7 +569,7 @@
         compiler_params=params(12),
         cost_estimate=cost(16 * macs, 2**20),
         name="pair_first",
-    )(gw_cut[0], i_keep, y, weight, inverse)
+    )(gl_last[0], i_keep, y, weight, inverse)
     gw_last = reduce(*gw_cut, "col", n_col, early)
     gr_last = reduce(*gr_cut, "row", n_row, gw_last[0])
     pair_out = pl.pallas_call(

time: 43.4 us -> 40.9 us (0.942)
  waiting for transfers between devices: 5.11 us -> 1.62 us
  starting transfers between devices: 14.2 us -> 16.8 us
  Pallas kernels: 23.2 us -> 21.5 us
    ppermute x12, waiting for transfers between devices: 5.11 us -> 1.62 us  [swap(): return lax.ppermute(array, axis, [(s, s ^ bit) for s in range(n)])]
    ppermute x12, starting transfers between devices: 14.2 us -> 16.8 us  [swap(): return lax.ppermute(array, axis, [(s, s ^ bit) for s in range(n)])]
    pallas_call x3, Pallas kernels: 7.97 us -> 5.79 us  [the longest x1 2.53 us: shards(): pl.pallas_call(functools.partial(left_kernel, dims, n_col), in_specs=[hbm...]
    pallas_call x1, Pallas kernels: 6.63 us -> 5.27 us  [shards(): pl.pallas_call(functools.partial(outer_kernel, dims, n_row, n_col), in_sp...]
    pallas_call x1, Pallas kernels: 2.33 us -> 3.61 us  [shards(): pl.pallas_call(functools.partial(right_kernel, dims, n_row), in_specs=[hb...]
    pallas_call x1, Pallas kernels: 2.03 us -> 2.53 us  [shards(): pl.pallas_call(functools.partial(scale_kernel, dims), in_specs=[hbm()] *...]
  transfers between devices with their start and end apart: 12 -> 12, of which waited for: 4 -> 3; matrix products, arithmetic and copies ran while one was open for 0% -> 0% of each run, Pallas kernels for 52% -> 38%
where the time goes in v8:
time: 40.9 us; the launch traced here: 40.7 us
  Pallas kernels  21.5 us (53%)
  starting transfers between devices  16.8 us (41%)
  waiting for transfers between devices  1.62 us (4%)
  between operations  0.77 us (2%)
    ppermute x12, starting transfers between devices, swap(): return lax.ppermute(array, axis, [(s, s ^ bit) for s in range(n)])  16.8 us
    pallas_call x1, Pallas kernels, shards(): pl.pallas_call(functools.partial(outer_kernel, dims, n_row, n_col), in_sp...  5.27 us
    pallas_call x1, Pallas kernels, shards(): pl.pallas_call(functools.partial(right_kernel, dims, n_row), in_specs=[hb...  3.61 us
    pallas_call x1, Pallas kernels, shards(): pl.pallas_call(functools.partial(scale_kernel, dims), in_specs=[hbm()] *...  2.53 us
    pallas_call x1, Pallas kernels, shards(): pl.pallas_call(functools.partial(left_kernel, dims, n_col), in_specs=[hbm...  2.53 us
    pallas_call x1, Pallas kernels, shards(): pl.pallas_call(functools.partial(inner_kernel, dims, early_steps), in_spe...  2.19 us
    pallas_call x1, Pallas kernels, shards(): pl.pallas_call(functools.partial(pair_kernel, dims), in_specs=[hbm()] * 2...  2.07 us
    ppermute x12, waiting for transfers between devices, swap(): return lax.ppermute(array, axis, [(s, s ^ bit) for s in range(n)])  1.62 us
  transfers between devices with their start and end apart: 12, of which 3 were waited for; matrix products, arithmetic and copies ran while one was open for 0% of the time, Pallas kernels for 38%

profile of v8, /device:TPU:0, one launch (start us, length us, event | category | flops | bytes accessed | tf_op | source)
XLA Modules:
  0.0 40.7 jit_solution(10336229041129942815)
XLA Ops:
  0.6 3.0 %collective-permute-start.1 = (bf16[1,16,2048]{2,1,0:T(8,128)(2,1)}, bf16[1,16,2048]{2,1,0:T(8,128)(2,1)S(1)}, u32[]{:S(2)}, u32[]{:S(2)}) collective-permute-start(bf16[1,16,2048]{2,1,0:T(8,128)(2,1)} %bitcast.5), channel_id=1, source_target_pairs={{0,8},{4,12},{8,0},{12,4},{1,9},{5,13},{9,1},{13,5},{2,10},{6,14},... | collective-permute-start | bytes 196616 | tf_op jit(solution)/shard_map/ppermute | solution.py:368
  3.6 2.6 %collective-permute-start = (bf16[1,16,2048]{2,1,0:T(8,128)(2,1)}, bf16[1,16,2048]{2,1,0:T(8,128)(2,1)S(1)}, u32[]{:S(2)}, u32[]{:S(2)}) collective-permute-start(bf16[1,16,2048]{2,1,0:T(8,128)(2,1)} %bitcast.4), channel_id=1, source_target_pairs={{0,2},{1,3},{2,0},{3,1},{4,6},{5,7},{6,4},{7,5},{8,10},{9,11},{10,... | collective-permute-start | bytes 196616 | tf_op jit(solution)/shard_map/ppermute | solution.py:368
  6.2 2.5 %scale.1 = (bf16[64,64,128]{2,1,0:T(8,128)(2,1)S(1)}, f32[64,128]{1,0:T(8,128)S(1)}, bf16[1024,128]{1,0:T(8,128)(2,1)S(1)}, f32[1,2048]{1,0:T(1,128)S(1)}, f32[6...) custom-call(s32[1,256]{1,0:T(1,128)} %bitcast.6, ...), custom_call_target="tpu_custom_call" | custom-call | flops 8589934592 | bytes 1048576 | tf_op jit(solution)/shard_map/scale/pallas_call | solution.py:454
  8.8 0.5 %collective-permute-done.came_ref = bf16[1,16,2048]{2,1,0:T(8,128)(2,1)S(1)} collective-permute-done((bf16[1,16,2048]{2,1,0:T(8,128)(2,1)}, bf16[1,16,2048]{2,1,0:T(8,128)(2,1)S(1)}, u32[]{:S(2)}, u32[]{:S(2)}) %collective-permute-start) | collective-permute-done | bytes 65568 | tf_op jit(solution)/shard_map/ppermute | solution.py:368
  9.3 1.3 %collective-permute-start.3 = (bf16[2,16,2048]{2,1,0:T(8,128)(2,1)S(1)}, bf16[2,16,2048]{2,1,0:T(8,128)(2,1)S(1)}, u32[]{:S(2)}, u32[]{:S(2)}) collective-permute-start(bf16[2,16,2048]{2,1,0:T(8,128)(2,1)S(1)} %join.2.after.refs_4_), channel_id=1, source_target_pairs={{0,1},{1,0},{2,3},{3,2},{4,5},{5,4},{6,7},{7,6},{8,9},{9,8},{10,11... | collective-permute-start | bytes 393224 | tf_op jit(solution)/shard_map/ppermute | solution.py:368
  10.7 0.1 collective-permute-start.2
  10.8 2.2 %inner.1.after.refs_1_ = bf16[3,512,2048]{2,1,0:T(8,128)(2,1)S(1)} custom-call(bf16[2,16,2048]{2,1,0:T(8,128)(2,1)S(1)} %join.3.after.right_held, bf16[64,64,128]{2,1,0:T(8,128)(2,1)S(1)} %get-tuple-element.38.scaled_ref.refs_2_, bf16[1024,128]{1,0:T(8,128)(2,1)S(1)} %get-tuple-element.41.wp_ref.refs_4_), custom_call_target="tpu_custom_call" | custom-call | flops 8589934592 | bytes 1048576 | tf_op jit(solution)/shard_map/inner/pallas_call | solution.py:486
  13.0 1.1 %right_rows.1 = (bf16[512,256]{1,0:T(8,128)(2,1)S(1)}, bf16[256,512]{1,0:T(8,128)(2,1)S(1)}) custom-call(bf16[3,512,2048]{2,1,0:T(8,128)(2,1)S(1)} %inner.1.after.refs_1_, f32[64,128]{1,0:T(8,128)S(1)} %get-tuple-element.42.rj_ref, f32[1,2048]{1,0:T(1,128)S(1)} %get-tuple-element.37.keep_ref.refs_1_, bf16[2,16,2048]{2,1,0:T(8,128)(2,1)S(1)} %join.3.after.right_held, ...), custom_call_target="tpu_custom_call" | custom-call | flops 8589934592 | bytes 1048576 | tf_op jit(solution)/shard_map/right_rows/pallas_call | solution.py:497
  14.0 0.3 collective-permute-done.3.refs_5_
  14.4 5.3 %outer.1 = (bf16[64,64,1024]{2,1,0:T(8,128)(2,1)S(1)}, bf16[4,256,2048]{2,1,0:T(8,128)(2,1)S(1)}, bf16[2,256,128]{2,1,0:T(8,128)(2,1)S(1)}, bf16[2,256,128]{2,1,0:T(8,128)(2,1)S(1)}) custom-call(f32[64,128]{1,0:T(8,128)S(1)} %get-tuple-element.36.refs_0_.ri_ref.refs_2_, f32[1,2048]{1,0:T(1,128)S(1)} %get-tuple-element.37.keep_ref.refs_1_, ...), custom_call_target="tpu_custom_call" | custom-call | flops 8589934592 | bytes 1048576 | tf_op jit(solution)/shard_map/outer/pallas_call | solution.py:508
  19.6 0.3 collective-permute-start.4
  19.9 2.5 %left.1 = (bf16[2,256,128]{2,1,0:T(8,128)(2,1)S(1)}, bf16[2,256,128]{2,1,0:T(8,128)(2,1)S(1)}) custom-call(bf16[2,256,128]{2,1,0:T(8,128)(2,1)S(1)} %get-tuple-element.44.after.held_ref, bf16[256,512]{1,0:T(8,128)(2,1)S(1)} %get-tuple-element.45.rbt_ref, bf16[1,512,2048]{2,1,0:T(8,128)(2,1)S(1)} %get-tuple-element.46.refs_0_, ...), custom_call_target="tpu_custom_call" | custom-call | flops 8589934592 | bytes 1048576 | tf_op jit(solution)/shard_map/left/pallas_call | solution.py:529
  22.4 1.2 %collective-permute-start.6 = (bf16[2,256,128]{2,1,0:T(8,128)(2,1)S(1)}, bf16[2,256,128]{2,1,0:T(8,128)(2,1)S(1)}, u32[]{:S(2)}, u32[]{:S(2)}) collective-permute-start(bf16[2,256,128]{2,1,0:T(8,128)(2,1)S(1)} %get-tuple-element.54), channel_id=1, source_target_pairs={{0,1},{1,0},{2,3},{3,2},{4,5},{5,4},{6,7},{7,6},{8,9},{9,8},{10,11... | collective-permute-start | bytes 393224 | tf_op jit(solution)/shard_map/ppermute | solution.py:368
  23.6 0.6 %collective-permute-start.5 = (bf16[1,256,128]{2,1,0:T(8,128)(2,1)S(1)}, bf16[1,256,128]{2,1,0:T(8,128)(2,1)S(1)}, u32[]{:S(2)}, u32[]{:S(2)}) collective-permute-start(bf16[1,256,128]{2,1,0:T(8,128)(2,1)S(1)} %get-tuple-element.52), channel_id=1, source_target_pairs={{0,8},{4,12},{8,0},{12,4},{1,9},{5,13},{9,1},{13,5},{2,10},{6,14},... | collective-permute-start | bytes 196616 | tf_op jit(solution)/shard_map/ppermute | solution.py:368
  24.2 3.6 %right.1 = (bf16[2,256,128]{2,1,0:T(8,128)(2,1)S(1)}, bf16[2,256,128]{2,1,0:T(8,128)(2,1)S(1)}) custom-call(f32[1,256,128]{2,1,0:T(8,128)S(1)} %get-tuple-element.49.after.held_ref, bf16[4,256,2048]{2,1,0:T(8,128)(2,1)S(1)} %get-tuple-element.50.diag_ref, bf16[1,512,2048]{2,1,0:T(8,128)(2,1)S(1)} %get-tuple-element.46.refs_0_, ...), custom_call_target="tpu_custom_call" | custom-call | flops 8589934592 | bytes 1048576 | tf_op jit(solution)/shard_map/right/pallas_call | solution.py:541
  27.9 0.1 collective-permute-start.9
  28.0 1.0 %collective-permute-start.8 = (bf16[2,64,128]{2,1,0:T(8,128)(2,1)S(1)}, bf16[2,64,128]{2,1,0:T(8,128)(2,1)S(1)}, u32[]{:S(2)}, u32[]{:S(2)}) collective-permute-start(bf16[2,64,128]{2,1,0:T(8,128)(2,1)S(1)} %get-tuple-element.59), channel_id=1, source_target_pairs={{0,1},{1,0},{2,3},{3,2},{4,5},{5,4},{6,7},{7,6},{8,9},{9,8},{10,11... | collective-permute-start | bytes 98312 | tf_op jit(solution)/shard_map/ppermute | solution.py:368
  29.0 3.2 %collective-permute-start.7 = (bf16[1,256,128]{2,1,0:T(8,128)(2,1)S(1)}, bf16[1,256,128]{2,1,0:T(8,128)(2,1)S(1)}, u32[]{:S(2)}, u32[]{:S(2)}) collective-permute-start(bf16[1,256,128]{2,1,0:T(8,128)(2,1)S(1)} %get-tuple-element.55), channel_id=1, source_target_pairs={{0,2},{1,3},{2,0},{3,1},{4,6},{5,7},{6,4},{7,5},{8,10},{9,11},{10,... | collective-permute-start | bytes 196616 | tf_op jit(solution)/shard_map/ppermute | solution.py:368
  32.3 1.2 %pair_first.1.after.refs_6_ = bf16[32,64,128]{2,1,0:T(8,128)(2,1)S(1)} custom-call(f32[1,256,128]{2,1,0:T(8,128)S(1)} %get-tuple-element.56.after.refs_0_, f32[64,128]{1,0:T(8,128)S(1)} %get-tuple-element.36.refs_0_.ri_ref.refs_2_, bf16[64,64,1024]{2,1,0:T(8,128)(2,1)S(1)} %get-tuple-element.57.y_ref.refs_3_, ...), custom_call_target="tpu_custom_call" | custom-call | flops 8589934592 | bytes 1048576 | tf_op jit(solution)/shard_map/pair_first/pallas_call | solution.py:564
  33.6 2.0 %collective-permute-start.11 = (bf16[1,64,128]{2,1,0:T(8,128)(2,1)S(1)}, bf16[1,64,128]{2,1,0:T(8,128)(2,1)S(1)}, u32[]{:S(2)}, u32[]{:S(2)}) collective-permute-start(bf16[1,64,128]{2,1,0:T(8,128)(2,1)S(1)} %get-tuple-element.64), channel_id=1, source_target_pairs={{0,2},{1,3},{2,0},{3,1},{4,6},{5,7},{6,4},{7,5},{8,10},{9,11},{10,... | collective-permute-start | bytes 49160 | tf_op jit(solution)/shard_map/ppermute | solution.py:368
  35.5 1.5 %collective-permute-start.10 = (bf16[1,256,128]{2,1,0:T(8,128)(2,1)S(1)}, bf16[1,256,128]{2,1,0:T(8,128)(2,1)S(1)}, u32[]{:S(2)}, u32[]{:S(2)}) collective-permute-start(bf16[1,256,128]{2,1,0:T(8,128)(2,1)S(1)} %get-tuple-element.63), channel_id=1, source_target_pairs={{0,8},{4,12},{8,0},{12,4},{1,9},{5,13},{9,1},{13,5},{2,10},{6,14},... | collective-permute-start | bytes 196616 | tf_op jit(solution)/shard_map/ppermute | solution.py:368
  37.1 2.1 %pair.1.after = bf16[64,64,128]{2,1,0:T(8,128)(2,1)} custom-call(bf16[1,256,128]{2,1,0:T(8,128)(2,1)S(1)} %collective-permute-done.7.refs_0_.refs_1_, f32[1,256,128]{2,1,0:T(8,128)S(1)} %get-tuple-element.62.refs_1_.refs_2_, f32[64,128]{1,0:T(8,128)S(1)} %get-tuple-element.36.refs_0_.ri_ref.refs_2_, ...), custom_call_target="tpu_custom_call" | custom-call | flops 8589934592 | bytes 1048576 | tf_op jit(solution)/shard_map/pair/pallas_call | solution.py:575
  39.2 0.7 %collective-permute-done.10.refs_3_ = bf16[1,256,128]{2,1,0:T(8,128)(2,1)S(1)} collective-permute-done((bf16[1,256,128]{2,1,0:T(8,128)(2,1)S(1)}, bf16[1,256,128]{2,1,0:T(8,128)(2,1)S(1)}, u32[]{:S(2)}, u32[]{:S(2)}) %collective-permute-start.10) | collective-permute-done | bytes 65568 | tf_op jit(solution)/shard_map/ppermute | solution.py:368
  39.9 0.8 %final_sums.1 = (f32[16,2048]{1,0:T(8,128)}, f32[16,2048]{1,0:T(8,128)}, f32[64,128]{1,0:T(8,128)}) custom-call(bf16[64,64,128]{2,1,0:T(8,128)(2,1)} %pair.1.after, f32[64,128]{1,0:T(8,128)S(1)} %get-tuple-element.36.refs_0_.ri_ref.refs_2_, f32[64,128]{1,0:T(8,128)S(1)} %get-tuple-element.42.rj_ref, f32[1,2048]{1,0:T(1,128)S(1)} %get-tuple-element.37.keep_ref.refs_1_, ...), custom_call_target="tpu_custom_call" | custom-call | flops 1000 | bytes 1000 | tf_op jit(solution)/shard_map/final_sums/pallas_call | solution.py:589
  (16 shorter events, 0.2 us)
Async XLA Ops:
  0.6 10.0 %collective-permute-start.1 = (bf16[1,16,2048]{2,1,0:T(8,128)(2,1)}, bf16[1,16,2048]{2,1,0:T(8,128)(2,1)S(1)}, u32[]{:S(2)}, u32[]{:S(2)}) collective-permute-start(bf16[1,16,2048]{2,1,0:T(8,128)(2,1)} %bitcast.5), channel_id=1, source_target_pairs={{0,8},{4,12},{8,0},{12,4},{1,9},{5,13},{9,1},{13,5},{2,10},{6,14},... | collective-permute-start | bytes 196616 | tf_op jit(solution)/shard_map/ppermute | solution.py:368
  3.6 5.7 %collective-permute-start = (bf16[1,16,2048]{2,1,0:T(8,128)(2,1)}, bf16[1,16,2048]{2,1,0:T(8,128)(2,1)S(1)}, u32[]{:S(2)}, u32[]{:S(2)}) collective-permute-start(bf16[1,16,2048]{2,1,0:T(8,128)(2,1)} %bitcast.4), channel_id=1, source_target_pairs={{0,2},{1,3},{2,0},{3,1},{4,6},{5,7},{6,4},{7,5},{8,10},{9,11},{10,... | collective-permute-start | bytes 196616 | tf_op jit(solution)/shard_map/ppermute | solution.py:368
  9.3 5.0 %collective-permute-start.3 = (bf16[2,16,2048]{2,1,0:T(8,128)(2,1)S(1)}, bf16[2,16,2048]{2,1,0:T(8,128)(2,1)S(1)}, u32[]{:S(2)}, u32[]{:S(2)}) collective-permute-start(bf16[2,16,2048]{2,1,0:T(8,128)(2,1)S(1)} %join.2.after.refs_4_), channel_id=1, source_target_pairs={{0,1},{1,0},{2,3},{3,2},{4,5},{5,4},{6,7},{7,6},{8,9},{9,8},{10,11... | collective-permute-start | bytes 393224 | tf_op jit(solution)/shard_map/ppermute | solution.py:368
  10.7 2.3 %collective-permute-start.2 = (bf16[2,16,2048]{2,1,0:T(8,128)(2,1)S(1)}, bf16[2,16,2048]{2,1,0:T(8,128)(2,1)S(1)}, u32[]{:S(2)}, u32[]{:S(2)}) collective-permute-start(bf16[2,16,2048]{2,1,0:T(8,128)(2,1)S(1)} %join.3.after.right_held), channel_id=1, source_target_pairs={{0,4},{4,0},{8,12},{12,8},{1,5},{5,1},{9,13},{13,9},{2,6},{6,2},{1... | collective-permute-start | bytes 393224 | tf_op jit(solution)/shard_map/ppermute | solution.py:368
  19.6 4.0 %collective-permute-start.4 = (bf16[2,256,128]{2,1,0:T(8,128)(2,1)S(1)}, bf16[2,256,128]{2,1,0:T(8,128)(2,1)S(1)}, u32[]{:S(2)}, u32[]{:S(2)}) collective-permute-start(bf16[2,256,128]{2,1,0:T(8,128)(2,1)S(1)} %get-tuple-element.48), channel_id=1, source_target_pairs={{0,4},{4,0},{8,12},{12,8},{1,5},{5,1},{9,13},{13,9},{2,6},{6,2},{1... | collective-permute-start | bytes 393224 | tf_op jit(solution)/shard_map/ppermute | solution.py:368
  22.4 6.6 %collective-permute-start.6 = (bf16[2,256,128]{2,1,0:T(8,128)(2,1)S(1)}, bf16[2,256,128]{2,1,0:T(8,128)(2,1)S(1)}, u32[]{:S(2)}, u32[]{:S(2)}) collective-permute-start(bf16[2,256,128]{2,1,0:T(8,128)(2,1)S(1)} %get-tuple-element.54), channel_id=1, source_target_pairs={{0,1},{1,0},{2,3},{3,2},{4,5},{5,4},{6,7},{7,6},{8,9},{9,8},{10,11... | collective-permute-start | bytes 393224 | tf_op jit(solution)/shard_map/ppermute | solution.py:368
  23.6 4.3 %collective-permute-start.5 = (bf16[1,256,128]{2,1,0:T(8,128)(2,1)S(1)}, bf16[1,256,128]{2,1,0:T(8,128)(2,1)S(1)}, u32[]{:S(2)}, u32[]{:S(2)}) collective-permute-start(bf16[1,256,128]{2,1,0:T(8,128)(2,1)S(1)} %get-tuple-element.52), channel_id=1, source_target_pairs={{0,8},{4,12},{8,0},{12,4},{1,9},{5,13},{9,1},{13,5},{2,10},{6,14},... | collective-permute-start | bytes 196616 | tf_op jit(solution)/shard_map/ppermute | solution.py:368
  27.9 7.7 %collective-permute-start.9 = (bf16[2,256,128]{2,1,0:T(8,128)(2,1)S(1)}, bf16[2,256,128]{2,1,0:T(8,128)(2,1)S(1)}, u32[]{:S(2)}, u32[]{:S(2)}) collective-permute-start(bf16[2,256,128]{2,1,0:T(8,128)(2,1)S(1)} %get-tuple-element.61), channel_id=1, source_target_pairs={{0,4},{4,0},{8,12},{12,8},{1,5},{5,1},{9,13},{13,9},{2,6},{6,2},{1... | collective-permute-start | bytes 393224 | tf_op jit(solution)/shard_map/ppermute | solution.py:368
  28.0 5.5 %collective-permute-start.8 = (bf16[2,64,128]{2,1,0:T(8,128)(2,1)S(1)}, bf16[2,64,128]{2,1,0:T(8,128)(2,1)S(1)}, u32[]{:S(2)}, u32[]{:S(2)}) collective-permute-start(bf16[2,64,128]{2,1,0:T(8,128)(2,1)S(1)} %get-tuple-element.59), channel_id=1, source_target_pairs={{0,1},{1,0},{2,3},{3,2},{4,5},{5,4},{6,7},{7,6},{8,9},{9,8},{10,11... | collective-permute-start | bytes 98312 | tf_op jit(solution)/shard_map/ppermute | solution.py:368
  29.0 8.1 %collective-permute-start.7 = (bf16[1,256,128]{2,1,0:T(8,128)(2,1)S(1)}, bf16[1,256,128]{2,1,0:T(8,128)(2,1)S(1)}, u32[]{:S(2)}, u32[]{:S(2)}) collective-permute-start(bf16[1,256,128]{2,1,0:T(8,128)(2,1)S(1)} %get-tuple-element.55), channel_id=1, source_target_pairs={{0,2},{1,3},{2,0},{3,1},{4,6},{5,7},{6,4},{7,5},{8,10},{9,11},{10,... | collective-permute-start | bytes 196616 | tf_op jit(solution)/shard_map/ppermute | solution.py:368
  33.6 5.6 %collective-permute-start.11 = (bf16[1,64,128]{2,1,0:T(8,128)(2,1)S(1)}, bf16[1,64,128]{2,1,0:T(8,128)(2,1)S(1)}, u32[]{:S(2)}, u32[]{:S(2)}) collective-permute-start(bf16[1,64,128]{2,1,0:T(8,128)(2,1)S(1)} %get-tuple-element.64), channel_id=1, source_target_pairs={{0,2},{1,3},{2,0},{3,1},{4,6},{5,7},{6,4},{7,5},{8,10},{9,11},{10,... | collective-permute-start | bytes 49160 | tf_op jit(solution)/shard_map/ppermute | solution.py:368
  35.5 4.3 %collective-permute-start.10 = (bf16[1,256,128]{2,1,0:T(8,128)(2,1)S(1)}, bf16[1,256,128]{2,1,0:T(8,128)(2,1)S(1)}, u32[]{:S(2)}, u32[]{:S(2)}) collective-permute-start(bf16[1,256,128]{2,1,0:T(8,128)(2,1)S(1)} %get-tuple-element.63), channel_id=1, source_target_pairs={{0,8},{4,12},{8,0},{12,4},{1,9},{5,13},{9,1},{13,5},{2,10},{6,14},... | collective-permute-start | bytes 196616 | tf_op jit(solution)/shard_map/ppermute | solution.py:368

commit v9 on v8

--- a/solution.py
+++ b/solution.py
@@ -141,9 +141,9 @@
 def outer_kernel(dims, n_row, n_col, *refs):
     chans, groups, blocks, i_rows, j_rows, step_rows, sequences = dims
     tiles = sequences * chans // LANES
-    ri_ref, keep_ref, scaled_ref, rbig, left_held, left_came = refs[:6]
-    y_ref, diag_ref, keep_out, send_out = refs[6:10]
-    flat, lsplit, expand, gwt, gwr = refs[10:]
+    after, ri_ref, keep_ref, scaled_ref, rbig, left_held, left_came = refs[:7]
+    y_ref, diag_ref, keep_out, send_out = refs[7:11]
+    flat, lsplit, expand, gwt, gwr = refs[11:]
     place((left_held, left_came), lax.axis_index("col"), n_col, flat)
     for t in range(tiles):
         lanes = slice(t * LANES, (t + 1) * LANES)
@@ -197,16 +197,25 @@
     cut(gwr, lax.axis_index("row"), n_row, keep_out, send_out)
 
 
-def right_kernel(dims, n_row, after, diag_ref, *refs):
+def right_sum(first, last, z_refs, diag_ref, acc, so_far=None):
+    for step in range(first, last):
+        part = lax.dot_general(
+            diag_ref[step], at_step(z_refs, step)[...], NT, preferred_element_type=F32
+        )
+        acc[...] = part if so_far is None else so_far[...] + part
+        so_far = acc
+
+
+def right_first_kernel(steps, after, diag_ref, *refs):
+    right_sum(0, steps, refs[:-1], diag_ref, refs[-1])
+
+
+def right_kernel(dims, n_row, first, after, diag_ref, acc_first, *refs):
     chans, groups, blocks, i_rows, j_rows, step_rows, sequences = dims
     tiles = sequences * chans // LANES
     j_pad = -(-j_rows // LANES) * LANES
     z_refs, (keep_out, send_out, acc, turned, gr_all) = refs[:-5], refs[-5:]
-    for step in range(i_rows // step_rows):
-        part = lax.dot_general(
-            diag_ref[step], at_step(z_refs, step)[...], NT, preferred_element_type=F32
-        )
-        acc[...] = acc[...] + part if step else part
+    right_sum(first, i_rows // step_rows, z_refs, diag_ref, acc, acc_first)
     for a in range(blocks):
         at, shift = divmod(a * j_rows, LANES)
         mine = acc[:, at * LANES : at * LANES + j_pad]
@@ -443,7 +452,7 @@
     inner = chans * chans
     step_rows = 16
     steps = i_rows // step_rows
-    early_steps = steps // 4
+    early_steps = steps // 2
     dims = (chans, groups, blocks, i_rows, j_rows, step_rows, sequences)
     j_pad = -(-j_rows // LANES) * LANES
     span = blocks * j_rows
@@ -476,7 +485,7 @@
             pltpu.SemaphoreType.DMA((5,)),
         ],
         compiler_params=params(16),
-        cost_estimate=cost(16 * macs, 2**20),
+        cost_estimate=cost(1000, 1000),
         name="scale",
     )(*map(in_hbm, (*mask_row, cotangent, out_weight, left_act, right_act)))
 
@@ -505,9 +514,19 @@
         name="right_rows",
     )(z_last, j_keep, keep, *rights)
 
+    gl_cut = pl.pallas_call(
+        functools.partial(left_kernel, dims, n_col),
+        in_specs=[hbm()] + vmem(1 + len(z)),
+        out_specs=vmem(2),
+        out_shape=halves(i_rows * tiles, n_col),
+        scratch_shapes=[pltpu.VMEM((i_rows * tiles, LANES), F32)],
+        compiler_params=params(16),
+        cost_estimate=cost(16 * macs, 2**20),
+        name="left",
+    )(rbig, right_turned, *z)
     y, diag, *gw_cut = pl.pallas_call(
         functools.partial(outer_kernel, dims, n_row, n_col),
-        in_specs=vmem(6),
+        in_specs=[hbm()] + vmem(6),
         out_specs=vmem(4),
         out_shape=[
             pltpu.VMEM((i_rows, j_rows, inner), BF16),
@@ -524,23 +543,25 @@
         compiler_params=params(16),
         cost_estimate=cost(16 * macs, 2**20),
         name="outer",
-    )(i_keep, keep, scaled, rbig, *lefts)
-
-    gl_cut = pl.pallas_call(
-        functools.partial(left_kernel, dims, n_col),
+    )(gl_cut[0], i_keep, keep, scaled, rbig, *lefts)
+
+    gl_last = reduce(*gl_cut, "col", n_col, gw_cut[0])
+
+    right_steps = steps // 4
+    acc = pl.pallas_call(
+        functools.partial(right_first_kernel, right_steps),
         in_specs=[hbm()] + vmem(1 + len(z)),
-        out_specs=vmem(2),
-        out_shape=halves(i_rows * tiles, n_col),
-        scratch_shapes=[pltpu.VMEM((i_rows * tiles, LANES), F32)],
+        out_specs=vmem()[0],
+        out_shape=pltpu.VMEM((depth, span), F32),
         compiler_params=params(16),
         cost_estimate=cost(16 * macs, 2**20),
-        name="left",
-    )(gw_cut[0], right_turned, *z)
-    gw_row = reduce(*gw_cut, "row", n_row, gl_cut[0])
+        name="right_first",
+    )(gl_last[0], diag, *z)
+    gw_row = reduce(*gw_cut, "row", n_row, acc)
 
     gr_cut = pl.pallas_call(
-        functools.partial(right_kernel, dims, n_row),
-        in_specs=[hbm()] + vmem(1 + len(z)),
+        functools.partial(right_kernel, dims, n_row, right_steps),
+        in_specs=[hbm()] + vmem(2 + len(z)),
         out_specs=vmem(2),
         out_shape=halves(j_rows * tiles, n_row),
         scratch_shapes=[
@@ -551,14 +572,13 @@
         compiler_params=params(20),
         cost_estimate=cost(16 * macs, 2**20),
         name="right",
-    )(gw_row[0], diag, *z)
+    )(gw_row[0], diag, acc, *z)
     gw_cut = small_call(
         functools.partial(turn_kernel, n_col),
         halves(inner // n_row, n_col),
         "turn",
         [pltpu.VMEM((inner // n_row, pair_width), F32)],
     )(gr_cut[0], *gw_row)
-    gl_last = reduce(*gl_cut, "col", n_col, gw_cut[0])
 
     half = steps // 2
     early = pl.pallas_call(
@@ -569,7 +589,7 @@
         compiler_params=params(12),
         cost_estimate=cost(16 * macs, 2**20),
         name="pair_first",
-    )(gl_last[0], i_keep, y, weight, inverse)
+    )(gw_cut[0], i_keep, y, weight, inverse)
     gw_last = reduce(*gw_cut, "col", n_col, early)
     gr_last = reduce(*gr_cut, "row", n_row, gw_last[0])
     pair_out = pl.pallas_call(

time: 40.9 us -> 40.3 us (0.985)
  starting transfers between devices: 16.8 us -> 15.1 us
  waiting for transfers between devices: 1.62 us -> 2.46 us
    ppermute x12, starting transfers between devices: 16.8 us -> 15.1 us  [swap(): return lax.ppermute(array, axis, [(s, s ^ bit) for s in range(n)])]
    ppermute x12, waiting for transfers between devices: 1.62 us -> 2.46 us  [swap(): return lax.ppermute(array, axis, [(s, s ^ bit) for s in range(n)])]
    pallas_call x1, Pallas kernels: 2.53 us -> 3.33 us  [shards(): pl.pallas_call(functools.partial(scale_kernel, dims), in_specs=[hbm()] *...]
    pallas_call x1, Pallas kernels: 2.19 us -> 1.51 us  [shards(): pl.pallas_call(functools.partial(inner_kernel, dims, early_steps), in_spe...]
    pallas_call x1 -> x2, Pallas kernels: 3.61 us -> 3.8 us  [the longest x1 2.87 us: shards(): pl.pallas_call(functools.partial(right_kernel, dims, n_row, right_steps),...]
  transfers between devices with their start and end apart: 12 -> 12, of which waited for: 3 -> 3; matrix products, arithmetic and copies ran while one was open for 0% -> 0% of each run, Pallas kernels for 38% -> 52%
where the time goes in v9:
time: 40.3 us; the launch traced here: 40.2 us
  Pallas kernels  21.8 us (54%)
  starting transfers between devices  15.1 us (37%)
  waiting for transfers between devices  2.46 us (6%)
  between operations  0.79 us (2%)
    ppermute x12, starting transfers between devices, swap(): return lax.ppermute(array, axis, [(s, s ^ bit) for s in range(n)])  15.1 us
    pallas_call x1, Pallas kernels, shards(): pl.pallas_call(functools.partial(outer_kernel, dims, n_row, n_col), in_sp...  5.27 us
    pallas_call x1, Pallas kernels, shards(): pl.pallas_call(functools.partial(scale_kernel, dims), in_specs=[hbm()] *...  3.33 us
    pallas_call x1, Pallas kernels, shards(): pl.pallas_call(functools.partial(right_kernel, dims, n_row, right_steps),...  2.87 us
    pallas_call x1, Pallas kernels, shards(): pl.pallas_call(functools.partial(left_kernel, dims, n_col), in_specs=[hbm...  2.53 us
    ppermute x12, waiting for transfers between devices, swap(): return lax.ppermute(array, axis, [(s, s ^ bit) for s in range(n)])  2.46 us
    pallas_call x1, Pallas kernels, shards(): pl.pallas_call(functools.partial(pair_kernel, dims), in_specs=[hbm()] * 2...  2.06 us
    pallas_call x1, Pallas kernels, shards(): pl.pallas_call(functools.partial(inner_kernel, dims, early_steps), in_spe...  1.51 us
  transfers between devices with their start and end apart: 12, of which 3 were waited for; matrix products, arithmetic and copies ran while one was open for 0% of the time, Pallas kernels for 52%

profile of v9, /device:TPU:0, one launch (start us, length us, event | category | flops | bytes accessed | tf_op | source)
XLA Modules:
  0.0 40.2 jit_solution(11487226899288807742)
XLA Ops:
  0.6 4.1 %collective-permute-start = (bf16[1,16,2048]{2,1,0:T(8,128)(2,1)}, bf16[1,16,2048]{2,1,0:T(8,128)(2,1)S(1)}, u32[]{:S(2)}, u32[]{:S(2)}) collective-permute-start(bf16[1,16,2048]{2,1,0:T(8,128)(2,1)} %bitcast.4), channel_id=1, source_target_pairs={{0,2},{1,3},{2,0},{3,1},{4,6},{5,7},{6,4},{7,5},{8,10},{9,11},{10,... | collective-permute-start | bytes 196616 | tf_op jit(solution)/shard_map/ppermute | solution.py:377
  4.7 1.5 %collective-permute-start.1 = (bf16[1,16,2048]{2,1,0:T(8,128)(2,1)}, bf16[1,16,2048]{2,1,0:T(8,128)(2,1)S(1)}, u32[]{:S(2)}, u32[]{:S(2)}) collective-permute-start(bf16[1,16,2048]{2,1,0:T(8,128)(2,1)} %bitcast.5), channel_id=1, source_target_pairs={{0,8},{4,12},{8,0},{12,4},{1,9},{5,13},{9,1},{13,5},{2,10},{6,14},... | collective-permute-start | bytes 196616 | tf_op jit(solution)/shard_map/ppermute | solution.py:377
  6.2 3.3 %scale.1 = (bf16[64,64,128]{2,1,0:T(8,128)(2,1)S(1)}, f32[64,128]{1,0:T(8,128)S(1)}, bf16[1024,128]{1,0:T(8,128)(2,1)S(1)}, f32[1,2048]{1,0:T(1,128)S(1)}, f32[6...) custom-call(s32[1,256]{1,0:T(1,128)} %bitcast.6, ...), custom_call_target="tpu_custom_call" | custom-call | flops 1000 | bytes 1000 | tf_op jit(solution)/shard_map/scale/pallas_call | solution.py:463
  9.6 1.6 %collective-permute-start.3 = (bf16[2,16,2048]{2,1,0:T(8,128)(2,1)S(1)}, bf16[2,16,2048]{2,1,0:T(8,128)(2,1)S(1)}, u32[]{:S(2)}, u32[]{:S(2)}) collective-permute-start(bf16[2,16,2048]{2,1,0:T(8,128)(2,1)S(1)} %join.2.after.refs_5_), channel_id=1, source_target_pairs={{0,1},{1,0},{2,3},{3,2},{4,5},{5,4},{6,7},{7,6},{8,9},{9,8},{10,11... | collective-permute-start | bytes 393224 | tf_op jit(solution)/shard_map/ppermute | solution.py:377
  11.2 0.1 collective-permute-start.2
  11.3 1.5 %inner.1.after.refs_1_ = bf16[2,512,2048]{2,1,0:T(8,128)(2,1)S(1)} custom-call(bf16[2,16,2048]{2,1,0:T(8,128)(2,1)S(1)} %join.3.after.right_held, bf16[64,64,128]{2,1,0:T(8,128)(2,1)S(1)} %get-tuple-element.38.scaled_ref.refs_3_, bf16[1024,128]{1,0:T(8,128)(2,1)S(1)} %get-tuple-element.39.wp_ref.refs_4_), custom_call_target="tpu_custom_call" | custom-call | flops 8589934592 | bytes 1048576 | tf_op jit(solution)/shard_map/inner/pallas_call | solution.py:495
  12.8 1.1 %right_rows.1 = (bf16[512,256]{1,0:T(8,128)(2,1)S(1)}, bf16[256,512]{1,0:T(8,128)(2,1)S(1)}) custom-call(bf16[2,512,2048]{2,1,0:T(8,128)(2,1)S(1)} %inner.1.after.refs_1_, f32[64,128]{1,0:T(8,128)S(1)} %get-tuple-element.40.rj_ref, f32[1,2048]{1,0:T(1,128)S(1)} %get-tuple-element.41.keep_ref.refs_2_, bf16[2,16,2048]{2,1,0:T(8,128)(2,1)S(1)} %join.3.after.right_held, ...), custom_call_target="tpu_custom_call" | custom-call | flops 8589934592 | bytes 1048576 | tf_op jit(solution)/shard_map/right_rows/pallas_call | solution.py:506
  13.9 2.5 %left.1 = (bf16[2,256,128]{2,1,0:T(8,128)(2,1)S(1)}, bf16[2,256,128]{2,1,0:T(8,128)(2,1)S(1)}) custom-call(bf16[512,256]{1,0:T(8,128)(2,1)S(1)} %get-tuple-element.42.after.refs_4_, bf16[256,512]{1,0:T(8,128)(2,1)S(1)} %get-tuple-element.43.rbt_ref, bf16[2,512,2048]{2,1,0:T(8,128)(2,1)S(1)} %get-tuple-element.44.refs_0_, ...), custom_call_target="tpu_custom_call" | custom-call | flops 8589934592 | bytes 1048576 | tf_op jit(solution)/shard_map/left/pallas_call | solution.py:517
  16.5 0.5 %collective-permute-start.4 = (bf16[2,256,128]{2,1,0:T(8,128)(2,1)S(1)}, bf16[2,256,128]{2,1,0:T(8,128)(2,1)S(1)}, u32[]{:S(2)}, u32[]{:S(2)}) collective-permute-start(bf16[2,256,128]{2,1,0:T(8,128)(2,1)S(1)} %get-tuple-element.48), channel_id=1, source_target_pairs={{0,1},{1,0},{2,3},{3,2},{4,5},{5,4},{6,7},{7,6},{8,9},{9,8},{10,11... | collective-permute-start | bytes 393224 | tf_op jit(solution)/shard_map/ppermute | solution.py:377
  17.0 5.3 %outer.1 = (bf16[64,64,1024]{2,1,0:T(8,128)(2,1)S(1)}, bf16[4,256,2048]{2,1,0:T(8,128)(2,1)S(1)}, bf16[2,256,128]{2,1,0:T(8,128)(2,1)S(1)}, bf16[2,256,128]{2,1,0:T(8,128)(2,1)S(1)}) custom-call(bf16[2,256,128]{2,1,0:T(8,128)(2,1)S(1)} %get-tuple-element.45.refs_0_.held_ref, f32[64,128]{1,0:T(8,128)S(1)} %get-tuple-element.46.refs_1_.ri_ref.refs_2_, ...), custom_call_target="tpu_custom_call" | custom-call | flops 8589934592 | bytes 1048576 | tf_op jit(solution)/shard_map/outer/pallas_call | solution.py:527
  22.3 0.3 collective-permute-start.6
  22.6 1.3 %collective-permute-start.5 = (bf16[1,256,128]{2,1,0:T(8,128)(2,1)S(1)}, bf16[1,256,128]{2,1,0:T(8,128)(2,1)S(1)}, u32[]{:S(2)}, u32[]{:S(2)}) collective-permute-start(bf16[1,256,128]{2,1,0:T(8,128)(2,1)S(1)} %get-tuple-element.49), channel_id=1, source_target_pairs={{0,2},{1,3},{2,0},{3,1},{4,6},{5,7},{6,4},{7,5},{8,10},{9,11},{10,... | collective-permute-start | bytes 196616 | tf_op jit(solution)/shard_map/ppermute | solution.py:377
  23.9 0.9 %right_first.1.after.acc_first = f32[256,512]{1,0:T(8,128)S(1)} custom-call(f32[1,256,128]{2,1,0:T(8,128)S(1)} %get-tuple-element.50.after.refs_0_, bf16[4,256,2048]{2,1,0:T(8,128)(2,1)S(1)} %get-tuple-element.51.diag_ref, bf16[2,512,2048]{2,1,0:T(8,128)(2,1)S(1)} %get-tuple-element.44.refs_0_, bf16[2,512,2048]{2,1,0:T(8,128)(2,1)S(1)} %inner.1.after.refs_1_), custom_call_target="tpu_custom_call" | custom-call | flops 8589934592 | bytes 1048576 | tf_op jit(solution)/shard_map/right_first/pallas_call | solution.py:551
  24.9 1.6 %collective-permute-start.7 = (bf16[1,256,128]{2,1,0:T(8,128)(2,1)S(1)}, bf16[1,256,128]{2,1,0:T(8,128)(2,1)S(1)}, u32[]{:S(2)}, u32[]{:S(2)}) collective-permute-start(bf16[1,256,128]{2,1,0:T(8,128)(2,1)S(1)} %get-tuple-element.55), channel_id=1, source_target_pairs={{0,8},{4,12},{8,0},{12,4},{1,9},{5,13},{9,1},{13,5},{2,10},{6,14},... | collective-permute-start | bytes 196616 | tf_op jit(solution)/shard_map/ppermute | solution.py:377
  26.5 2.9 %right.1 = (bf16[2,256,128]{2,1,0:T(8,128)(2,1)S(1)}, bf16[2,256,128]{2,1,0:T(8,128)(2,1)S(1)}) custom-call(f32[1,256,128]{2,1,0:T(8,128)S(1)} %get-tuple-element.53.after.held_ref, bf16[4,256,2048]{2,1,0:T(8,128)(2,1)S(1)} %get-tuple-element.51.diag_ref, f32[256,512]{1,0:T(8,128)S(1)} %right_first.1.after.acc_first, ...), custom_call_target="tpu_custom_call" | custom-call | flops 8589934592 | bytes 1048576 | tf_op jit(solution)/shard_map/right/pallas_call | solution.py:562
  29.5 1.8 %collective-permute-start.8 = (bf16[2,64,128]{2,1,0:T(8,128)(2,1)S(1)}, bf16[2,64,128]{2,1,0:T(8,128)(2,1)S(1)}, u32[]{:S(2)}, u32[]{:S(2)}) collective-permute-start(bf16[2,64,128]{2,1,0:T(8,128)(2,1)S(1)} %get-tuple-element.59), channel_id=1, source_target_pairs={{0,1},{1,0},{2,3},{3,2},{4,5},{5,4},{6,7},{7,6},{8,9},{9,8},{10,11... | collective-permute-start | bytes 98312 | tf_op jit(solution)/shard_map/ppermute | solution.py:377
  31.2 1.2 %pair_first.1.after.refs_6_ = bf16[32,64,128]{2,1,0:T(8,128)(2,1)S(1)} custom-call(bf16[2,64,128]{2,1,0:T(8,128)(2,1)S(1)} %get-tuple-element.56.after.held_ref, f32[64,128]{1,0:T(8,128)S(1)} %get-tuple-element.46.refs_1_.ri_ref.refs_2_, bf16[64,64,1024]{2,1,0:T(8,128)(2,1)S(1)} %get-tuple-element.57.y_ref.refs_3_, ...), custom_call_target="tpu_custom_call" | custom-call | flops 8589934592 | bytes 1048576 | tf_op jit(solution)/shard_map/pair_first/pallas_call | solution.py:584
  32.5 1.0 %collective-permute-done.8.came_ref = bf16[2,64,128]{2,1,0:T(8,128)(2,1)S(1)} collective-permute-done((bf16[2,64,128]{2,1,0:T(8,128)(2,1)S(1)}, bf16[2,64,128]{2,1,0:T(8,128)(2,1)S(1)}, u32[]{:S(2)}, u32[]{:S(2)}) %collective-permute-start.8) | collective-permute-done | bytes 32800 | tf_op jit(solution)/shard_map/ppermute | solution.py:377
  33.5 1.5 %collective-permute-start.11 = (bf16[1,64,128]{2,1,0:T(8,128)(2,1)S(1)}, bf16[1,64,128]{2,1,0:T(8,128)(2,1)S(1)}, u32[]{:S(2)}, u32[]{:S(2)}) collective-permute-start(bf16[1,64,128]{2,1,0:T(8,128)(2,1)S(1)} %get-tuple-element.64), channel_id=1, source_target_pairs={{0,2},{1,3},{2,0},{3,1},{4,6},{5,7},{6,4},{7,5},{8,10},{9,11},{10,... | collective-permute-start | bytes 49160 | tf_op jit(solution)/shard_map/ppermute | solution.py:377
  35.0 0.8 %collective-permute-start.10 = (bf16[1,256,128]{2,1,0:T(8,128)(2,1)S(1)}, bf16[1,256,128]{2,1,0:T(8,128)(2,1)S(1)}, u32[]{:S(2)}, u32[]{:S(2)}) collective-permute-start(bf16[1,256,128]{2,1,0:T(8,128)(2,1)S(1)} %get-tuple-element.63), channel_id=1, source_target_pairs={{0,8},{4,12},{8,0},{12,4},{1,9},{5,13},{9,1},{13,5},{2,10},{6,14},... | collective-permute-start | bytes 196616 | tf_op jit(solution)/shard_map/ppermute | solution.py:377
  35.8 2.1 %pair.1.after = bf16[64,64,128]{2,1,0:T(8,128)(2,1)} custom-call(bf16[1,256,128]{2,1,0:T(8,128)(2,1)S(1)} %collective-permute-done.5.refs_0_.refs_1_, f32[1,256,128]{2,1,0:T(8,128)S(1)} %get-tuple-element.62.refs_1_.refs_2_, f32[64,128]{1,0:T(8,128)S(1)} %get-tuple-element.46.refs_1_.ri_ref.refs_2_, ...), custom_call_target="tpu_custom_call" | custom-call | flops 8589934592 | bytes 1048576 | tf_op jit(solution)/shard_map/pair/pallas_call | solution.py:595
  37.9 0.3 collective-permute-done.11.refs_5_
  38.2 1.2 %collective-permute-done.10.refs_3_ = bf16[1,256,128]{2,1,0:T(8,128)(2,1)S(1)} collective-permute-done((bf16[1,256,128]{2,1,0:T(8,128)(2,1)S(1)}, bf16[1,256,128]{2,1,0:T(8,128)(2,1)S(1)}, u32[]{:S(2)}, u32[]{:S(2)}) %collective-permute-start.10) | collective-permute-done | bytes 65568 | tf_op jit(solution)/shard_map/ppermute | solution.py:377
  39.4 0.8 %final_sums.1 = (f32[16,2048]{1,0:T(8,128)}, f32[16,2048]{1,0:T(8,128)}, f32[64,128]{1,0:T(8,128)}) custom-call(bf16[64,64,128]{2,1,0:T(8,128)(2,1)} %pair.1.after, f32[64,128]{1,0:T(8,128)S(1)} %get-tuple-element.46.refs_1_.ri_ref.refs_2_, f32[64,128]{1,0:T(8,128)S(1)} %get-tuple-element.40.rj_ref, f32[1,2048]{1,0:T(1,128)S(1)} %get-tuple-element.41.keep_ref.refs_2_, ...), custom_call_target="tpu_custom_call" | custom-call | flops 1000 | bytes 1000 | tf_op jit(solution)/shard_map/final_sums/pallas_call | solution.py:609
  (17 shorter events, 0.2 us)
Async XLA Ops:
  0.6 8.9 %collective-permute-start = (bf16[1,16,2048]{2,1,0:T(8,128)(2,1)}, bf16[1,16,2048]{2,1,0:T(8,128)(2,1)S(1)}, u32[]{:S(2)}, u32[]{:S(2)}) collective-permute-start(bf16[1,16,2048]{2,1,0:T(8,128)(2,1)} %bitcast.4), channel_id=1, source_target_pairs={{0,2},{1,3},{2,0},{3,1},{4,6},{5,7},{6,4},{7,5},{8,10},{9,11},{10,... | collective-permute-start | bytes 196616 | tf_op jit(solution)/shard_map/ppermute | solution.py:377
  4.7 6.5 %collective-permute-start.1 = (bf16[1,16,2048]{2,1,0:T(8,128)(2,1)}, bf16[1,16,2048]{2,1,0:T(8,128)(2,1)S(1)}, u32[]{:S(2)}, u32[]{:S(2)}) collective-permute-start(bf16[1,16,2048]{2,1,0:T(8,128)(2,1)} %bitcast.5), channel_id=1, source_target_pairs={{0,8},{4,12},{8,0},{12,4},{1,9},{5,13},{9,1},{13,5},{2,10},{6,14},... | collective-permute-start | bytes 196616 | tf_op jit(solution)/shard_map/ppermute | solution.py:377
  9.6 7.4 %collective-permute-start.3 = (bf16[2,16,2048]{2,1,0:T(8,128)(2,1)S(1)}, bf16[2,16,2048]{2,1,0:T(8,128)(2,1)S(1)}, u32[]{:S(2)}, u32[]{:S(2)}) collective-permute-start(bf16[2,16,2048]{2,1,0:T(8,128)(2,1)S(1)} %join.2.after.refs_5_), channel_id=1, source_target_pairs={{0,1},{1,0},{2,3},{3,2},{4,5},{5,4},{6,7},{7,6},{8,9},{9,8},{10,11... | collective-permute-start | bytes 393224 | tf_op jit(solution)/shard_map/ppermute | solution.py:377
  11.2 1.6 %collective-permute-start.2 = (bf16[2,16,2048]{2,1,0:T(8,128)(2,1)S(1)}, bf16[2,16,2048]{2,1,0:T(8,128)(2,1)S(1)}, u32[]{:S(2)}, u32[]{:S(2)}) collective-permute-start(bf16[2,16,2048]{2,1,0:T(8,128)(2,1)S(1)} %join.3.after.right_held), channel_id=1, source_target_pairs={{0,4},{4,0},{8,12},{12,8},{1,5},{5,1},{9,13},{13,9},{2,6},{6,2},{1... | collective-permute-start | bytes 393224 | tf_op jit(solution)/shard_map/ppermute | solution.py:377
  16.5 6.1 %collective-permute-start.4 = (bf16[2,256,128]{2,1,0:T(8,128)(2,1)S(1)}, bf16[2,256,128]{2,1,0:T(8,128)(2,1)S(1)}, u32[]{:S(2)}, u32[]{:S(2)}) collective-permute-start(bf16[2,256,128]{2,1,0:T(8,128)(2,1)S(1)} %get-tuple-element.48), channel_id=1, source_target_pairs={{0,1},{1,0},{2,3},{3,2},{4,5},{5,4},{6,7},{7,6},{8,9},{9,8},{10,11... | collective-permute-start | bytes 393224 | tf_op jit(solution)/shard_map/ppermute | solution.py:377
  22.3 2.6 %collective-permute-start.6 = (bf16[2,256,128]{2,1,0:T(8,128)(2,1)S(1)}, bf16[2,256,128]{2,1,0:T(8,128)(2,1)S(1)}, u32[]{:S(2)}, u32[]{:S(2)}) collective-permute-start(bf16[2,256,128]{2,1,0:T(8,128)(2,1)S(1)} %get-tuple-element.52), channel_id=1, source_target_pairs={{0,4},{4,0},{8,12},{12,8},{1,5},{5,1},{9,13},{13,9},{2,6},{6,2},{1... | collective-permute-start | bytes 393224 | tf_op jit(solution)/shard_map/ppermute | solution.py:377
  22.6 13.2 %collective-permute-start.5 = (bf16[1,256,128]{2,1,0:T(8,128)(2,1)S(1)}, bf16[1,256,128]{2,1,0:T(8,128)(2,1)S(1)}, u32[]{:S(2)}, u32[]{:S(2)}) collective-permute-start(bf16[1,256,128]{2,1,0:T(8,128)(2,1)S(1)} %get-tuple-element.49), channel_id=1, source_target_pairs={{0,2},{1,3},{2,0},{3,1},{4,6},{5,7},{6,4},{7,5},{8,10},{9,11},{10,... | collective-permute-start | bytes 196616 | tf_op jit(solution)/shard_map/ppermute | solution.py:377
  24.9 4.5 %collective-permute-start.7 = (bf16[1,256,128]{2,1,0:T(8,128)(2,1)S(1)}, bf16[1,256,128]{2,1,0:T(8,128)(2,1)S(1)}, u32[]{:S(2)}, u32[]{:S(2)}) collective-permute-start(bf16[1,256,128]{2,1,0:T(8,128)(2,1)S(1)} %get-tuple-element.55), channel_id=1, source_target_pairs={{0,8},{4,12},{8,0},{12,4},{1,9},{5,13},{9,1},{13,5},{2,10},{6,14},... | collective-permute-start | bytes 196616 | tf_op jit(solution)/shard_map/ppermute | solution.py:377
  29.3 5.6 %collective-permute-start.9 = (bf16[2,256,128]{2,1,0:T(8,128)(2,1)S(1)}, bf16[2,256,128]{2,1,0:T(8,128)(2,1)S(1)}, u32[]{:S(2)}, u32[]{:S(2)}) collective-permute-start(bf16[2,256,128]{2,1,0:T(8,128)(2,1)S(1)} %get-tuple-element.61), channel_id=1, source_target_pairs={{0,4},{4,0},{8,12},{12,8},{1,5},{5,1},{9,13},{13,9},{2,6},{6,2},{1... | collective-permute-start | bytes 393224 | tf_op jit(solution)/shard_map/ppermute | solution.py:377
  29.5 4.0 %collective-permute-start.8 = (bf16[2,64,128]{2,1,0:T(8,128)(2,1)S(1)}, bf16[2,64,128]{2,1,0:T(8,128)(2,1)S(1)}, u32[]{:S(2)}, u32[]{:S(2)}) collective-permute-start(bf16[2,64,128]{2,1,0:T(8,128)(2,1)S(1)} %get-tuple-element.59), channel_id=1, source_target_pairs={{0,1},{1,0},{2,3},{3,2},{4,5},{5,4},{6,7},{7,6},{8,9},{9,8},{10,11... | collective-permute-start | bytes 98312 | tf_op jit(solution)/shard_map/ppermute | solution.py:377
  33.5 4.7 %collective-permute-start.11 = (bf16[1,64,128]{2,1,0:T(8,128)(2,1)S(1)}, bf16[1,64,128]{2,1,0:T(8,128)(2,1)S(1)}, u32[]{:S(2)}, u32[]{:S(2)}) collective-permute-start(bf16[1,64,128]{2,1,0:T(8,128)(2,1)S(1)} %get-tuple-element.64), channel_id=1, source_target_pairs={{0,2},{1,3},{2,0},{3,1},{4,6},{5,7},{6,4},{7,5},{8,10},{9,11},{10,... | collective-permute-start | bytes 49160 | tf_op jit(solution)/shard_map/ppermute | solution.py:377
  35.0 4.3 %collective-permute-start.10 = (bf16[1,256,128]{2,1,0:T(8,128)(2,1)S(1)}, bf16[1,256,128]{2,1,0:T(8,128)(2,1)S(1)}, u32[]{:S(2)}, u32[]{:S(2)}) collective-permute-start(bf16[1,256,128]{2,1,0:T(8,128)(2,1)S(1)} %get-tuple-element.63), channel_id=1, source_target_pairs={{0,8},{4,12},{8,0},{12,4},{1,9},{5,13},{9,1},{13,5},{2,10},{6,14},... | collective-permute-start | bytes 196616 | tf_op jit(solution)/shard_map/ppermute | solution.py:377

commit v10 on v9

--- a/solution.py
+++ b/solution.py
@@ -8,6 +8,8 @@
 from jax.sharding import PartitionSpec as P
 
 LANES = 128
+CHUNK = 4
+PIECE = 8
 NT = (((1,), (1,)), ((), ()))
 F32 = jnp.float32
 BF16 = jnp.bfloat16
@@ -57,9 +59,9 @@
     res_ref, seq_ref, w_ref, w32, cot, sems, more_sems = refs[15:]
     steps = i_rows // step_rows
 
-    def fetch(step):
-        rows = pl.ds(step * step_rows, step_rows)
-        return pltpu.make_async_copy(cot_ref.at[rows], cot.at[rows], sems.at[step])
+    def fetch(piece):
+        rows = pl.ds(piece * PIECE, PIECE)
+        return pltpu.make_async_copy(cot_ref.at[rows], cot.at[rows], sems.at[piece])
 
     pairs = [
         (res_hbm, res_ref),
@@ -73,8 +75,8 @@
     ]
     for copy in more[:3]:
         copy.start()
-    for step in range(steps):
-        fetch(step).start()
+    for piece in range(i_rows // PIECE):
+        fetch(piece).start()
     for copy in more[3:]:
         copy.start()
     shape = (sequences, tiles * LANES)
@@ -95,9 +97,9 @@
     for e in range(chans):
         wp_ref[e * chans : (e + 1) * chans, :] = w32[pl.ds(e, chans, stride=chans), :].astype(BF16)
     for step in range(steps):
-        fetch(step).wait()
-        for i in range(step_rows):
-            at = step * step_rows + i
+        for at in range(step * step_rows, (step + 1) * step_rows):
+            if at % PIECE == 0:
+                fetch(at // PIECE).wait()
             inverse = jnp.where(ri_ref[at : at + 1, :] > 0, inv_ref[...], 1.0)
             scaled_ref[at] = (cot[at].astype(F32) * inverse).astype(BF16)
         if step < z_ref.shape[0]:
@@ -109,15 +111,15 @@
 
 def inner_rows(dims, scaled, wp_ref, z_ref, at):
     chans, groups, blocks, i_rows, j_rows, step_rows, sequences = dims
-    for pair in range(0, blocks, 2):
+    for first in range(0, blocks, CHUNK):
         part = lax.dot_general(
             scaled.reshape(step_rows * j_rows, LANES),
-            wp_ref[pair * LANES : (pair + 2) * LANES, :],
+            wp_ref[first * LANES : (first + CHUNK) * LANES, :],
             NT,
             preferred_element_type=F32,
         ).astype(BF16)
-        for k in range(2):
-            a = pair + k
+        for k in range(CHUNK):
+            a = first + k
             for i in range(step_rows):
                 z_ref[at, a * j_rows : (a + 1) * j_rows, i * LANES : (i + 1) * LANES] = part[
                     i * j_rows : (i + 1) * j_rows, k * LANES : (k + 1) * LANES
@@ -172,15 +174,15 @@
                     diag_ref[step, at : at + tiles, i * LANES : (i + 1) * LANES] = (
                         spread[i * tiles : (i + 1) * tiles, lo * LANES : (lo + 1) * LANES] * chosen
                     )
-        for pair in range(0, step_rows, 2):
+        for first in range(0, step_rows, CHUNK):
             part = jnp.dot(
                 rbig[...],
-                diag_ref[step, :, pair * LANES : (pair + 2) * LANES],
+                diag_ref[step, :, first * LANES : (first + CHUNK) * LANES],
                 preferred_element_type=F32,
             ).astype(BF16)
-            for k in range(2):
+            for k in range(CHUNK):
                 for a in range(blocks):
-                    y_ref[step * step_rows + pair + k, :, a * LANES : (a + 1) * LANES] = part[
+                    y_ref[step * step_rows + first + k, :, a * LANES : (a + 1) * LANES] = part[
                         a * j_rows : (a + 1) * j_rows, k * LANES : (k + 1) * LANES
                     ]
         block = slice(step * step_rows, (step + 1) * step_rows)
@@ -265,13 +267,13 @@
 
     for step in range(i_rows // step_rows):
         z_ref = at_step(z_refs, step)
-        for pair in range(0, step_rows, 2):
+        for first in range(0, step_rows, CHUNK):
             part = jnp.dot(
                 rbt_ref[...],
-                z_ref[:, pair * LANES : (pair + 2) * LANES],
+                z_ref[:, first * LANES : (first + CHUNK) * LANES],
                 preferred_element_type=F32,
             )
-            for k in range(2):
+            for k in range(CHUNK):
                 mine = part[:, k * LANES : (k + 1) * LANES]
                 total = mine[0:sequences]
                 for b in range(1, groups):
@@ -283,7 +285,7 @@
                 merged = total[0:tiles]
                 for lo in range(1, groups):
                     merged = jnp.where(group_t == lo, total[lo * tiles : (lo + 1) * tiles], merged)
-                at = (step * step_rows + pair + k) * tiles
+                at = (step * step_rows + first + k) * tiles
                 gl_all[at : at + tiles, :] = merged
     cut(gl_all, lax.axis_index("col"), n_col, keep_out, send_out)
 
@@ -319,36 +321,38 @@
         )
 
 
-def pair_rows(dims, step, ri_ref, y_ref, wp_ref, inv_ref, out_ref, at):
-    chans, groups, blocks, i_rows, j_rows, step_rows, sequences = dims
-    pairs = step_rows * j_rows
-    y_flat = y_ref[step * step_rows : (step + 1) * step_rows].reshape(pairs, blocks * LANES)
+def pair_rows(dims, row, ri_ref, y_ref, wp_ref, inv_ref, out_ref, at):
+    j_rows = dims[4]
+    y_flat = y_ref[row : row + PIECE].reshape(PIECE * j_rows, y_ref.shape[2])
     projected = jnp.dot(y_flat, wp_ref[...], preferred_element_type=F32)
-    for i in range(step_rows):
-        row = step * step_rows + i
-        inverse = jnp.where(ri_ref[row : row + 1, :] > 0, inv_ref[...], 1.0)
+    for i in range(PIECE):
+        inverse = jnp.where(ri_ref[row + i : row + i + 1, :] > 0, inv_ref[...], 1.0)
         out_ref[at + i] = (projected[i * j_rows : (i + 1) * j_rows] * inverse).astype(BF16)
 
 
-def pair_first_kernel(dims, steps, after, ri_ref, y_ref, wp_ref, inv_ref, out_ref):
-    for step in range(steps):
-        pair_rows(dims, step, ri_ref, y_ref, wp_ref, inv_ref, out_ref, step * dims[5])
+def pair_first_kernel(dims, after, ri_ref, y_ref, wp_ref, inv_ref, out_ref):
+    for row in range(0, out_ref.shape[0], PIECE):
+        pair_rows(dims, row, ri_ref, y_ref, wp_ref, inv_ref, out_ref, row)
 
 
 def pair_kernel(dims, *refs):
-    i_rows, j_rows, step_rows = dims[3:6]
-    after_left, after_right, ri_ref, y_ref, wp_ref, inv_ref, early = refs[:7]
-    out_ref, staged, sems = refs[7:]
+    after, ri_ref, y_ref, wp_ref, inv_ref, early, keep_ref, held, came = refs[:9]
+    out_ref, gl_out, staged, whole, left, sems = refs[9:]
     begin = early.shape[0]
     copies = [pltpu.make_async_copy(early, out_ref.at[pl.ds(0, begin)], sems.at[0])]
     copies[0].start()
-    for step in range(begin // step_rows, i_rows // step_rows):
-        at = step * step_rows - begin
-        pair_rows(dims, step, ri_ref, y_ref, wp_ref, inv_ref, staged, at)
+    own = left.shape[0]
+    first = pl.multiple_of(lax.axis_index("col") * own, 8)
+    whole[...] = total_of(held, came)
+    write_rows(whole, ri_ref[pl.ds(first, own), :], keep_ref, left, whole.shape[0] // own)
+    copies.append(pltpu.make_async_copy(left, gl_out, sems.at[1]))
+    copies[1].start()
+    for row in range(begin, dims[3], PIECE):
+        pair_rows(dims, row, ri_ref, y_ref, wp_ref, inv_ref, staged, row - begin)
         copies.append(
             pltpu.make_async_copy(
-                staged.at[pl.ds(at, step_rows)],
-                out_ref.at[pl.ds(begin + at, step_rows)],
+                staged.at[pl.ds(row - begin, PIECE)],
+                out_ref.at[pl.ds(row, PIECE)],
                 sems.at[len(copies)],
             )
         )
@@ -357,20 +361,20 @@
         copy.wait()
 
 
-def final_kernel(dims, after, ri_ref, rj_ref, keep_ref, *refs):
-    chans, groups, blocks, i_rows, j_rows, step_rows, sequences = dims
-    tiles = sequences * chans // LANES
-    left, right, weight = refs[0:2], refs[2:4], refs[4:6]
-    gl_out, gr_out, gw_out, whole = refs[6:]
-    for refs_in, out, rows_ref, axis in (
-        (left, gl_out, ri_ref, "col"),
-        (right, gr_out, rj_ref, "row"),
-    ):
-        own = out.shape[0]
-        whole[0 : own * tiles, :] = total_of(*refs_in)
-        first = pl.multiple_of(lax.axis_index(axis) * own, 8)
-        write_rows(whole, rows_ref[pl.ds(first, own), :], keep_ref, out, tiles)
-    gw_out[...] = total_of(*weight)
+def final_kernel(after, rj_ref, keep_ref, *refs):
+    right, weight = refs[0:2], refs[2:4]
+    gr_out, gw_out, whole, rows, weight_rows, sems = refs[4:]
+    weight_rows[...] = total_of(*weight)
+    copies = [pltpu.make_async_copy(weight_rows, gw_out, sems.at[0])]
+    copies[0].start()
+    own = rows.shape[0]
+    first = pl.multiple_of(lax.axis_index("row") * own, 8)
+    whole[...] = total_of(*right)
+    write_rows(whole, rj_ref[pl.ds(first, own), :], keep_ref, rows, whole.shape[0] // own)
+    copies.append(pltpu.make_async_copy(rows, gr_out, sems.at[1]))
+    copies[1].start()
+    for copy in copies:
+        copy.wait()
 
 
 def swap(array, axis, n, bit):
@@ -450,7 +454,7 @@
     tiles = width // LANES
     depth = groups * sequences
     inner = chans * chans
-    step_rows = 16
+    step_rows = 32
     steps = i_rows // step_rows
     early_steps = steps // 2
     dims = (chans, groups, blocks, i_rows, j_rows, step_rows, sequences)
@@ -481,7 +485,7 @@
             pltpu.VMEM(out_weight.shape, BF16),
             pltpu.VMEM(out_weight.shape, F32),
             pltpu.VMEM(cotangent.shape, BF16),
-            pltpu.SemaphoreType.DMA((steps,)),
+            pltpu.SemaphoreType.DMA((i_rows // PIECE,)),
             pltpu.SemaphoreType.DMA((5,)),
         ],
         compiler_params=params(16),
@@ -547,7 +551,7 @@
 
     gl_last = reduce(*gl_cut, "col", n_col, gw_cut[0])
 
-    right_steps = steps // 4
+    right_steps = max(1, steps // 4)
     acc = pl.pallas_call(
         functools.partial(right_first_kernel, right_steps),
         in_specs=[hbm()] + vmem(1 + len(z)),
@@ -580,46 +584,56 @@
         [pltpu.VMEM((inner // n_row, pair_width), F32)],
     )(gr_cut[0], *gw_row)
 
-    half = steps // 2
+    begin = i_rows // PIECE // 2 * PIECE
     early = pl.pallas_call(
-        functools.partial(pair_first_kernel, dims, half),
+        functools.partial(pair_first_kernel, dims),
         in_specs=[hbm()] + vmem(4),
         out_specs=vmem()[0],
-        out_shape=pltpu.VMEM((half * step_rows, j_rows, pair_width), BF16),
+        out_shape=pltpu.VMEM((begin, j_rows, pair_width), BF16),
         compiler_params=params(12),
         cost_estimate=cost(16 * macs, 2**20),
         name="pair_first",
     )(gw_cut[0], i_keep, y, weight, inverse)
     gw_last = reduce(*gw_cut, "col", n_col, early)
     gr_last = reduce(*gr_cut, "row", n_row, gw_last[0])
-    pair_out = pl.pallas_call(
+    pair_out, grad_left = pl.pallas_call(
         functools.partial(pair_kernel, dims),
-        in_specs=[hbm()] * 2 + vmem(5),
-        out_specs=hbm(),
-        out_shape=jax.ShapeDtypeStruct(cotangent.shape, BF16),
+        in_specs=[hbm()] + vmem(8),
+        out_specs=[hbm()] * 2,
+        out_shape=[
+            jax.ShapeDtypeStruct(cotangent.shape, BF16),
+            jax.ShapeDtypeStruct((own_left, width), F32),
+        ],
         scratch_shapes=[
-            pltpu.VMEM((i_rows - half * step_rows, j_rows, pair_width), BF16),
-            pltpu.SemaphoreType.DMA((1 + steps - half,)),
+            pltpu.VMEM((i_rows - begin, j_rows, pair_width), BF16),
+            pltpu.VMEM((own_left * tiles, LANES), F32),
+            pltpu.VMEM((own_left, width), F32),
+            pltpu.SemaphoreType.DMA((2 + (i_rows - begin) // PIECE,)),
         ],
         compiler_params=params(12),
         cost_estimate=cost(16 * macs, 2**20),
         name="pair",
-    )(gl_last[1], gr_last[0], i_keep, y, weight, inverse, early)
-
-    grad_left, grad_right, grad_weight = pl.pallas_call(
-        functools.partial(final_kernel, dims),
-        in_specs=[hbm()] + vmem(9),
-        out_specs=vmem(3),
+    )(gr_last[0], i_keep, y, weight, inverse, early, keep, *gl_last)
+
+    owned = (inner // n_row // n_col, pair_width)
+    grad_right, grad_weight = pl.pallas_call(
+        final_kernel,
+        in_specs=[hbm()] + vmem(6),
+        out_specs=[hbm()] * 2,
         out_shape=[
-            jax.ShapeDtypeStruct((own_left, width), F32),
             jax.ShapeDtypeStruct((own_right, width), F32),
-            jax.ShapeDtypeStruct((inner // n_row // n_col, pair_width), F32),
-        ],
-        scratch_shapes=[pltpu.VMEM((max(own_left, own_right) * tiles, LANES), F32)],
+            jax.ShapeDtypeStruct(owned, F32),
+        ],
+        scratch_shapes=[
+            pltpu.VMEM((own_right * tiles, LANES), F32),
+            pltpu.VMEM((own_right, width), F32),
+            pltpu.VMEM(owned, F32),
+            pltpu.SemaphoreType.DMA((2,)),
+        ],
         compiler_params=params(4),
         cost_estimate=cost(1000, 1000),
         name="final_sums",
-    )(in_hbm(pair_out), i_keep, j_keep, keep, *gl_last, *gr_last, *gw_last)
+    )(in_hbm(pair_out), j_keep, keep, *gr_last, *gw_last)
     return (pair_out, grad_left, grad_right, grad_weight)
 
 

time: 40.3 us -> 41 us (1.017)
  waiting for transfers between devices: 2.46 us -> 3.7 us
    ppermute x12, waiting for transfers between devices: 2.46 us -> 3.7 us  [swap(): return lax.ppermute(array, axis, [(s, s ^ bit) for s in range(n)])]
    pallas_call x1, Pallas kernels: 2.87 us -> 2.33 us  [shards(): pl.pallas_call(functools.partial(right_kernel, dims, n_row, right_steps),...]
    pallas_call x1, Pallas kernels: 0.93 us -> 1.47 us  [shards(): pl.pallas_call(functools.partial(right_first_kernel, right_steps), in_spe...]
  transfers between devices with their start and end apart: 12 -> 12, of which waited for: 3 -> 5; matrix products, arithmetic and copies ran while one was open for 0% -> 0% of each run, Pallas kernels for 52% -> 51%
where the time goes in v10:
time: 41 us; the launch traced here: 40.9 us
  Pallas kernels  21.5 us (52%)
  starting transfers between devices  14.8 us (36%)
  waiting for transfers between devices  3.7 us (9%)
  between operations  0.94 us (2%)
    ppermute x12, starting transfers between devices, swap(): return lax.ppermute(array, axis, [(s, s ^ bit) for s in range(n)])  14.8 us
    pallas_call x1, Pallas kernels, shards(): pl.pallas_call(functools.partial(outer_kernel, dims, n_row, n_col), in_sp...  4.89 us
    ppermute x12, waiting for transfers between devices, swap(): return lax.ppermute(array, axis, [(s, s ^ bit) for s in range(n)])  3.7 us
    pallas_call x1, Pallas kernels, shards(): pl.pallas_call(functools.partial(scale_kernel, dims), in_specs=[hbm()] *...  3.51 us
    pallas_call x1, Pallas kernels, shards(): pl.pallas_call(functools.partial(left_kernel, dims, n_col), in_specs=[hbm...  2.53 us
    pallas_call x1, Pallas kernels, shards(): pl.pallas_call(functools.partial(right_kernel, dims, n_row, right_steps),...  2.33 us
    pallas_call x1, Pallas kernels, shards(): pl.pallas_call(functools.partial(pair_kernel, dims), in_specs=[hbm()] + v...  2.02 us
    pallas_call x1, Pallas kernels, shards(): pl.pallas_call(functools.partial(inner_kernel, dims, early_steps), in_spe...  1.51 us
  transfers between devices with their start and end apart: 12, of which 5 were waited for; matrix products, arithmetic and copies ran while one was open for 0% of the time, Pallas kernels for 51%

profile of v10, /device:TPU:0, one launch (start us, length us, event | category | flops | bytes accessed | tf_op | source)
XLA Modules:
  0.0 40.9 jit_solution(11098301622613762029)
XLA Ops:
  0.6 4.1 %collective-permute-start = (bf16[1,16,2048]{2,1,0:T(8,128)(2,1)}, bf16[1,16,2048]{2,1,0:T(8,128)(2,1)S(1)}, u32[]{:S(2)}, u32[]{:S(2)}) collective-permute-start(bf16[1,16,2048]{2,1,0:T(8,128)(2,1)} %bitcast.4), channel_id=1, source_target_pairs={{0,2},{1,3},{2,0},{3,1},{4,6},{5,7},{6,4},{7,5},{8,10},{9,11},{10,... | collective-permute-start | bytes 196616 | tf_op jit(solution)/shard_map/ppermute | solution.py:381
  4.7 1.5 %collective-permute-start.1 = (bf16[1,16,2048]{2,1,0:T(8,128)(2,1)}, bf16[1,16,2048]{2,1,0:T(8,128)(2,1)S(1)}, u32[]{:S(2)}, u32[]{:S(2)}) collective-permute-start(bf16[1,16,2048]{2,1,0:T(8,128)(2,1)} %bitcast.5), channel_id=1, source_target_pairs={{0,8},{4,12},{8,0},{12,4},{1,9},{5,13},{9,1},{13,5},{2,10},{6,14},... | collective-permute-start | bytes 196616 | tf_op jit(solution)/shard_map/ppermute | solution.py:381
  6.2 3.5 %scale.1 = (bf16[64,64,128]{2,1,0:T(8,128)(2,1)S(1)}, f32[64,128]{1,0:T(8,128)S(1)}, bf16[1024,128]{1,0:T(8,128)(2,1)S(1)}, f32[1,2048]{1,0:T(1,128)S(1)}, f32[6...) custom-call(s32[1,256]{1,0:T(1,128)} %bitcast.6, ...), custom_call_target="tpu_custom_call" | custom-call | flops 1000 | bytes 1000 | tf_op jit(solution)/shard_map/scale/pallas_call | solution.py:467
  9.8 1.6 %collective-permute-start.3 = (bf16[2,16,2048]{2,1,0:T(8,128)(2,1)S(1)}, bf16[2,16,2048]{2,1,0:T(8,128)(2,1)S(1)}, u32[]{:S(2)}, u32[]{:S(2)}) collective-permute-start(bf16[2,16,2048]{2,1,0:T(8,128)(2,1)S(1)} %join.2.after.refs_5_), channel_id=1, source_target_pairs={{0,1},{1,0},{2,3},{3,2},{4,5},{5,4},{6,7},{7,6},{8,9},{9,8},{10,11... | collective-permute-start | bytes 393224 | tf_op jit(solution)/shard_map/ppermute | solution.py:381
  11.5 1.5 %inner.1.after.refs_1_ = bf16[1,512,4096]{2,1,0:T(8,128)(2,1)S(1)} custom-call(bf16[2,16,2048]{2,1,0:T(8,128)(2,1)S(1)} %join.3.after.right_held, bf16[64,64,128]{2,1,0:T(8,128)(2,1)S(1)} %get-tuple-element.39.scaled_ref.refs_3_, bf16[1024,128]{1,0:T(8,128)(2,1)S(1)} %get-tuple-element.40.wp_ref.refs_3_), custom_call_target="tpu_custom_call" | custom-call | flops 8589934592 | bytes 1048576 | tf_op jit(solution)/shard_map/inner/pallas_call | solution.py:499
  13.0 1.1 %right_rows.1 = (bf16[512,256]{1,0:T(8,128)(2,1)S(1)}, bf16[256,512]{1,0:T(8,128)(2,1)S(1)}) custom-call(bf16[1,512,4096]{2,1,0:T(8,128)(2,1)S(1)} %inner.1.after.refs_1_, f32[64,128]{1,0:T(8,128)S(1)} %get-tuple-element.41.rj_ref, f32[1,2048]{1,0:T(1,128)S(1)} %get-tuple-element.42.keep_ref.refs_2_.refs_6_, bf16[2,16,2048]{2,1,0:T(8,128)(2,1)S(1)} %join.3.after.right_held, ...), custom_call_target="tpu_custom_call" | custom-call | flops 8589934592 | bytes 1048576 | tf_op jit(solution)/shard_map/right_rows/pallas_call | solution.py:510
  14.1 2.5 %left.1 = (bf16[2,256,128]{2,1,0:T(8,128)(2,1)S(1)}, bf16[2,256,128]{2,1,0:T(8,128)(2,1)S(1)}) custom-call(bf16[512,256]{1,0:T(8,128)(2,1)S(1)} %get-tuple-element.43.after.refs_4_, bf16[256,512]{1,0:T(8,128)(2,1)S(1)} %get-tuple-element.44.rbt_ref, bf16[1,512,4096]{2,1,0:T(8,128)(2,1)S(1)} %get-tuple-element.45.refs_0_, ...), custom_call_target="tpu_custom_call" | custom-call | flops 8589934592 | bytes 1048576 | tf_op jit(solution)/shard_map/left/pallas_call | solution.py:521
  16.7 0.5 %collective-permute-start.4 = (bf16[2,256,128]{2,1,0:T(8,128)(2,1)S(1)}, bf16[2,256,128]{2,1,0:T(8,128)(2,1)S(1)}, u32[]{:S(2)}, u32[]{:S(2)}) collective-permute-start(bf16[2,256,128]{2,1,0:T(8,128)(2,1)S(1)} %get-tuple-element.49), channel_id=1, source_target_pairs={{0,1},{1,0},{2,3},{3,2},{4,5},{5,4},{6,7},{7,6},{8,9},{9,8},{10,11... | collective-permute-start | bytes 393224 | tf_op jit(solution)/shard_map/ppermute | solution.py:381
  17.2 4.9 %outer.1 = (bf16[64,64,1024]{2,1,0:T(8,128)(2,1)S(1)}, bf16[2,256,4096]{2,1,0:T(8,128)(2,1)S(1)}, bf16[2,256,128]{2,1,0:T(8,128)(2,1)S(1)}, bf16[2,256,128]{2,1,0:T(8,128)(2,1)S(1)}) custom-call(bf16[2,256,128]{2,1,0:T(8,128)(2,1)S(1)} %get-tuple-element.46.refs_0_.held_ref, f32[64,128]{1,0:T(8,128)S(1)} %get-tuple-element.47.refs_1_.ri_ref, ...), custom_call_target="tpu_custom_call" | custom-call | flops 8589934592 | bytes 1048576 | tf_op jit(solution)/shard_map/outer/pallas_call | solution.py:531
  22.1 0.3 collective-permute-start.5
  22.3 0.3 collective-permute-done.4.came_ref
  22.7 1.3 %collective-permute-start.9 = (bf16[1,256,128]{2,1,0:T(8,128)(2,1)S(1)}, bf16[1,256,128]{2,1,0:T(8,128)(2,1)S(1)}, u32[]{:S(2)}, u32[]{:S(2)}) collective-permute-start(bf16[1,256,128]{2,1,0:T(8,128)(2,1)S(1)} %get-tuple-element.63), channel_id=1, source_target_pairs={{0,2},{1,3},{2,0},{3,1},{4,6},{5,7},{6,4},{7,5},{8,10},{9,11},{10,... | collective-permute-start | bytes 196616 | tf_op jit(solution)/shard_map/ppermute | solution.py:381
  23.9 1.5 %right_first.1.after.acc_first = f32[256,512]{1,0:T(8,128)S(1)} custom-call(f32[1,256,128]{2,1,0:T(8,128)S(1)} %get-tuple-element.50.after.refs_7_, bf16[2,256,4096]{2,1,0:T(8,128)(2,1)S(1)} %get-tuple-element.51.diag_ref, bf16[1,512,4096]{2,1,0:T(8,128)(2,1)S(1)} %get-tuple-element.45.refs_0_, bf16[1,512,4096]{2,1,0:T(8,128)(2,1)S(1)} %inner.1.after.refs_1_), custom_call_target="tpu_custom_call" | custom-call | flops 8589934592 | bytes 1048576 | tf_op jit(solution)/shard_map/right_first/pallas_call | solution.py:555
  25.5 1.6 %collective-permute-start.6 = (bf16[1,256,128]{2,1,0:T(8,128)(2,1)S(1)}, bf16[1,256,128]{2,1,0:T(8,128)(2,1)S(1)}, u32[]{:S(2)}, u32[]{:S(2)}) collective-permute-start(bf16[1,256,128]{2,1,0:T(8,128)(2,1)S(1)} %get-tuple-element.55), channel_id=1, source_target_pairs={{0,8},{4,12},{8,0},{12,4},{1,9},{5,13},{9,1},{13,5},{2,10},{6,14},... | collective-permute-start | bytes 196616 | tf_op jit(solution)/shard_map/ppermute | solution.py:381
  27.0 2.3 %right.1 = (bf16[2,256,128]{2,1,0:T(8,128)(2,1)S(1)}, bf16[2,256,128]{2,1,0:T(8,128)(2,1)S(1)}) custom-call(f32[1,256,128]{2,1,0:T(8,128)S(1)} %get-tuple-element.53.after.held_ref, bf16[2,256,4096]{2,1,0:T(8,128)(2,1)S(1)} %get-tuple-element.51.diag_ref, f32[256,512]{1,0:T(8,128)S(1)} %right_first.1.after.acc_first, ...), custom_call_target="tpu_custom_call" | custom-call | flops 8589934592 | bytes 1048576 | tf_op jit(solution)/shard_map/right/pallas_call | solution.py:566
  29.4 0.4 collective-permute-done.6.came_ref
  29.8 1.4 %collective-permute-start.7 = (bf16[2,64,128]{2,1,0:T(8,128)(2,1)S(1)}, bf16[2,64,128]{2,1,0:T(8,128)(2,1)S(1)}, u32[]{:S(2)}, u32[]{:S(2)}) collective-permute-start(bf16[2,64,128]{2,1,0:T(8,128)(2,1)S(1)} %get-tuple-element.59), channel_id=1, source_target_pairs={{0,1},{1,0},{2,3},{3,2},{4,5},{5,4},{6,7},{7,6},{8,9},{9,8},{10,11... | collective-permute-start | bytes 98312 | tf_op jit(solution)/shard_map/ppermute | solution.py:381
  31.2 1.2 %pair_first.1.after.refs_5_ = bf16[32,64,128]{2,1,0:T(8,128)(2,1)S(1)} custom-call(bf16[2,64,128]{2,1,0:T(8,128)(2,1)S(1)} %get-tuple-element.56.after.held_ref, f32[64,128]{1,0:T(8,128)S(1)} %get-tuple-element.47.refs_1_.ri_ref, bf16[64,64,1024]{2,1,0:T(8,128)(2,1)S(1)} %get-tuple-element.57.y_ref.refs_2_, ...), custom_call_target="tpu_custom_call" | custom-call | flops 8589934592 | bytes 1048576 | tf_op jit(solution)/shard_map/pair_first/pallas_call | solution.py:588
  32.4 1.4 %collective-permute-done.7.came_ref = bf16[2,64,128]{2,1,0:T(8,128)(2,1)S(1)} collective-permute-done((bf16[2,64,128]{2,1,0:T(8,128)(2,1)S(1)}, bf16[2,64,128]{2,1,0:T(8,128)(2,1)S(1)}, u32[]{:S(2)}, u32[]{:S(2)}) %collective-permute-start.7) | collective-permute-done | bytes 32800 | tf_op jit(solution)/shard_map/ppermute | solution.py:381
  33.8 1.8 %collective-permute-start.11 = (bf16[1,64,128]{2,1,0:T(8,128)(2,1)S(1)}, bf16[1,64,128]{2,1,0:T(8,128)(2,1)S(1)}, u32[]{:S(2)}, u32[]{:S(2)}) collective-permute-start(bf16[1,64,128]{2,1,0:T(8,128)(2,1)S(1)} %get-tuple-element.67), channel_id=1, source_target_pairs={{0,2},{1,3},{2,0},{3,1},{4,6},{5,7},{6,4},{7,5},{8,10},{9,11},{10,... | collective-permute-start | bytes 49160 | tf_op jit(solution)/shard_map/ppermute | solution.py:381
  35.6 0.6 %collective-permute-start.10 = (bf16[1,256,128]{2,1,0:T(8,128)(2,1)S(1)}, bf16[1,256,128]{2,1,0:T(8,128)(2,1)S(1)}, u32[]{:S(2)}, u32[]{:S(2)}) collective-permute-start(bf16[1,256,128]{2,1,0:T(8,128)(2,1)S(1)} %get-tuple-element.66), channel_id=1, source_target_pairs={{0,8},{4,12},{8,0},{12,4},{1,9},{5,13},{9,1},{13,5},{2,10},{6,14},... | collective-permute-start | bytes 196616 | tf_op jit(solution)/shard_map/ppermute | solution.py:381
  36.2 2.0 %pair.1 = (bf16[64,64,128]{2,1,0:T(8,128)(2,1)}, f32[16,2048]{1,0:T(8,128)}) custom-call(f32[1,256,128]{2,1,0:T(8,128)S(1)} %get-tuple-element.62.refs_0_, f32[64,128]{1,0:T(8,128)S(1)} %get-tuple-element.47.refs_1_.ri_ref, bf16[64,64,1024]{2,1,0:T(8,128)(2,1)S(1)} %get-tuple-element.57.y_ref.refs_2_, ...), custom_call_target="tpu_custom_call" | custom-call | flops 8589934592 | bytes 1048576 | tf_op jit(solution)/shard_map/pair/pallas_call | solution.py:599
  38.5 1.4 %collective-permute-done.10.refs_1_ = bf16[1,256,128]{2,1,0:T(8,128)(2,1)S(1)} collective-permute-done((bf16[1,256,128]{2,1,0:T(8,128)(2,1)S(1)}, bf16[1,256,128]{2,1,0:T(8,128)(2,1)S(1)}, u32[]{:S(2)}, u32[]{:S(2)}) %collective-permute-start.10) | collective-permute-done | bytes 65568 | tf_op jit(solution)/shard_map/ppermute | solution.py:381
  40.0 0.7 %final_sums.1 = (f32[16,2048]{1,0:T(8,128)}, f32[64,128]{1,0:T(8,128)}) custom-call(bf16[64,64,128]{2,1,0:T(8,128)(2,1)} %get-tuple-element.33.after, f32[64,128]{1,0:T(8,128)S(1)} %get-tuple-element.41.rj_ref, f32[1,2048]{1,0:T(1,128)S(1)} %get-tuple-element.42.keep_ref.refs_2_.refs_6_, f32[1,256,128]{2,1,0:T(8,128)S(1)} %get-tuple-element.62.refs_0_, ...), custom_call_target="tpu_custom_call" | custom-call | flops 1000 | bytes 1000 | tf_op jit(solution)/shard_map/final_sums/pallas_call | solution.py:619
  (17 shorter events, 0.6 us)
Async XLA Ops:
  0.6 9.1 %collective-permute-start = (bf16[1,16,2048]{2,1,0:T(8,128)(2,1)}, bf16[1,16,2048]{2,1,0:T(8,128)(2,1)S(1)}, u32[]{:S(2)}, u32[]{:S(2)}) collective-permute-start(bf16[1,16,2048]{2,1,0:T(8,128)(2,1)} %bitcast.4), channel_id=1, source_target_pairs={{0,2},{1,3},{2,0},{3,1},{4,6},{5,7},{6,4},{7,5},{8,10},{9,11},{10,... | collective-permute-start | bytes 196616 | tf_op jit(solution)/shard_map/ppermute | solution.py:381
  4.7 6.7 %collective-permute-start.1 = (bf16[1,16,2048]{2,1,0:T(8,128)(2,1)}, bf16[1,16,2048]{2,1,0:T(8,128)(2,1)S(1)}, u32[]{:S(2)}, u32[]{:S(2)}) collective-permute-start(bf16[1,16,2048]{2,1,0:T(8,128)(2,1)} %bitcast.5), channel_id=1, source_target_pairs={{0,8},{4,12},{8,0},{12,4},{1,9},{5,13},{9,1},{13,5},{2,10},{6,14},... | collective-permute-start | bytes 196616 | tf_op jit(solution)/shard_map/ppermute | solution.py:381
  9.8 7.4 %collective-permute-start.3 = (bf16[2,16,2048]{2,1,0:T(8,128)(2,1)S(1)}, bf16[2,16,2048]{2,1,0:T(8,128)(2,1)S(1)}, u32[]{:S(2)}, u32[]{:S(2)}) collective-permute-start(bf16[2,16,2048]{2,1,0:T(8,128)(2,1)S(1)} %join.2.after.refs_5_), channel_id=1, source_target_pairs={{0,1},{1,0},{2,3},{3,2},{4,5},{5,4},{6,7},{7,6},{8,9},{9,8},{10,11... | collective-permute-start | bytes 393224 | tf_op jit(solution)/shard_map/ppermute | solution.py:381
  11.4 1.6 %collective-permute-start.2 = (bf16[2,16,2048]{2,1,0:T(8,128)(2,1)S(1)}, bf16[2,16,2048]{2,1,0:T(8,128)(2,1)S(1)}, u32[]{:S(2)}, u32[]{:S(2)}) collective-permute-start(bf16[2,16,2048]{2,1,0:T(8,128)(2,1)S(1)} %join.3.after.right_held), channel_id=1, source_target_pairs={{0,4},{4,0},{8,12},{12,8},{1,5},{5,1},{9,13},{13,9},{2,6},{6,2},{1... | collective-permute-start | bytes 393224 | tf_op jit(solution)/shard_map/ppermute | solution.py:381
  16.7 6.0 %collective-permute-start.4 = (bf16[2,256,128]{2,1,0:T(8,128)(2,1)S(1)}, bf16[2,256,128]{2,1,0:T(8,128)(2,1)S(1)}, u32[]{:S(2)}, u32[]{:S(2)}) collective-permute-start(bf16[2,256,128]{2,1,0:T(8,128)(2,1)S(1)} %get-tuple-element.49), channel_id=1, source_target_pairs={{0,1},{1,0},{2,3},{3,2},{4,5},{5,4},{6,7},{7,6},{8,9},{9,8},{10,11... | collective-permute-start | bytes 393224 | tf_op jit(solution)/shard_map/ppermute | solution.py:381
  22.1 3.3 %collective-permute-start.5 = (bf16[2,256,128]{2,1,0:T(8,128)(2,1)S(1)}, bf16[2,256,128]{2,1,0:T(8,128)(2,1)S(1)}, u32[]{:S(2)}, u32[]{:S(2)}) collective-permute-start(bf16[2,256,128]{2,1,0:T(8,128)(2,1)S(1)} %get-tuple-element.52), channel_id=1, source_target_pairs={{0,4},{4,0},{8,12},{12,8},{1,5},{5,1},{9,13},{13,9},{2,6},{6,2},{1... | collective-permute-start | bytes 393224 | tf_op jit(solution)/shard_map/ppermute | solution.py:381
  22.7 13.6 %collective-permute-start.9 = (bf16[1,256,128]{2,1,0:T(8,128)(2,1)S(1)}, bf16[1,256,128]{2,1,0:T(8,128)(2,1)S(1)}, u32[]{:S(2)}, u32[]{:S(2)}) collective-permute-start(bf16[1,256,128]{2,1,0:T(8,128)(2,1)S(1)} %get-tuple-element.63), channel_id=1, source_target_pairs={{0,2},{1,3},{2,0},{3,1},{4,6},{5,7},{6,4},{7,5},{8,10},{9,11},{10,... | collective-permute-start | bytes 196616 | tf_op jit(solution)/shard_map/ppermute | solution.py:381
  25.5 4.3 %collective-permute-start.6 = (bf16[1,256,128]{2,1,0:T(8,128)(2,1)S(1)}, bf16[1,256,128]{2,1,0:T(8,128)(2,1)S(1)}, u32[]{:S(2)}, u32[]{:S(2)}) collective-permute-start(bf16[1,256,128]{2,1,0:T(8,128)(2,1)S(1)} %get-tuple-element.55), channel_id=1, source_target_pairs={{0,8},{4,12},{8,0},{12,4},{1,9},{5,13},{9,1},{13,5},{2,10},{6,14},... | collective-permute-start | bytes 196616 | tf_op jit(solution)/shard_map/ppermute | solution.py:381
  29.3 6.2 %collective-permute-start.8 = (bf16[2,256,128]{2,1,0:T(8,128)(2,1)S(1)}, bf16[2,256,128]{2,1,0:T(8,128)(2,1)S(1)}, u32[]{:S(2)}, u32[]{:S(2)}) collective-permute-start(bf16[2,256,128]{2,1,0:T(8,128)(2,1)S(1)} %get-tuple-element.61), channel_id=1, source_target_pairs={{0,4},{4,0},{8,12},{12,8},{1,5},{5,1},{9,13},{13,9},{2,6},{6,2},{1... | collective-permute-start | bytes 393224 | tf_op jit(solution)/shard_map/ppermute | solution.py:381
  29.8 4.0 %collective-permute-start.7 = (bf16[2,64,128]{2,1,0:T(8,128)(2,1)S(1)}, bf16[2,64,128]{2,1,0:T(8,128)(2,1)S(1)}, u32[]{:S(2)}, u32[]{:S(2)}) collective-permute-start(bf16[2,64,128]{2,1,0:T(8,128)(2,1)S(1)} %get-tuple-element.59), channel_id=1, source_target_pairs={{0,1},{1,0},{2,3},{3,2},{4,5},{5,4},{6,7},{7,6},{8,9},{9,8},{10,11... | collective-permute-start | bytes 98312 | tf_op jit(solution)/shard_map/ppermute | solution.py:381
  33.8 4.7 %collective-permute-start.11 = (bf16[1,64,128]{2,1,0:T(8,128)(2,1)S(1)}, bf16[1,64,128]{2,1,0:T(8,128)(2,1)S(1)}, u32[]{:S(2)}, u32[]{:S(2)}) collective-permute-start(bf16[1,64,128]{2,1,0:T(8,128)(2,1)S(1)} %get-tuple-element.67), channel_id=1, source_target_pairs={{0,2},{1,3},{2,0},{3,1},{4,6},{5,7},{6,4},{7,5},{8,10},{9,11},{10,... | collective-permute-start | bytes 49160 | tf_op jit(solution)/shard_map/ppermute | solution.py:381
  35.6 4.3 %collective-permute-start.10 = (bf16[1,256,128]{2,1,0:T(8,128)(2,1)S(1)}, bf16[1,256,128]{2,1,0:T(8,128)(2,1)S(1)}, u32[]{:S(2)}, u32[]{:S(2)}) collective-permute-start(bf16[1,256,128]{2,1,0:T(8,128)(2,1)S(1)} %get-tuple-element.66), channel_id=1, source_target_pairs={{0,8},{4,12},{8,0},{12,4},{1,9},{5,13},{9,1},{13,5},{2,10},{6,14},... | collective-permute-start | bytes 196616 | tf_op jit(solution)/shard_map/ppermute | solution.py:381

commit v11 on v10

--- a/solution.py
+++ b/solution.py
@@ -157,7 +157,7 @@
     same = (source // chans == target // LANES) & (source % chans == target % chans)
     expand[...] = same.astype(F32).astype(BF16)
     rows = step_rows * tiles
-    pairs = step_rows * j_rows
+    deep_rows = 2 * step_rows if i_rows % (2 * step_rows) == 0 else step_rows
     group = lane_group((tiles, LANES), chans)
 
     for step in range(i_rows // step_rows):
@@ -185,11 +185,12 @@
                     y_ref[step * step_rows + first + k, :, a * LANES : (a + 1) * LANES] = part[
                         a * j_rows : (a + 1) * j_rows, k * LANES : (k + 1) * LANES
                     ]
-        block = slice(step * step_rows, (step + 1) * step_rows)
-        scaled_t = scaled_ref[block].reshape(pairs, LANES).T
-        y_flat = y_ref[block].reshape(pairs, blocks * LANES)
-        part = jnp.dot(scaled_t, y_flat, preferred_element_type=F32)
-        gwt[...] = gwt[...] + part if step else part
+        if (step + 1) * step_rows % deep_rows == 0:
+            block = slice((step + 1) * step_rows - deep_rows, (step + 1) * step_rows)
+            scaled_t = scaled_ref[block].reshape(deep_rows * j_rows, LANES).T
+            y_flat = y_ref[block].reshape(deep_rows * j_rows, blocks * LANES)
+            part = jnp.dot(scaled_t, y_flat, preferred_element_type=F32)
+            gwt[...] = gwt[...] + part if block.start else part
     for k in range(blocks):
         turned_tile = gwt[:, k * LANES : (k + 1) * LANES].T
         for q in range(groups):
@@ -336,17 +337,21 @@
 
 
 def pair_kernel(dims, *refs):
-    after, ri_ref, y_ref, wp_ref, inv_ref, early, keep_ref, held, came = refs[:9]
-    out_ref, gl_out, staged, whole, left, sems = refs[9:]
+    after, ri_ref, y_ref, wp_ref, inv_ref, early, keep_ref = refs[:7]
+    left_sums, weight_sums = refs[7:9], refs[9:11]
+    out_ref, gl_out, gw_out, staged, whole, left, weight, sems = refs[11:]
     begin = early.shape[0]
     copies = [pltpu.make_async_copy(early, out_ref.at[pl.ds(0, begin)], sems.at[0])]
     copies[0].start()
     own = left.shape[0]
     first = pl.multiple_of(lax.axis_index("col") * own, 8)
-    whole[...] = total_of(held, came)
+    whole[...] = total_of(*left_sums)
     write_rows(whole, ri_ref[pl.ds(first, own), :], keep_ref, left, whole.shape[0] // own)
+    weight[...] = total_of(*weight_sums)
     copies.append(pltpu.make_async_copy(left, gl_out, sems.at[1]))
+    copies.append(pltpu.make_async_copy(weight, gw_out, sems.at[2]))
     copies[1].start()
+    copies[2].start()
     for row in range(begin, dims[3], PIECE):
         pair_rows(dims, row, ri_ref, y_ref, wp_ref, inv_ref, staged, row - begin)
         copies.append(
@@ -361,20 +366,11 @@
         copy.wait()
 
 
-def final_kernel(after, rj_ref, keep_ref, *refs):
-    right, weight = refs[0:2], refs[2:4]
-    gr_out, gw_out, whole, rows, weight_rows, sems = refs[4:]
-    weight_rows[...] = total_of(*weight)
-    copies = [pltpu.make_async_copy(weight_rows, gw_out, sems.at[0])]
-    copies[0].start()
-    own = rows.shape[0]
+def final_kernel(after, rj_ref, keep_ref, held, came, gr_out, whole):
+    own = gr_out.shape[0]
     first = pl.multiple_of(lax.axis_index("row") * own, 8)
-    whole[...] = total_of(*right)
-    write_rows(whole, rj_ref[pl.ds(first, own), :], keep_ref, rows, whole.shape[0] // own)
-    copies.append(pltpu.make_async_copy(rows, gr_out, sems.at[1]))
-    copies[1].start()
-    for copy in copies:
-        copy.wait()
+    whole[...] = total_of(held, came)
+    write_rows(whole, rj_ref[pl.ds(first, own), :], keep_ref, gr_out, whole.shape[0] // own)
 
 
 def swap(array, axis, n, bit):
@@ -454,7 +450,7 @@
     tiles = width // LANES
     depth = groups * sequences
     inner = chans * chans
-    step_rows = 32
+    step_rows = 16
     steps = i_rows // step_rows
     early_steps = steps // 2
     dims = (chans, groups, blocks, i_rows, j_rows, step_rows, sequences)
@@ -549,9 +545,10 @@
         name="outer",
     )(gl_cut[0], i_keep, keep, scaled, rbig, *lefts)
 
-    gl_last = reduce(*gl_cut, "col", n_col, gw_cut[0])
-
-    right_steps = max(1, steps // 4)
+    gw_row = reduce(*gw_cut, "row", n_row, gw_cut[0])
+    gl_last = reduce(*gl_cut, "col", n_col, gw_row[0])
+
+    right_steps = steps // 2
     acc = pl.pallas_call(
         functools.partial(right_first_kernel, right_steps),
         in_specs=[hbm()] + vmem(1 + len(z)),
@@ -561,7 +558,12 @@
         cost_estimate=cost(16 * macs, 2**20),
         name="right_first",
     )(gl_last[0], diag, *z)
-    gw_row = reduce(*gw_cut, "row", n_row, acc)
+    gw_cut = small_call(
+        functools.partial(turn_kernel, n_col),
+        halves(inner // n_row, n_col),
+        "turn",
+        [pltpu.VMEM((inner // n_row, pair_width), F32)],
+    )(acc, *gw_row)
 
     gr_cut = pl.pallas_call(
         functools.partial(right_kernel, dims, n_row, right_steps),
@@ -576,13 +578,8 @@
         compiler_params=params(20),
         cost_estimate=cost(16 * macs, 2**20),
         name="right",
-    )(gw_row[0], diag, acc, *z)
-    gw_cut = small_call(
-        functools.partial(turn_kernel, n_col),
-        halves(inner // n_row, n_col),
-        "turn",
-        [pltpu.VMEM((inner // n_row, pair_width), F32)],
-    )(gr_cut[0], *gw_row)
+    )(gw_cut[0], diag, acc, *z)
+    gw_last = reduce(*gw_cut, "col", n_col, gr_cut[0])
 
     begin = i_rows // PIECE // 2 * PIECE
     early = pl.pallas_call(
@@ -593,47 +590,40 @@
         compiler_params=params(12),
         cost_estimate=cost(16 * macs, 2**20),
         name="pair_first",
-    )(gw_cut[0], i_keep, y, weight, inverse)
-    gw_last = reduce(*gw_cut, "col", n_col, early)
-    gr_last = reduce(*gr_cut, "row", n_row, gw_last[0])
-    pair_out, grad_left = pl.pallas_call(
+    )(gw_last[0], i_keep, y, weight, inverse)
+    gr_last = reduce(*gr_cut, "row", n_row, early)
+    owned = (inner // n_row // n_col, pair_width)
+    pair_out, grad_left, grad_weight = pl.pallas_call(
         functools.partial(pair_kernel, dims),
-        in_specs=[hbm()] + vmem(8),
-        out_specs=[hbm()] * 2,
+        in_specs=[hbm()] + vmem(10),
+        out_specs=[hbm()] * 3,
         out_shape=[
             jax.ShapeDtypeStruct(cotangent.shape, BF16),
             jax.ShapeDtypeStruct((own_left, width), F32),
+            jax.ShapeDtypeStruct(owned, F32),
         ],
         scratch_shapes=[
             pltpu.VMEM((i_rows - begin, j_rows, pair_width), BF16),
             pltpu.VMEM((own_left * tiles, LANES), F32),
             pltpu.VMEM((own_left, width), F32),
-            pltpu.SemaphoreType.DMA((2 + (i_rows - begin) // PIECE,)),
+            pltpu.VMEM(owned, F32),
+            pltpu.SemaphoreType.DMA((3 + (i_rows - begin) // PIECE,)),
         ],
         compiler_params=params(12),
         cost_estimate=cost(16 * macs, 2**20),
         name="pair",
-    )(gr_last[0], i_keep, y, weight, inverse, early, keep, *gl_last)
-
-    owned = (inner // n_row // n_col, pair_width)
-    grad_right, grad_weight = pl.pallas_call(
+    )(gr_last[0], i_keep, y, weight, inverse, early, keep, *gl_last, *gw_last)
+
+    grad_right = pl.pallas_call(
         final_kernel,
-        in_specs=[hbm()] + vmem(6),
-        out_specs=[hbm()] * 2,
-        out_shape=[
-            jax.ShapeDtypeStruct((own_right, width), F32),
-            jax.ShapeDtypeStruct(owned, F32),
-        ],
-        scratch_shapes=[
-            pltpu.VMEM((own_right * tiles, LANES), F32),
-            pltpu.VMEM((own_right, width), F32),
-            pltpu.VMEM(owned, F32),
-            pltpu.SemaphoreType.DMA((2,)),
-        ],
+        in_specs=[hbm()] + vmem(4),
+        out_specs=vmem()[0],
+        out_shape=jax.ShapeDtypeStruct((own_right, width), F32),
+        scratch_shapes=[pltpu.VMEM((own_right * tiles, LANES), F32)],
         compiler_params=params(4),
         cost_estimate=cost(1000, 1000),
         name="final_sums",
-    )(in_hbm(pair_out), j_keep, keep, *gr_last, *gw_last)
+    )(in_hbm(pair_out), j_keep, keep, *gr_last)
     return (pair_out, grad_left, grad_right, grad_weight)
 
 

time: 41 us -> 46 us (1.12)
  waiting for transfers between devices: 3.7 us -> 9.21 us
  starting transfers between devices: 14.8 us -> 13.9 us
  Pallas kernels: 21.5 us -> 22 us
    ppermute x12, waiting for transfers between devices: 3.7 us -> 9.21 us  [swap(): return lax.ppermute(array, axis, [(s, s ^ bit) for s in range(n)])]
    ppermute x12, starting transfers between devices: 14.8 us -> 13.9 us  [swap(): return lax.ppermute(array, axis, [(s, s ^ bit) for s in range(n)])]
  transfers between devices with their start and end apart: 12 -> 12, of which waited for: 5 -> 6; matrix products, arithmetic and copies ran while one was open for 0% -> 0% of each run, Pallas kernels for 51% -> 35%
where the time goes in v11:
time: 46 us; the launch traced here: 45.8 us
  Pallas kernels  22 us (48%)
  starting transfers between devices  13.9 us (30%)
  waiting for transfers between devices  9.21 us (20%)
  between operations  0.79 us (2%)
    ppermute x12, starting transfers between devices, swap(): return lax.ppermute(array, axis, [(s, s ^ bit) for s in range(n)])  13.9 us
    ppermute x12, waiting for transfers between devices, swap(): return lax.ppermute(array, axis, [(s, s ^ bit) for s in range(n)])  9.21 us
    pallas_call x1, Pallas kernels, shards(): pl.pallas_call(functools.partial(outer_kernel, dims, n_row, n_col), in_sp...  5.24 us
    pallas_call x1, Pallas kernels, shards(): pl.pallas_call(functools.partial(scale_kernel, dims), in_specs=[hbm()] *...  3.65 us
    pallas_call x1, Pallas kernels, shards(): pl.pallas_call(functools.partial(left_kernel, dims, n_col), in_specs=[hbm...  2.53 us
    pallas_call x1, Pallas kernels, shards(): pl.pallas_call(functools.partial(right_kernel, dims, n_row, right_steps),...  2.33 us
    pallas_call x1, Pallas kernels, shards(): pl.pallas_call(functools.partial(pair_kernel, dims), in_specs=[hbm()] + v...  2.05 us
    pallas_call x1, Pallas kernels, shards(): pl.pallas_call(functools.partial(inner_kernel, dims, early_steps), in_spe...  1.51 us
  transfers between devices with their start and end apart: 12, of which 6 were waited for; matrix products, arithmetic and copies ran while one was open for 0% of the time, Pallas kernels for 35%

profile of v11, /device:TPU:0, one launch (start us, length us, event | category | flops | bytes accessed | tf_op | source)
XLA Modules:
  0.0 45.8 jit_solution(16014596236436434612)
XLA Ops:
  0.6 4.1 %collective-permute-start = (bf16[1,16,2048]{2,1,0:T(8,128)(2,1)}, bf16[1,16,2048]{2,1,0:T(8,128)(2,1)S(1)}, u32[]{:S(2)}, u32[]{:S(2)}) collective-permute-start(bf16[1,16,2048]{2,1,0:T(8,128)(2,1)} %bitcast.4), channel_id=1, source_target_pairs={{0,2},{1,3},{2,0},{3,1},{4,6},{5,7},{6,4},{7,5},{8,10},{9,11},{10,... | collective-permute-start | bytes 196616 | tf_op jit(solution)/shard_map/ppermute | solution.py:377
  4.7 1.5 %collective-permute-start.1 = (bf16[1,16,2048]{2,1,0:T(8,128)(2,1)}, bf16[1,16,2048]{2,1,0:T(8,128)(2,1)S(1)}, u32[]{:S(2)}, u32[]{:S(2)}) collective-permute-start(bf16[1,16,2048]{2,1,0:T(8,128)(2,1)} %bitcast.5), channel_id=1, source_target_pairs={{0,8},{4,12},{8,0},{12,4},{1,9},{5,13},{9,1},{13,5},{2,10},{6,14},... | collective-permute-start | bytes 196616 | tf_op jit(solution)/shard_map/ppermute | solution.py:377
  6.2 3.6 %scale.1 = (bf16[64,64,128]{2,1,0:T(8,128)(2,1)S(1)}, f32[64,128]{1,0:T(8,128)S(1)}, bf16[1024,128]{1,0:T(8,128)(2,1)S(1)}, f32[1,2048]{1,0:T(1,128)S(1)}, f32[6...) custom-call(s32[1,256]{1,0:T(1,128)} %bitcast.6, ...), custom_call_target="tpu_custom_call" | custom-call | flops 1000 | bytes 1000 | tf_op jit(solution)/shard_map/scale/pallas_call | solution.py:463
  9.9 1.6 %collective-permute-start.3 = (bf16[2,16,2048]{2,1,0:T(8,128)(2,1)S(1)}, bf16[2,16,2048]{2,1,0:T(8,128)(2,1)S(1)}, u32[]{:S(2)}, u32[]{:S(2)}) collective-permute-start(bf16[2,16,2048]{2,1,0:T(8,128)(2,1)S(1)} %join.2.after.refs_5_), channel_id=1, source_target_pairs={{0,1},{1,0},{2,3},{3,2},{4,5},{5,4},{6,7},{7,6},{8,9},{9,8},{10,11... | collective-permute-start | bytes 393224 | tf_op jit(solution)/shard_map/ppermute | solution.py:377
  11.7 1.5 %inner.1.after.refs_1_ = bf16[2,512,2048]{2,1,0:T(8,128)(2,1)S(1)} custom-call(bf16[2,16,2048]{2,1,0:T(8,128)(2,1)S(1)} %join.3.after.right_held, bf16[64,64,128]{2,1,0:T(8,128)(2,1)S(1)} %get-tuple-element.38.scaled_ref.refs_3_, bf16[1024,128]{1,0:T(8,128)(2,1)S(1)} %get-tuple-element.39.wp_ref.refs_3_), custom_call_target="tpu_custom_call" | custom-call | flops 8589934592 | bytes 1048576 | tf_op jit(solution)/shard_map/inner/pallas_call | solution.py:495
  13.2 1.1 %right_rows.1 = (bf16[512,256]{1,0:T(8,128)(2,1)S(1)}, bf16[256,512]{1,0:T(8,128)(2,1)S(1)}) custom-call(bf16[2,512,2048]{2,1,0:T(8,128)(2,1)S(1)} %inner.1.after.refs_1_, f32[64,128]{1,0:T(8,128)S(1)} %get-tuple-element.40.rj_ref, f32[1,2048]{1,0:T(1,128)S(1)} %get-tuple-element.41.keep_ref.refs_2_.refs_6_, bf16[2,16,2048]{2,1,0:T(8,128)(2,1)S(1)} %join.3.after.right_held, ...), custom_call_target="tpu_custom_call" | custom-call | flops 8589934592 | bytes 1048576 | tf_op jit(solution)/shard_map/right_rows/pallas_call | solution.py:506
  14.3 2.5 %left.1 = (bf16[2,256,128]{2,1,0:T(8,128)(2,1)S(1)}, bf16[2,256,128]{2,1,0:T(8,128)(2,1)S(1)}) custom-call(bf16[512,256]{1,0:T(8,128)(2,1)S(1)} %get-tuple-element.42.after.refs_4_, bf16[256,512]{1,0:T(8,128)(2,1)S(1)} %get-tuple-element.43.rbt_ref, bf16[2,512,2048]{2,1,0:T(8,128)(2,1)S(1)} %get-tuple-element.44.refs_0_, ...), custom_call_target="tpu_custom_call" | custom-call | flops 8589934592 | bytes 1048576 | tf_op jit(solution)/shard_map/left/pallas_call | solution.py:517
  16.8 5.2 %outer.1 = (bf16[64,64,1024]{2,1,0:T(8,128)(2,1)S(1)}, bf16[4,256,2048]{2,1,0:T(8,128)(2,1)S(1)}, bf16[2,256,128]{2,1,0:T(8,128)(2,1)S(1)}, bf16[2,256,128]{2,1,0:T(8,128)(2,1)S(1)}) custom-call(bf16[2,256,128]{2,1,0:T(8,128)(2,1)S(1)} %get-tuple-element.45.refs_0_.held_ref, f32[64,128]{1,0:T(8,128)S(1)} %get-tuple-element.46.refs_1_.ri_ref, ...), custom_call_target="tpu_custom_call" | custom-call | flops 8589934592 | bytes 1048576 | tf_op jit(solution)/shard_map/outer/pallas_call | solution.py:527
  22.1 0.6 %collective-permute-start.4 = (bf16[2,256,128]{2,1,0:T(8,128)(2,1)S(1)}, bf16[2,256,128]{2,1,0:T(8,128)(2,1)S(1)}, u32[]{:S(2)}, u32[]{:S(2)}) collective-permute-start(bf16[2,256,128]{2,1,0:T(8,128)(2,1)S(1)} %get-tuple-element.48), channel_id=1, source_target_pairs={{0,4},{4,0},{8,12},{12,8},{1,5},{5,1},{9,13},{13,9},{2,6},{6,2},{1... | collective-permute-start | bytes 393224 | tf_op jit(solution)/shard_map/ppermute | solution.py:377
  23.1 0.5 %collective-permute-done.4.came_ref = bf16[2,256,128]{2,1,0:T(8,128)(2,1)S(1)} collective-permute-done((bf16[2,256,128]{2,1,0:T(8,128)(2,1)S(1)}, bf16[2,256,128]{2,1,0:T(8,128)(2,1)S(1)}, u32[]{:S(2)}, u32[]{:S(2)}) %collective-permute-start.4) | collective-permute-done | bytes 131104 | tf_op jit(solution)/shard_map/ppermute | solution.py:377
  23.7 4.5 %collective-permute-done.5.came_ref = bf16[2,256,128]{2,1,0:T(8,128)(2,1)S(1)} collective-permute-done((bf16[2,256,128]{2,1,0:T(8,128)(2,1)S(1)}, bf16[2,256,128]{2,1,0:T(8,128)(2,1)S(1)}, u32[]{:S(2)}, u32[]{:S(2)}) %collective-permute-start.5) | collective-permute-done | bytes 131104 | tf_op jit(solution)/shard_map/ppermute | solution.py:377
  28.1 1.1 %collective-permute-start.9 = (bf16[1,256,128]{2,1,0:T(8,128)(2,1)S(1)}, bf16[1,256,128]{2,1,0:T(8,128)(2,1)S(1)}, u32[]{:S(2)}, u32[]{:S(2)}) collective-permute-start(bf16[1,256,128]{2,1,0:T(8,128)(2,1)S(1)} %get-tuple-element.62), channel_id=1, source_target_pairs={{0,2},{1,3},{2,0},{3,1},{4,6},{5,7},{6,4},{7,5},{8,10},{9,11},{10,... | collective-permute-start | bytes 196616 | tf_op jit(solution)/shard_map/ppermute | solution.py:377
  29.3 1.5 %collective-permute-start.6 = (bf16[1,256,128]{2,1,0:T(8,128)(2,1)S(1)}, bf16[1,256,128]{2,1,0:T(8,128)(2,1)S(1)}, u32[]{:S(2)}, u32[]{:S(2)}) collective-permute-start(bf16[1,256,128]{2,1,0:T(8,128)(2,1)S(1)} %get-tuple-element.53), channel_id=1, source_target_pairs={{0,8},{4,12},{8,0},{12,4},{1,9},{5,13},{9,1},{13,5},{2,10},{6,14},... | collective-permute-start | bytes 196616 | tf_op jit(solution)/shard_map/ppermute | solution.py:377
  30.8 1.5 %right_first.1.after.acc_first = f32[256,512]{1,0:T(8,128)S(1)} custom-call(f32[1,256,128]{2,1,0:T(8,128)S(1)} %get-tuple-element.51.after.refs_7_, bf16[4,256,2048]{2,1,0:T(8,128)(2,1)S(1)} %get-tuple-element.52.diag_ref, bf16[2,512,2048]{2,1,0:T(8,128)(2,1)S(1)} %get-tuple-element.44.refs_0_, bf16[2,512,2048]{2,1,0:T(8,128)(2,1)S(1)} %inner.1.after.refs_1_), custom_call_target="tpu_custom_call" | custom-call | flops 8589934592 | bytes 1048576 | tf_op jit(solution)/shard_map/right_first/pallas_call | solution.py:552
  32.2 1.3 %collective-permute-done.6.came_ref = bf16[1,256,128]{2,1,0:T(8,128)(2,1)S(1)} collective-permute-done((bf16[1,256,128]{2,1,0:T(8,128)(2,1)S(1)}, bf16[1,256,128]{2,1,0:T(8,128)(2,1)S(1)}, u32[]{:S(2)}, u32[]{:S(2)}) %collective-permute-start.6) | collective-permute-done | bytes 65568 | tf_op jit(solution)/shard_map/ppermute | solution.py:377
  33.9 2.3 %right.1 = (bf16[2,256,128]{2,1,0:T(8,128)(2,1)S(1)}, bf16[2,256,128]{2,1,0:T(8,128)(2,1)S(1)}) custom-call(bf16[2,64,128]{2,1,0:T(8,128)(2,1)S(1)} %get-tuple-element.54.after.held_ref, bf16[4,256,2048]{2,1,0:T(8,128)(2,1)S(1)} %get-tuple-element.52.diag_ref, f32[256,512]{1,0:T(8,128)S(1)} %right_first.1.after.acc_first, ...), custom_call_target="tpu_custom_call" | custom-call | flops 8589934592 | bytes 1048576 | tf_op jit(solution)/shard_map/right/pallas_call | solution.py:568
  36.3 1.2 %collective-permute-done.7.came_ref = bf16[2,64,128]{2,1,0:T(8,128)(2,1)S(1)} collective-permute-done((bf16[2,64,128]{2,1,0:T(8,128)(2,1)S(1)}, bf16[2,64,128]{2,1,0:T(8,128)(2,1)S(1)}, u32[]{:S(2)}, u32[]{:S(2)}) %collective-permute-start.7) | collective-permute-done | bytes 32800 | tf_op jit(solution)/shard_map/ppermute | solution.py:377
  37.6 1.9 %collective-permute-start.10 = (bf16[1,64,128]{2,1,0:T(8,128)(2,1)S(1)}, bf16[1,64,128]{2,1,0:T(8,128)(2,1)S(1)}, u32[]{:S(2)}, u32[]{:S(2)}) collective-permute-start(bf16[1,64,128]{2,1,0:T(8,128)(2,1)S(1)} %get-tuple-element.63), channel_id=1, source_target_pairs={{0,2},{1,3},{2,0},{3,1},{4,6},{5,7},{6,4},{7,5},{8,10},{9,11},{10,... | collective-permute-start | bytes 49160 | tf_op jit(solution)/shard_map/ppermute | solution.py:377
  39.5 1.2 %pair_first.1.after.refs_5_ = bf16[32,64,128]{2,1,0:T(8,128)(2,1)S(1)} custom-call(f32[1,64,128]{2,1,0:T(8,128)S(1)} %get-tuple-element.57.after.refs_9_, f32[64,128]{1,0:T(8,128)S(1)} %get-tuple-element.46.refs_1_.ri_ref, bf16[64,64,1024]{2,1,0:T(8,128)(2,1)S(1)} %get-tuple-element.58.y_ref.refs_2_, bf16[1024,128]{1,0:T(8,128)(2,1)S(1)} %get-tuple-element.39.wp_ref.refs_3_, ...), custom_call_target="tpu_custom_call" | custom-call | flops 8589934592 | bytes 1048576 | tf_op jit(solution)/shard_map/pair_first/pallas_call | solution.py:585
  40.8 0.6 %collective-permute-start.11 = (bf16[1,256,128]{2,1,0:T(8,128)(2,1)S(1)}, bf16[1,256,128]{2,1,0:T(8,128)(2,1)S(1)}, u32[]{:S(2)}, u32[]{:S(2)}) collective-permute-start(bf16[1,256,128]{2,1,0:T(8,128)(2,1)S(1)} %get-tuple-element.66), channel_id=1, source_target_pairs={{0,8},{4,12},{8,0},{12,4},{1,9},{5,13},{9,1},{13,5},{2,10},{6,14},... | collective-permute-start | bytes 196616 | tf_op jit(solution)/shard_map/ppermute | solution.py:377
  41.4 1.0 %collective-permute-done.10.refs_10_ = bf16[1,64,128]{2,1,0:T(8,128)(2,1)S(1)} collective-permute-done((bf16[1,64,128]{2,1,0:T(8,128)(2,1)S(1)}, bf16[1,64,128]{2,1,0:T(8,128)(2,1)S(1)}, u32[]{:S(2)}, u32[]{:S(2)}) %collective-permute-start.10) | collective-permute-done | bytes 16416 | tf_op jit(solution)/shard_map/ppermute | solution.py:377
  42.4 2.0 %pair.1 = (bf16[64,64,128]{2,1,0:T(8,128)(2,1)}, f32[16,2048]{1,0:T(8,128)}, f32[64,128]{1,0:T(8,128)}) custom-call(f32[1,256,128]{2,1,0:T(8,128)S(1)} %get-tuple-element.61.refs_0_.held, f32[64,128]{1,0:T(8,128)S(1)} %get-tuple-element.46.refs_1_.ri_ref, bf16[64,64,1024]{2,1,0:T(8,128)(2,1)S(1)} %get-tuple-element.58.y_ref.refs_2_, ...), custom_call_target="tpu_custom_call" | custom-call | flops 8589934592 | bytes 1048576 | tf_op jit(solution)/shard_map/pair/pallas_call | solution.py:596
  44.5 0.7 %collective-permute-done.11.came = bf16[1,256,128]{2,1,0:T(8,128)(2,1)S(1)} collective-permute-done((bf16[1,256,128]{2,1,0:T(8,128)(2,1)S(1)}, bf16[1,256,128]{2,1,0:T(8,128)(2,1)S(1)}, u32[]{:S(2)}, u32[]{:S(2)}) %collective-permute-start.11) | collective-permute-done | bytes 65568 | tf_op jit(solution)/shard_map/ppermute | solution.py:377
  45.1 0.7 %final_sums.1 = f32[16,2048]{1,0:T(8,128)} custom-call(bf16[64,64,128]{2,1,0:T(8,128)(2,1)} %get-tuple-element.32.after, f32[64,128]{1,0:T(8,128)S(1)} %get-tuple-element.40.rj_ref, f32[1,2048]{1,0:T(1,128)S(1)} %get-tuple-element.41.keep_ref.refs_2_.refs_6_, f32[1,256,128]{2,1,0:T(8,128)S(1)} %get-tuple-element.61.refs_0_.held, ...), custom_call_target="tpu_custom_call" | custom-call | flops 1000 | bytes 1000 | tf_op jit(solution)/shard_map/final_sums/pallas_call | solution.py:617
  (17 shorter events, 1.1 us)
Async XLA Ops:
  0.6 9.3 %collective-permute-start = (bf16[1,16,2048]{2,1,0:T(8,128)(2,1)}, bf16[1,16,2048]{2,1,0:T(8,128)(2,1)S(1)}, u32[]{:S(2)}, u32[]{:S(2)}) collective-permute-start(bf16[1,16,2048]{2,1,0:T(8,128)(2,1)} %bitcast.4), channel_id=1, source_target_pairs={{0,2},{1,3},{2,0},{3,1},{4,6},{5,7},{6,4},{7,5},{8,10},{9,11},{10,... | collective-permute-start | bytes 196616 | tf_op jit(solution)/shard_map/ppermute | solution.py:377
  4.7 6.8 %collective-permute-start.1 = (bf16[1,16,2048]{2,1,0:T(8,128)(2,1)}, bf16[1,16,2048]{2,1,0:T(8,128)(2,1)S(1)}, u32[]{:S(2)}, u32[]{:S(2)}) collective-permute-start(bf16[1,16,2048]{2,1,0:T(8,128)(2,1)} %bitcast.5), channel_id=1, source_target_pairs={{0,8},{4,12},{8,0},{12,4},{1,9},{5,13},{9,1},{13,5},{2,10},{6,14},... | collective-permute-start | bytes 196616 | tf_op jit(solution)/shard_map/ppermute | solution.py:377
  9.9 6.9 %collective-permute-start.3 = (bf16[2,16,2048]{2,1,0:T(8,128)(2,1)S(1)}, bf16[2,16,2048]{2,1,0:T(8,128)(2,1)S(1)}, u32[]{:S(2)}, u32[]{:S(2)}) collective-permute-start(bf16[2,16,2048]{2,1,0:T(8,128)(2,1)S(1)} %join.2.after.refs_5_), channel_id=1, source_target_pairs={{0,1},{1,0},{2,3},{3,2},{4,5},{5,4},{6,7},{7,6},{8,9},{9,8},{10,11... | collective-permute-start | bytes 393224 | tf_op jit(solution)/shard_map/ppermute | solution.py:377
  11.6 1.6 %collective-permute-start.2 = (bf16[2,16,2048]{2,1,0:T(8,128)(2,1)S(1)}, bf16[2,16,2048]{2,1,0:T(8,128)(2,1)S(1)}, u32[]{:S(2)}, u32[]{:S(2)}) collective-permute-start(bf16[2,16,2048]{2,1,0:T(8,128)(2,1)S(1)} %join.3.after.right_held), channel_id=1, source_target_pairs={{0,4},{4,0},{8,12},{12,8},{1,5},{5,1},{9,13},{13,9},{2,6},{6,2},{1... | collective-permute-start | bytes 393224 | tf_op jit(solution)/shard_map/ppermute | solution.py:377
  22.1 1.6 %collective-permute-start.4 = (bf16[2,256,128]{2,1,0:T(8,128)(2,1)S(1)}, bf16[2,256,128]{2,1,0:T(8,128)(2,1)S(1)}, u32[]{:S(2)}, u32[]{:S(2)}) collective-permute-start(bf16[2,256,128]{2,1,0:T(8,128)(2,1)S(1)} %get-tuple-element.48), channel_id=1, source_target_pairs={{0,4},{4,0},{8,12},{12,8},{1,5},{5,1},{9,13},{13,9},{2,6},{6,2},{1... | collective-permute-start | bytes 393224 | tf_op jit(solution)/shard_map/ppermute | solution.py:377
  22.6 5.5 %collective-permute-start.5 = (bf16[2,256,128]{2,1,0:T(8,128)(2,1)S(1)}, bf16[2,256,128]{2,1,0:T(8,128)(2,1)S(1)}, u32[]{:S(2)}, u32[]{:S(2)}) collective-permute-start(bf16[2,256,128]{2,1,0:T(8,128)(2,1)S(1)} %get-tuple-element.50), channel_id=1, source_target_pairs={{0,1},{1,0},{2,3},{3,2},{4,5},{5,4},{6,7},{7,6},{8,9},{9,8},{10,11... | collective-permute-start | bytes 393224 | tf_op jit(solution)/shard_map/ppermute | solution.py:377
  28.1 13.2 %collective-permute-start.9 = (bf16[1,256,128]{2,1,0:T(8,128)(2,1)S(1)}, bf16[1,256,128]{2,1,0:T(8,128)(2,1)S(1)}, u32[]{:S(2)}, u32[]{:S(2)}) collective-permute-start(bf16[1,256,128]{2,1,0:T(8,128)(2,1)S(1)} %get-tuple-element.62), channel_id=1, source_target_pairs={{0,2},{1,3},{2,0},{3,1},{4,6},{5,7},{6,4},{7,5},{8,10},{9,11},{10,... | collective-permute-start | bytes 196616 | tf_op jit(solution)/shard_map/ppermute | solution.py:377
  29.3 4.3 %collective-permute-start.6 = (bf16[1,256,128]{2,1,0:T(8,128)(2,1)S(1)}, bf16[1,256,128]{2,1,0:T(8,128)(2,1)S(1)}, u32[]{:S(2)}, u32[]{:S(2)}) collective-permute-start(bf16[1,256,128]{2,1,0:T(8,128)(2,1)S(1)} %get-tuple-element.53), channel_id=1, source_target_pairs={{0,8},{4,12},{8,0},{12,4},{1,9},{5,13},{9,1},{13,5},{2,10},{6,14},... | collective-permute-start | bytes 196616 | tf_op jit(solution)/shard_map/ppermute | solution.py:377
  33.6 4.0 %collective-permute-start.7 = (bf16[2,64,128]{2,1,0:T(8,128)(2,1)S(1)}, bf16[2,64,128]{2,1,0:T(8,128)(2,1)S(1)}, u32[]{:S(2)}, u32[]{:S(2)}) collective-permute-start(bf16[2,64,128]{2,1,0:T(8,128)(2,1)S(1)} %get-tuple-element.56), channel_id=1, source_target_pairs={{0,1},{1,0},{2,3},{3,2},{4,5},{5,4},{6,7},{7,6},{8,9},{9,8},{10,11... | collective-permute-start | bytes 98312 | tf_op jit(solution)/shard_map/ppermute | solution.py:377
  36.2 4.5 %collective-permute-start.8 = (bf16[2,256,128]{2,1,0:T(8,128)(2,1)S(1)}, bf16[2,256,128]{2,1,0:T(8,128)(2,1)S(1)}, u32[]{:S(2)}, u32[]{:S(2)}) collective-permute-start(bf16[2,256,128]{2,1,0:T(8,128)(2,1)S(1)} %get-tuple-element.60), channel_id=1, source_target_pairs={{0,4},{4,0},{8,12},{12,8},{1,5},{5,1},{9,13},{13,9},{2,6},{6,2},{1... | collective-permute-start | bytes 393224 | tf_op jit(solution)/shard_map/ppermute | solution.py:377
  37.6 4.9 %collective-permute-start.10 = (bf16[1,64,128]{2,1,0:T(8,128)(2,1)S(1)}, bf16[1,64,128]{2,1,0:T(8,128)(2,1)S(1)}, u32[]{:S(2)}, u32[]{:S(2)}) collective-permute-start(bf16[1,64,128]{2,1,0:T(8,128)(2,1)S(1)} %get-tuple-element.63), channel_id=1, source_target_pairs={{0,2},{1,3},{2,0},{3,1},{4,6},{5,7},{6,4},{7,5},{8,10},{9,11},{10,... | collective-permute-start | bytes 49160 | tf_op jit(solution)/shard_map/ppermute | solution.py:377
  40.8 4.3 %collective-permute-start.11 = (bf16[1,256,128]{2,1,0:T(8,128)(2,1)S(1)}, bf16[1,256,128]{2,1,0:T(8,128)(2,1)S(1)}, u32[]{:S(2)}, u32[]{:S(2)}) collective-permute-start(bf16[1,256,128]{2,1,0:T(8,128)(2,1)S(1)} %get-tuple-element.66), channel_id=1, source_target_pairs={{0,8},{4,12},{8,0},{12,4},{1,9},{5,13},{9,1},{13,5},{2,10},{6,14},... | collective-permute-start | bytes 196616 | tf_op jit(solution)/shard_map/ppermute | solution.py:377

commit v12 on v10

--- a/solution.py
+++ b/solution.py
@@ -157,7 +157,7 @@
     same = (source // chans == target // LANES) & (source % chans == target % chans)
     expand[...] = same.astype(F32).astype(BF16)
     rows = step_rows * tiles
-    pairs = step_rows * j_rows
+    deep_rows = 2 * step_rows if i_rows % (2 * step_rows) == 0 else step_rows
     group = lane_group((tiles, LANES), chans)
 
     for step in range(i_rows // step_rows):
@@ -185,11 +185,12 @@
                     y_ref[step * step_rows + first + k, :, a * LANES : (a + 1) * LANES] = part[
                         a * j_rows : (a + 1) * j_rows, k * LANES : (k + 1) * LANES
                     ]
-        block = slice(step * step_rows, (step + 1) * step_rows)
-        scaled_t = scaled_ref[block].reshape(pairs, LANES).T
-        y_flat = y_ref[block].reshape(pairs, blocks * LANES)
-        part = jnp.dot(scaled_t, y_flat, preferred_element_type=F32)
-        gwt[...] = gwt[...] + part if step else part
+        if (step + 1) * step_rows % deep_rows == 0:
+            block = slice((step + 1) * step_rows - deep_rows, (step + 1) * step_rows)
+            scaled_t = scaled_ref[block].reshape(deep_rows * j_rows, LANES).T
+            y_flat = y_ref[block].reshape(deep_rows * j_rows, blocks * LANES)
+            part = jnp.dot(scaled_t, y_flat, preferred_element_type=F32)
+            gwt[...] = gwt[...] + part if block.start else part
     for k in range(blocks):
         turned_tile = gwt[:, k * LANES : (k + 1) * LANES].T
         for q in range(groups):
@@ -307,6 +308,12 @@
         into[k // 2] = total_of(held_ref, came_ref, k).astype(into.dtype)
 
 
+def copy_kernel(after, *refs):
+    count = len(refs) // 2
+    for source, to in zip(refs[:count], refs[count:]):
+        to[...] = source[...]
+
+
 def turn_kernel(n_col, after, held_ref, came_ref, keep_out, send_out, whole):
     whole[...] = total_of(held_ref, came_ref)
     cut(whole, lax.axis_index("col"), n_col, keep_out, send_out)
@@ -321,40 +328,25 @@
         )
 
 
-def pair_rows(dims, row, ri_ref, y_ref, wp_ref, inv_ref, out_ref, at):
-    j_rows = dims[4]
-    y_flat = y_ref[row : row + PIECE].reshape(PIECE * j_rows, y_ref.shape[2])
-    projected = jnp.dot(y_flat, wp_ref[...], preferred_element_type=F32)
-    for i in range(PIECE):
-        inverse = jnp.where(ri_ref[row + i : row + i + 1, :] > 0, inv_ref[...], 1.0)
-        out_ref[at + i] = (projected[i * j_rows : (i + 1) * j_rows] * inverse).astype(BF16)
-
-
-def pair_first_kernel(dims, after, ri_ref, y_ref, wp_ref, inv_ref, out_ref):
-    for row in range(0, out_ref.shape[0], PIECE):
-        pair_rows(dims, row, ri_ref, y_ref, wp_ref, inv_ref, out_ref, row)
-
-
 def pair_kernel(dims, *refs):
-    after, ri_ref, y_ref, wp_ref, inv_ref, early, keep_ref, held, came = refs[:9]
-    out_ref, gl_out, staged, whole, left, sems = refs[9:]
-    begin = early.shape[0]
-    copies = [pltpu.make_async_copy(early, out_ref.at[pl.ds(0, begin)], sems.at[0])]
-    copies[0].start()
+    after, ri_ref, y_ref, wp_ref, inv_ref, keep_ref, held, came = refs[:8]
+    out_ref, gl_out, staged, whole, left, sems = refs[8:]
+    i_rows, j_rows = dims[3:5]
     own = left.shape[0]
     first = pl.multiple_of(lax.axis_index("col") * own, 8)
     whole[...] = total_of(held, came)
     write_rows(whole, ri_ref[pl.ds(first, own), :], keep_ref, left, whole.shape[0] // own)
-    copies.append(pltpu.make_async_copy(left, gl_out, sems.at[1]))
-    copies[1].start()
-    for row in range(begin, dims[3], PIECE):
-        pair_rows(dims, row, ri_ref, y_ref, wp_ref, inv_ref, staged, row - begin)
+    copies = [pltpu.make_async_copy(left, gl_out, sems.at[0])]
+    copies[0].start()
+    for row in range(0, i_rows, PIECE):
+        y_flat = y_ref[row : row + PIECE].reshape(PIECE * j_rows, y_ref.shape[2])
+        projected = jnp.dot(y_flat, wp_ref[...], preferred_element_type=F32)
+        for i in range(PIECE):
+            inverse = jnp.where(ri_ref[row + i : row + i + 1, :] > 0, inv_ref[...], 1.0)
+            staged[row + i] = (projected[i * j_rows : (i + 1) * j_rows] * inverse).astype(BF16)
+        rows = pl.ds(row, PIECE)
         copies.append(
-            pltpu.make_async_copy(
-                staged.at[pl.ds(row - begin, PIECE)],
-                out_ref.at[pl.ds(row, PIECE)],
-                sems.at[len(copies)],
-            )
+            pltpu.make_async_copy(staged.at[rows], out_ref.at[rows], sems.at[len(copies)])
         )
         copies[-1].start()
     for copy in copies:
@@ -398,19 +390,24 @@
     return held, swap(sent, axis, n, 1)
 
 
-def reduce(keep, send, axis, n, after):
+def reduce(keep, send, axis, n, after, between=None):
     bit = 1
     while True:
         came = swap(send, axis, n, bit)
         bit *= 2
         if bit >= n:
+            if between is not None:
+                between(keep)
             return keep, came
         half = (keep.shape[0] // 2,) + keep.shape[1:]
         outs = [pltpu.VMEM(half, F32), pltpu.VMEM(half, BF16)]
         keep, send = small_call(fold_kernel, outs, "fold")(after, keep, came)
-
-
-def small_call(body, outs, name, scratch=()):
+        if between is not None:
+            gate, between = between(keep), None
+            keep, send = hold(gate, keep, send)
+
+
+def small_call(body, outs, name, scratch=(), flops=1000):
     def call(after, *operands):
         return pl.pallas_call(
             body,
@@ -419,11 +416,16 @@
             out_shape=outs,
             scratch_shapes=list(scratch),
             compiler_params=params(4),
-            cost_estimate=cost(1000, 1000),
+            cost_estimate=cost(flops, 1000),
             name=name,
         )(after, *operands)
 
     return call
+
+
+def hold(after, *arrays):
+    outs = [pltpu.VMEM(array.shape, array.dtype) for array in arrays]
+    return small_call(copy_kernel, outs, "hold", flops=10**10)(after, *arrays)
 
 
 def halves(rows, n):
@@ -454,7 +456,7 @@
     tiles = width // LANES
     depth = groups * sequences
     inner = chans * chans
-    step_rows = 32
+    step_rows = 16
     steps = i_rows // step_rows
     early_steps = steps // 2
     dims = (chans, groups, blocks, i_rows, j_rows, step_rows, sequences)
@@ -549,19 +551,30 @@
         name="outer",
     )(gl_cut[0], i_keep, keep, scaled, rbig, *lefts)
 
-    gl_last = reduce(*gl_cut, "col", n_col, gw_cut[0])
-
-    right_steps = max(1, steps // 4)
+    gw_row = []
+
+    def weight_rounds(after):
+        gw_row.extend(reduce(*gw_cut, "row", n_row, after))
+        return gw_row[0]
+
+    gl_last = reduce(*gl_cut, "col", n_col, gw_cut[0], weight_rounds)
+
+    right_steps = steps // 2
     acc = pl.pallas_call(
         functools.partial(right_first_kernel, right_steps),
         in_specs=[hbm()] + vmem(1 + len(z)),
         out_specs=vmem()[0],
         out_shape=pltpu.VMEM((depth, span), F32),
         compiler_params=params(16),
-        cost_estimate=cost(16 * macs, 2**20),
+        cost_estimate=cost(1000, 1000),
         name="right_first",
     )(gl_last[0], diag, *z)
-    gw_row = reduce(*gw_cut, "row", n_row, acc)
+    gw_turned = small_call(
+        functools.partial(turn_kernel, n_col),
+        halves(inner // n_row, n_col),
+        "turn",
+        [pltpu.VMEM((inner // n_row, pair_width), F32)],
+    )(acc, *gw_row)
 
     gr_cut = pl.pallas_call(
         functools.partial(right_kernel, dims, n_row, right_steps),
@@ -576,44 +589,34 @@
         compiler_params=params(20),
         cost_estimate=cost(16 * macs, 2**20),
         name="right",
-    )(gw_row[0], diag, acc, *z)
-    gw_cut = small_call(
-        functools.partial(turn_kernel, n_col),
-        halves(inner // n_row, n_col),
-        "turn",
-        [pltpu.VMEM((inner // n_row, pair_width), F32)],
-    )(gr_cut[0], *gw_row)
-
-    begin = i_rows // PIECE // 2 * PIECE
-    early = pl.pallas_call(
-        functools.partial(pair_first_kernel, dims),
-        in_specs=[hbm()] + vmem(4),
-        out_specs=vmem()[0],
-        out_shape=pltpu.VMEM((begin, j_rows, pair_width), BF16),
-        compiler_params=params(12),
-        cost_estimate=cost(16 * macs, 2**20),
-        name="pair_first",
-    )(gw_cut[0], i_keep, y, weight, inverse)
-    gw_last = reduce(*gw_cut, "col", n_col, early)
-    gr_last = reduce(*gr_cut, "row", n_row, gw_last[0])
+    )(gw_turned[0], diag, acc, *z)
+    gr_held = []
+
+    def right_rounds(after):
+        gr_held.extend(hold(after, *gr_cut))
+        return gr_held[0]
+
+    gw_last = reduce(*gw_turned, "col", n_col, gr_cut[0], right_rounds)
+    gr_last = reduce(*gr_held, "row", n_row, gw_last[0])
+
     pair_out, grad_left = pl.pallas_call(
         functools.partial(pair_kernel, dims),
-        in_specs=[hbm()] + vmem(8),
+        in_specs=[hbm()] + vmem(7),
         out_specs=[hbm()] * 2,
         out_shape=[
             jax.ShapeDtypeStruct(cotangent.shape, BF16),
             jax.ShapeDtypeStruct((own_left, width), F32),
         ],
         scratch_shapes=[
-            pltpu.VMEM((i_rows - begin, j_rows, pair_width), BF16),
+            pltpu.VMEM(cotangent.shape, BF16),
             pltpu.VMEM((own_left * tiles, LANES), F32),
             pltpu.VMEM((own_left, width), F32),
-            pltpu.SemaphoreType.DMA((2 + (i_rows - begin) // PIECE,)),
+            pltpu.SemaphoreType.DMA((1 + i_rows // PIECE,)),
         ],
         compiler_params=params(12),
         cost_estimate=cost(16 * macs, 2**20),
         name="pair",
-    )(gr_last[0], i_keep, y, weight, inverse, early, keep, *gl_last)
+    )(gr_last[0], i_keep, y, weight, inverse, keep, *gl_last)
 
     owned = (inner // n_row // n_col, pair_width)
     grad_right, grad_weight = pl.pallas_call(

time: 41 us -> 39.5 us (0.963)
  waiting for transfers between devices: 3.7 us -> 1.75 us
    ppermute x12, waiting for transfers between devices: 3.7 us -> 1.75 us  [swap(): return lax.ppermute(array, axis, [(s, s ^ bit) for s in range(n)])]
    pallas_call x1 -> x0, Pallas kernels: 1.25 us -> none  [shards(): pl.pallas_call(functools.partial(pair_first_kernel, dims), in_specs=[hbm(...]
    pallas_call x1, Pallas kernels: 2.02 us -> 3.15 us  [shards(): pl.pallas_call(functools.partial(pair_kernel, dims), in_specs=[hbm()] + v...]
  transfers between devices with their start and end apart: 12 -> 12, of which waited for: 5 -> 3; matrix products, arithmetic and copies ran while one was open for 0% -> 0% of each run, Pallas kernels for 51% -> 54%
where the time goes in v12:
time: 39.5 us; the launch traced here: 39.3 us
  Pallas kernels  21.9 us (55%)
  starting transfers between devices  14.7 us (37%)
  waiting for transfers between devices  1.75 us (4%)
  between operations  0.97 us (2%)
    ppermute x12, starting transfers between devices, swap(): return lax.ppermute(array, axis, [(s, s ^ bit) for s in range(n)])  14.7 us
    pallas_call x1, Pallas kernels, shards(): pl.pallas_call(functools.partial(outer_kernel, dims, n_row, n_col), in_sp...  5.24 us
    pallas_call x1, Pallas kernels, shards(): pl.pallas_call(functools.partial(scale_kernel, dims), in_specs=[hbm()] *...  3.66 us
    pallas_call x1, Pallas kernels, shards(): pl.pallas_call(functools.partial(pair_kernel, dims), in_specs=[hbm()] + v...  3.15 us
    pallas_call x1, Pallas kernels, shards(): pl.pallas_call(functools.partial(left_kernel, dims, n_col), in_specs=[hbm...  2.53 us
    pallas_call x1, Pallas kernels, shards(): pl.pallas_call(functools.partial(right_kernel, dims, n_row, right_steps),...  2.33 us
    ppermute x12, waiting for transfers between devices, swap(): return lax.ppermute(array, axis, [(s, s ^ bit) for s in range(n)])  1.75 us
    pallas_call x1, Pallas kernels, shards(): pl.pallas_call(functools.partial(inner_kernel, dims, early_steps), in_spe...  1.52 us
  transfers between devices with their start and end apart: 12, of which 3 were waited for; matrix products, arithmetic and copies ran while one was open for 0% of the time, Pallas kernels for 54%

profile of v12, /device:TPU:0, one launch (start us, length us, event | category | flops | bytes accessed | tf_op | source)
XLA Modules:
  0.0 39.3 jit_solution(5343458864790720412)
XLA Ops:
  0.6 4.1 %collective-permute-start = (bf16[1,16,2048]{2,1,0:T(8,128)(2,1)}, bf16[1,16,2048]{2,1,0:T(8,128)(2,1)S(1)}, u32[]{:S(2)}, u32[]{:S(2)}) collective-permute-start(bf16[1,16,2048]{2,1,0:T(8,128)(2,1)} %bitcast.4), channel_id=1, source_target_pairs={{0,2},{1,3},{2,0},{3,1},{4,6},{5,7},{6,4},{7,5},{8,10},{9,11},{10,... | collective-permute-start | bytes 196616 | tf_op jit(solution)/shard_map/ppermute | solution.py:373
  4.7 1.5 %collective-permute-start.1 = (bf16[1,16,2048]{2,1,0:T(8,128)(2,1)}, bf16[1,16,2048]{2,1,0:T(8,128)(2,1)S(1)}, u32[]{:S(2)}, u32[]{:S(2)}) collective-permute-start(bf16[1,16,2048]{2,1,0:T(8,128)(2,1)} %bitcast.5), channel_id=1, source_target_pairs={{0,8},{4,12},{8,0},{12,4},{1,9},{5,13},{9,1},{13,5},{2,10},{6,14},... | collective-permute-start | bytes 196616 | tf_op jit(solution)/shard_map/ppermute | solution.py:373
  6.2 3.7 %scale.1 = (bf16[64,64,128]{2,1,0:T(8,128)(2,1)S(1)}, f32[64,128]{1,0:T(8,128)S(1)}, bf16[1024,128]{1,0:T(8,128)(2,1)S(1)}, f32[1,2048]{1,0:T(1,128)S(1)}, f32[6...) custom-call(s32[1,256]{1,0:T(1,128)} %bitcast.6, ...), custom_call_target="tpu_custom_call" | custom-call | flops 1000 | bytes 1000 | tf_op jit(solution)/shard_map/scale/pallas_call | solution.py:469
  9.9 1.6 %collective-permute-start.3 = (bf16[2,16,2048]{2,1,0:T(8,128)(2,1)S(1)}, bf16[2,16,2048]{2,1,0:T(8,128)(2,1)S(1)}, u32[]{:S(2)}, u32[]{:S(2)}) collective-permute-start(bf16[2,16,2048]{2,1,0:T(8,128)(2,1)S(1)} %join.2.after.refs_5_), channel_id=1, source_target_pairs={{0,1},{1,0},{2,3},{3,2},{4,5},{5,4},{6,7},{7,6},{8,9},{9,8},{10,11... | collective-permute-start | bytes 393224 | tf_op jit(solution)/shard_map/ppermute | solution.py:373
  11.6 0.1 collective-permute-start.2
  11.7 1.5 %inner.1.after.refs_1_ = bf16[2,512,2048]{2,1,0:T(8,128)(2,1)S(1)} custom-call(bf16[2,16,2048]{2,1,0:T(8,128)(2,1)S(1)} %join.3.after.right_held, bf16[64,64,128]{2,1,0:T(8,128)(2,1)S(1)} %get-tuple-element.45.scaled_ref.refs_3_, bf16[1024,128]{1,0:T(8,128)(2,1)S(1)} %get-tuple-element.46.wp_ref.refs_3_), custom_call_target="tpu_custom_call" | custom-call | flops 8589934592 | bytes 1048576 | tf_op jit(solution)/shard_map/inner/pallas_call | solution.py:501
  13.2 1.1 %right_rows.1 = (bf16[512,256]{1,0:T(8,128)(2,1)S(1)}, bf16[256,512]{1,0:T(8,128)(2,1)S(1)}) custom-call(bf16[2,512,2048]{2,1,0:T(8,128)(2,1)S(1)} %inner.1.after.refs_1_, f32[64,128]{1,0:T(8,128)S(1)} %get-tuple-element.47.rj_ref, f32[1,2048]{1,0:T(1,128)S(1)} %get-tuple-element.48.keep_ref.refs_2_.refs_5_, bf16[2,16,2048]{2,1,0:T(8,128)(2,1)S(1)} %join.3.after.right_held, ...), custom_call_target="tpu_custom_call" | custom-call | flops 8589934592 | bytes 1048576 | tf_op jit(solution)/shard_map/right_rows/pallas_call | solution.py:512
  14.3 2.5 %left.1 = (bf16[2,256,128]{2,1,0:T(8,128)(2,1)S(1)}, bf16[2,256,128]{2,1,0:T(8,128)(2,1)S(1)}) custom-call(bf16[512,256]{1,0:T(8,128)(2,1)S(1)} %get-tuple-element.49.after.refs_4_, bf16[256,512]{1,0:T(8,128)(2,1)S(1)} %get-tuple-element.50.rbt_ref, bf16[2,512,2048]{2,1,0:T(8,128)(2,1)S(1)} %get-tuple-element.51.refs_0_, ...), custom_call_target="tpu_custom_call" | custom-call | flops 8589934592 | bytes 1048576 | tf_op jit(solution)/shard_map/left/pallas_call | solution.py:523
  16.8 0.5 %collective-permute-start.4 = (bf16[2,256,128]{2,1,0:T(8,128)(2,1)S(1)}, bf16[2,256,128]{2,1,0:T(8,128)(2,1)S(1)}, u32[]{:S(2)}, u32[]{:S(2)}) collective-permute-start(bf16[2,256,128]{2,1,0:T(8,128)(2,1)S(1)} %get-tuple-element.55), channel_id=1, source_target_pairs={{0,1},{1,0},{2,3},{3,2},{4,5},{5,4},{6,7},{7,6},{8,9},{9,8},{10,11... | collective-permute-start | bytes 393224 | tf_op jit(solution)/shard_map/ppermute | solution.py:373
  17.3 5.2 %outer.1 = (bf16[64,64,1024]{2,1,0:T(8,128)(2,1)S(1)}, bf16[4,256,2048]{2,1,0:T(8,128)(2,1)S(1)}, bf16[2,256,128]{2,1,0:T(8,128)(2,1)S(1)}, bf16[2,256,128]{2,1,0:T(8,128)(2,1)S(1)}) custom-call(bf16[2,256,128]{2,1,0:T(8,128)(2,1)S(1)} %get-tuple-element.52.refs_0_.held_ref, f32[64,128]{1,0:T(8,128)S(1)} %get-tuple-element.53.refs_1_, ...), custom_call_target="tpu_custom_call" | custom-call | flops 8589934592 | bytes 1048576 | tf_op jit(solution)/shard_map/outer/pallas_call | solution.py:533
  22.6 0.3 collective-permute-start.5
  22.9 1.1 %collective-permute-done.5.came_ref = bf16[2,256,128]{2,1,0:T(8,128)(2,1)S(1)} collective-permute-done((bf16[2,256,128]{2,1,0:T(8,128)(2,1)S(1)}, bf16[2,256,128]{2,1,0:T(8,128)(2,1)S(1)}, u32[]{:S(2)}, u32[]{:S(2)}) %collective-permute-start.5) | collective-permute-done | bytes 131104 | tf_op jit(solution)/shard_map/ppermute | solution.py:373
  24.0 0.6 %collective-permute-start.6 = (bf16[1,256,128]{2,1,0:T(8,128)(2,1)S(1)}, bf16[1,256,128]{2,1,0:T(8,128)(2,1)S(1)}, u32[]{:S(2)}, u32[]{:S(2)}) collective-permute-start(bf16[1,256,128]{2,1,0:T(8,128)(2,1)S(1)} %get-tuple-element.62), channel_id=1, source_target_pairs={{0,8},{4,12},{8,0},{12,4},{1,9},{5,13},{9,1},{13,5},{2,10},{6,14},... | collective-permute-start | bytes 196616 | tf_op jit(solution)/shard_map/ppermute | solution.py:373
  24.6 1.8 %collective-permute-start.9 = (bf16[1,256,128]{2,1,0:T(8,128)(2,1)S(1)}, bf16[1,256,128]{2,1,0:T(8,128)(2,1)S(1)}, u32[]{:S(2)}, u32[]{:S(2)}) collective-permute-start(bf16[1,256,128]{2,1,0:T(8,128)(2,1)S(1)} %get-tuple-element.75), channel_id=1, source_target_pairs={{0,2},{1,3},{2,0},{3,1},{4,6},{5,7},{6,4},{7,5},{8,10},{9,11},{10,... | collective-permute-start | bytes 196616 | tf_op jit(solution)/shard_map/ppermute | solution.py:373
  26.5 1.5 %right_first.1.after.acc_first = f32[256,512]{1,0:T(8,128)S(1)} custom-call(f32[1,256,128]{2,1,0:T(8,128)S(1)} %get-tuple-element.60.after.refs_6_, bf16[4,256,2048]{2,1,0:T(8,128)(2,1)S(1)} %get-tuple-element.61.diag_ref, bf16[2,512,2048]{2,1,0:T(8,128)(2,1)S(1)} %get-tuple-element.51.refs_0_, bf16[2,512,2048]{2,1,0:T(8,128)(2,1)S(1)} %inner.1.after.refs_1_), custom_call_target="tpu_custom_call" | custom-call | flops 1000 | bytes 1000 | tf_op jit(solution)/shard_map/right_first/pallas_call | solution.py:563
  27.9 0.4 %collective-permute-done.6.came_ref = bf16[1,256,128]{2,1,0:T(8,128)(2,1)S(1)} collective-permute-done((bf16[1,256,128]{2,1,0:T(8,128)(2,1)S(1)}, bf16[1,256,128]{2,1,0:T(8,128)(2,1)S(1)}, u32[]{:S(2)}, u32[]{:S(2)}) %collective-permute-start.6) | collective-permute-done | bytes 65568 | tf_op jit(solution)/shard_map/ppermute | solution.py:373
  28.4 1.6 %collective-permute-start.7 = (bf16[2,64,128]{2,1,0:T(8,128)(2,1)S(1)}, bf16[2,64,128]{2,1,0:T(8,128)(2,1)S(1)}, u32[]{:S(2)}, u32[]{:S(2)}) collective-permute-start(bf16[2,64,128]{2,1,0:T(8,128)(2,1)S(1)} %get-tuple-element.65), channel_id=1, source_target_pairs={{0,1},{1,0},{2,3},{3,2},{4,5},{5,4},{6,7},{7,6},{8,9},{9,8},{10,11... | collective-permute-start | bytes 98312 | tf_op jit(solution)/shard_map/ppermute | solution.py:373
  30.0 2.3 %right.1 = (bf16[2,256,128]{2,1,0:T(8,128)(2,1)S(1)}, bf16[2,256,128]{2,1,0:T(8,128)(2,1)S(1)}) custom-call(bf16[2,64,128]{2,1,0:T(8,128)(2,1)S(1)} %get-tuple-element.63.after.held_ref, bf16[4,256,2048]{2,1,0:T(8,128)(2,1)S(1)} %get-tuple-element.61.diag_ref, f32[256,512]{1,0:T(8,128)S(1)} %right_first.1.after.acc_first, ...), custom_call_target="tpu_custom_call" | custom-call | flops 8589934592 | bytes 1048576 | tf_op jit(solution)/shard_map/right/pallas_call | solution.py:579
  32.4 0.1 collective-permute-start.8
  32.5 1.1 %collective-permute-start.11 = (bf16[1,64,128]{2,1,0:T(8,128)(2,1)S(1)}, bf16[1,64,128]{2,1,0:T(8,128)(2,1)S(1)}, u32[]{:S(2)}, u32[]{:S(2)}) collective-permute-start(bf16[1,64,128]{2,1,0:T(8,128)(2,1)S(1)} %get-tuple-element.79), channel_id=1, source_target_pairs={{0,2},{1,3},{2,0},{3,1},{4,6},{5,7},{6,4},{7,5},{8,10},{9,11},{10,... | collective-permute-start | bytes 49160 | tf_op jit(solution)/shard_map/ppermute | solution.py:373
  33.6 0.2 collective-permute-done.8.came_ref
  33.9 1.4 %collective-permute-start.10 = (bf16[1,256,128]{2,1,0:T(8,128)(2,1)S(1)}, bf16[1,256,128]{2,1,0:T(8,128)(2,1)S(1)}, u32[]{:S(2)}, u32[]{:S(2)}) collective-permute-start(bf16[1,256,128]{2,1,0:T(8,128)(2,1)S(1)} %get-tuple-element.78), channel_id=1, source_target_pairs={{0,8},{4,12},{8,0},{12,4},{1,9},{5,13},{9,1},{13,5},{2,10},{6,14},... | collective-permute-start | bytes 196616 | tf_op jit(solution)/shard_map/ppermute | solution.py:373
  35.2 3.1 %pair.1 = (bf16[64,64,128]{2,1,0:T(8,128)(2,1)}, f32[16,2048]{1,0:T(8,128)}) custom-call(f32[1,256,128]{2,1,0:T(8,128)S(1)} %get-tuple-element.72.refs_0_, f32[64,128]{1,0:T(8,128)S(1)} %get-tuple-element.53.refs_1_, bf16[64,64,1024]{2,1,0:T(8,128)(2,1)S(1)} %get-tuple-element.73.refs_2_, bf16[1024,128]{1,0:T(8,128)(2,1)S(1)} %get-tuple-element.46.wp_ref.refs_3_, ...), custom_call_target="tpu_custom_call" | custom-call | flops 8589934592 | bytes 1048576 | tf_op jit(solution)/shard_map/pair/pallas_call | solution.py:602
  38.4 0.7 %final_sums.1 = (f32[16,2048]{1,0:T(8,128)}, f32[64,128]{1,0:T(8,128)}) custom-call(bf16[64,64,128]{2,1,0:T(8,128)(2,1)} %get-tuple-element.39.after, f32[64,128]{1,0:T(8,128)S(1)} %get-tuple-element.47.rj_ref, f32[1,2048]{1,0:T(1,128)S(1)} %get-tuple-element.48.keep_ref.refs_2_.refs_5_, f32[1,256,128]{2,1,0:T(8,128)S(1)} %get-tuple-element.72.refs_0_, ...), custom_call_target="tpu_custom_call" | custom-call | flops 1000 | bytes 1000 | tf_op jit(solution)/shard_map/final_sums/pallas_call | solution.py:622
  (19 shorter events, 0.2 us)
Async XLA Ops:
  0.6 9.3 %collective-permute-start = (bf16[1,16,2048]{2,1,0:T(8,128)(2,1)}, bf16[1,16,2048]{2,1,0:T(8,128)(2,1)S(1)}, u32[]{:S(2)}, u32[]{:S(2)}) collective-permute-start(bf16[1,16,2048]{2,1,0:T(8,128)(2,1)} %bitcast.4), channel_id=1, source_target_pairs={{0,2},{1,3},{2,0},{3,1},{4,6},{5,7},{6,4},{7,5},{8,10},{9,11},{10,... | collective-permute-start | bytes 196616 | tf_op jit(solution)/shard_map/ppermute | solution.py:373
  4.7 6.8 %collective-permute-start.1 = (bf16[1,16,2048]{2,1,0:T(8,128)(2,1)}, bf16[1,16,2048]{2,1,0:T(8,128)(2,1)S(1)}, u32[]{:S(2)}, u32[]{:S(2)}) collective-permute-start(bf16[1,16,2048]{2,1,0:T(8,128)(2,1)} %bitcast.5), channel_id=1, source_target_pairs={{0,8},{4,12},{8,0},{12,4},{1,9},{5,13},{9,1},{13,5},{2,10},{6,14},... | collective-permute-start | bytes 196616 | tf_op jit(solution)/shard_map/ppermute | solution.py:373
  9.9 7.4 %collective-permute-start.3 = (bf16[2,16,2048]{2,1,0:T(8,128)(2,1)S(1)}, bf16[2,16,2048]{2,1,0:T(8,128)(2,1)S(1)}, u32[]{:S(2)}, u32[]{:S(2)}) collective-permute-start(bf16[2,16,2048]{2,1,0:T(8,128)(2,1)S(1)} %join.2.after.refs_5_), channel_id=1, source_target_pairs={{0,1},{1,0},{2,3},{3,2},{4,5},{5,4},{6,7},{7,6},{8,9},{9,8},{10,11... | collective-permute-start | bytes 393224 | tf_op jit(solution)/shard_map/ppermute | solution.py:373
  11.6 1.6 %collective-permute-start.2 = (bf16[2,16,2048]{2,1,0:T(8,128)(2,1)S(1)}, bf16[2,16,2048]{2,1,0:T(8,128)(2,1)S(1)}, u32[]{:S(2)}, u32[]{:S(2)}) collective-permute-start(bf16[2,16,2048]{2,1,0:T(8,128)(2,1)S(1)} %join.3.after.right_held), channel_id=1, source_target_pairs={{0,4},{4,0},{8,12},{12,8},{1,5},{5,1},{9,13},{13,9},{2,6},{6,2},{1... | collective-permute-start | bytes 393224 | tf_op jit(solution)/shard_map/ppermute | solution.py:373
  16.8 6.1 %collective-permute-start.4 = (bf16[2,256,128]{2,1,0:T(8,128)(2,1)S(1)}, bf16[2,256,128]{2,1,0:T(8,128)(2,1)S(1)}, u32[]{:S(2)}, u32[]{:S(2)}) collective-permute-start(bf16[2,256,128]{2,1,0:T(8,128)(2,1)S(1)} %get-tuple-element.55), channel_id=1, source_target_pairs={{0,1},{1,0},{2,3},{3,2},{4,5},{5,4},{6,7},{7,6},{8,9},{9,8},{10,11... | collective-permute-start | bytes 393224 | tf_op jit(solution)/shard_map/ppermute | solution.py:373
  22.6 1.4 %collective-permute-start.5 = (bf16[2,256,128]{2,1,0:T(8,128)(2,1)S(1)}, bf16[2,256,128]{2,1,0:T(8,128)(2,1)S(1)}, u32[]{:S(2)}, u32[]{:S(2)}) collective-permute-start(bf16[2,256,128]{2,1,0:T(8,128)(2,1)S(1)} %get-tuple-element.57), channel_id=1, source_target_pairs={{0,4},{4,0},{8,12},{12,8},{1,5},{5,1},{9,13},{13,9},{2,6},{6,2},{1... | collective-permute-start | bytes 393224 | tf_op jit(solution)/shard_map/ppermute | solution.py:373
  24.0 4.3 %collective-permute-start.6 = (bf16[1,256,128]{2,1,0:T(8,128)(2,1)S(1)}, bf16[1,256,128]{2,1,0:T(8,128)(2,1)S(1)}, u32[]{:S(2)}, u32[]{:S(2)}) collective-permute-start(bf16[1,256,128]{2,1,0:T(8,128)(2,1)S(1)} %get-tuple-element.62), channel_id=1, source_target_pairs={{0,8},{4,12},{8,0},{12,4},{1,9},{5,13},{9,1},{13,5},{2,10},{6,14},... | collective-permute-start | bytes 196616 | tf_op jit(solution)/shard_map/ppermute | solution.py:373
  24.6 10.6 %collective-permute-start.9 = (bf16[1,256,128]{2,1,0:T(8,128)(2,1)S(1)}, bf16[1,256,128]{2,1,0:T(8,128)(2,1)S(1)}, u32[]{:S(2)}, u32[]{:S(2)}) collective-permute-start(bf16[1,256,128]{2,1,0:T(8,128)(2,1)S(1)} %get-tuple-element.75), channel_id=1, source_target_pairs={{0,2},{1,3},{2,0},{3,1},{4,6},{5,7},{6,4},{7,5},{8,10},{9,11},{10,... | collective-permute-start | bytes 196616 | tf_op jit(solution)/shard_map/ppermute | solution.py:373
  28.4 4.0 %collective-permute-start.7 = (bf16[2,64,128]{2,1,0:T(8,128)(2,1)S(1)}, bf16[2,64,128]{2,1,0:T(8,128)(2,1)S(1)}, u32[]{:S(2)}, u32[]{:S(2)}) collective-permute-start(bf16[2,64,128]{2,1,0:T(8,128)(2,1)S(1)} %get-tuple-element.65), channel_id=1, source_target_pairs={{0,1},{1,0},{2,3},{3,2},{4,5},{5,4},{6,7},{7,6},{8,9},{9,8},{10,11... | collective-permute-start | bytes 98312 | tf_op jit(solution)/shard_map/ppermute | solution.py:373
  32.4 1.4 %collective-permute-start.8 = (bf16[2,256,128]{2,1,0:T(8,128)(2,1)S(1)}, bf16[2,256,128]{2,1,0:T(8,128)(2,1)S(1)}, u32[]{:S(2)}, u32[]{:S(2)}) collective-permute-start(bf16[2,256,128]{2,1,0:T(8,128)(2,1)S(1)} %get-tuple-element.71), channel_id=1, source_target_pairs={{0,4},{4,0},{8,12},{12,8},{1,5},{5,1},{9,13},{13,9},{2,6},{6,2},{1... | collective-permute-start | bytes 393224 | tf_op jit(solution)/shard_map/ppermute | solution.py:373
  32.5 5.9 %collective-permute-start.11 = (bf16[1,64,128]{2,1,0:T(8,128)(2,1)S(1)}, bf16[1,64,128]{2,1,0:T(8,128)(2,1)S(1)}, u32[]{:S(2)}, u32[]{:S(2)}) collective-permute-start(bf16[1,64,128]{2,1,0:T(8,128)(2,1)S(1)} %get-tuple-element.79), channel_id=1, source_target_pairs={{0,2},{1,3},{2,0},{3,1},{4,6},{5,7},{6,4},{7,5},{8,10},{9,11},{10,... | collective-permute-start | bytes 49160 | tf_op jit(solution)/shard_map/ppermute | solution.py:373
  33.9 4.5 %collective-permute-start.10 = (bf16[1,256,128]{2,1,0:T(8,128)(2,1)S(1)}, bf16[1,256,128]{2,1,0:T(8,128)(2,1)S(1)}, u32[]{:S(2)}, u32[]{:S(2)}) collective-permute-start(bf16[1,256,128]{2,1,0:T(8,128)(2,1)S(1)} %get-tuple-element.78), channel_id=1, source_target_pairs={{0,8},{4,12},{8,0},{12,4},{1,9},{5,13},{9,1},{13,5},{2,10},{6,14},... | collective-permute-start | bytes 196616 | tf_op jit(solution)/shard_map/ppermute | solution.py:373

commit v13 on v12

--- a/solution.py
+++ b/solution.py
@@ -60,7 +60,7 @@
     steps = i_rows // step_rows
 
     def fetch(piece):
-        rows = pl.ds(piece * PIECE, PIECE)
+        rows = pl.ds(piece * step_rows, step_rows)
         return pltpu.make_async_copy(cot_ref.at[rows], cot.at[rows], sems.at[piece])
 
     pairs = [
@@ -75,7 +75,7 @@
     ]
     for copy in more[:3]:
         copy.start()
-    for piece in range(i_rows // PIECE):
+    for piece in range(i_rows // step_rows):
         fetch(piece).start()
     for copy in more[3:]:
         copy.start()
@@ -96,10 +96,10 @@
     w32[...] = w_ref[...].astype(F32)
     for e in range(chans):
         wp_ref[e * chans : (e + 1) * chans, :] = w32[pl.ds(e, chans, stride=chans), :].astype(BF16)
+    for piece in range(i_rows // step_rows):
+        fetch(piece).wait()
     for step in range(steps):
         for at in range(step * step_rows, (step + 1) * step_rows):
-            if at % PIECE == 0:
-                fetch(at // PIECE).wait()
             inverse = jnp.where(ri_ref[at : at + 1, :] > 0, inv_ref[...], 1.0)
             scaled_ref[at] = (cot[at].astype(F32) * inverse).astype(BF16)
         if step < z_ref.shape[0]:
@@ -156,24 +156,27 @@
     target = lax.broadcasted_iota(jnp.int32, shape, 1)
     same = (source // chans == target // LANES) & (source % chans == target % chans)
     expand[...] = same.astype(F32).astype(BF16)
-    rows = step_rows * tiles
+    group = lane_group((tiles, LANES), chans)
+    masks = [(group == b).astype(F32).astype(BF16) for b in range(groups)]
     deep_rows = 2 * step_rows if i_rows % (2 * step_rows) == 0 else step_rows
-    group = lane_group((tiles, LANES), chans)
 
     for step in range(i_rows // step_rows):
-        spread = jnp.dot(
-            lsplit[step * rows : (step + 1) * rows, :].astype(BF16),
-            expand[...],
-            preferred_element_type=F32,
-        ).astype(BF16)
-        for b in range(groups):
-            chosen = (group == b).astype(F32).astype(BF16)
-            for lo in range(groups):
-                at = b * sequences + lo * tiles
-                for i in range(step_rows):
-                    diag_ref[step, at : at + tiles, i * LANES : (i + 1) * LANES] = (
-                        spread[i * tiles : (i + 1) * tiles, lo * LANES : (lo + 1) * LANES] * chosen
-                    )
+        if step * step_rows % deep_rows == 0:
+            rows = slice(step * step_rows * tiles, (step * step_rows + deep_rows) * tiles)
+            spread = jnp.dot(
+                lsplit[rows, :].astype(BF16), expand[...], preferred_element_type=F32
+            ).astype(BF16)
+            for i in range(deep_rows):
+                block, at = divmod(step * step_rows + i, step_rows)
+                for b in range(groups):
+                    for lo in range(groups):
+                        first = b * sequences + lo * tiles
+                        diag_ref[
+                            block, first : first + tiles, at * LANES : (at + 1) * LANES
+                        ] = (
+                            spread[i * tiles : (i + 1) * tiles, lo * LANES : (lo + 1) * LANES]
+                            * masks[b]
+                        )
         for first in range(0, step_rows, CHUNK):
             part = jnp.dot(
                 rbig[...],
@@ -209,8 +212,8 @@
         so_far = acc
 
 
-def right_first_kernel(steps, after, diag_ref, *refs):
-    right_sum(0, steps, refs[:-1], diag_ref, refs[-1])
+def right_part_kernel(first, last, parts, after, diag_ref, *refs):
+    right_sum(first, last, refs[:parts], diag_ref, refs[-1], *refs[parts:-1])
 
 
 def right_kernel(dims, n_row, first, after, diag_ref, acc_first, *refs):
@@ -487,7 +490,7 @@
             pltpu.VMEM(out_weight.shape, BF16),
             pltpu.VMEM(out_weight.shape, F32),
             pltpu.VMEM(cotangent.shape, BF16),
-            pltpu.SemaphoreType.DMA((i_rows // PIECE,)),
+            pltpu.SemaphoreType.DMA((steps,)),
             pltpu.SemaphoreType.DMA((5,)),
         ],
         compiler_params=params(16),
@@ -551,24 +554,27 @@
         name="outer",
     )(gl_cut[0], i_keep, keep, scaled, rbig, *lefts)
 
-    gw_row = []
+    def right_part(first, last, after, *so_far):
+        return pl.pallas_call(
+            functools.partial(right_part_kernel, first, last, len(z)),
+            in_specs=[hbm()] + vmem(1 + len(z) + len(so_far)),
+            out_specs=vmem()[0],
+            out_shape=pltpu.VMEM((depth, span), F32),
+            compiler_params=params(16),
+            cost_estimate=cost(1000, 1000),
+            name="right_part",
+        )(after, diag, *z, *so_far)
+
+    gw_row, acc = [], []
+    right_steps = max(1, steps // 4)
 
     def weight_rounds(after):
-        gw_row.extend(reduce(*gw_cut, "row", n_row, after))
+        acc.append(right_part(0, right_steps, after))
+        gw_row.extend(reduce(*gw_cut, "row", n_row, acc[0]))
         return gw_row[0]
 
     gl_last = reduce(*gl_cut, "col", n_col, gw_cut[0], weight_rounds)
-
-    right_steps = steps // 2
-    acc = pl.pallas_call(
-        functools.partial(right_first_kernel, right_steps),
-        in_specs=[hbm()] + vmem(1 + len(z)),
-        out_specs=vmem()[0],
-        out_shape=pltpu.VMEM((depth, span), F32),
-        compiler_params=params(16),
-        cost_estimate=cost(1000, 1000),
-        name="right_first",
-    )(gl_last[0], diag, *z)
+    acc = right_part(right_steps, 2 * right_steps, gl_last[0], acc[0])
     gw_turned = small_call(
         functools.partial(turn_kernel, n_col),
         halves(inner // n_row, n_col),
@@ -577,7 +583,7 @@
     )(acc, *gw_row)
 
     gr_cut = pl.pallas_call(
-        functools.partial(right_kernel, dims, n_row, right_steps),
+        functools.partial(right_kernel, dims, n_row, 2 * right_steps),
         in_specs=[hbm()] + vmem(2 + len(z)),
         out_specs=vmem(2),
         out_shape=halves(j_rows * tiles, n_row),

time: 39.5 us -> 39.2 us (level)
  starting transfers between devices: 14.7 us -> 16.1 us
  waiting for transfers between devices: 1.75 us -> 0.8 us
  Pallas kernels: 21.9 us -> 21.1 us
    ppermute x12, starting transfers between devices: 14.7 us -> 16.1 us  [swap(): return lax.ppermute(array, axis, [(s, s ^ bit) for s in range(n)])]
    ppermute x12, waiting for transfers between devices: 1.75 us -> 0.8 us  [swap(): return lax.ppermute(array, axis, [(s, s ^ bit) for s in range(n)])]
    pallas_call x1, Pallas kernels: 3.66 us -> 3.02 us  [shards(): pl.pallas_call(functools.partial(scale_kernel, dims), in_specs=[hbm()] *...]
    pallas_call x2 -> x3, Pallas kernels: 3.79 us -> 3.99 us  [the longest x1 2.33 us: shards(): pl.pallas_call(functools.partial(right_kernel, dims, n_row, 2 * right_ste...]
  transfers between devices with their start and end apart: 12 -> 12, of which waited for: 3 -> 4; matrix products, arithmetic and copies ran while one was open for 0% -> 0% of each run, Pallas kernels for 54% -> 52%
where the time goes in v13:
time: 39.2 us; the launch traced here: 39 us
  Pallas kernels  21.1 us (54%)
  starting transfers between devices  16.1 us (41%)
  between operations  0.96 us (2%)
  waiting for transfers between devices  0.8 us (2%)
    ppermute x12, starting transfers between devices, swap(): return lax.ppermute(array, axis, [(s, s ^ bit) for s in range(n)])  16.1 us
    pallas_call x1, Pallas kernels, shards(): pl.pallas_call(functools.partial(outer_kernel, dims, n_row, n_col), in_sp...  4.94 us
    pallas_call x1, Pallas kernels, shards(): pl.pallas_call(functools.partial(pair_kernel, dims), in_specs=[hbm()] + v...  3.15 us
    pallas_call x1, Pallas kernels, shards(): pl.pallas_call(functools.partial(scale_kernel, dims), in_specs=[hbm()] *...  3.02 us
    pallas_call x1, Pallas kernels, shards(): pl.pallas_call(functools.partial(left_kernel, dims, n_col), in_specs=[hbm...  2.53 us
    pallas_call x1, Pallas kernels, shards(): pl.pallas_call(functools.partial(right_kernel, dims, n_row, 2 * right_ste...  2.33 us
    pallas_call x2, Pallas kernels, right_part(): pl.pallas_call(functools.partial(right_part_kernel, first, last, len(z)),...  1.66 us
    pallas_call x1, Pallas kernels, shards(): pl.pallas_call(functools.partial(inner_kernel, dims, early_steps), in_spe...  1.51 us
  transfers between devices with their start and end apart: 12, of which 4 were waited for; matrix products, arithmetic and copies ran while one was open for 0% of the time, Pallas kernels for 52%

profile of v13, /device:TPU:0, one launch (start us, length us, event | category | flops | bytes accessed | tf_op | source)
XLA Modules:
  0.0 39.0 jit_solution(10280254240328041301)
XLA Ops:
  0.6 4.1 %collective-permute-start = (bf16[1,16,2048]{2,1,0:T(8,128)(2,1)}, bf16[1,16,2048]{2,1,0:T(8,128)(2,1)S(1)}, u32[]{:S(2)}, u32[]{:S(2)}) collective-permute-start(bf16[1,16,2048]{2,1,0:T(8,128)(2,1)} %bitcast.4), channel_id=1, source_target_pairs={{0,2},{1,3},{2,0},{3,1},{4,6},{5,7},{6,4},{7,5},{8,10},{9,11},{10,... | collective-permute-start | bytes 196616 | tf_op jit(solution)/shard_map/ppermute | solution.py:376
  4.7 1.5 %collective-permute-start.1 = (bf16[1,16,2048]{2,1,0:T(8,128)(2,1)}, bf16[1,16,2048]{2,1,0:T(8,128)(2,1)S(1)}, u32[]{:S(2)}, u32[]{:S(2)}) collective-permute-start(bf16[1,16,2048]{2,1,0:T(8,128)(2,1)} %bitcast.5), channel_id=1, source_target_pairs={{0,8},{4,12},{8,0},{12,4},{1,9},{5,13},{9,1},{13,5},{2,10},{6,14},... | collective-permute-start | bytes 196616 | tf_op jit(solution)/shard_map/ppermute | solution.py:376
  6.2 3.0 %scale.1 = (bf16[64,64,128]{2,1,0:T(8,128)(2,1)S(1)}, f32[64,128]{1,0:T(8,128)S(1)}, bf16[1024,128]{1,0:T(8,128)(2,1)S(1)}, f32[1,2048]{1,0:T(1,128)S(1)}, f32[6...) custom-call(s32[1,256]{1,0:T(1,128)} %bitcast.6, ...), custom_call_target="tpu_custom_call" | custom-call | flops 1000 | bytes 1000 | tf_op jit(solution)/shard_map/scale/pallas_call | solution.py:472
  9.3 1.6 %collective-permute-start.3 = (bf16[2,16,2048]{2,1,0:T(8,128)(2,1)S(1)}, bf16[2,16,2048]{2,1,0:T(8,128)(2,1)S(1)}, u32[]{:S(2)}, u32[]{:S(2)}) collective-permute-start(bf16[2,16,2048]{2,1,0:T(8,128)(2,1)S(1)} %join.2.after.refs_5_), channel_id=1, source_target_pairs={{0,1},{1,0},{2,3},{3,2},{4,5},{5,4},{6,7},{7,6},{8,9},{9,8},{10,11... | collective-permute-start | bytes 393224 | tf_op jit(solution)/shard_map/ppermute | solution.py:376
  11.0 1.5 %inner.1.after.refs_1_ = bf16[2,512,2048]{2,1,0:T(8,128)(2,1)S(1)} custom-call(bf16[2,16,2048]{2,1,0:T(8,128)(2,1)S(1)} %join.3.after.right_held, bf16[64,64,128]{2,1,0:T(8,128)(2,1)S(1)} %get-tuple-element.45.scaled_ref.refs_3_, bf16[1024,128]{1,0:T(8,128)(2,1)S(1)} %get-tuple-element.46.wp_ref.refs_3_), custom_call_target="tpu_custom_call" | custom-call | flops 8589934592 | bytes 1048576 | tf_op jit(solution)/shard_map/inner/pallas_call | solution.py:504
  12.6 1.1 %right_rows.1 = (bf16[512,256]{1,0:T(8,128)(2,1)S(1)}, bf16[256,512]{1,0:T(8,128)(2,1)S(1)}) custom-call(bf16[2,512,2048]{2,1,0:T(8,128)(2,1)S(1)} %inner.1.after.refs_1_, f32[64,128]{1,0:T(8,128)S(1)} %get-tuple-element.47.rj_ref, f32[1,2048]{1,0:T(1,128)S(1)} %get-tuple-element.48.keep_ref.refs_2_.refs_5_, bf16[2,16,2048]{2,1,0:T(8,128)(2,1)S(1)} %join.3.after.right_held, ...), custom_call_target="tpu_custom_call" | custom-call | flops 8589934592 | bytes 1048576 | tf_op jit(solution)/shard_map/right_rows/pallas_call | solution.py:515
  13.6 2.5 %left.1 = (bf16[2,256,128]{2,1,0:T(8,128)(2,1)S(1)}, bf16[2,256,128]{2,1,0:T(8,128)(2,1)S(1)}) custom-call(bf16[512,256]{1,0:T(8,128)(2,1)S(1)} %get-tuple-element.49.after.refs_4_, bf16[256,512]{1,0:T(8,128)(2,1)S(1)} %get-tuple-element.50.rbt_ref, bf16[2,512,2048]{2,1,0:T(8,128)(2,1)S(1)} %get-tuple-element.51.refs_0_, ...), custom_call_target="tpu_custom_call" | custom-call | flops 8589934592 | bytes 1048576 | tf_op jit(solution)/shard_map/left/pallas_call | solution.py:526
  16.2 0.5 %collective-permute-start.4 = (bf16[2,256,128]{2,1,0:T(8,128)(2,1)S(1)}, bf16[2,256,128]{2,1,0:T(8,128)(2,1)S(1)}, u32[]{:S(2)}, u32[]{:S(2)}) collective-permute-start(bf16[2,256,128]{2,1,0:T(8,128)(2,1)S(1)} %get-tuple-element.55), channel_id=1, source_target_pairs={{0,1},{1,0},{2,3},{3,2},{4,5},{5,4},{6,7},{7,6},{8,9},{9,8},{10,11... | collective-permute-start | bytes 393224 | tf_op jit(solution)/shard_map/ppermute | solution.py:376
  16.7 4.9 %outer.1 = (bf16[64,64,1024]{2,1,0:T(8,128)(2,1)S(1)}, bf16[4,256,2048]{2,1,0:T(8,128)(2,1)S(1)}, bf16[2,256,128]{2,1,0:T(8,128)(2,1)S(1)}, bf16[2,256,128]{2,1,0:T(8,128)(2,1)S(1)}) custom-call(bf16[2,256,128]{2,1,0:T(8,128)(2,1)S(1)} %get-tuple-element.52.refs_0_.held_ref, f32[64,128]{1,0:T(8,128)S(1)} %get-tuple-element.53.refs_1_, ...), custom_call_target="tpu_custom_call" | custom-call | flops 8589934592 | bytes 1048576 | tf_op jit(solution)/shard_map/outer/pallas_call | solution.py:536
  21.6 0.3 collective-permute-start.5
  21.9 0.2 collective-permute-done.4.came_ref
  22.2 0.7 %right_part.2.after.refs_2_ = f32[256,512]{1,0:T(8,128)S(1)} custom-call(f32[1,256,128]{2,1,0:T(8,128)S(1)} %get-tuple-element.56.after.refs_0_, bf16[4,256,2048]{2,1,0:T(8,128)(2,1)S(1)} %get-tuple-element.57.diag_ref, bf16[2,512,2048]{2,1,0:T(8,128)(2,1)S(1)} %get-tuple-element.51.refs_0_, bf16[2,512,2048]{2,1,0:T(8,128)(2,1)S(1)} %inner.1.after.refs_1_), custom_call_target="tpu_custom_call" | custom-call | flops 1000 | bytes 1000 | tf_op jit(solution)/shard_map/right_part/pallas_call | solution.py:558
  22.9 0.1 collective-permute-done.5.came_ref
  23.1 1.1 %collective-permute-start.6 = (bf16[1,256,128]{2,1,0:T(8,128)(2,1)S(1)}, bf16[1,256,128]{2,1,0:T(8,128)(2,1)S(1)}, u32[]{:S(2)}, u32[]{:S(2)}) collective-permute-start(bf16[1,256,128]{2,1,0:T(8,128)(2,1)S(1)} %get-tuple-element.62), channel_id=1, source_target_pairs={{0,8},{4,12},{8,0},{12,4},{1,9},{5,13},{9,1},{13,5},{2,10},{6,14},... | collective-permute-start | bytes 196616 | tf_op jit(solution)/shard_map/ppermute | solution.py:376
  24.2 0.9 %right_part.3.after.acc_first = f32[256,512]{1,0:T(8,128)S(1)} custom-call(f32[1,256,128]{2,1,0:T(8,128)S(1)} %get-tuple-element.61.after.refs_6_, bf16[4,256,2048]{2,1,0:T(8,128)(2,1)S(1)} %get-tuple-element.57.diag_ref, bf16[2,512,2048]{2,1,0:T(8,128)(2,1)S(1)} %get-tuple-element.51.refs_0_, bf16[2,512,2048]{2,1,0:T(8,128)(2,1)S(1)} %inner.1.after.refs_1_, ...), custom_call_target="tpu_custom_call" | custom-call | flops 1000 | bytes 1000 | tf_op jit(solution)/shard_map/right_part/pallas_call | solution.py:558
  25.1 2.1 %collective-permute-start.9 = (bf16[1,256,128]{2,1,0:T(8,128)(2,1)S(1)}, bf16[1,256,128]{2,1,0:T(8,128)(2,1)S(1)}, u32[]{:S(2)}, u32[]{:S(2)}) collective-permute-start(bf16[1,256,128]{2,1,0:T(8,128)(2,1)S(1)} %get-tuple-element.75), channel_id=1, source_target_pairs={{0,2},{1,3},{2,0},{3,1},{4,6},{5,7},{6,4},{7,5},{8,10},{9,11},{10,... | collective-permute-start | bytes 196616 | tf_op jit(solution)/shard_map/ppermute | solution.py:376
  27.2 0.2 collective-permute-done.6.came_ref
  27.4 1.6 %collective-permute-start.7 = (bf16[2,64,128]{2,1,0:T(8,128)(2,1)S(1)}, bf16[2,64,128]{2,1,0:T(8,128)(2,1)S(1)}, u32[]{:S(2)}, u32[]{:S(2)}) collective-permute-start(bf16[2,64,128]{2,1,0:T(8,128)(2,1)S(1)} %get-tuple-element.65), channel_id=1, source_target_pairs={{0,1},{1,0},{2,3},{3,2},{4,5},{5,4},{6,7},{7,6},{8,9},{9,8},{10,11... | collective-permute-start | bytes 98312 | tf_op jit(solution)/shard_map/ppermute | solution.py:376
  29.1 2.3 %right.1 = (bf16[2,256,128]{2,1,0:T(8,128)(2,1)S(1)}, bf16[2,256,128]{2,1,0:T(8,128)(2,1)S(1)}) custom-call(bf16[2,64,128]{2,1,0:T(8,128)(2,1)S(1)} %get-tuple-element.63.after.held_ref, bf16[4,256,2048]{2,1,0:T(8,128)(2,1)S(1)} %get-tuple-element.57.diag_ref, f32[256,512]{1,0:T(8,128)S(1)} %right_part.3.after.acc_first, ...), custom_call_target="tpu_custom_call" | custom-call | flops 8589934592 | bytes 1048576 | tf_op jit(solution)/shard_map/right/pallas_call | solution.py:585
  31.4 0.2 collective-permute-done.7.came_ref
  31.8 1.5 %collective-permute-start.11 = (bf16[1,64,128]{2,1,0:T(8,128)(2,1)S(1)}, bf16[1,64,128]{2,1,0:T(8,128)(2,1)S(1)}, u32[]{:S(2)}, u32[]{:S(2)}) collective-permute-start(bf16[1,64,128]{2,1,0:T(8,128)(2,1)S(1)} %get-tuple-element.79), channel_id=1, source_target_pairs={{0,2},{1,3},{2,0},{3,1},{4,6},{5,7},{6,4},{7,5},{8,10},{9,11},{10,... | collective-permute-start | bytes 49160 | tf_op jit(solution)/shard_map/ppermute | solution.py:376
  33.4 1.6 %collective-permute-start.10 = (bf16[1,256,128]{2,1,0:T(8,128)(2,1)S(1)}, bf16[1,256,128]{2,1,0:T(8,128)(2,1)S(1)}, u32[]{:S(2)}, u32[]{:S(2)}) collective-permute-start(bf16[1,256,128]{2,1,0:T(8,128)(2,1)S(1)} %get-tuple-element.78), channel_id=1, source_target_pairs={{0,8},{4,12},{8,0},{12,4},{1,9},{5,13},{9,1},{13,5},{2,10},{6,14},... | collective-permute-start | bytes 196616 | tf_op jit(solution)/shard_map/ppermute | solution.py:376
  34.9 3.2 %pair.1 = (bf16[64,64,128]{2,1,0:T(8,128)(2,1)}, f32[16,2048]{1,0:T(8,128)}) custom-call(f32[1,256,128]{2,1,0:T(8,128)S(1)} %get-tuple-element.72.refs_0_, f32[64,128]{1,0:T(8,128)S(1)} %get-tuple-element.53.refs_1_, bf16[64,64,1024]{2,1,0:T(8,128)(2,1)S(1)} %get-tuple-element.73.refs_2_, bf16[1024,128]{1,0:T(8,128)(2,1)S(1)} %get-tuple-element.46.wp_ref.refs_3_, ...), custom_call_target="tpu_custom_call" | custom-call | flops 8589934592 | bytes 1048576 | tf_op jit(solution)/shard_map/pair/pallas_call | solution.py:608
  38.1 0.7 %final_sums.1 = (f32[16,2048]{1,0:T(8,128)}, f32[64,128]{1,0:T(8,128)}) custom-call(bf16[64,64,128]{2,1,0:T(8,128)(2,1)} %get-tuple-element.39.after, f32[64,128]{1,0:T(8,128)S(1)} %get-tuple-element.47.rj_ref, f32[1,2048]{1,0:T(1,128)S(1)} %get-tuple-element.48.keep_ref.refs_2_.refs_5_, f32[1,256,128]{2,1,0:T(8,128)S(1)} %get-tuple-element.72.refs_0_, ...), custom_call_target="tpu_custom_call" | custom-call | flops 1000 | bytes 1000 | tf_op jit(solution)/shard_map/final_sums/pallas_call | solution.py:628
  (20 shorter events, 0.4 us)
Async XLA Ops:
  0.6 8.6 %collective-permute-start = (bf16[1,16,2048]{2,1,0:T(8,128)(2,1)}, bf16[1,16,2048]{2,1,0:T(8,128)(2,1)S(1)}, u32[]{:S(2)}, u32[]{:S(2)}) collective-permute-start(bf16[1,16,2048]{2,1,0:T(8,128)(2,1)} %bitcast.4), channel_id=1, source_target_pairs={{0,2},{1,3},{2,0},{3,1},{4,6},{5,7},{6,4},{7,5},{8,10},{9,11},{10,... | collective-permute-start | bytes 196616 | tf_op jit(solution)/shard_map/ppermute | solution.py:376
  4.7 6.2 %collective-permute-start.1 = (bf16[1,16,2048]{2,1,0:T(8,128)(2,1)}, bf16[1,16,2048]{2,1,0:T(8,128)(2,1)S(1)}, u32[]{:S(2)}, u32[]{:S(2)}) collective-permute-start(bf16[1,16,2048]{2,1,0:T(8,128)(2,1)} %bitcast.5), channel_id=1, source_target_pairs={{0,8},{4,12},{8,0},{12,4},{1,9},{5,13},{9,1},{13,5},{2,10},{6,14},... | collective-permute-start | bytes 196616 | tf_op jit(solution)/shard_map/ppermute | solution.py:376
  9.3 7.4 %collective-permute-start.3 = (bf16[2,16,2048]{2,1,0:T(8,128)(2,1)S(1)}, bf16[2,16,2048]{2,1,0:T(8,128)(2,1)S(1)}, u32[]{:S(2)}, u32[]{:S(2)}) collective-permute-start(bf16[2,16,2048]{2,1,0:T(8,128)(2,1)S(1)} %join.2.after.refs_5_), channel_id=1, source_target_pairs={{0,1},{1,0},{2,3},{3,2},{4,5},{5,4},{6,7},{7,6},{8,9},{9,8},{10,11... | collective-permute-start | bytes 393224 | tf_op jit(solution)/shard_map/ppermute | solution.py:376
  10.9 1.6 %collective-permute-start.2 = (bf16[2,16,2048]{2,1,0:T(8,128)(2,1)S(1)}, bf16[2,16,2048]{2,1,0:T(8,128)(2,1)S(1)}, u32[]{:S(2)}, u32[]{:S(2)}) collective-permute-start(bf16[2,16,2048]{2,1,0:T(8,128)(2,1)S(1)} %join.3.after.right_held), channel_id=1, source_target_pairs={{0,4},{4,0},{8,12},{12,8},{1,5},{5,1},{9,13},{13,9},{2,6},{6,2},{1... | collective-permute-start | bytes 393224 | tf_op jit(solution)/shard_map/ppermute | solution.py:376
  16.2 6.0 %collective-permute-start.4 = (bf16[2,256,128]{2,1,0:T(8,128)(2,1)S(1)}, bf16[2,256,128]{2,1,0:T(8,128)(2,1)S(1)}, u32[]{:S(2)}, u32[]{:S(2)}) collective-permute-start(bf16[2,256,128]{2,1,0:T(8,128)(2,1)S(1)} %get-tuple-element.55), channel_id=1, source_target_pairs={{0,1},{1,0},{2,3},{3,2},{4,5},{5,4},{6,7},{7,6},{8,9},{9,8},{10,11... | collective-permute-start | bytes 393224 | tf_op jit(solution)/shard_map/ppermute | solution.py:376
  21.6 1.4 %collective-permute-start.5 = (bf16[2,256,128]{2,1,0:T(8,128)(2,1)S(1)}, bf16[2,256,128]{2,1,0:T(8,128)(2,1)S(1)}, u32[]{:S(2)}, u32[]{:S(2)}) collective-permute-start(bf16[2,256,128]{2,1,0:T(8,128)(2,1)S(1)} %get-tuple-element.58), channel_id=1, source_target_pairs={{0,4},{4,0},{8,12},{12,8},{1,5},{5,1},{9,13},{13,9},{2,6},{6,2},{1... | collective-permute-start | bytes 393224 | tf_op jit(solution)/shard_map/ppermute | solution.py:376
  23.1 4.3 %collective-permute-start.6 = (bf16[1,256,128]{2,1,0:T(8,128)(2,1)S(1)}, bf16[1,256,128]{2,1,0:T(8,128)(2,1)S(1)}, u32[]{:S(2)}, u32[]{:S(2)}) collective-permute-start(bf16[1,256,128]{2,1,0:T(8,128)(2,1)S(1)} %get-tuple-element.62), channel_id=1, source_target_pairs={{0,8},{4,12},{8,0},{12,4},{1,9},{5,13},{9,1},{13,5},{2,10},{6,14},... | collective-permute-start | bytes 196616 | tf_op jit(solution)/shard_map/ppermute | solution.py:376
  25.1 9.8 %collective-permute-start.9 = (bf16[1,256,128]{2,1,0:T(8,128)(2,1)S(1)}, bf16[1,256,128]{2,1,0:T(8,128)(2,1)S(1)}, u32[]{:S(2)}, u32[]{:S(2)}) collective-permute-start(bf16[1,256,128]{2,1,0:T(8,128)(2,1)S(1)} %get-tuple-element.75), channel_id=1, source_target_pairs={{0,2},{1,3},{2,0},{3,1},{4,6},{5,7},{6,4},{7,5},{8,10},{9,11},{10,... | collective-permute-start | bytes 196616 | tf_op jit(solution)/shard_map/ppermute | solution.py:376
  27.4 4.2 %collective-permute-start.7 = (bf16[2,64,128]{2,1,0:T(8,128)(2,1)S(1)}, bf16[2,64,128]{2,1,0:T(8,128)(2,1)S(1)}, u32[]{:S(2)}, u32[]{:S(2)}) collective-permute-start(bf16[2,64,128]{2,1,0:T(8,128)(2,1)S(1)} %get-tuple-element.65), channel_id=1, source_target_pairs={{0,1},{1,0},{2,3},{3,2},{4,5},{5,4},{6,7},{7,6},{8,9},{9,8},{10,11... | collective-permute-start | bytes 98312 | tf_op jit(solution)/shard_map/ppermute | solution.py:376
  31.7 1.6 %collective-permute-start.8 = (bf16[2,256,128]{2,1,0:T(8,128)(2,1)S(1)}, bf16[2,256,128]{2,1,0:T(8,128)(2,1)S(1)}, u32[]{:S(2)}, u32[]{:S(2)}) collective-permute-start(bf16[2,256,128]{2,1,0:T(8,128)(2,1)S(1)} %get-tuple-element.71), channel_id=1, source_target_pairs={{0,4},{4,0},{8,12},{12,8},{1,5},{5,1},{9,13},{13,9},{2,6},{6,2},{1... | collective-permute-start | bytes 393224 | tf_op jit(solution)/shard_map/ppermute | solution.py:376
  31.8 6.3 %collective-permute-start.11 = (bf16[1,64,128]{2,1,0:T(8,128)(2,1)S(1)}, bf16[1,64,128]{2,1,0:T(8,128)(2,1)S(1)}, u32[]{:S(2)}, u32[]{:S(2)}) collective-permute-start(bf16[1,64,128]{2,1,0:T(8,128)(2,1)S(1)} %get-tuple-element.79), channel_id=1, source_target_pairs={{0,2},{1,3},{2,0},{3,1},{4,6},{5,7},{6,4},{7,5},{8,10},{9,11},{10,... | collective-permute-start | bytes 49160 | tf_op jit(solution)/shard_map/ppermute | solution.py:376
  33.4 4.7 %collective-permute-start.10 = (bf16[1,256,128]{2,1,0:T(8,128)(2,1)S(1)}, bf16[1,256,128]{2,1,0:T(8,128)(2,1)S(1)}, u32[]{:S(2)}, u32[]{:S(2)}) collective-permute-start(bf16[1,256,128]{2,1,0:T(8,128)(2,1)S(1)} %get-tuple-element.78), channel_id=1, source_target_pairs={{0,8},{4,12},{8,0},{12,4},{1,9},{5,13},{9,1},{13,5},{2,10},{6,14},... | collective-permute-start | bytes 196616 | tf_op jit(solution)/shard_map/ppermute | solution.py:376

commit v14 on v13

--- a/solution.py
+++ b/solution.py
@@ -206,7 +206,7 @@
 def right_sum(first, last, z_refs, diag_ref, acc, so_far=None):
     for step in range(first, last):
         part = lax.dot_general(
-            diag_ref[step], at_step(z_refs, step)[...], NT, preferred_element_type=F32
+            at_step(z_refs, step)[...], diag_ref[step], NT, preferred_element_type=F32
         )
         acc[...] = part if so_far is None else so_far[...] + part
         so_far = acc
@@ -222,9 +222,10 @@
     j_pad = -(-j_rows // LANES) * LANES
     z_refs, (keep_out, send_out, acc, turned, gr_all) = refs[:-5], refs[-5:]
     right_sum(first, i_rows // step_rows, z_refs, diag_ref, acc, acc_first)
+    flipped = acc[...].T
     for a in range(blocks):
         at, shift = divmod(a * j_rows, LANES)
-        mine = acc[:, at * LANES : at * LANES + j_pad]
+        mine = flipped[:, at * LANES : at * LANES + j_pad]
         if shift:
             mine = pltpu.roll(mine, LANES - shift, axis=1)
         for b in range(groups):
@@ -461,7 +462,7 @@
     inner = chans * chans
     step_rows = 16
     steps = i_rows // step_rows
-    early_steps = steps // 2
+    early_steps = 3 * steps // 4
     dims = (chans, groups, blocks, i_rows, j_rows, step_rows, sequences)
     j_pad = -(-j_rows // LANES) * LANES
     span = blocks * j_rows
@@ -559,7 +560,7 @@
             functools.partial(right_part_kernel, first, last, len(z)),
             in_specs=[hbm()] + vmem(1 + len(z) + len(so_far)),
             out_specs=vmem()[0],
-            out_shape=pltpu.VMEM((depth, span), F32),
+            out_shape=pltpu.VMEM((span, depth), F32),
             compiler_params=params(16),
             cost_estimate=cost(1000, 1000),
             name="right_part",
@@ -588,7 +589,7 @@
         out_specs=vmem(2),
         out_shape=halves(j_rows * tiles, n_row),
         scratch_shapes=[
-            pltpu.VMEM((depth, span), F32),
+            pltpu.VMEM((span, depth), F32),
             pltpu.VMEM((width, j_pad), F32),
             pltpu.VMEM((j_rows * tiles, LANES), F32),
         ],

time: 39.2 us -> 39 us (level)
  starting transfers between devices: 16.1 us -> 14.3 us
  waiting for transfers between devices: 0.8 us -> 2.45 us
    ppermute x12, starting transfers between devices: 16.1 us -> 14.3 us  [swap(): return lax.ppermute(array, axis, [(s, s ^ bit) for s in range(n)])]
    ppermute x12, waiting for transfers between devices: 0.8 us -> 2.45 us  [swap(): return lax.ppermute(array, axis, [(s, s ^ bit) for s in range(n)])]
    pallas_call x1, Pallas kernels: 1.51 us -> 0.83 us  [shards(): pl.pallas_call(functools.partial(inner_kernel, dims, early_steps), in_spe...]
    pallas_call x1, Pallas kernels: 3.02 us -> 3.64 us  [shards(): pl.pallas_call(functools.partial(scale_kernel, dims), in_specs=[hbm()] *...]
  transfers between devices with their start and end apart: 12 -> 12, of which waited for: 4 -> 6; matrix products, arithmetic and copies ran while one was open for 0% -> 0% of each run, Pallas kernels for 52% -> 52%
where the time goes in v14:
time: 39 us; the launch traced here: 38.8 us
  Pallas kernels  21.1 us (54%)
  starting transfers between devices  14.3 us (37%)
  waiting for transfers between devices  2.45 us (6%)
  between operations  0.96 us (2%)
    ppermute x12, starting transfers between devices, swap(): return lax.ppermute(array, axis, [(s, s ^ bit) for s in range(n)])  14.3 us
    pallas_call x1, Pallas kernels, shards(): pl.pallas_call(functools.partial(outer_kernel, dims, n_row, n_col), in_sp...  4.89 us
    pallas_call x1, Pallas kernels, shards(): pl.pallas_call(functools.partial(scale_kernel, dims), in_specs=[hbm()] *...  3.64 us
    pallas_call x1, Pallas kernels, shards(): pl.pallas_call(functools.partial(pair_kernel, dims), in_specs=[hbm()] + v...  3.14 us
    pallas_call x1, Pallas kernels, shards(): pl.pallas_call(functools.partial(left_kernel, dims, n_col), in_specs=[hbm...  2.53 us
    ppermute x12, waiting for transfers between devices, swap(): return lax.ppermute(array, axis, [(s, s ^ bit) for s in range(n)])  2.45 us
    pallas_call x1, Pallas kernels, shards(): pl.pallas_call(functools.partial(right_kernel, dims, n_row, 2 * right_ste...  2.37 us
    pallas_call x2, Pallas kernels, right_part(): pl.pallas_call(functools.partial(right_part_kernel, first, last, len(z)),...  1.68 us
  transfers between devices with their start and end apart: 12, of which 6 were waited for; matrix products, arithmetic and copies ran while one was open for 0% of the time, Pallas kernels for 52%

profile of v14, /device:TPU:0, one launch (start us, length us, event | category | flops | bytes accessed | tf_op | source)
XLA Modules:
  0.0 38.8 jit_solution(15134163689948478916)
XLA Ops:
  0.6 4.1 %collective-permute-start = (bf16[1,16,2048]{2,1,0:T(8,128)(2,1)}, bf16[1,16,2048]{2,1,0:T(8,128)(2,1)S(1)}, u32[]{:S(2)}, u32[]{:S(2)}) collective-permute-start(bf16[1,16,2048]{2,1,0:T(8,128)(2,1)} %bitcast.4), channel_id=1, source_target_pairs={{0,2},{1,3},{2,0},{3,1},{4,6},{5,7},{6,4},{7,5},{8,10},{9,11},{10,... | collective-permute-start | bytes 196616 | tf_op jit(solution)/shard_map/ppermute | solution.py:377
  4.7 1.5 %collective-permute-start.1 = (bf16[1,16,2048]{2,1,0:T(8,128)(2,1)}, bf16[1,16,2048]{2,1,0:T(8,128)(2,1)S(1)}, u32[]{:S(2)}, u32[]{:S(2)}) collective-permute-start(bf16[1,16,2048]{2,1,0:T(8,128)(2,1)} %bitcast.5), channel_id=1, source_target_pairs={{0,8},{4,12},{8,0},{12,4},{1,9},{5,13},{9,1},{13,5},{2,10},{6,14},... | collective-permute-start | bytes 196616 | tf_op jit(solution)/shard_map/ppermute | solution.py:377
  6.2 3.6 %scale.1 = (bf16[64,64,128]{2,1,0:T(8,128)(2,1)S(1)}, f32[64,128]{1,0:T(8,128)S(1)}, bf16[1024,128]{1,0:T(8,128)(2,1)S(1)}, f32[1,2048]{1,0:T(1,128)S(1)}, f32[6...) custom-call(s32[1,256]{1,0:T(1,128)} %bitcast.6, ...), custom_call_target="tpu_custom_call" | custom-call | flops 1000 | bytes 1000 | tf_op jit(solution)/shard_map/scale/pallas_call | solution.py:473
  9.9 1.6 %collective-permute-start.3 = (bf16[2,16,2048]{2,1,0:T(8,128)(2,1)S(1)}, bf16[2,16,2048]{2,1,0:T(8,128)(2,1)S(1)}, u32[]{:S(2)}, u32[]{:S(2)}) collective-permute-start(bf16[2,16,2048]{2,1,0:T(8,128)(2,1)S(1)} %join.2.after.refs_5_), channel_id=1, source_target_pairs={{0,1},{1,0},{2,3},{3,2},{4,5},{5,4},{6,7},{7,6},{8,9},{9,8},{10,11... | collective-permute-start | bytes 393224 | tf_op jit(solution)/shard_map/ppermute | solution.py:377
  11.6 0.8 %inner.1.after.refs_1_ = bf16[1,512,2048]{2,1,0:T(8,128)(2,1)S(1)} custom-call(bf16[2,16,2048]{2,1,0:T(8,128)(2,1)S(1)} %join.3.after.right_held, bf16[64,64,128]{2,1,0:T(8,128)(2,1)S(1)} %get-tuple-element.45.scaled_ref.refs_3_, bf16[1024,128]{1,0:T(8,128)(2,1)S(1)} %get-tuple-element.46.wp_ref.refs_3_), custom_call_target="tpu_custom_call" | custom-call | flops 8589934592 | bytes 1048576 | tf_op jit(solution)/shard_map/inner/pallas_call | solution.py:505
  12.5 0.5 %collective-permute-done.2.right_came = bf16[2,16,2048]{2,1,0:T(8,128)(2,1)S(1)} collective-permute-done((bf16[2,16,2048]{2,1,0:T(8,128)(2,1)S(1)}, bf16[2,16,2048]{2,1,0:T(8,128)(2,1)S(1)}, u32[]{:S(2)}, u32[]{:S(2)}) %collective-permute-start.2) | collective-permute-done | bytes 131104 | tf_op jit(solution)/shard_map/ppermute | solution.py:377
  13.0 1.1 %right_rows.1 = (bf16[512,256]{1,0:T(8,128)(2,1)S(1)}, bf16[256,512]{1,0:T(8,128)(2,1)S(1)}) custom-call(bf16[1,512,2048]{2,1,0:T(8,128)(2,1)S(1)} %inner.1.after.refs_1_, f32[64,128]{1,0:T(8,128)S(1)} %get-tuple-element.47.rj_ref, f32[1,2048]{1,0:T(1,128)S(1)} %get-tuple-element.48.keep_ref.refs_2_.refs_5_, bf16[2,16,2048]{2,1,0:T(8,128)(2,1)S(1)} %join.3.after.right_held, ...), custom_call_target="tpu_custom_call" | custom-call | flops 8589934592 | bytes 1048576 | tf_op jit(solution)/shard_map/right_rows/pallas_call | solution.py:516
  14.0 2.5 %left.1 = (bf16[2,256,128]{2,1,0:T(8,128)(2,1)S(1)}, bf16[2,256,128]{2,1,0:T(8,128)(2,1)S(1)}) custom-call(bf16[512,256]{1,0:T(8,128)(2,1)S(1)} %get-tuple-element.49.after.refs_4_, bf16[256,512]{1,0:T(8,128)(2,1)S(1)} %get-tuple-element.50.rbt_ref, bf16[3,512,2048]{2,1,0:T(8,128)(2,1)S(1)} %get-tuple-element.51.refs_0_, ...), custom_call_target="tpu_custom_call" | custom-call | flops 8589934592 | bytes 1048576 | tf_op jit(solution)/shard_map/left/pallas_call | solution.py:527
  16.6 0.5 %collective-permute-start.4 = (bf16[2,256,128]{2,1,0:T(8,128)(2,1)S(1)}, bf16[2,256,128]{2,1,0:T(8,128)(2,1)S(1)}, u32[]{:S(2)}, u32[]{:S(2)}) collective-permute-start(bf16[2,256,128]{2,1,0:T(8,128)(2,1)S(1)} %get-tuple-element.55), channel_id=1, source_target_pairs={{0,1},{1,0},{2,3},{3,2},{4,5},{5,4},{6,7},{7,6},{8,9},{9,8},{10,11... | collective-permute-start | bytes 393224 | tf_op jit(solution)/shard_map/ppermute | solution.py:377
  17.1 4.9 %outer.1 = (bf16[64,64,1024]{2,1,0:T(8,128)(2,1)S(1)}, bf16[4,256,2048]{2,1,0:T(8,128)(2,1)S(1)}, bf16[2,256,128]{2,1,0:T(8,128)(2,1)S(1)}, bf16[2,256,128]{2,1,0:T(8,128)(2,1)S(1)}) custom-call(bf16[2,256,128]{2,1,0:T(8,128)(2,1)S(1)} %get-tuple-element.52.refs_0_.held_ref, f32[64,128]{1,0:T(8,128)S(1)} %get-tuple-element.53.refs_1_, ...), custom_call_target="tpu_custom_call" | custom-call | flops 8589934592 | bytes 1048576 | tf_op jit(solution)/shard_map/outer/pallas_call | solution.py:537
  22.1 0.1 collective-permute-done.4.came_ref
  22.2 0.7 %right_part.2.after.refs_2_ = f32[512,256]{1,0:T(8,128)S(1)} custom-call(f32[1,256,128]{2,1,0:T(8,128)S(1)} %get-tuple-element.56.after.refs_0_, bf16[4,256,2048]{2,1,0:T(8,128)(2,1)S(1)} %get-tuple-element.57.diag_ref, bf16[3,512,2048]{2,1,0:T(8,128)(2,1)S(1)} %get-tuple-element.51.refs_0_, bf16[1,512,2048]{2,1,0:T(8,128)(2,1)S(1)} %inner.1.after.refs_1_), custom_call_target="tpu_custom_call" | custom-call | flops 1000 | bytes 1000 | tf_op jit(solution)/shard_map/right_part/pallas_call | solution.py:559
  23.0 0.4 %collective-permute-done.5.came_ref = bf16[2,256,128]{2,1,0:T(8,128)(2,1)S(1)} collective-permute-done((bf16[2,256,128]{2,1,0:T(8,128)(2,1)S(1)}, bf16[2,256,128]{2,1,0:T(8,128)(2,1)S(1)}, u32[]{:S(2)}, u32[]{:S(2)}) %collective-permute-start.5) | collective-permute-done | bytes 131104 | tf_op jit(solution)/shard_map/ppermute | solution.py:377
  23.5 0.6 %collective-permute-start.6 = (bf16[1,256,128]{2,1,0:T(8,128)(2,1)S(1)}, bf16[1,256,128]{2,1,0:T(8,128)(2,1)S(1)}, u32[]{:S(2)}, u32[]{:S(2)}) collective-permute-start(bf16[1,256,128]{2,1,0:T(8,128)(2,1)S(1)} %get-tuple-element.62), channel_id=1, source_target_pairs={{0,8},{4,12},{8,0},{12,4},{1,9},{5,13},{9,1},{13,5},{2,10},{6,14},... | collective-permute-start | bytes 196616 | tf_op jit(solution)/shard_map/ppermute | solution.py:377
  24.1 0.9 %right_part.3.after.acc_first = f32[512,256]{1,0:T(8,128)S(1)} custom-call(f32[1,256,128]{2,1,0:T(8,128)S(1)} %get-tuple-element.61.after.refs_6_, bf16[4,256,2048]{2,1,0:T(8,128)(2,1)S(1)} %get-tuple-element.57.diag_ref, bf16[3,512,2048]{2,1,0:T(8,128)(2,1)S(1)} %get-tuple-element.51.refs_0_, bf16[1,512,2048]{2,1,0:T(8,128)(2,1)S(1)} %inner.1.after.refs_1_, ...), custom_call_target="tpu_custom_call" | custom-call | flops 1000 | bytes 1000 | tf_op jit(solution)/shard_map/right_part/pallas_call | solution.py:559
  25.0 1.7 %collective-permute-start.9 = (bf16[1,256,128]{2,1,0:T(8,128)(2,1)S(1)}, bf16[1,256,128]{2,1,0:T(8,128)(2,1)S(1)}, u32[]{:S(2)}, u32[]{:S(2)}) collective-permute-start(bf16[1,256,128]{2,1,0:T(8,128)(2,1)S(1)} %get-tuple-element.75), channel_id=1, source_target_pairs={{0,2},{1,3},{2,0},{3,1},{4,6},{5,7},{6,4},{7,5},{8,10},{9,11},{10,... | collective-permute-start | bytes 196616 | tf_op jit(solution)/shard_map/ppermute | solution.py:377
  26.7 1.1 %collective-permute-done.6.came_ref = bf16[1,256,128]{2,1,0:T(8,128)(2,1)S(1)} collective-permute-done((bf16[1,256,128]{2,1,0:T(8,128)(2,1)S(1)}, bf16[1,256,128]{2,1,0:T(8,128)(2,1)S(1)}, u32[]{:S(2)}, u32[]{:S(2)}) %collective-permute-start.6) | collective-permute-done | bytes 65568 | tf_op jit(solution)/shard_map/ppermute | solution.py:377
  27.8 1.6 %collective-permute-start.7 = (bf16[2,64,128]{2,1,0:T(8,128)(2,1)S(1)}, bf16[2,64,128]{2,1,0:T(8,128)(2,1)S(1)}, u32[]{:S(2)}, u32[]{:S(2)}) collective-permute-start(bf16[2,64,128]{2,1,0:T(8,128)(2,1)S(1)} %get-tuple-element.65), channel_id=1, source_target_pairs={{0,1},{1,0},{2,3},{3,2},{4,5},{5,4},{6,7},{7,6},{8,9},{9,8},{10,11... | collective-permute-start | bytes 98312 | tf_op jit(solution)/shard_map/ppermute | solution.py:377
  29.5 2.4 %right.1 = (bf16[2,256,128]{2,1,0:T(8,128)(2,1)S(1)}, bf16[2,256,128]{2,1,0:T(8,128)(2,1)S(1)}) custom-call(bf16[2,64,128]{2,1,0:T(8,128)(2,1)S(1)} %get-tuple-element.63.after.held_ref, bf16[4,256,2048]{2,1,0:T(8,128)(2,1)S(1)} %get-tuple-element.57.diag_ref, f32[512,256]{1,0:T(8,128)S(1)} %right_part.3.after.acc_first, ...), custom_call_target="tpu_custom_call" | custom-call | flops 8589934592 | bytes 1048576 | tf_op jit(solution)/shard_map/right/pallas_call | solution.py:586
  32.0 1.1 %collective-permute-start.11 = (bf16[1,64,128]{2,1,0:T(8,128)(2,1)S(1)}, bf16[1,64,128]{2,1,0:T(8,128)(2,1)S(1)}, u32[]{:S(2)}, u32[]{:S(2)}) collective-permute-start(bf16[1,64,128]{2,1,0:T(8,128)(2,1)S(1)} %get-tuple-element.79), channel_id=1, source_target_pairs={{0,2},{1,3},{2,0},{3,1},{4,6},{5,7},{6,4},{7,5},{8,10},{9,11},{10,... | collective-permute-start | bytes 49160 | tf_op jit(solution)/shard_map/ppermute | solution.py:377
  33.1 0.2 collective-permute-done.8.came_ref
  33.4 1.3 %collective-permute-start.10 = (bf16[1,256,128]{2,1,0:T(8,128)(2,1)S(1)}, bf16[1,256,128]{2,1,0:T(8,128)(2,1)S(1)}, u32[]{:S(2)}, u32[]{:S(2)}) collective-permute-start(bf16[1,256,128]{2,1,0:T(8,128)(2,1)S(1)} %get-tuple-element.78), channel_id=1, source_target_pairs={{0,8},{4,12},{8,0},{12,4},{1,9},{5,13},{9,1},{13,5},{2,10},{6,14},... | collective-permute-start | bytes 196616 | tf_op jit(solution)/shard_map/ppermute | solution.py:377
  34.7 3.1 %pair.1 = (bf16[64,64,128]{2,1,0:T(8,128)(2,1)}, f32[16,2048]{1,0:T(8,128)}) custom-call(f32[1,256,128]{2,1,0:T(8,128)S(1)} %get-tuple-element.72.refs_0_, f32[64,128]{1,0:T(8,128)S(1)} %get-tuple-element.53.refs_1_, bf16[64,64,1024]{2,1,0:T(8,128)(2,1)S(1)} %get-tuple-element.73.refs_2_, bf16[1024,128]{1,0:T(8,128)(2,1)S(1)} %get-tuple-element.46.wp_ref.refs_3_, ...), custom_call_target="tpu_custom_call" | custom-call | flops 8589934592 | bytes 1048576 | tf_op jit(solution)/shard_map/pair/pallas_call | solution.py:609
  37.9 0.7 %final_sums.1 = (f32[16,2048]{1,0:T(8,128)}, f32[64,128]{1,0:T(8,128)}) custom-call(bf16[64,64,128]{2,1,0:T(8,128)(2,1)} %get-tuple-element.39.after, f32[64,128]{1,0:T(8,128)S(1)} %get-tuple-element.47.rj_ref, f32[1,2048]{1,0:T(1,128)S(1)} %get-tuple-element.48.keep_ref.refs_2_.refs_5_, f32[1,256,128]{2,1,0:T(8,128)S(1)} %get-tuple-element.72.refs_0_, ...), custom_call_target="tpu_custom_call" | custom-call | flops 1000 | bytes 1000 | tf_op jit(solution)/shard_map/final_sums/pallas_call | solution.py:629
  (20 shorter events, 0.5 us)
Async XLA Ops:
  0.6 9.2 %collective-permute-start = (bf16[1,16,2048]{2,1,0:T(8,128)(2,1)}, bf16[1,16,2048]{2,1,0:T(8,128)(2,1)S(1)}, u32[]{:S(2)}, u32[]{:S(2)}) collective-permute-start(bf16[1,16,2048]{2,1,0:T(8,128)(2,1)} %bitcast.4), channel_id=1, source_target_pairs={{0,2},{1,3},{2,0},{3,1},{4,6},{5,7},{6,4},{7,5},{8,10},{9,11},{10,... | collective-permute-start | bytes 196616 | tf_op jit(solution)/shard_map/ppermute | solution.py:377
  4.7 6.8 %collective-permute-start.1 = (bf16[1,16,2048]{2,1,0:T(8,128)(2,1)}, bf16[1,16,2048]{2,1,0:T(8,128)(2,1)S(1)}, u32[]{:S(2)}, u32[]{:S(2)}) collective-permute-start(bf16[1,16,2048]{2,1,0:T(8,128)(2,1)} %bitcast.5), channel_id=1, source_target_pairs={{0,8},{4,12},{8,0},{12,4},{1,9},{5,13},{9,1},{13,5},{2,10},{6,14},... | collective-permute-start | bytes 196616 | tf_op jit(solution)/shard_map/ppermute | solution.py:377
  9.9 7.2 %collective-permute-start.3 = (bf16[2,16,2048]{2,1,0:T(8,128)(2,1)S(1)}, bf16[2,16,2048]{2,1,0:T(8,128)(2,1)S(1)}, u32[]{:S(2)}, u32[]{:S(2)}) collective-permute-start(bf16[2,16,2048]{2,1,0:T(8,128)(2,1)S(1)} %join.2.after.refs_5_), channel_id=1, source_target_pairs={{0,1},{1,0},{2,3},{3,2},{4,5},{5,4},{6,7},{7,6},{8,9},{9,8},{10,11... | collective-permute-start | bytes 393224 | tf_op jit(solution)/shard_map/ppermute | solution.py:377
  11.6 1.4 %collective-permute-start.2 = (bf16[2,16,2048]{2,1,0:T(8,128)(2,1)S(1)}, bf16[2,16,2048]{2,1,0:T(8,128)(2,1)S(1)}, u32[]{:S(2)}, u32[]{:S(2)}) collective-permute-start(bf16[2,16,2048]{2,1,0:T(8,128)(2,1)S(1)} %join.3.after.right_held), channel_id=1, source_target_pairs={{0,4},{4,0},{8,12},{12,8},{1,5},{5,1},{9,13},{13,9},{2,6},{6,2},{1... | collective-permute-start | bytes 393224 | tf_op jit(solution)/shard_map/ppermute | solution.py:377
  16.6 5.6 %collective-permute-start.4 = (bf16[2,256,128]{2,1,0:T(8,128)(2,1)S(1)}, bf16[2,256,128]{2,1,0:T(8,128)(2,1)S(1)}, u32[]{:S(2)}, u32[]{:S(2)}) collective-permute-start(bf16[2,256,128]{2,1,0:T(8,128)(2,1)S(1)} %get-tuple-element.55), channel_id=1, source_target_pairs={{0,1},{1,0},{2,3},{3,2},{4,5},{5,4},{6,7},{7,6},{8,9},{9,8},{10,11... | collective-permute-start | bytes 393224 | tf_op jit(solution)/shard_map/ppermute | solution.py:377
  22.0 1.4 %collective-permute-start.5 = (bf16[2,256,128]{2,1,0:T(8,128)(2,1)S(1)}, bf16[2,256,128]{2,1,0:T(8,128)(2,1)S(1)}, u32[]{:S(2)}, u32[]{:S(2)}) collective-permute-start(bf16[2,256,128]{2,1,0:T(8,128)(2,1)S(1)} %get-tuple-element.58), channel_id=1, source_target_pairs={{0,4},{4,0},{8,12},{12,8},{1,5},{5,1},{9,13},{13,9},{2,6},{6,2},{1... | collective-permute-start | bytes 393224 | tf_op jit(solution)/shard_map/ppermute | solution.py:377
  23.5 4.3 %collective-permute-start.6 = (bf16[1,256,128]{2,1,0:T(8,128)(2,1)S(1)}, bf16[1,256,128]{2,1,0:T(8,128)(2,1)S(1)}, u32[]{:S(2)}, u32[]{:S(2)}) collective-permute-start(bf16[1,256,128]{2,1,0:T(8,128)(2,1)S(1)} %get-tuple-element.62), channel_id=1, source_target_pairs={{0,8},{4,12},{8,0},{12,4},{1,9},{5,13},{9,1},{13,5},{2,10},{6,14},... | collective-permute-start | bytes 196616 | tf_op jit(solution)/shard_map/ppermute | solution.py:377
  25.0 9.7 %collective-permute-start.9 = (bf16[1,256,128]{2,1,0:T(8,128)(2,1)S(1)}, bf16[1,256,128]{2,1,0:T(8,128)(2,1)S(1)}, u32[]{:S(2)}, u32[]{:S(2)}) collective-permute-start(bf16[1,256,128]{2,1,0:T(8,128)(2,1)S(1)} %get-tuple-element.75), channel_id=1, source_target_pairs={{0,2},{1,3},{2,0},{3,1},{4,6},{5,7},{6,4},{7,5},{8,10},{9,11},{10,... | collective-permute-start | bytes 196616 | tf_op jit(solution)/shard_map/ppermute | solution.py:377
  27.8 4.1 %collective-permute-start.7 = (bf16[2,64,128]{2,1,0:T(8,128)(2,1)S(1)}, bf16[2,64,128]{2,1,0:T(8,128)(2,1)S(1)}, u32[]{:S(2)}, u32[]{:S(2)}) collective-permute-start(bf16[2,64,128]{2,1,0:T(8,128)(2,1)S(1)} %get-tuple-element.65), channel_id=1, source_target_pairs={{0,1},{1,0},{2,3},{3,2},{4,5},{5,4},{6,7},{7,6},{8,9},{9,8},{10,11... | collective-permute-start | bytes 98312 | tf_op jit(solution)/shard_map/ppermute | solution.py:377
  31.9 1.4 %collective-permute-start.8 = (bf16[2,256,128]{2,1,0:T(8,128)(2,1)S(1)}, bf16[2,256,128]{2,1,0:T(8,128)(2,1)S(1)}, u32[]{:S(2)}, u32[]{:S(2)}) collective-permute-start(bf16[2,256,128]{2,1,0:T(8,128)(2,1)S(1)} %get-tuple-element.71), channel_id=1, source_target_pairs={{0,4},{4,0},{8,12},{12,8},{1,5},{5,1},{9,13},{13,9},{2,6},{6,2},{1... | collective-permute-start | bytes 393224 | tf_op jit(solution)/shard_map/ppermute | solution.py:377
  32.0 5.8 %collective-permute-start.11 = (bf16[1,64,128]{2,1,0:T(8,128)(2,1)S(1)}, bf16[1,64,128]{2,1,0:T(8,128)(2,1)S(1)}, u32[]{:S(2)}, u32[]{:S(2)}) collective-permute-start(bf16[1,64,128]{2,1,0:T(8,128)(2,1)S(1)} %get-tuple-element.79), channel_id=1, source_target_pairs={{0,2},{1,3},{2,0},{3,1},{4,6},{5,7},{6,4},{7,5},{8,10},{9,11},{10,... | collective-permute-start | bytes 49160 | tf_op jit(solution)/shard_map/ppermute | solution.py:377
  33.4 4.5 %collective-permute-start.10 = (bf16[1,256,128]{2,1,0:T(8,128)(2,1)S(1)}, bf16[1,256,128]{2,1,0:T(8,128)(2,1)S(1)}, u32[]{:S(2)}, u32[]{:S(2)}) collective-permute-start(bf16[1,256,128]{2,1,0:T(8,128)(2,1)S(1)} %get-tuple-element.78), channel_id=1, source_target_pairs={{0,8},{4,12},{8,0},{12,4},{1,9},{5,13},{9,1},{13,5},{2,10},{6,14},... | collective-permute-start | bytes 196616 | tf_op jit(solution)/shard_map/ppermute | solution.py:377

commit v15 on v13

--- a/solution.py
+++ b/solution.py
@@ -37,6 +37,22 @@
         for k, owner in enumerate(owners):
             at = pl.multiple_of((index ^ owner) * rows, 8)
             flat[pl.ds(at, rows), :] = buffer[k].astype(F32)
+
+
+def paired(j_rows):
+    return 2 * j_rows == LANES
+
+
+def slot_of(tile, tiles, j_rows):
+    return tile % 2 * (tiles // 2) + tile // 2 if paired(j_rows) else tile
+
+
+def swap_halves(low, first, second):
+    half = LANES // 2
+    return (
+        jnp.where(low, first, pltpu.roll(second, half, axis=1)),
+        jnp.where(low, pltpu.roll(first, half, axis=1), second),
+    )
 
 
 def lane_group(shape, chans):
@@ -150,7 +166,7 @@
     for t in range(tiles):
         lanes = slice(t * LANES, (t + 1) * LANES)
         masked = flat[0:i_rows, lanes] * ri_ref[...] * keep_ref[:, lanes]
-        lsplit[pl.ds(t, i_rows, stride=tiles), :] = masked
+        lsplit[pl.ds(slot_of(t, tiles, j_rows), i_rows, stride=tiles), :] = masked
     shape = (LANES, groups * LANES)
     source = lax.broadcasted_iota(jnp.int32, shape, 0)
     target = lax.broadcasted_iota(jnp.int32, shape, 1)
@@ -222,20 +238,43 @@
     j_pad = -(-j_rows // LANES) * LANES
     z_refs, (keep_out, send_out, acc, turned, gr_all) = refs[:-5], refs[-5:]
     right_sum(first, i_rows // step_rows, z_refs, diag_ref, acc, acc_first)
-    for a in range(blocks):
-        at, shift = divmod(a * j_rows, LANES)
-        mine = acc[:, at * LANES : at * LANES + j_pad]
-        if shift:
-            mine = pltpu.roll(mine, LANES - shift, axis=1)
-        for b in range(groups):
-            for lo in range(groups):
-                first = b * sequences + lo * tiles
-                turned[pl.ds(lo * chans + groups * a + b, tiles, stride=LANES), :] = mine[
-                    first : first + tiles
+    if paired(j_rows):
+        half = tiles // 2
+        low = lane_group((half, LANES), LANES // 2) == 0
+        for a in range(0, blocks, 2):
+            lanes = slice(a * j_rows, (a + 2) * j_rows)
+            for b in range(groups):
+                for lo in range(groups):
+                    first = b * sequences + lo * tiles
+                    both = swap_halves(
+                        low,
+                        acc[first : first + half, lanes],
+                        acc[first + half : first + tiles, lanes],
+                    )
+                    at = lo * chans + groups * a + b
+                    turned[pl.ds(at, half, stride=LANES), :] = both[0]
+                    turned[pl.ds(at + groups, half, stride=LANES), :] = both[1]
+        for pair in range(half):
+            block = turned[pair * LANES : (pair + 1) * LANES, :].T
+            for k in range(2):
+                gr_all[pl.ds(2 * pair + k, j_rows, stride=tiles), :] = block[
+                    k * j_rows : (k + 1) * j_rows
                 ]
-    for t in range(tiles):
-        lanes = slice(t * LANES, (t + 1) * LANES)
-        gr_all[pl.ds(t, j_rows, stride=tiles), :] = turned[lanes, :].T[:j_rows]
+    else:
+        for a in range(blocks):
+            at, shift = divmod(a * j_rows, LANES)
+            mine = acc[:, at * LANES : at * LANES + j_pad]
+            if shift:
+                mine = pltpu.roll(mine, LANES - shift, axis=1)
+            for b in range(groups):
+                for lo in range(groups):
+                    first = b * sequences + lo * tiles
+                    turned[pl.ds(lo * chans + groups * a + b, tiles, stride=LANES), :] = mine[
+                        first : first + tiles
+                    ]
+        for t in range(tiles):
+            lanes = slice(t * LANES, (t + 1) * LANES)
+            gr_all[pl.ds(t, j_rows, stride=tiles), :] = turned[lanes, :].T[:j_rows]
     cut(gr_all, lax.axis_index("row"), n_row, keep_out, send_out)
 
 
@@ -245,21 +284,45 @@
     j_pad = -(-j_rows // LANES) * LANES
     rbig, rbt_ref, flat, turned = refs
     place((right_held, right_came), lax.axis_index("row"), n_row, flat)
-    for t in range(tiles):
-        lanes = slice(t * LANES, (t + 1) * LANES)
-        masked = flat[0:j_rows, lanes] * rj_ref[...] * keep_ref[:, lanes]
-        if j_rows < j_pad:
-            masked = jnp.concatenate([masked, jnp.zeros((j_pad - j_rows, LANES), F32)], axis=0)
-        turned[lanes, :] = masked.T
-    for a in range(blocks):
-        parts = [
-            turned[pl.ds(lo * chans + groups * a + b, tiles, stride=LANES), :]
-            for b in range(groups)
-            for lo in range(groups)
-        ]
-        block = jnp.concatenate(parts, axis=0)
-        rbig[a * j_rows : (a + 1) * j_rows, :] = block.T[:j_rows].astype(BF16)
-    rbt_ref[...] = rbig[...].T
+    if paired(j_rows):
+        half = tiles // 2
+        low = lane_group((half, LANES), LANES // 2) == 0
+        for pair in range(half):
+            rows = []
+            for t in (2 * pair, 2 * pair + 1):
+                lanes = slice(t * LANES, (t + 1) * LANES)
+                rows.append(flat[0:j_rows, lanes] * rj_ref[...] * keep_ref[:, lanes])
+            turned[pair * LANES : (pair + 1) * LANES, :] = jnp.concatenate(rows, axis=0).T
+        for a in range(0, blocks, 2):
+            parts = []
+            for b in range(groups):
+                for lo in range(groups):
+                    at = lo * chans + groups * a + b
+                    parts += swap_halves(
+                        low,
+                        turned[pl.ds(at, half, stride=LANES), :],
+                        turned[pl.ds(at + groups, half, stride=LANES), :],
+                    )
+            block = jnp.concatenate(parts, axis=0)
+            lanes = slice(a * j_rows, (a + 2) * j_rows)
+            rbt_ref[:, lanes] = block.astype(BF16)
+            rbig[lanes, :] = block.T.astype(BF16)
+    else:
+        for t in range(tiles):
+            lanes = slice(t * LANES, (t + 1) * LANES)
+            masked = flat[0:j_rows, lanes] * rj_ref[...] * keep_ref[:, lanes]
+            if j_rows < j_pad:
+                masked = jnp.concatenate([masked, jnp.zeros((j_pad - j_rows, LANES), F32)], axis=0)
+            turned[lanes, :] = masked.T
+        for a in range(blocks):
+            parts = [
+                turned[pl.ds(lo * chans + groups * a + b, tiles, stride=LANES), :]
+                for b in range(groups)
+                for lo in range(groups)
+            ]
+            block = jnp.concatenate(parts, axis=0)
+            rbig[a * j_rows : (a + 1) * j_rows, :] = block.T[:j_rows].astype(BF16)
+        rbt_ref[...] = rbig[...].T
 
 
 def left_kernel(dims, n_col, after, rbt_ref, *refs):
@@ -322,11 +385,12 @@
     cut(whole, lax.axis_index("col"), n_col, keep_out, send_out)
 
 
-def write_rows(whole, rows, keep_ref, out_ref, tiles):
+def write_rows(whole, rows, keep_ref, out_ref, slots):
     own = out_ref.shape[0]
-    for t in range(tiles):
+    tiles = len(slots)
+    for t, slot in enumerate(slots):
         lanes = slice(t * LANES, (t + 1) * LANES)
-        out_ref[:, lanes] = whole[pl.ds(t, own, stride=tiles), :] * (
+        out_ref[:, lanes] = whole[pl.ds(slot, own, stride=tiles), :] * (
             rows * keep_ref[:, lanes]
         )
 
@@ -338,7 +402,9 @@
     own = left.shape[0]
     first = pl.multiple_of(lax.axis_index("col") * own, 8)
     whole[...] = total_of(held, came)
-    write_rows(whole, ri_ref[pl.ds(first, own), :], keep_ref, left, whole.shape[0] // own)
+    tiles = whole.shape[0] // own
+    slots = [slot_of(t, tiles, j_rows) for t in range(tiles)]
+    write_rows(whole, ri_ref[pl.ds(first, own), :], keep_ref, left, slots)
     copies = [pltpu.make_async_copy(left, gl_out, sems.at[0])]
     copies[0].start()
     for row in range(0, i_rows, PIECE):
@@ -365,7 +431,8 @@
     own = rows.shape[0]
     first = pl.multiple_of(lax.axis_index("row") * own, 8)
     whole[...] = total_of(*right)
-    write_rows(whole, rj_ref[pl.ds(first, own), :], keep_ref, rows, whole.shape[0] // own)
+    slots = range(whole.shape[0] // own)
+    write_rows(whole, rj_ref[pl.ds(first, own), :], keep_ref, rows, slots)
     copies.append(pltpu.make_async_copy(rows, gr_out, sems.at[1]))
     copies[1].start()
     for copy in copies:

time: 39.2 us -> 38.6 us (0.985)
  Pallas kernels: 21.1 us -> 20.3 us
  waiting for transfers between devices: 0.8 us -> 1.3 us
    ppermute x12, waiting for transfers between devices: 0.8 us -> 1.3 us  [swap(): return lax.ppermute(array, axis, [(s, s ^ bit) for s in range(n)])]
    pallas_call x1, Pallas kernels: 2.33 us -> 1.83 us  [shards(): pl.pallas_call(functools.partial(right_kernel, dims, n_row, 2 * right_ste...]
  transfers between devices with their start and end apart: 12 -> 12, of which waited for: 4 -> 4; matrix products, arithmetic and copies ran while one was open for 0% -> 0% of each run, Pallas kernels for 52% -> 51%
where the time goes in v15:
time: 38.6 us; the launch traced here: 38.5 us
  Pallas kernels  20.3 us (53%)
  starting transfers between devices  15.9 us (41%)
  waiting for transfers between devices  1.3 us (3%)
  between operations  0.96 us (2%)
    ppermute x12, starting transfers between devices, swap(): return lax.ppermute(array, axis, [(s, s ^ bit) for s in range(n)])  15.9 us
    pallas_call x1, Pallas kernels, shards(): pl.pallas_call(functools.partial(outer_kernel, dims, n_row, n_col), in_sp...  4.94 us
    pallas_call x1, Pallas kernels, shards(): pl.pallas_call(functools.partial(pair_kernel, dims), in_specs=[hbm()] + v...  3.15 us
    pallas_call x1, Pallas kernels, shards(): pl.pallas_call(functools.partial(scale_kernel, dims), in_specs=[hbm()] *...  3.02 us
    pallas_call x1, Pallas kernels, shards(): pl.pallas_call(functools.partial(left_kernel, dims, n_col), in_specs=[hbm...  2.53 us
    pallas_call x1, Pallas kernels, shards(): pl.pallas_call(functools.partial(right_kernel, dims, n_row, 2 * right_ste...  1.83 us
    pallas_call x2, Pallas kernels, right_part(): pl.pallas_call(functools.partial(right_part_kernel, first, last, len(z)),...  1.67 us
    pallas_call x1, Pallas kernels, shards(): pl.pallas_call(functools.partial(inner_kernel, dims, early_steps), in_spe...  1.51 us
  transfers between devices with their start and end apart: 12, of which 4 were waited for; matrix products, arithmetic and copies ran while one was open for 0% of the time, Pallas kernels for 51%

profile of v15, /device:TPU:0, one launch (start us, length us, event | category | flops | bytes accessed | tf_op | source)
XLA Modules:
  0.0 38.5 jit_solution(8339227237551904787)
XLA Ops:
  0.6 4.1 %collective-permute-start = (bf16[1,16,2048]{2,1,0:T(8,128)(2,1)}, bf16[1,16,2048]{2,1,0:T(8,128)(2,1)S(1)}, u32[]{:S(2)}, u32[]{:S(2)}) collective-permute-start(bf16[1,16,2048]{2,1,0:T(8,128)(2,1)} %bitcast.4), channel_id=1, source_target_pairs={{0,2},{1,3},{2,0},{3,1},{4,6},{5,7},{6,4},{7,5},{8,10},{9,11},{10,... | collective-permute-start | bytes 196616 | tf_op jit(solution)/shard_map/ppermute | solution.py:443
  4.7 1.5 %collective-permute-start.1 = (bf16[1,16,2048]{2,1,0:T(8,128)(2,1)}, bf16[1,16,2048]{2,1,0:T(8,128)(2,1)S(1)}, u32[]{:S(2)}, u32[]{:S(2)}) collective-permute-start(bf16[1,16,2048]{2,1,0:T(8,128)(2,1)} %bitcast.5), channel_id=1, source_target_pairs={{0,8},{4,12},{8,0},{12,4},{1,9},{5,13},{9,1},{13,5},{2,10},{6,14},... | collective-permute-start | bytes 196616 | tf_op jit(solution)/shard_map/ppermute | solution.py:443
  6.2 3.0 %scale.1 = (bf16[64,64,128]{2,1,0:T(8,128)(2,1)S(1)}, f32[64,128]{1,0:T(8,128)S(1)}, bf16[1024,128]{1,0:T(8,128)(2,1)S(1)}, f32[1,2048]{1,0:T(1,128)S(1)}, f32[6...) custom-call(s32[1,256]{1,0:T(1,128)} %bitcast.6, ...), custom_call_target="tpu_custom_call" | custom-call | flops 1000 | bytes 1000 | tf_op jit(solution)/shard_map/scale/pallas_call | solution.py:539
  9.3 1.6 %collective-permute-start.3 = (bf16[2,16,2048]{2,1,0:T(8,128)(2,1)S(1)}, bf16[2,16,2048]{2,1,0:T(8,128)(2,1)S(1)}, u32[]{:S(2)}, u32[]{:S(2)}) collective-permute-start(bf16[2,16,2048]{2,1,0:T(8,128)(2,1)S(1)} %join.2.after.refs_5_), channel_id=1, source_target_pairs={{0,1},{1,0},{2,3},{3,2},{4,5},{5,4},{6,7},{7,6},{8,9},{9,8},{10,11... | collective-permute-start | bytes 393224 | tf_op jit(solution)/shard_map/ppermute | solution.py:443
  11.0 1.5 %inner.1.after.refs_1_ = bf16[2,512,2048]{2,1,0:T(8,128)(2,1)S(1)} custom-call(bf16[2,16,2048]{2,1,0:T(8,128)(2,1)S(1)} %join.3.after.right_held, bf16[64,64,128]{2,1,0:T(8,128)(2,1)S(1)} %get-tuple-element.45.scaled_ref.refs_3_, bf16[1024,128]{1,0:T(8,128)(2,1)S(1)} %get-tuple-element.46.wp_ref.refs_3_), custom_call_target="tpu_custom_call" | custom-call | flops 8589934592 | bytes 1048576 | tf_op jit(solution)/shard_map/inner/pallas_call | solution.py:571
  12.6 0.7 %right_rows.1 = (bf16[512,256]{1,0:T(8,128)(2,1)S(1)}, bf16[256,512]{1,0:T(8,128)(2,1)S(1)}) custom-call(bf16[2,512,2048]{2,1,0:T(8,128)(2,1)S(1)} %inner.1.after.refs_1_, f32[64,128]{1,0:T(8,128)S(1)} %get-tuple-element.47.rj_ref, f32[1,2048]{1,0:T(1,128)S(1)} %get-tuple-element.48.keep_ref.refs_2_.refs_5_, bf16[2,16,2048]{2,1,0:T(8,128)(2,1)S(1)} %join.3.after.right_held, ...), custom_call_target="tpu_custom_call" | custom-call | flops 8589934592 | bytes 1048576 | tf_op jit(solution)/shard_map/right_rows/pallas_call | solution.py:582
  13.3 2.5 %left.1 = (bf16[2,256,128]{2,1,0:T(8,128)(2,1)S(1)}, bf16[2,256,128]{2,1,0:T(8,128)(2,1)S(1)}) custom-call(bf16[512,256]{1,0:T(8,128)(2,1)S(1)} %get-tuple-element.49.after.refs_4_, bf16[256,512]{1,0:T(8,128)(2,1)S(1)} %get-tuple-element.50.rbt_ref, bf16[2,512,2048]{2,1,0:T(8,128)(2,1)S(1)} %get-tuple-element.51.refs_0_, ...), custom_call_target="tpu_custom_call" | custom-call | flops 8589934592 | bytes 1048576 | tf_op jit(solution)/shard_map/left/pallas_call | solution.py:593
  15.8 0.5 %collective-permute-start.4 = (bf16[2,256,128]{2,1,0:T(8,128)(2,1)S(1)}, bf16[2,256,128]{2,1,0:T(8,128)(2,1)S(1)}, u32[]{:S(2)}, u32[]{:S(2)}) collective-permute-start(bf16[2,256,128]{2,1,0:T(8,128)(2,1)S(1)} %get-tuple-element.55), channel_id=1, source_target_pairs={{0,1},{1,0},{2,3},{3,2},{4,5},{5,4},{6,7},{7,6},{8,9},{9,8},{10,11... | collective-permute-start | bytes 393224 | tf_op jit(solution)/shard_map/ppermute | solution.py:443
  16.3 4.9 %outer.1 = (bf16[64,64,1024]{2,1,0:T(8,128)(2,1)S(1)}, bf16[4,256,2048]{2,1,0:T(8,128)(2,1)S(1)}, bf16[2,256,128]{2,1,0:T(8,128)(2,1)S(1)}, bf16[2,256,128]{2,1,0:T(8,128)(2,1)S(1)}) custom-call(bf16[2,256,128]{2,1,0:T(8,128)(2,1)S(1)} %get-tuple-element.52.refs_0_.held_ref, f32[64,128]{1,0:T(8,128)S(1)} %get-tuple-element.53.refs_1_, ...), custom_call_target="tpu_custom_call" | custom-call | flops 8589934592 | bytes 1048576 | tf_op jit(solution)/shard_map/outer/pallas_call | solution.py:603
  21.3 0.3 collective-permute-start.5
  21.5 0.2 collective-permute-done.4.came_ref
  21.8 0.7 %right_part.2.after.refs_2_ = f32[256,512]{1,0:T(8,128)S(1)} custom-call(f32[1,256,128]{2,1,0:T(8,128)S(1)} %get-tuple-element.56.after.refs_0_, bf16[4,256,2048]{2,1,0:T(8,128)(2,1)S(1)} %get-tuple-element.57.diag_ref, bf16[2,512,2048]{2,1,0:T(8,128)(2,1)S(1)} %get-tuple-element.51.refs_0_, bf16[2,512,2048]{2,1,0:T(8,128)(2,1)S(1)} %inner.1.after.refs_1_), custom_call_target="tpu_custom_call" | custom-call | flops 1000 | bytes 1000 | tf_op jit(solution)/shard_map/right_part/pallas_call | solution.py:625
  22.5 0.1 collective-permute-done.5.came_ref
  22.7 1.1 %collective-permute-start.6 = (bf16[1,256,128]{2,1,0:T(8,128)(2,1)S(1)}, bf16[1,256,128]{2,1,0:T(8,128)(2,1)S(1)}, u32[]{:S(2)}, u32[]{:S(2)}) collective-permute-start(bf16[1,256,128]{2,1,0:T(8,128)(2,1)S(1)} %get-tuple-element.62), channel_id=1, source_target_pairs={{0,8},{4,12},{8,0},{12,4},{1,9},{5,13},{9,1},{13,5},{2,10},{6,14},... | collective-permute-start | bytes 196616 | tf_op jit(solution)/shard_map/ppermute | solution.py:443
  23.8 0.9 %right_part.3.after.acc_first = f32[256,512]{1,0:T(8,128)S(1)} custom-call(f32[1,256,128]{2,1,0:T(8,128)S(1)} %get-tuple-element.61.after.refs_6_, bf16[4,256,2048]{2,1,0:T(8,128)(2,1)S(1)} %get-tuple-element.57.diag_ref, bf16[2,512,2048]{2,1,0:T(8,128)(2,1)S(1)} %get-tuple-element.51.refs_0_, bf16[2,512,2048]{2,1,0:T(8,128)(2,1)S(1)} %inner.1.after.refs_1_, ...), custom_call_target="tpu_custom_call" | custom-call | flops 1000 | bytes 1000 | tf_op jit(solution)/shard_map/right_part/pallas_call | solution.py:625
  24.7 2.1 %collective-permute-start.9 = (bf16[1,256,128]{2,1,0:T(8,128)(2,1)S(1)}, bf16[1,256,128]{2,1,0:T(8,128)(2,1)S(1)}, u32[]{:S(2)}, u32[]{:S(2)}) collective-permute-start(bf16[1,256,128]{2,1,0:T(8,128)(2,1)S(1)} %get-tuple-element.75), channel_id=1, source_target_pairs={{0,2},{1,3},{2,0},{3,1},{4,6},{5,7},{6,4},{7,5},{8,10},{9,11},{10,... | collective-permute-start | bytes 196616 | tf_op jit(solution)/shard_map/ppermute | solution.py:443
  26.9 0.2 collective-permute-done.6.came_ref
  27.1 1.6 %collective-permute-start.7 = (bf16[2,64,128]{2,1,0:T(8,128)(2,1)S(1)}, bf16[2,64,128]{2,1,0:T(8,128)(2,1)S(1)}, u32[]{:S(2)}, u32[]{:S(2)}) collective-permute-start(bf16[2,64,128]{2,1,0:T(8,128)(2,1)S(1)} %get-tuple-element.65), channel_id=1, source_target_pairs={{0,1},{1,0},{2,3},{3,2},{4,5},{5,4},{6,7},{7,6},{8,9},{9,8},{10,11... | collective-permute-start | bytes 98312 | tf_op jit(solution)/shard_map/ppermute | solution.py:443
  28.7 1.8 %right.1 = (bf16[2,256,128]{2,1,0:T(8,128)(2,1)S(1)}, bf16[2,256,128]{2,1,0:T(8,128)(2,1)S(1)}) custom-call(bf16[2,64,128]{2,1,0:T(8,128)(2,1)S(1)} %get-tuple-element.63.after.held_ref, bf16[4,256,2048]{2,1,0:T(8,128)(2,1)S(1)} %get-tuple-element.57.diag_ref, f32[256,512]{1,0:T(8,128)S(1)} %right_part.3.after.acc_first, ...), custom_call_target="tpu_custom_call" | custom-call | flops 8589934592 | bytes 1048576 | tf_op jit(solution)/shard_map/right/pallas_call | solution.py:652
  30.5 0.7 %collective-permute-done.7.came_ref = bf16[2,64,128]{2,1,0:T(8,128)(2,1)S(1)} collective-permute-done((bf16[2,64,128]{2,1,0:T(8,128)(2,1)S(1)}, bf16[2,64,128]{2,1,0:T(8,128)(2,1)S(1)}, u32[]{:S(2)}, u32[]{:S(2)}) %collective-permute-start.7) | collective-permute-done | bytes 32800 | tf_op jit(solution)/shard_map/ppermute | solution.py:443
  31.4 1.4 %collective-permute-start.11 = (bf16[1,64,128]{2,1,0:T(8,128)(2,1)S(1)}, bf16[1,64,128]{2,1,0:T(8,128)(2,1)S(1)}, u32[]{:S(2)}, u32[]{:S(2)}) collective-permute-start(bf16[1,64,128]{2,1,0:T(8,128)(2,1)S(1)} %get-tuple-element.79), channel_id=1, source_target_pairs={{0,2},{1,3},{2,0},{3,1},{4,6},{5,7},{6,4},{7,5},{8,10},{9,11},{10,... | collective-permute-start | bytes 49160 | tf_op jit(solution)/shard_map/ppermute | solution.py:443
  32.9 1.6 %collective-permute-start.10 = (bf16[1,256,128]{2,1,0:T(8,128)(2,1)S(1)}, bf16[1,256,128]{2,1,0:T(8,128)(2,1)S(1)}, u32[]{:S(2)}, u32[]{:S(2)}) collective-permute-start(bf16[1,256,128]{2,1,0:T(8,128)(2,1)S(1)} %get-tuple-element.78), channel_id=1, source_target_pairs={{0,8},{4,12},{8,0},{12,4},{1,9},{5,13},{9,1},{13,5},{2,10},{6,14},... | collective-permute-start | bytes 196616 | tf_op jit(solution)/shard_map/ppermute | solution.py:443
  34.4 3.1 %pair.1 = (bf16[64,64,128]{2,1,0:T(8,128)(2,1)}, f32[16,2048]{1,0:T(8,128)}) custom-call(f32[1,256,128]{2,1,0:T(8,128)S(1)} %get-tuple-element.72.refs_0_, f32[64,128]{1,0:T(8,128)S(1)} %get-tuple-element.53.refs_1_, bf16[64,64,1024]{2,1,0:T(8,128)(2,1)S(1)} %get-tuple-element.73.refs_2_, bf16[1024,128]{1,0:T(8,128)(2,1)S(1)} %get-tuple-element.46.wp_ref.refs_3_, ...), custom_call_target="tpu_custom_call" | custom-call | flops 8589934592 | bytes 1048576 | tf_op jit(solution)/shard_map/pair/pallas_call | solution.py:675
  37.6 0.7 %final_sums.1 = (f32[16,2048]{1,0:T(8,128)}, f32[64,128]{1,0:T(8,128)}) custom-call(bf16[64,64,128]{2,1,0:T(8,128)(2,1)} %get-tuple-element.39.after, f32[64,128]{1,0:T(8,128)S(1)} %get-tuple-element.47.rj_ref, f32[1,2048]{1,0:T(1,128)S(1)} %get-tuple-element.48.keep_ref.refs_2_.refs_5_, f32[1,256,128]{2,1,0:T(8,128)S(1)} %get-tuple-element.72.refs_0_, ...), custom_call_target="tpu_custom_call" | custom-call | flops 1000 | bytes 1000 | tf_op jit(solution)/shard_map/final_sums/pallas_call | solution.py:695
  (20 shorter events, 0.4 us)
Async XLA Ops:
  0.6 8.6 %collective-permute-start = (bf16[1,16,2048]{2,1,0:T(8,128)(2,1)}, bf16[1,16,2048]{2,1,0:T(8,128)(2,1)S(1)}, u32[]{:S(2)}, u32[]{:S(2)}) collective-permute-start(bf16[1,16,2048]{2,1,0:T(8,128)(2,1)} %bitcast.4), channel_id=1, source_target_pairs={{0,2},{1,3},{2,0},{3,1},{4,6},{5,7},{6,4},{7,5},{8,10},{9,11},{10,... | collective-permute-start | bytes 196616 | tf_op jit(solution)/shard_map/ppermute | solution.py:443
  4.7 6.2 %collective-permute-start.1 = (bf16[1,16,2048]{2,1,0:T(8,128)(2,1)}, bf16[1,16,2048]{2,1,0:T(8,128)(2,1)S(1)}, u32[]{:S(2)}, u32[]{:S(2)}) collective-permute-start(bf16[1,16,2048]{2,1,0:T(8,128)(2,1)} %bitcast.5), channel_id=1, source_target_pairs={{0,8},{4,12},{8,0},{12,4},{1,9},{5,13},{9,1},{13,5},{2,10},{6,14},... | collective-permute-start | bytes 196616 | tf_op jit(solution)/shard_map/ppermute | solution.py:443
  9.3 7.0 %collective-permute-start.3 = (bf16[2,16,2048]{2,1,0:T(8,128)(2,1)S(1)}, bf16[2,16,2048]{2,1,0:T(8,128)(2,1)S(1)}, u32[]{:S(2)}, u32[]{:S(2)}) collective-permute-start(bf16[2,16,2048]{2,1,0:T(8,128)(2,1)S(1)} %join.2.after.refs_5_), channel_id=1, source_target_pairs={{0,1},{1,0},{2,3},{3,2},{4,5},{5,4},{6,7},{7,6},{8,9},{9,8},{10,11... | collective-permute-start | bytes 393224 | tf_op jit(solution)/shard_map/ppermute | solution.py:443
  10.9 1.6 %collective-permute-start.2 = (bf16[2,16,2048]{2,1,0:T(8,128)(2,1)S(1)}, bf16[2,16,2048]{2,1,0:T(8,128)(2,1)S(1)}, u32[]{:S(2)}, u32[]{:S(2)}) collective-permute-start(bf16[2,16,2048]{2,1,0:T(8,128)(2,1)S(1)} %join.3.after.right_held), channel_id=1, source_target_pairs={{0,4},{4,0},{8,12},{12,8},{1,5},{5,1},{9,13},{13,9},{2,6},{6,2},{1... | collective-permute-start | bytes 393224 | tf_op jit(solution)/shard_map/ppermute | solution.py:443
  15.8 6.0 %collective-permute-start.4 = (bf16[2,256,128]{2,1,0:T(8,128)(2,1)S(1)}, bf16[2,256,128]{2,1,0:T(8,128)(2,1)S(1)}, u32[]{:S(2)}, u32[]{:S(2)}) collective-permute-start(bf16[2,256,128]{2,1,0:T(8,128)(2,1)S(1)} %get-tuple-element.55), channel_id=1, source_target_pairs={{0,1},{1,0},{2,3},{3,2},{4,5},{5,4},{6,7},{7,6},{8,9},{9,8},{10,11... | collective-permute-start | bytes 393224 | tf_op jit(solution)/shard_map/ppermute | solution.py:443
  21.3 1.4 %collective-permute-start.5 = (bf16[2,256,128]{2,1,0:T(8,128)(2,1)S(1)}, bf16[2,256,128]{2,1,0:T(8,128)(2,1)S(1)}, u32[]{:S(2)}, u32[]{:S(2)}) collective-permute-start(bf16[2,256,128]{2,1,0:T(8,128)(2,1)S(1)} %get-tuple-element.58), channel_id=1, source_target_pairs={{0,4},{4,0},{8,12},{12,8},{1,5},{5,1},{9,13},{13,9},{2,6},{6,2},{1... | collective-permute-start | bytes 393224 | tf_op jit(solution)/shard_map/ppermute | solution.py:443
  22.7 4.3 %collective-permute-start.6 = (bf16[1,256,128]{2,1,0:T(8,128)(2,1)S(1)}, bf16[1,256,128]{2,1,0:T(8,128)(2,1)S(1)}, u32[]{:S(2)}, u32[]{:S(2)}) collective-permute-start(bf16[1,256,128]{2,1,0:T(8,128)(2,1)S(1)} %get-tuple-element.62), channel_id=1, source_target_pairs={{0,8},{4,12},{8,0},{12,4},{1,9},{5,13},{9,1},{13,5},{2,10},{6,14},... | collective-permute-start | bytes 196616 | tf_op jit(solution)/shard_map/ppermute | solution.py:443
  24.7 9.7 %collective-permute-start.9 = (bf16[1,256,128]{2,1,0:T(8,128)(2,1)S(1)}, bf16[1,256,128]{2,1,0:T(8,128)(2,1)S(1)}, u32[]{:S(2)}, u32[]{:S(2)}) collective-permute-start(bf16[1,256,128]{2,1,0:T(8,128)(2,1)S(1)} %get-tuple-element.75), channel_id=1, source_target_pairs={{0,2},{1,3},{2,0},{3,1},{4,6},{5,7},{6,4},{7,5},{8,10},{9,11},{10,... | collective-permute-start | bytes 196616 | tf_op jit(solution)/shard_map/ppermute | solution.py:443
  27.1 4.2 %collective-permute-start.7 = (bf16[2,64,128]{2,1,0:T(8,128)(2,1)S(1)}, bf16[2,64,128]{2,1,0:T(8,128)(2,1)S(1)}, u32[]{:S(2)}, u32[]{:S(2)}) collective-permute-start(bf16[2,64,128]{2,1,0:T(8,128)(2,1)S(1)} %get-tuple-element.65), channel_id=1, source_target_pairs={{0,1},{1,0},{2,3},{3,2},{4,5},{5,4},{6,7},{7,6},{8,9},{9,8},{10,11... | collective-permute-start | bytes 98312 | tf_op jit(solution)/shard_map/ppermute | solution.py:443
  31.3 1.5 %collective-permute-start.8 = (bf16[2,256,128]{2,1,0:T(8,128)(2,1)S(1)}, bf16[2,256,128]{2,1,0:T(8,128)(2,1)S(1)}, u32[]{:S(2)}, u32[]{:S(2)}) collective-permute-start(bf16[2,256,128]{2,1,0:T(8,128)(2,1)S(1)} %get-tuple-element.71), channel_id=1, source_target_pairs={{0,4},{4,0},{8,12},{12,8},{1,5},{5,1},{9,13},{13,9},{2,6},{6,2},{1... | collective-permute-start | bytes 393224 | tf_op jit(solution)/shard_map/ppermute | solution.py:443
  31.4 6.2 %collective-permute-start.11 = (bf16[1,64,128]{2,1,0:T(8,128)(2,1)S(1)}, bf16[1,64,128]{2,1,0:T(8,128)(2,1)S(1)}, u32[]{:S(2)}, u32[]{:S(2)}) collective-permute-start(bf16[1,64,128]{2,1,0:T(8,128)(2,1)S(1)} %get-tuple-element.79), channel_id=1, source_target_pairs={{0,2},{1,3},{2,0},{3,1},{4,6},{5,7},{6,4},{7,5},{8,10},{9,11},{10,... | collective-permute-start | bytes 49160 | tf_op jit(solution)/shard_map/ppermute | solution.py:443
  32.9 4.7 %collective-permute-start.10 = (bf16[1,256,128]{2,1,0:T(8,128)(2,1)S(1)}, bf16[1,256,128]{2,1,0:T(8,128)(2,1)S(1)}, u32[]{:S(2)}, u32[]{:S(2)}) collective-permute-start(bf16[1,256,128]{2,1,0:T(8,128)(2,1)S(1)} %get-tuple-element.78), channel_id=1, source_target_pairs={{0,8},{4,12},{8,0},{12,4},{1,9},{5,13},{9,1},{13,5},{2,10},{6,14},... | collective-permute-start | bytes 196616 | tf_op jit(solution)/shard_map/ppermute | solution.py:443

commit v16 on v15

--- a/solution.py
+++ b/solution.py
@@ -232,12 +232,10 @@
     right_sum(first, last, refs[:parts], diag_ref, refs[-1], *refs[parts:-1])
 
 
-def right_kernel(dims, n_row, first, after, diag_ref, acc_first, *refs):
+def right_kernel(dims, n_row, after, acc, keep_out, send_out, turned, gr_all):
     chans, groups, blocks, i_rows, j_rows, step_rows, sequences = dims
     tiles = sequences * chans // LANES
     j_pad = -(-j_rows // LANES) * LANES
-    z_refs, (keep_out, send_out, acc, turned, gr_all) = refs[:-5], refs[-5:]
-    right_sum(first, i_rows // step_rows, z_refs, diag_ref, acc, acc_first)
     if paired(j_rows):
         half = tiles // 2
         low = lane_group((half, LANES), LANES // 2) == 0
@@ -628,41 +626,37 @@
             out_specs=vmem()[0],
             out_shape=pltpu.VMEM((depth, span), F32),
             compiler_params=params(16),
-            cost_estimate=cost(1000, 1000),
+            cost_estimate=cost(16 * macs, 1000),
             name="right_part",
         )(after, diag, *z, *so_far)
 
-    gw_row, acc = [], []
     right_steps = max(1, steps // 4)
-
-    def weight_rounds(after):
-        acc.append(right_part(0, right_steps, after))
-        gw_row.extend(reduce(*gw_cut, "row", n_row, acc[0]))
-        return gw_row[0]
-
-    gl_last = reduce(*gl_cut, "col", n_col, gw_cut[0], weight_rounds)
-    acc = right_part(right_steps, 2 * right_steps, gl_last[0], acc[0])
+    acc = right_part(0, right_steps, gw_cut[0])
+    gw_row = reduce(*gw_cut, "row", n_row, acc)
+    gl_held = hold(gw_row[0], *gl_cut)
+    acc = right_part(right_steps, steps, gl_held[0], acc)
     gw_turned = small_call(
         functools.partial(turn_kernel, n_col),
         halves(inner // n_row, n_col),
         "turn",
         [pltpu.VMEM((inner // n_row, pair_width), F32)],
     )(acc, *gw_row)
+    gl_last = reduce(*gl_held, "col", n_col, gw_turned[0])
+
 
     gr_cut = pl.pallas_call(
-        functools.partial(right_kernel, dims, n_row, 2 * right_steps),
-        in_specs=[hbm()] + vmem(2 + len(z)),
+        functools.partial(right_kernel, dims, n_row),
+        in_specs=[hbm()] + vmem(),
         out_specs=vmem(2),
         out_shape=halves(j_rows * tiles, n_row),
         scratch_shapes=[
-            pltpu.VMEM((depth, span), F32),
             pltpu.VMEM((width, j_pad), F32),
             pltpu.VMEM((j_rows * tiles, LANES), F32),
         ],
         compiler_params=params(20),
         cost_estimate=cost(16 * macs, 2**20),
         name="right",
-    )(gw_turned[0], diag, acc, *z)
+    )(gl_last[0], acc)
     gr_held = []
 
     def right_rounds(after):

time: 38.6 us -> 39.4 us (1.021)
  waiting for transfers between devices: 1.3 us -> 4.21 us
  starting transfers between devices: 15.9 us -> 13.9 us
    ppermute x12, waiting for transfers between devices: 1.3 us -> 4.21 us  [swap(): return lax.ppermute(array, axis, [(s, s ^ bit) for s in range(n)])]
    ppermute x12, starting transfers between devices: 15.9 us -> 13.9 us  [swap(): return lax.ppermute(array, axis, [(s, s ^ bit) for s in range(n)])]
    pallas_call x1, Pallas kernels: 1.83 us -> 0.68 us  [shards(): pl.pallas_call(functools.partial(right_kernel, dims, n_row), in_specs=[hb...]
    pallas_call x2, Pallas kernels: 1.67 us -> 2.74 us  [right_part(): pl.pallas_call(functools.partial(right_part_kernel, first, last, len(z)),...]
  transfers between devices with their start and end apart: 12 -> 12, of which waited for: 4 -> 5; matrix products, arithmetic and copies ran while one was open for 0% -> 0% of each run, Pallas kernels for 51% -> 37%
where the time goes in v16:
time: 39.4 us; the launch traced here: 39.2 us
  Pallas kernels  20.1 us (51%)
  starting transfers between devices  13.9 us (35%)
  waiting for transfers between devices  4.21 us (11%)
  between operations  0.97 us (2%)
    ppermute x12, starting transfers between devices, swap(): return lax.ppermute(array, axis, [(s, s ^ bit) for s in range(n)])  13.9 us
    pallas_call x1, Pallas kernels, shards(): pl.pallas_call(functools.partial(outer_kernel, dims, n_row, n_col), in_sp...  4.88 us
    ppermute x12, waiting for transfers between devices, swap(): return lax.ppermute(array, axis, [(s, s ^ bit) for s in range(n)])  4.21 us
    pallas_call x1, Pallas kernels, shards(): pl.pallas_call(functools.partial(pair_kernel, dims), in_specs=[hbm()] + v...  3.13 us
    pallas_call x1, Pallas kernels, shards(): pl.pallas_call(functools.partial(scale_kernel, dims), in_specs=[hbm()] *...  3.04 us
    pallas_call x2, Pallas kernels, right_part(): pl.pallas_call(functools.partial(right_part_kernel, first, last, len(z)),...  2.74 us
    pallas_call x1, Pallas kernels, shards(): pl.pallas_call(functools.partial(left_kernel, dims, n_col), in_specs=[hbm...  2.53 us
    pallas_call x1, Pallas kernels, shards(): pl.pallas_call(functools.partial(inner_kernel, dims, early_steps), in_spe...  1.51 us
  transfers between devices with their start and end apart: 12, of which 5 were waited for; matrix products, arithmetic and copies ran while one was open for 0% of the time, Pallas kernels for 37%

profile of v16, /device:TPU:0, one launch (start us, length us, event | category | flops | bytes accessed | tf_op | source)
XLA Modules:
  0.0 39.2 jit_solution(5067191927014225168)
XLA Ops:
  0.6 4.1 %collective-permute-start = (bf16[1,16,2048]{2,1,0:T(8,128)(2,1)}, bf16[1,16,2048]{2,1,0:T(8,128)(2,1)S(1)}, u32[]{:S(2)}, u32[]{:S(2)}) collective-permute-start(bf16[1,16,2048]{2,1,0:T(8,128)(2,1)} %bitcast.4), channel_id=1, source_target_pairs={{0,2},{1,3},{2,0},{3,1},{4,6},{5,7},{6,4},{7,5},{8,10},{9,11},{10,... | collective-permute-start | bytes 196616 | tf_op jit(solution)/shard_map/ppermute | solution.py:441
  4.7 1.5 %collective-permute-start.1 = (bf16[1,16,2048]{2,1,0:T(8,128)(2,1)}, bf16[1,16,2048]{2,1,0:T(8,128)(2,1)S(1)}, u32[]{:S(2)}, u32[]{:S(2)}) collective-permute-start(bf16[1,16,2048]{2,1,0:T(8,128)(2,1)} %bitcast.5), channel_id=1, source_target_pairs={{0,8},{4,12},{8,0},{12,4},{1,9},{5,13},{9,1},{13,5},{2,10},{6,14},... | collective-permute-start | bytes 196616 | tf_op jit(solution)/shard_map/ppermute | solution.py:441
  6.2 3.0 %scale.1 = (bf16[64,64,128]{2,1,0:T(8,128)(2,1)S(1)}, f32[64,128]{1,0:T(8,128)S(1)}, bf16[1024,128]{1,0:T(8,128)(2,1)S(1)}, f32[1,2048]{1,0:T(1,128)S(1)}, f32[6...) custom-call(s32[1,256]{1,0:T(1,128)} %bitcast.6, ...), custom_call_target="tpu_custom_call" | custom-call | flops 1000 | bytes 1000 | tf_op jit(solution)/shard_map/scale/pallas_call | solution.py:537
  9.3 1.6 %collective-permute-start.3 = (bf16[2,16,2048]{2,1,0:T(8,128)(2,1)S(1)}, bf16[2,16,2048]{2,1,0:T(8,128)(2,1)S(1)}, u32[]{:S(2)}, u32[]{:S(2)}) collective-permute-start(bf16[2,16,2048]{2,1,0:T(8,128)(2,1)S(1)} %join.2.after.refs_5_), channel_id=1, source_target_pairs={{0,1},{1,0},{2,3},{3,2},{4,5},{5,4},{6,7},{7,6},{8,9},{9,8},{10,11... | collective-permute-start | bytes 393224 | tf_op jit(solution)/shard_map/ppermute | solution.py:441
  11.0 1.5 %inner.1.after.refs_1_ = bf16[2,512,2048]{2,1,0:T(8,128)(2,1)S(1)} custom-call(bf16[2,16,2048]{2,1,0:T(8,128)(2,1)S(1)} %join.3.after.right_held, bf16[64,64,128]{2,1,0:T(8,128)(2,1)S(1)} %get-tuple-element.45.scaled_ref.refs_3_, bf16[1024,128]{1,0:T(8,128)(2,1)S(1)} %get-tuple-element.46.wp_ref.refs_3_), custom_call_target="tpu_custom_call" | custom-call | flops 8589934592 | bytes 1048576 | tf_op jit(solution)/shard_map/inner/pallas_call | solution.py:569
  12.6 0.7 %right_rows.1 = (bf16[512,256]{1,0:T(8,128)(2,1)S(1)}, bf16[256,512]{1,0:T(8,128)(2,1)S(1)}) custom-call(bf16[2,512,2048]{2,1,0:T(8,128)(2,1)S(1)} %inner.1.after.refs_1_, f32[64,128]{1,0:T(8,128)S(1)} %get-tuple-element.47.rj_ref, f32[1,2048]{1,0:T(1,128)S(1)} %get-tuple-element.48.keep_ref.refs_2_.refs_5_, bf16[2,16,2048]{2,1,0:T(8,128)(2,1)S(1)} %join.3.after.right_held, ...), custom_call_target="tpu_custom_call" | custom-call | flops 8589934592 | bytes 1048576 | tf_op jit(solution)/shard_map/right_rows/pallas_call | solution.py:580
  13.3 2.5 %left.1 = (bf16[2,256,128]{2,1,0:T(8,128)(2,1)S(1)}, bf16[2,256,128]{2,1,0:T(8,128)(2,1)S(1)}) custom-call(bf16[512,256]{1,0:T(8,128)(2,1)S(1)} %get-tuple-element.49.after.refs_4_, bf16[256,512]{1,0:T(8,128)(2,1)S(1)} %get-tuple-element.50.rbt_ref, bf16[2,512,2048]{2,1,0:T(8,128)(2,1)S(1)} %get-tuple-element.51.refs_0_, ...), custom_call_target="tpu_custom_call" | custom-call | flops 8589934592 | bytes 1048576 | tf_op jit(solution)/shard_map/left/pallas_call | solution.py:591
  15.8 4.9 %outer.1 = (bf16[64,64,1024]{2,1,0:T(8,128)(2,1)S(1)}, bf16[4,256,2048]{2,1,0:T(8,128)(2,1)S(1)}, bf16[2,256,128]{2,1,0:T(8,128)(2,1)S(1)}, bf16[2,256,128]{2,1,0:T(8,128)(2,1)S(1)}) custom-call(bf16[2,256,128]{2,1,0:T(8,128)(2,1)S(1)} %get-tuple-element.52.refs_0_, f32[64,128]{1,0:T(8,128)S(1)} %get-tuple-element.53.refs_1_, ...), custom_call_target="tpu_custom_call" | custom-call | flops 8589934592 | bytes 1048576 | tf_op jit(solution)/shard_map/outer/pallas_call | solution.py:601
  20.7 0.6 %collective-permute-start.4 = (bf16[2,256,128]{2,1,0:T(8,128)(2,1)S(1)}, bf16[2,256,128]{2,1,0:T(8,128)(2,1)S(1)}, u32[]{:S(2)}, u32[]{:S(2)}) collective-permute-start(bf16[2,256,128]{2,1,0:T(8,128)(2,1)S(1)} %get-tuple-element.56), channel_id=1, source_target_pairs={{0,4},{4,0},{8,12},{12,8},{1,5},{5,1},{9,13},{13,9},{2,6},{6,2},{1... | collective-permute-start | bytes 393224 | tf_op jit(solution)/shard_map/ppermute | solution.py:441
  21.3 0.7 %right_part.2.after.refs_2_ = f32[256,512]{1,0:T(8,128)S(1)} custom-call(bf16[2,256,128]{2,1,0:T(8,128)(2,1)S(1)} %get-tuple-element.54.after.held_ref, bf16[4,256,2048]{2,1,0:T(8,128)(2,1)S(1)} %get-tuple-element.55.diag_ref, bf16[2,512,2048]{2,1,0:T(8,128)(2,1)S(1)} %get-tuple-element.51.refs_0_, bf16[2,512,2048]{2,1,0:T(8,128)(2,1)S(1)} %inner.1.after.refs_1_), custom_call_target="tpu_custom_call" | custom-call | flops 8589934592 | bytes 1000 | tf_op jit(solution)/shard_map/right_part/pallas_call | solution.py:623
  22.0 0.2 collective-permute-done.4.came_ref
  22.3 0.6 %collective-permute-start.5 = (bf16[1,256,128]{2,1,0:T(8,128)(2,1)S(1)}, bf16[1,256,128]{2,1,0:T(8,128)(2,1)S(1)}, u32[]{:S(2)}, u32[]{:S(2)}) collective-permute-start(bf16[1,256,128]{2,1,0:T(8,128)(2,1)S(1)} %get-tuple-element.60), channel_id=1, source_target_pairs={{0,8},{4,12},{8,0},{12,4},{1,9},{5,13},{9,1},{13,5},{2,10},{6,14},... | collective-permute-start | bytes 196616 | tf_op jit(solution)/shard_map/ppermute | solution.py:441
  22.9 1.0 %collective-permute-start.6 = (bf16[2,256,128]{2,1,0:T(8,128)(2,1)S(1)}, bf16[2,256,128]{2,1,0:T(8,128)(2,1)S(1)}, u32[]{:S(2)}, u32[]{:S(2)}) collective-permute-start(bf16[2,256,128]{2,1,0:T(8,128)(2,1)S(1)} %get-tuple-element.62), channel_id=1, source_target_pairs={{0,1},{1,0},{2,3},{3,2},{4,5},{5,4},{6,7},{7,6},{8,9},{9,8},{10,11... | collective-permute-start | bytes 393224 | tf_op jit(solution)/shard_map/ppermute | solution.py:441
  23.9 2.0 %right_part.3.after.acc = f32[256,512]{1,0:T(8,128)S(1)} custom-call(bf16[2,256,128]{2,1,0:T(8,128)(2,1)S(1)} %get-tuple-element.59.after.held_ref, bf16[4,256,2048]{2,1,0:T(8,128)(2,1)S(1)} %get-tuple-element.55.diag_ref, bf16[2,512,2048]{2,1,0:T(8,128)(2,1)S(1)} %get-tuple-element.51.refs_0_, bf16[2,512,2048]{2,1,0:T(8,128)(2,1)S(1)} %inner.1.after.refs_1_, ...), custom_call_target="tpu_custom_call" | custom-call | flops 8589934592 | bytes 1000 | tf_op jit(solution)/shard_map/right_part/pallas_call | solution.py:623
  25.9 0.8 %collective-permute-done.5.came_ref = bf16[1,256,128]{2,1,0:T(8,128)(2,1)S(1)} collective-permute-done((bf16[1,256,128]{2,1,0:T(8,128)(2,1)S(1)}, bf16[1,256,128]{2,1,0:T(8,128)(2,1)S(1)}, u32[]{:S(2)}, u32[]{:S(2)}) %collective-permute-start.5) | collective-permute-done | bytes 65568 | tf_op jit(solution)/shard_map/ppermute | solution.py:441
  26.7 0.5 %collective-permute-start.7 = (bf16[2,64,128]{2,1,0:T(8,128)(2,1)S(1)}, bf16[2,64,128]{2,1,0:T(8,128)(2,1)S(1)}, u32[]{:S(2)}, u32[]{:S(2)}) collective-permute-start(bf16[2,64,128]{2,1,0:T(8,128)(2,1)S(1)} %get-tuple-element.65), channel_id=1, source_target_pairs={{0,1},{1,0},{2,3},{3,2},{4,5},{5,4},{6,7},{7,6},{8,9},{9,8},{10,11... | collective-permute-start | bytes 98312 | tf_op jit(solution)/shard_map/ppermute | solution.py:441
  27.2 1.2 %collective-permute-done.6.came_ref = bf16[2,256,128]{2,1,0:T(8,128)(2,1)S(1)} collective-permute-done((bf16[2,256,128]{2,1,0:T(8,128)(2,1)S(1)}, bf16[2,256,128]{2,1,0:T(8,128)(2,1)S(1)}, u32[]{:S(2)}, u32[]{:S(2)}) %collective-permute-start.6) | collective-permute-done | bytes 131104 | tf_op jit(solution)/shard_map/ppermute | solution.py:441
  28.5 0.7 %right.1 = (bf16[2,256,128]{2,1,0:T(8,128)(2,1)S(1)}, bf16[2,256,128]{2,1,0:T(8,128)(2,1)S(1)}) custom-call(f32[1,256,128]{2,1,0:T(8,128)S(1)} %get-tuple-element.63.after.refs_6_, f32[256,512]{1,0:T(8,128)S(1)} %right_part.3.after.acc), custom_call_target="tpu_custom_call" | custom-call | flops 8589934592 | bytes 1048576 | tf_op jit(solution)/shard_map/right/pallas_call | solution.py:647
  29.2 3.0 %collective-permute-start.9 = (bf16[1,256,128]{2,1,0:T(8,128)(2,1)S(1)}, bf16[1,256,128]{2,1,0:T(8,128)(2,1)S(1)}, u32[]{:S(2)}, u32[]{:S(2)}) collective-permute-start(bf16[1,256,128]{2,1,0:T(8,128)(2,1)S(1)} %get-tuple-element.75), channel_id=1, source_target_pairs={{0,2},{1,3},{2,0},{3,1},{4,6},{5,7},{6,4},{7,5},{8,10},{9,11},{10,... | collective-permute-start | bytes 196616 | tf_op jit(solution)/shard_map/ppermute | solution.py:441
  32.6 1.1 %collective-permute-done.8.came_ref = bf16[2,256,128]{2,1,0:T(8,128)(2,1)S(1)} collective-permute-done((bf16[2,256,128]{2,1,0:T(8,128)(2,1)S(1)}, bf16[2,256,128]{2,1,0:T(8,128)(2,1)S(1)}, u32[]{:S(2)}, u32[]{:S(2)}) %collective-permute-start.8) | collective-permute-done | bytes 131104 | tf_op jit(solution)/shard_map/ppermute | solution.py:441
  33.7 0.6 %collective-permute-start.10 = (bf16[1,256,128]{2,1,0:T(8,128)(2,1)S(1)}, bf16[1,256,128]{2,1,0:T(8,128)(2,1)S(1)}, u32[]{:S(2)}, u32[]{:S(2)}) collective-permute-start(bf16[1,256,128]{2,1,0:T(8,128)(2,1)S(1)} %get-tuple-element.78), channel_id=1, source_target_pairs={{0,8},{4,12},{8,0},{12,4},{1,9},{5,13},{9,1},{13,5},{2,10},{6,14},... | collective-permute-start | bytes 196616 | tf_op jit(solution)/shard_map/ppermute | solution.py:441
  34.3 0.9 %collective-permute-done.9.refs_7_ = bf16[1,256,128]{2,1,0:T(8,128)(2,1)S(1)} collective-permute-done((bf16[1,256,128]{2,1,0:T(8,128)(2,1)S(1)}, bf16[1,256,128]{2,1,0:T(8,128)(2,1)S(1)}, u32[]{:S(2)}, u32[]{:S(2)}) %collective-permute-start.9) | collective-permute-done | bytes 65568 | tf_op jit(solution)/shard_map/ppermute | solution.py:441
  35.2 3.1 %pair.1 = (bf16[64,64,128]{2,1,0:T(8,128)(2,1)}, f32[16,2048]{1,0:T(8,128)}) custom-call(f32[1,256,128]{2,1,0:T(8,128)S(1)} %get-tuple-element.72.refs_0_, f32[64,128]{1,0:T(8,128)S(1)} %get-tuple-element.53.refs_1_, bf16[64,64,1024]{2,1,0:T(8,128)(2,1)S(1)} %get-tuple-element.73.refs_2_, bf16[1024,128]{1,0:T(8,128)(2,1)S(1)} %get-tuple-element.46.wp_ref.refs_3_, ...), custom_call_target="tpu_custom_call" | custom-call | flops 8589934592 | bytes 1048576 | tf_op jit(solution)/shard_map/pair/pallas_call | solution.py:669
  38.3 0.7 %final_sums.1 = (f32[16,2048]{1,0:T(8,128)}, f32[64,128]{1,0:T(8,128)}) custom-call(bf16[64,64,128]{2,1,0:T(8,128)(2,1)} %get-tuple-element.39.after, f32[64,128]{1,0:T(8,128)S(1)} %get-tuple-element.47.rj_ref, f32[1,2048]{1,0:T(1,128)S(1)} %get-tuple-element.48.keep_ref.refs_2_.refs_5_, f32[1,256,128]{2,1,0:T(8,128)S(1)} %get-tuple-element.72.refs_0_, ...), custom_call_target="tpu_custom_call" | custom-call | flops 1000 | bytes 1000 | tf_op jit(solution)/shard_map/final_sums/pallas_call | solution.py:689
  (20 shorter events, 0.6 us)
Async XLA Ops:
  0.6 8.6 %collective-permute-start = (bf16[1,16,2048]{2,1,0:T(8,128)(2,1)}, bf16[1,16,2048]{2,1,0:T(8,128)(2,1)S(1)}, u32[]{:S(2)}, u32[]{:S(2)}) collective-permute-start(bf16[1,16,2048]{2,1,0:T(8,128)(2,1)} %bitcast.4), channel_id=1, source_target_pairs={{0,2},{1,3},{2,0},{3,1},{4,6},{5,7},{6,4},{7,5},{8,10},{9,11},{10,... | collective-permute-start | bytes 196616 | tf_op jit(solution)/shard_map/ppermute | solution.py:441
  4.7 6.2 %collective-permute-start.1 = (bf16[1,16,2048]{2,1,0:T(8,128)(2,1)}, bf16[1,16,2048]{2,1,0:T(8,128)(2,1)S(1)}, u32[]{:S(2)}, u32[]{:S(2)}) collective-permute-start(bf16[1,16,2048]{2,1,0:T(8,128)(2,1)} %bitcast.5), channel_id=1, source_target_pairs={{0,8},{4,12},{8,0},{12,4},{1,9},{5,13},{9,1},{13,5},{2,10},{6,14},... | collective-permute-start | bytes 196616 | tf_op jit(solution)/shard_map/ppermute | solution.py:441
  9.3 6.5 %collective-permute-start.3 = (bf16[2,16,2048]{2,1,0:T(8,128)(2,1)S(1)}, bf16[2,16,2048]{2,1,0:T(8,128)(2,1)S(1)}, u32[]{:S(2)}, u32[]{:S(2)}) collective-permute-start(bf16[2,16,2048]{2,1,0:T(8,128)(2,1)S(1)} %join.2.after.refs_5_), channel_id=1, source_target_pairs={{0,1},{1,0},{2,3},{3,2},{4,5},{5,4},{6,7},{7,6},{8,9},{9,8},{10,11... | collective-permute-start | bytes 393224 | tf_op jit(solution)/shard_map/ppermute | solution.py:441
  11.0 1.6 %collective-permute-start.2 = (bf16[2,16,2048]{2,1,0:T(8,128)(2,1)S(1)}, bf16[2,16,2048]{2,1,0:T(8,128)(2,1)S(1)}, u32[]{:S(2)}, u32[]{:S(2)}) collective-permute-start(bf16[2,16,2048]{2,1,0:T(8,128)(2,1)S(1)} %join.3.after.right_held), channel_id=1, source_target_pairs={{0,4},{4,0},{8,12},{12,8},{1,5},{5,1},{9,13},{13,9},{2,6},{6,2},{1... | collective-permute-start | bytes 393224 | tf_op jit(solution)/shard_map/ppermute | solution.py:441
  20.7 1.5 %collective-permute-start.4 = (bf16[2,256,128]{2,1,0:T(8,128)(2,1)S(1)}, bf16[2,256,128]{2,1,0:T(8,128)(2,1)S(1)}, u32[]{:S(2)}, u32[]{:S(2)}) collective-permute-start(bf16[2,256,128]{2,1,0:T(8,128)(2,1)S(1)} %get-tuple-element.56), channel_id=1, source_target_pairs={{0,4},{4,0},{8,12},{12,8},{1,5},{5,1},{9,13},{13,9},{2,6},{6,2},{1... | collective-permute-start | bytes 393224 | tf_op jit(solution)/shard_map/ppermute | solution.py:441
  22.3 4.4 %collective-permute-start.5 = (bf16[1,256,128]{2,1,0:T(8,128)(2,1)S(1)}, bf16[1,256,128]{2,1,0:T(8,128)(2,1)S(1)}, u32[]{:S(2)}, u32[]{:S(2)}) collective-permute-start(bf16[1,256,128]{2,1,0:T(8,128)(2,1)S(1)} %get-tuple-element.60), channel_id=1, source_target_pairs={{0,8},{4,12},{8,0},{12,4},{1,9},{5,13},{9,1},{13,5},{2,10},{6,14},... | collective-permute-start | bytes 196616 | tf_op jit(solution)/shard_map/ppermute | solution.py:441
  22.9 5.5 %collective-permute-start.6 = (bf16[2,256,128]{2,1,0:T(8,128)(2,1)S(1)}, bf16[2,256,128]{2,1,0:T(8,128)(2,1)S(1)}, u32[]{:S(2)}, u32[]{:S(2)}) collective-permute-start(bf16[2,256,128]{2,1,0:T(8,128)(2,1)S(1)} %get-tuple-element.62), channel_id=1, source_target_pairs={{0,1},{1,0},{2,3},{3,2},{4,5},{5,4},{6,7},{7,6},{8,9},{9,8},{10,11... | collective-permute-start | bytes 393224 | tf_op jit(solution)/shard_map/ppermute | solution.py:441
  26.7 5.5 %collective-permute-start.7 = (bf16[2,64,128]{2,1,0:T(8,128)(2,1)S(1)}, bf16[2,64,128]{2,1,0:T(8,128)(2,1)S(1)}, u32[]{:S(2)}, u32[]{:S(2)}) collective-permute-start(bf16[2,64,128]{2,1,0:T(8,128)(2,1)S(1)} %get-tuple-element.65), channel_id=1, source_target_pairs={{0,1},{1,0},{2,3},{3,2},{4,5},{5,4},{6,7},{7,6},{8,9},{9,8},{10,11... | collective-permute-start | bytes 98312 | tf_op jit(solution)/shard_map/ppermute | solution.py:441
  29.2 6.0 %collective-permute-start.9 = (bf16[1,256,128]{2,1,0:T(8,128)(2,1)S(1)}, bf16[1,256,128]{2,1,0:T(8,128)(2,1)S(1)}, u32[]{:S(2)}, u32[]{:S(2)}) collective-permute-start(bf16[1,256,128]{2,1,0:T(8,128)(2,1)S(1)} %get-tuple-element.75), channel_id=1, source_target_pairs={{0,2},{1,3},{2,0},{3,1},{4,6},{5,7},{6,4},{7,5},{8,10},{9,11},{10,... | collective-permute-start | bytes 196616 | tf_op jit(solution)/shard_map/ppermute | solution.py:441
  32.3 1.4 %collective-permute-start.8 = (bf16[2,256,128]{2,1,0:T(8,128)(2,1)S(1)}, bf16[2,256,128]{2,1,0:T(8,128)(2,1)S(1)}, u32[]{:S(2)}, u32[]{:S(2)}) collective-permute-start(bf16[2,256,128]{2,1,0:T(8,128)(2,1)S(1)} %get-tuple-element.71), channel_id=1, source_target_pairs={{0,4},{4,0},{8,12},{12,8},{1,5},{5,1},{9,13},{13,9},{2,6},{6,2},{1... | collective-permute-start | bytes 393224 | tf_op jit(solution)/shard_map/ppermute | solution.py:441
  32.4 6.0 %collective-permute-start.11 = (bf16[1,64,128]{2,1,0:T(8,128)(2,1)S(1)}, bf16[1,64,128]{2,1,0:T(8,128)(2,1)S(1)}, u32[]{:S(2)}, u32[]{:S(2)}) collective-permute-start(bf16[1,64,128]{2,1,0:T(8,128)(2,1)S(1)} %get-tuple-element.79), channel_id=1, source_target_pairs={{0,2},{1,3},{2,0},{3,1},{4,6},{5,7},{6,4},{7,5},{8,10},{9,11},{10,... | collective-permute-start | bytes 49160 | tf_op jit(solution)/shard_map/ppermute | solution.py:441
  33.7 4.6 %collective-permute-start.10 = (bf16[1,256,128]{2,1,0:T(8,128)(2,1)S(1)}, bf16[1,256,128]{2,1,0:T(8,128)(2,1)S(1)}, u32[]{:S(2)}, u32[]{:S(2)}) collective-permute-start(bf16[1,256,128]{2,1,0:T(8,128)(2,1)S(1)} %get-tuple-element.78), channel_id=1, source_target_pairs={{0,8},{4,12},{8,0},{12,4},{1,9},{5,13},{9,1},{13,5},{2,10},{6,14},... | collective-permute-start | bytes 196616 | tf_op jit(solution)/shard_map/ppermute | solution.py:441

commit v17 on v15

--- a/solution.py
+++ b/solution.py
@@ -450,12 +450,14 @@
     return held, [k ^ 1 for k in held]
 
 
-def gather(block, own, axis, n, after):
+def gather(block, own, axis, n, after, flops=1000):
     held, sent, bit = own, block[None], n // 2
     while bit > 1:
         came = swap(sent, axis, n, bit)
         shape = (2 * held.shape[0],) + held.shape[1:]
-        held = small_call(join_kernel, [pltpu.VMEM(shape, BF16)], "join")(after, held, came)[0]
+        held = small_call(join_kernel, [pltpu.VMEM(shape, BF16)], "join", (), flops)(
+            after, held, came
+        )[0]
         sent, bit = held, bit // 2
     return held, swap(sent, axis, n, 1)
 
@@ -565,8 +567,7 @@
         name="scale",
     )(*map(in_hbm, (*mask_row, cotangent, out_weight, left_act, right_act)))
 
-    lefts = gather(left_act, own_l, "col", n_col, own_l)
-    rights = gather(right_act, own_r, "row", n_row, lefts[0])
+    rights = gather(right_act, own_r, "row", n_row, own_r)
 
     z_last = pl.pallas_call(
         functools.partial(inner_kernel, dims, early_steps),
@@ -574,10 +575,11 @@
         out_specs=vmem()[0],
         out_shape=pltpu.VMEM((steps - early_steps, span, step_rows * LANES), BF16),
         compiler_params=params(16),
-        cost_estimate=cost(16 * macs, 2**20),
+        cost_estimate=cost(1000, 1000),
         name="inner",
     )(rights[0], scaled, weight)
     z = (z_first, z_last)
+    lefts = gather(left_act, own_l, "col", n_col, z_last, 10**10)
 
     rbig, right_turned = pl.pallas_call(
         functools.partial(right_rows_kernel, dims, n_row),
@@ -588,7 +590,7 @@
         compiler_params=params(12),
         cost_estimate=cost(16 * macs, 2**20),
         name="right_rows",
-    )(z_last, j_keep, keep, *rights)
+    )(lefts[0], j_keep, keep, *rights)
 
     gl_cut = pl.pallas_call(
         functools.partial(left_kernel, dims, n_col),

time: 38.6 us -> 38.6 us (level)
  waiting for transfers between devices: 1.3 us -> 5.15 us
  starting transfers between devices: 15.9 us -> 12.1 us
    ppermute x12, starting transfers between devices: 15.9 us -> 12.1 us  [swap(): return lax.ppermute(array, axis, [(s, s ^ bit) for s in range(n)])]
    ppermute x12, waiting for transfers between devices: 1.3 us -> 5.15 us  [swap(): return lax.ppermute(array, axis, [(s, s ^ bit) for s in range(n)])]
  transfers between devices with their start and end apart: 12 -> 12, of which waited for: 4 -> 6; matrix products, arithmetic and copies ran while one was open for 0% -> 0% of each run, Pallas kernels for 51% -> 51%
where the time goes in v17:
time: 38.6 us; the launch traced here: 38.4 us
  Pallas kernels  20.2 us (52%)
  starting transfers between devices  12.1 us (31%)
  waiting for transfers between devices  5.15 us (13%)
  between operations  0.98 us (3%)
    ppermute x12, starting transfers between devices, swap(): return lax.ppermute(array, axis, [(s, s ^ bit) for s in range(n)])  12.1 us
    ppermute x12, waiting for transfers between devices, swap(): return lax.ppermute(array, axis, [(s, s ^ bit) for s in range(n)])  5.15 us
    pallas_call x1, Pallas kernels, shards(): pl.pallas_call(functools.partial(outer_kernel, dims, n_row, n_col), in_sp...  4.89 us
    pallas_call x1, Pallas kernels, shards(): pl.pallas_call(functools.partial(pair_kernel, dims), in_specs=[hbm()] + v...  3.13 us
    pallas_call x1, Pallas kernels, shards(): pl.pallas_call(functools.partial(scale_kernel, dims), in_specs=[hbm()] *...  3.02 us
    pallas_call x1, Pallas kernels, shards(): pl.pallas_call(functools.partial(left_kernel, dims, n_col), in_specs=[hbm...  2.53 us
    pallas_call x1, Pallas kernels, shards(): pl.pallas_call(functools.partial(right_kernel, dims, n_row, 2 * right_ste...  1.83 us
    pallas_call x2, Pallas kernels, right_part(): pl.pallas_call(functools.partial(right_part_kernel, first, last, len(z)),...  1.67 us
  transfers between devices with their start and end apart: 12, of which 6 were waited for; matrix products, arithmetic and copies ran while one was open for 0% of the time, Pallas kernels for 51%

profile of v17, /device:TPU:0, one launch (start us, length us, event | category | flops | bytes accessed | tf_op | source)
XLA Modules:
  0.0 38.4 jit_solution(5212897226764732027)
XLA Ops:
  0.6 3.0 %collective-permute-start = (bf16[1,16,2048]{2,1,0:T(8,128)(2,1)}, bf16[1,16,2048]{2,1,0:T(8,128)(2,1)S(1)}, u32[]{:S(2)}, u32[]{:S(2)}) collective-permute-start(bf16[1,16,2048]{2,1,0:T(8,128)(2,1)} %bitcast.4), channel_id=1, source_target_pairs={{0,8},{4,12},{8,0},{12,4},{1,9},{5,13},{9,1},{13,5},{2,10},{6,14},... | collective-permute-start | bytes 196616 | tf_op jit(solution)/shard_map/ppermute | solution.py:443
  3.6 2.6 %collective-permute-start.1 = (bf16[1,16,2048]{2,1,0:T(8,128)(2,1)}, bf16[1,16,2048]{2,1,0:T(8,128)(2,1)S(1)}, u32[]{:S(2)}, u32[]{:S(2)}) collective-permute-start(bf16[1,16,2048]{2,1,0:T(8,128)(2,1)} %bitcast.5), channel_id=1, source_target_pairs={{0,2},{1,3},{2,0},{3,1},{4,6},{5,7},{6,4},{7,5},{8,10},{9,11},{10,... | collective-permute-start | bytes 196616 | tf_op jit(solution)/shard_map/ppermute | solution.py:443
  6.2 3.0 %scale.1 = (bf16[64,64,128]{2,1,0:T(8,128)(2,1)S(1)}, f32[64,128]{1,0:T(8,128)S(1)}, bf16[1024,128]{1,0:T(8,128)(2,1)S(1)}, f32[1,2048]{1,0:T(1,128)S(1)}, f32[6...) custom-call(s32[1,256]{1,0:T(1,128)} %bitcast.6, ...), custom_call_target="tpu_custom_call" | custom-call | flops 1000 | bytes 1000 | tf_op jit(solution)/shard_map/scale/pallas_call | solution.py:541
  9.4 1.5 %inner.1.after.refs_1_ = bf16[2,512,2048]{2,1,0:T(8,128)(2,1)S(1)} custom-call(bf16[2,16,2048]{2,1,0:T(8,128)(2,1)S(1)} %join.2.after.right_held, bf16[64,64,128]{2,1,0:T(8,128)(2,1)S(1)} %get-tuple-element.44.scaled_ref.refs_3_, bf16[1024,128]{1,0:T(8,128)(2,1)S(1)} %get-tuple-element.45.wp_ref.refs_3_), custom_call_target="tpu_custom_call" | custom-call | flops 1000 | bytes 1000 | tf_op jit(solution)/shard_map/inner/pallas_call | solution.py:572
  10.9 1.6 %collective-permute-start.3 = (bf16[2,16,2048]{2,1,0:T(8,128)(2,1)S(1)}, bf16[2,16,2048]{2,1,0:T(8,128)(2,1)S(1)}, u32[]{:S(2)}, u32[]{:S(2)}) collective-permute-start(bf16[2,16,2048]{2,1,0:T(8,128)(2,1)S(1)} %join.3.after.refs_5_), channel_id=1, source_target_pairs={{0,1},{1,0},{2,3},{3,2},{4,5},{5,4},{6,7},{7,6},{8,9},{9,8},{10,11... | collective-permute-start | bytes 393224 | tf_op jit(solution)/shard_map/ppermute | solution.py:443
  12.6 0.7 %right_rows.1 = (bf16[512,256]{1,0:T(8,128)(2,1)S(1)}, bf16[256,512]{1,0:T(8,128)(2,1)S(1)}) custom-call(bf16[2,16,2048]{2,1,0:T(8,128)(2,1)S(1)} %join.3.after.refs_5_, f32[64,128]{1,0:T(8,128)S(1)} %get-tuple-element.47.rj_ref, f32[1,2048]{1,0:T(1,128)S(1)} %get-tuple-element.48.keep_ref.refs_2_.refs_5_, bf16[2,16,2048]{2,1,0:T(8,128)(2,1)S(1)} %join.2.after.right_held, ...), custom_call_target="tpu_custom_call" | custom-call | flops 8589934592 | bytes 1048576 | tf_op jit(solution)/shard_map/right_rows/pallas_call | solution.py:584
  13.3 2.5 %left.1 = (bf16[2,256,128]{2,1,0:T(8,128)(2,1)S(1)}, bf16[2,256,128]{2,1,0:T(8,128)(2,1)S(1)}) custom-call(bf16[512,256]{1,0:T(8,128)(2,1)S(1)} %get-tuple-element.49.after.refs_4_, bf16[256,512]{1,0:T(8,128)(2,1)S(1)} %get-tuple-element.50.rbt_ref, bf16[2,512,2048]{2,1,0:T(8,128)(2,1)S(1)} %get-tuple-element.51.refs_0_, ...), custom_call_target="tpu_custom_call" | custom-call | flops 8589934592 | bytes 1048576 | tf_op jit(solution)/shard_map/left/pallas_call | solution.py:595
  15.8 0.5 %collective-permute-start.4 = (bf16[2,256,128]{2,1,0:T(8,128)(2,1)S(1)}, bf16[2,256,128]{2,1,0:T(8,128)(2,1)S(1)}, u32[]{:S(2)}, u32[]{:S(2)}) collective-permute-start(bf16[2,256,128]{2,1,0:T(8,128)(2,1)S(1)} %get-tuple-element.55), channel_id=1, source_target_pairs={{0,1},{1,0},{2,3},{3,2},{4,5},{5,4},{6,7},{7,6},{8,9},{9,8},{10,11... | collective-permute-start | bytes 393224 | tf_op jit(solution)/shard_map/ppermute | solution.py:443
  16.3 0.6 %collective-permute-done.3.refs_6_ = bf16[2,16,2048]{2,1,0:T(8,128)(2,1)S(1)} collective-permute-done((bf16[2,16,2048]{2,1,0:T(8,128)(2,1)S(1)}, bf16[2,16,2048]{2,1,0:T(8,128)(2,1)S(1)}, u32[]{:S(2)}, u32[]{:S(2)}) %collective-permute-start.3) | collective-permute-done | bytes 131104 | tf_op jit(solution)/shard_map/ppermute | solution.py:443
  16.9 4.9 %outer.1 = (bf16[64,64,1024]{2,1,0:T(8,128)(2,1)S(1)}, bf16[4,256,2048]{2,1,0:T(8,128)(2,1)S(1)}, bf16[2,256,128]{2,1,0:T(8,128)(2,1)S(1)}, bf16[2,256,128]{2,1,0:T(8,128)(2,1)S(1)}) custom-call(bf16[2,256,128]{2,1,0:T(8,128)(2,1)S(1)} %get-tuple-element.52.refs_0_.held_ref, f32[64,128]{1,0:T(8,128)S(1)} %get-tuple-element.53.refs_1_, ...), custom_call_target="tpu_custom_call" | custom-call | flops 8589934592 | bytes 1048576 | tf_op jit(solution)/shard_map/outer/pallas_call | solution.py:605
  21.9 0.7 %right_part.2.after.refs_2_ = f32[256,512]{1,0:T(8,128)S(1)} custom-call(f32[1,256,128]{2,1,0:T(8,128)S(1)} %get-tuple-element.56.after.refs_0_, bf16[4,256,2048]{2,1,0:T(8,128)(2,1)S(1)} %get-tuple-element.57.diag_ref, bf16[2,512,2048]{2,1,0:T(8,128)(2,1)S(1)} %get-tuple-element.51.refs_0_, bf16[2,512,2048]{2,1,0:T(8,128)(2,1)S(1)} %inner.1.after.refs_1_), custom_call_target="tpu_custom_call" | custom-call | flops 1000 | bytes 1000 | tf_op jit(solution)/shard_map/right_part/pallas_call | solution.py:627
  22.6 0.5 %collective-permute-done.5.came_ref = bf16[2,256,128]{2,1,0:T(8,128)(2,1)S(1)} collective-permute-done((bf16[2,256,128]{2,1,0:T(8,128)(2,1)S(1)}, bf16[2,256,128]{2,1,0:T(8,128)(2,1)S(1)}, u32[]{:S(2)}, u32[]{:S(2)}) %collective-permute-start.5) | collective-permute-done | bytes 131104 | tf_op jit(solution)/shard_map/ppermute | solution.py:443
  23.2 0.6 %collective-permute-start.6 = (bf16[1,256,128]{2,1,0:T(8,128)(2,1)S(1)}, bf16[1,256,128]{2,1,0:T(8,128)(2,1)S(1)}, u32[]{:S(2)}, u32[]{:S(2)}) collective-permute-start(bf16[1,256,128]{2,1,0:T(8,128)(2,1)S(1)} %get-tuple-element.62), channel_id=1, source_target_pairs={{0,8},{4,12},{8,0},{12,4},{1,9},{5,13},{9,1},{13,5},{2,10},{6,14},... | collective-permute-start | bytes 196616 | tf_op jit(solution)/shard_map/ppermute | solution.py:443
  23.8 0.9 %right_part.3.after.acc_first = f32[256,512]{1,0:T(8,128)S(1)} custom-call(f32[1,256,128]{2,1,0:T(8,128)S(1)} %get-tuple-element.61.after.refs_6_, bf16[4,256,2048]{2,1,0:T(8,128)(2,1)S(1)} %get-tuple-element.57.diag_ref, bf16[2,512,2048]{2,1,0:T(8,128)(2,1)S(1)} %get-tuple-element.51.refs_0_, bf16[2,512,2048]{2,1,0:T(8,128)(2,1)S(1)} %inner.1.after.refs_1_, ...), custom_call_target="tpu_custom_call" | custom-call | flops 1000 | bytes 1000 | tf_op jit(solution)/shard_map/right_part/pallas_call | solution.py:627
  24.8 1.0 %collective-permute-start.9 = (bf16[1,256,128]{2,1,0:T(8,128)(2,1)S(1)}, bf16[1,256,128]{2,1,0:T(8,128)(2,1)S(1)}, u32[]{:S(2)}, u32[]{:S(2)}) collective-permute-start(bf16[1,256,128]{2,1,0:T(8,128)(2,1)S(1)} %get-tuple-element.75), channel_id=1, source_target_pairs={{0,2},{1,3},{2,0},{3,1},{4,6},{5,7},{6,4},{7,5},{8,10},{9,11},{10,... | collective-permute-start | bytes 196616 | tf_op jit(solution)/shard_map/ppermute | solution.py:443
  25.7 1.8 %collective-permute-done.6.came_ref = bf16[1,256,128]{2,1,0:T(8,128)(2,1)S(1)} collective-permute-done((bf16[1,256,128]{2,1,0:T(8,128)(2,1)S(1)}, bf16[1,256,128]{2,1,0:T(8,128)(2,1)S(1)}, u32[]{:S(2)}, u32[]{:S(2)}) %collective-permute-start.6) | collective-permute-done | bytes 65568 | tf_op jit(solution)/shard_map/ppermute | solution.py:443
  27.6 1.6 %collective-permute-start.7 = (bf16[2,64,128]{2,1,0:T(8,128)(2,1)S(1)}, bf16[2,64,128]{2,1,0:T(8,128)(2,1)S(1)}, u32[]{:S(2)}, u32[]{:S(2)}) collective-permute-start(bf16[2,64,128]{2,1,0:T(8,128)(2,1)S(1)} %get-tuple-element.65), channel_id=1, source_target_pairs={{0,1},{1,0},{2,3},{3,2},{4,5},{5,4},{6,7},{7,6},{8,9},{9,8},{10,11... | collective-permute-start | bytes 98312 | tf_op jit(solution)/shard_map/ppermute | solution.py:443
  29.2 1.8 %right.1 = (bf16[2,256,128]{2,1,0:T(8,128)(2,1)S(1)}, bf16[2,256,128]{2,1,0:T(8,128)(2,1)S(1)}) custom-call(bf16[2,64,128]{2,1,0:T(8,128)(2,1)S(1)} %get-tuple-element.63.after.held_ref, bf16[4,256,2048]{2,1,0:T(8,128)(2,1)S(1)} %get-tuple-element.57.diag_ref, f32[256,512]{1,0:T(8,128)S(1)} %right_part.3.after.acc_first, ...), custom_call_target="tpu_custom_call" | custom-call | flops 8589934592 | bytes 1048576 | tf_op jit(solution)/shard_map/right/pallas_call | solution.py:654
  31.1 0.6 %collective-permute-done.7.came_ref = bf16[2,64,128]{2,1,0:T(8,128)(2,1)S(1)} collective-permute-done((bf16[2,64,128]{2,1,0:T(8,128)(2,1)S(1)}, bf16[2,64,128]{2,1,0:T(8,128)(2,1)S(1)}, u32[]{:S(2)}, u32[]{:S(2)}) %collective-permute-start.7) | collective-permute-done | bytes 32800 | tf_op jit(solution)/shard_map/ppermute | solution.py:443
  32.1 1.0 %collective-permute-done.8.came_ref = bf16[2,256,128]{2,1,0:T(8,128)(2,1)S(1)} collective-permute-done((bf16[2,256,128]{2,1,0:T(8,128)(2,1)S(1)}, bf16[2,256,128]{2,1,0:T(8,128)(2,1)S(1)}, u32[]{:S(2)}, u32[]{:S(2)}) %collective-permute-start.8) | collective-permute-done | bytes 131104 | tf_op jit(solution)/shard_map/ppermute | solution.py:443
  33.2 0.6 %collective-permute-start.10 = (bf16[1,256,128]{2,1,0:T(8,128)(2,1)S(1)}, bf16[1,256,128]{2,1,0:T(8,128)(2,1)S(1)}, u32[]{:S(2)}, u32[]{:S(2)}) collective-permute-start(bf16[1,256,128]{2,1,0:T(8,128)(2,1)S(1)} %get-tuple-element.78), channel_id=1, source_target_pairs={{0,8},{4,12},{8,0},{12,4},{1,9},{5,13},{9,1},{13,5},{2,10},{6,14},... | collective-permute-start | bytes 196616 | tf_op jit(solution)/shard_map/ppermute | solution.py:443
  33.7 3.1 %pair.1 = (bf16[64,64,128]{2,1,0:T(8,128)(2,1)}, f32[16,2048]{1,0:T(8,128)}) custom-call(f32[1,256,128]{2,1,0:T(8,128)S(1)} %get-tuple-element.72.refs_0_, f32[64,128]{1,0:T(8,128)S(1)} %get-tuple-element.53.refs_1_, bf16[64,64,1024]{2,1,0:T(8,128)(2,1)S(1)} %get-tuple-element.73.refs_2_, bf16[1024,128]{1,0:T(8,128)(2,1)S(1)} %get-tuple-element.45.wp_ref.refs_3_, ...), custom_call_target="tpu_custom_call" | custom-call | flops 8589934592 | bytes 1048576 | tf_op jit(solution)/shard_map/pair/pallas_call | solution.py:677
  36.9 0.6 %collective-permute-done.10.refs_1_ = bf16[1,256,128]{2,1,0:T(8,128)(2,1)S(1)} collective-permute-done((bf16[1,256,128]{2,1,0:T(8,128)(2,1)S(1)}, bf16[1,256,128]{2,1,0:T(8,128)(2,1)S(1)}, u32[]{:S(2)}, u32[]{:S(2)}) %collective-permute-start.10) | collective-permute-done | bytes 65568 | tf_op jit(solution)/shard_map/ppermute | solution.py:443
  37.5 0.7 %final_sums.1 = (f32[16,2048]{1,0:T(8,128)}, f32[64,128]{1,0:T(8,128)}) custom-call(bf16[64,64,128]{2,1,0:T(8,128)(2,1)} %get-tuple-element.39.after, f32[64,128]{1,0:T(8,128)S(1)} %get-tuple-element.47.rj_ref, f32[1,2048]{1,0:T(1,128)S(1)} %get-tuple-element.48.keep_ref.refs_2_.refs_5_, f32[1,256,128]{2,1,0:T(8,128)S(1)} %get-tuple-element.72.refs_0_, ...), custom_call_target="tpu_custom_call" | custom-call | flops 1000 | bytes 1000 | tf_op jit(solution)/shard_map/final_sums/pallas_call | solution.py:697
  (20 shorter events, 0.7 us)
Async XLA Ops:
  0.6 8.6 %collective-permute-start = (bf16[1,16,2048]{2,1,0:T(8,128)(2,1)}, bf16[1,16,2048]{2,1,0:T(8,128)(2,1)S(1)}, u32[]{:S(2)}, u32[]{:S(2)}) collective-permute-start(bf16[1,16,2048]{2,1,0:T(8,128)(2,1)} %bitcast.4), channel_id=1, source_target_pairs={{0,8},{4,12},{8,0},{12,4},{1,9},{5,13},{9,1},{13,5},{2,10},{6,14},... | collective-permute-start | bytes 196616 | tf_op jit(solution)/shard_map/ppermute | solution.py:443
  3.6 7.3 %collective-permute-start.1 = (bf16[1,16,2048]{2,1,0:T(8,128)(2,1)}, bf16[1,16,2048]{2,1,0:T(8,128)(2,1)S(1)}, u32[]{:S(2)}, u32[]{:S(2)}) collective-permute-start(bf16[1,16,2048]{2,1,0:T(8,128)(2,1)} %bitcast.5), channel_id=1, source_target_pairs={{0,2},{1,3},{2,0},{3,1},{4,6},{5,7},{6,4},{7,5},{8,10},{9,11},{10,... | collective-permute-start | bytes 196616 | tf_op jit(solution)/shard_map/ppermute | solution.py:443
  9.3 3.3 %collective-permute-start.2 = (bf16[2,16,2048]{2,1,0:T(8,128)(2,1)S(1)}, bf16[2,16,2048]{2,1,0:T(8,128)(2,1)S(1)}, u32[]{:S(2)}, u32[]{:S(2)}) collective-permute-start(bf16[2,16,2048]{2,1,0:T(8,128)(2,1)S(1)} %join.2.after.right_held), channel_id=1, source_target_pairs={{0,4},{4,0},{8,12},{12,8},{1,5},{5,1},{9,13},{13,9},{2,6},{6,2},{1... | collective-permute-start | bytes 393224 | tf_op jit(solution)/shard_map/ppermute | solution.py:443
  10.9 6.0 %collective-permute-start.3 = (bf16[2,16,2048]{2,1,0:T(8,128)(2,1)S(1)}, bf16[2,16,2048]{2,1,0:T(8,128)(2,1)S(1)}, u32[]{:S(2)}, u32[]{:S(2)}) collective-permute-start(bf16[2,16,2048]{2,1,0:T(8,128)(2,1)S(1)} %join.3.after.refs_5_), channel_id=1, source_target_pairs={{0,1},{1,0},{2,3},{3,2},{4,5},{5,4},{6,7},{7,6},{8,9},{9,8},{10,11... | collective-permute-start | bytes 393224 | tf_op jit(solution)/shard_map/ppermute | solution.py:443
  15.8 6.1 %collective-permute-start.4 = (bf16[2,256,128]{2,1,0:T(8,128)(2,1)S(1)}, bf16[2,256,128]{2,1,0:T(8,128)(2,1)S(1)}, u32[]{:S(2)}, u32[]{:S(2)}) collective-permute-start(bf16[2,256,128]{2,1,0:T(8,128)(2,1)S(1)} %get-tuple-element.55), channel_id=1, source_target_pairs={{0,1},{1,0},{2,3},{3,2},{4,5},{5,4},{6,7},{7,6},{8,9},{9,8},{10,11... | collective-permute-start | bytes 393224 | tf_op jit(solution)/shard_map/ppermute | solution.py:443
  21.8 1.4 %collective-permute-start.5 = (bf16[2,256,128]{2,1,0:T(8,128)(2,1)S(1)}, bf16[2,256,128]{2,1,0:T(8,128)(2,1)S(1)}, u32[]{:S(2)}, u32[]{:S(2)}) collective-permute-start(bf16[2,256,128]{2,1,0:T(8,128)(2,1)S(1)} %get-tuple-element.58), channel_id=1, source_target_pairs={{0,4},{4,0},{8,12},{12,8},{1,5},{5,1},{9,13},{13,9},{2,6},{6,2},{1... | collective-permute-start | bytes 393224 | tf_op jit(solution)/shard_map/ppermute | solution.py:443
  23.2 4.3 %collective-permute-start.6 = (bf16[1,256,128]{2,1,0:T(8,128)(2,1)S(1)}, bf16[1,256,128]{2,1,0:T(8,128)(2,1)S(1)}, u32[]{:S(2)}, u32[]{:S(2)}) collective-permute-start(bf16[1,256,128]{2,1,0:T(8,128)(2,1)S(1)} %get-tuple-element.62), channel_id=1, source_target_pairs={{0,8},{4,12},{8,0},{12,4},{1,9},{5,13},{9,1},{13,5},{2,10},{6,14},... | collective-permute-start | bytes 196616 | tf_op jit(solution)/shard_map/ppermute | solution.py:443
  24.8 9.0 %collective-permute-start.9 = (bf16[1,256,128]{2,1,0:T(8,128)(2,1)S(1)}, bf16[1,256,128]{2,1,0:T(8,128)(2,1)S(1)}, u32[]{:S(2)}, u32[]{:S(2)}) collective-permute-start(bf16[1,256,128]{2,1,0:T(8,128)(2,1)S(1)} %get-tuple-element.75), channel_id=1, source_target_pairs={{0,2},{1,3},{2,0},{3,1},{4,6},{5,7},{6,4},{7,5},{8,10},{9,11},{10,... | collective-permute-start | bytes 196616 | tf_op jit(solution)/shard_map/ppermute | solution.py:443
  27.6 4.1 %collective-permute-start.7 = (bf16[2,64,128]{2,1,0:T(8,128)(2,1)S(1)}, bf16[2,64,128]{2,1,0:T(8,128)(2,1)S(1)}, u32[]{:S(2)}, u32[]{:S(2)}) collective-permute-start(bf16[2,64,128]{2,1,0:T(8,128)(2,1)S(1)} %get-tuple-element.65), channel_id=1, source_target_pairs={{0,1},{1,0},{2,3},{3,2},{4,5},{5,4},{6,7},{7,6},{8,9},{9,8},{10,11... | collective-permute-start | bytes 98312 | tf_op jit(solution)/shard_map/ppermute | solution.py:443
  31.7 1.4 %collective-permute-start.8 = (bf16[2,256,128]{2,1,0:T(8,128)(2,1)S(1)}, bf16[2,256,128]{2,1,0:T(8,128)(2,1)S(1)}, u32[]{:S(2)}, u32[]{:S(2)}) collective-permute-start(bf16[2,256,128]{2,1,0:T(8,128)(2,1)S(1)} %get-tuple-element.71), channel_id=1, source_target_pairs={{0,4},{4,0},{8,12},{12,8},{1,5},{5,1},{9,13},{13,9},{2,6},{6,2},{1... | collective-permute-start | bytes 393224 | tf_op jit(solution)/shard_map/ppermute | solution.py:443
  31.8 5.1 %collective-permute-start.11 = (bf16[1,64,128]{2,1,0:T(8,128)(2,1)S(1)}, bf16[1,64,128]{2,1,0:T(8,128)(2,1)S(1)}, u32[]{:S(2)}, u32[]{:S(2)}) collective-permute-start(bf16[1,64,128]{2,1,0:T(8,128)(2,1)S(1)} %get-tuple-element.79), channel_id=1, source_target_pairs={{0,2},{1,3},{2,0},{3,1},{4,6},{5,7},{6,4},{7,5},{8,10},{9,11},{10,... | collective-permute-start | bytes 49160 | tf_op jit(solution)/shard_map/ppermute | solution.py:443
  33.2 4.3 %collective-permute-start.10 = (bf16[1,256,128]{2,1,0:T(8,128)(2,1)S(1)}, bf16[1,256,128]{2,1,0:T(8,128)(2,1)S(1)}, u32[]{:S(2)}, u32[]{:S(2)}) collective-permute-start(bf16[1,256,128]{2,1,0:T(8,128)(2,1)S(1)} %get-tuple-element.78), channel_id=1, source_target_pairs={{0,8},{4,12},{8,0},{12,4},{1,9},{5,13},{9,1},{13,5},{2,10},{6,14},... | collective-permute-start | bytes 196616 | tf_op jit(solution)/shard_map/ppermute | solution.py:443

commit v18 on v15

--- a/solution.py
+++ b/solution.py
@@ -641,16 +641,16 @@
         return gw_row[0]
 
     gl_last = reduce(*gl_cut, "col", n_col, gw_cut[0], weight_rounds)
-    acc = right_part(right_steps, 2 * right_steps, gl_last[0], acc[0])
+    acc = acc[0]
     gw_turned = small_call(
         functools.partial(turn_kernel, n_col),
         halves(inner // n_row, n_col),
         "turn",
         [pltpu.VMEM((inner // n_row, pair_width), F32)],
-    )(acc, *gw_row)
+    )(gl_last[0], *gw_row)
 
     gr_cut = pl.pallas_call(
-        functools.partial(right_kernel, dims, n_row, 2 * right_steps),
+        functools.partial(right_kernel, dims, n_row, right_steps),
         in_specs=[hbm()] + vmem(2 + len(z)),
         out_specs=vmem(2),
         out_shape=halves(j_rows * tiles, n_row),

time: 38.6 us -> 39 us (1.010)
  starting transfers between devices: 15.9 us -> 16.3 us
    pallas_call x2 -> x1, Pallas kernels: 1.67 us -> 0.74 us  [right_part(): pl.pallas_call(functools.partial(right_part_kernel, first, last, len(z)),...]
    pallas_call x1, Pallas kernels: 1.83 us -> 2.57 us  [shards(): pl.pallas_call(functools.partial(right_kernel, dims, n_row, right_steps),...]
  transfers between devices with their start and end apart: 12 -> 12, of which waited for: 4 -> 3; matrix products, arithmetic and copies ran while one was open for 0% -> 0% of each run, Pallas kernels for 51% -> 50%
where the time goes in v18:
time: 39 us; the launch traced here: 38.8 us
  Pallas kernels  20.1 us (52%)
  starting transfers between devices  16.3 us (42%)
  waiting for transfers between devices  1.51 us (4%)
  between operations  0.97 us (2%)
    ppermute x12, starting transfers between devices, swap(): return lax.ppermute(array, axis, [(s, s ^ bit) for s in range(n)])  16.3 us
    pallas_call x1, Pallas kernels, shards(): pl.pallas_call(functools.partial(outer_kernel, dims, n_row, n_col), in_sp...  4.92 us
    pallas_call x1, Pallas kernels, shards(): pl.pallas_call(functools.partial(pair_kernel, dims), in_specs=[hbm()] + v...  3.14 us
    pallas_call x1, Pallas kernels, shards(): pl.pallas_call(functools.partial(scale_kernel, dims), in_specs=[hbm()] *...  3.05 us
    pallas_call x1, Pallas kernels, shards(): pl.pallas_call(functools.partial(right_kernel, dims, n_row, right_steps),...  2.57 us
    pallas_call x1, Pallas kernels, shards(): pl.pallas_call(functools.partial(left_kernel, dims, n_col), in_specs=[hbm...  2.53 us
    pallas_call x1, Pallas kernels, shards(): pl.pallas_call(functools.partial(inner_kernel, dims, early_steps), in_spe...  1.52 us
    ppermute x12, waiting for transfers between devices, swap(): return lax.ppermute(array, axis, [(s, s ^ bit) for s in range(n)])  1.51 us
  transfers between devices with their start and end apart: 12, of which 3 were waited for; matrix products, arithmetic and copies ran while one was open for 0% of the time, Pallas kernels for 50%

profile of v18, /device:TPU:0, one launch (start us, length us, event | category | flops | bytes accessed | tf_op | source)
XLA Modules:
  0.0 38.8 jit_solution(11922132480770395914)
XLA Ops:
  0.6 4.1 %collective-permute-start = (bf16[1,16,2048]{2,1,0:T(8,128)(2,1)}, bf16[1,16,2048]{2,1,0:T(8,128)(2,1)S(1)}, u32[]{:S(2)}, u32[]{:S(2)}) collective-permute-start(bf16[1,16,2048]{2,1,0:T(8,128)(2,1)} %bitcast.4), channel_id=1, source_target_pairs={{0,2},{1,3},{2,0},{3,1},{4,6},{5,7},{6,4},{7,5},{8,10},{9,11},{10,... | collective-permute-start | bytes 196616 | tf_op jit(solution)/shard_map/ppermute | solution.py:443
  4.7 1.5 %collective-permute-start.1 = (bf16[1,16,2048]{2,1,0:T(8,128)(2,1)}, bf16[1,16,2048]{2,1,0:T(8,128)(2,1)S(1)}, u32[]{:S(2)}, u32[]{:S(2)}) collective-permute-start(bf16[1,16,2048]{2,1,0:T(8,128)(2,1)} %bitcast.5), channel_id=1, source_target_pairs={{0,8},{4,12},{8,0},{12,4},{1,9},{5,13},{9,1},{13,5},{2,10},{6,14},... | collective-permute-start | bytes 196616 | tf_op jit(solution)/shard_map/ppermute | solution.py:443
  6.2 3.0 %scale.1 = (bf16[64,64,128]{2,1,0:T(8,128)(2,1)S(1)}, f32[64,128]{1,0:T(8,128)S(1)}, bf16[1024,128]{1,0:T(8,128)(2,1)S(1)}, f32[1,2048]{1,0:T(1,128)S(1)}, f32[6...) custom-call(s32[1,256]{1,0:T(1,128)} %bitcast.6, ...), custom_call_target="tpu_custom_call" | custom-call | flops 1000 | bytes 1000 | tf_op jit(solution)/shard_map/scale/pallas_call | solution.py:539
  9.3 1.6 %collective-permute-start.3 = (bf16[2,16,2048]{2,1,0:T(8,128)(2,1)S(1)}, bf16[2,16,2048]{2,1,0:T(8,128)(2,1)S(1)}, u32[]{:S(2)}, u32[]{:S(2)}) collective-permute-start(bf16[2,16,2048]{2,1,0:T(8,128)(2,1)S(1)} %join.2.after.refs_5_), channel_id=1, source_target_pairs={{0,1},{1,0},{2,3},{3,2},{4,5},{5,4},{6,7},{7,6},{8,9},{9,8},{10,11... | collective-permute-start | bytes 393224 | tf_op jit(solution)/shard_map/ppermute | solution.py:443
  11.0 0.1 collective-permute-start.2
  11.1 1.5 %inner.1.after.refs_1_ = bf16[2,512,2048]{2,1,0:T(8,128)(2,1)S(1)} custom-call(bf16[2,16,2048]{2,1,0:T(8,128)(2,1)S(1)} %join.3.after.right_held, bf16[64,64,128]{2,1,0:T(8,128)(2,1)S(1)} %get-tuple-element.45.scaled_ref.refs_3_, bf16[1024,128]{1,0:T(8,128)(2,1)S(1)} %get-tuple-element.46.wp_ref.refs_3_), custom_call_target="tpu_custom_call" | custom-call | flops 8589934592 | bytes 1048576 | tf_op jit(solution)/shard_map/inner/pallas_call | solution.py:571
  12.6 0.7 %right_rows.1 = (bf16[512,256]{1,0:T(8,128)(2,1)S(1)}, bf16[256,512]{1,0:T(8,128)(2,1)S(1)}) custom-call(bf16[2,512,2048]{2,1,0:T(8,128)(2,1)S(1)} %inner.1.after.refs_1_, f32[64,128]{1,0:T(8,128)S(1)} %get-tuple-element.47.rj_ref, f32[1,2048]{1,0:T(1,128)S(1)} %get-tuple-element.48.keep_ref.refs_2_.refs_5_, bf16[2,16,2048]{2,1,0:T(8,128)(2,1)S(1)} %join.3.after.right_held, ...), custom_call_target="tpu_custom_call" | custom-call | flops 8589934592 | bytes 1048576 | tf_op jit(solution)/shard_map/right_rows/pallas_call | solution.py:582
  13.3 2.5 %left.1 = (bf16[2,256,128]{2,1,0:T(8,128)(2,1)S(1)}, bf16[2,256,128]{2,1,0:T(8,128)(2,1)S(1)}) custom-call(bf16[512,256]{1,0:T(8,128)(2,1)S(1)} %get-tuple-element.49.after.refs_4_, bf16[256,512]{1,0:T(8,128)(2,1)S(1)} %get-tuple-element.50.rbt_ref, bf16[2,512,2048]{2,1,0:T(8,128)(2,1)S(1)} %get-tuple-element.51.refs_0_, ...), custom_call_target="tpu_custom_call" | custom-call | flops 8589934592 | bytes 1048576 | tf_op jit(solution)/shard_map/left/pallas_call | solution.py:593
  15.8 0.5 %collective-permute-start.4 = (bf16[2,256,128]{2,1,0:T(8,128)(2,1)S(1)}, bf16[2,256,128]{2,1,0:T(8,128)(2,1)S(1)}, u32[]{:S(2)}, u32[]{:S(2)}) collective-permute-start(bf16[2,256,128]{2,1,0:T(8,128)(2,1)S(1)} %get-tuple-element.55), channel_id=1, source_target_pairs={{0,1},{1,0},{2,3},{3,2},{4,5},{5,4},{6,7},{7,6},{8,9},{9,8},{10,11... | collective-permute-start | bytes 393224 | tf_op jit(solution)/shard_map/ppermute | solution.py:443
  16.3 4.9 %outer.1 = (bf16[64,64,1024]{2,1,0:T(8,128)(2,1)S(1)}, bf16[4,256,2048]{2,1,0:T(8,128)(2,1)S(1)}, bf16[2,256,128]{2,1,0:T(8,128)(2,1)S(1)}, bf16[2,256,128]{2,1,0:T(8,128)(2,1)S(1)}) custom-call(bf16[2,256,128]{2,1,0:T(8,128)(2,1)S(1)} %get-tuple-element.52.refs_0_.held_ref, f32[64,128]{1,0:T(8,128)S(1)} %get-tuple-element.53.refs_1_, ...), custom_call_target="tpu_custom_call" | custom-call | flops 8589934592 | bytes 1048576 | tf_op jit(solution)/shard_map/outer/pallas_call | solution.py:603
  21.3 0.3 collective-permute-start.5
  21.5 0.2 collective-permute-done.4.came_ref
  21.8 0.7 %right_part.1.after.acc_first = f32[256,512]{1,0:T(8,128)S(1)} custom-call(f32[1,256,128]{2,1,0:T(8,128)S(1)} %get-tuple-element.56.after.refs_0_, bf16[4,256,2048]{2,1,0:T(8,128)(2,1)S(1)} %get-tuple-element.57.diag_ref, bf16[2,512,2048]{2,1,0:T(8,128)(2,1)S(1)} %get-tuple-element.51.refs_0_, bf16[2,512,2048]{2,1,0:T(8,128)(2,1)S(1)} %inner.1.after.refs_1_), custom_call_target="tpu_custom_call" | custom-call | flops 1000 | bytes 1000 | tf_op jit(solution)/shard_map/right_part/pallas_call | solution.py:625
  22.6 0.1 collective-permute-done.5.came_ref
  22.7 1.1 %collective-permute-start.6 = (bf16[1,256,128]{2,1,0:T(8,128)(2,1)S(1)}, bf16[1,256,128]{2,1,0:T(8,128)(2,1)S(1)}, u32[]{:S(2)}, u32[]{:S(2)}) collective-permute-start(bf16[1,256,128]{2,1,0:T(8,128)(2,1)S(1)} %get-tuple-element.62), channel_id=1, source_target_pairs={{0,8},{4,12},{8,0},{12,4},{1,9},{5,13},{9,1},{13,5},{2,10},{6,14},... | collective-permute-start | bytes 196616 | tf_op jit(solution)/shard_map/ppermute | solution.py:443
  23.8 2.1 %collective-permute-start.9 = (bf16[1,256,128]{2,1,0:T(8,128)(2,1)S(1)}, bf16[1,256,128]{2,1,0:T(8,128)(2,1)S(1)}, u32[]{:S(2)}, u32[]{:S(2)}) collective-permute-start(bf16[1,256,128]{2,1,0:T(8,128)(2,1)S(1)} %get-tuple-element.75), channel_id=1, source_target_pairs={{0,2},{1,3},{2,0},{3,1},{4,6},{5,7},{6,4},{7,5},{8,10},{9,11},{10,... | collective-permute-start | bytes 196616 | tf_op jit(solution)/shard_map/ppermute | solution.py:443
  25.9 1.1 %collective-permute-done.6.came_ref = bf16[1,256,128]{2,1,0:T(8,128)(2,1)S(1)} collective-permute-done((bf16[1,256,128]{2,1,0:T(8,128)(2,1)S(1)}, bf16[1,256,128]{2,1,0:T(8,128)(2,1)S(1)}, u32[]{:S(2)}, u32[]{:S(2)}) %collective-permute-start.6) | collective-permute-done | bytes 65568 | tf_op jit(solution)/shard_map/ppermute | solution.py:443
  27.1 1.6 %collective-permute-start.7 = (bf16[2,64,128]{2,1,0:T(8,128)(2,1)S(1)}, bf16[2,64,128]{2,1,0:T(8,128)(2,1)S(1)}, u32[]{:S(2)}, u32[]{:S(2)}) collective-permute-start(bf16[2,64,128]{2,1,0:T(8,128)(2,1)S(1)} %get-tuple-element.65), channel_id=1, source_target_pairs={{0,1},{1,0},{2,3},{3,2},{4,5},{5,4},{6,7},{7,6},{8,9},{9,8},{10,11... | collective-permute-start | bytes 98312 | tf_op jit(solution)/shard_map/ppermute | solution.py:443
  28.7 2.6 %right.1 = (bf16[2,256,128]{2,1,0:T(8,128)(2,1)S(1)}, bf16[2,256,128]{2,1,0:T(8,128)(2,1)S(1)}) custom-call(bf16[2,64,128]{2,1,0:T(8,128)(2,1)S(1)} %get-tuple-element.63.after.held_ref, bf16[4,256,2048]{2,1,0:T(8,128)(2,1)S(1)} %get-tuple-element.57.diag_ref, f32[256,512]{1,0:T(8,128)S(1)} %right_part.1.after.acc_first, ...), custom_call_target="tpu_custom_call" | custom-call | flops 8589934592 | bytes 1048576 | tf_op jit(solution)/shard_map/right/pallas_call | solution.py:652
  31.4 0.1 collective-permute-start.8
  31.4 1.7 %collective-permute-start.11 = (bf16[1,64,128]{2,1,0:T(8,128)(2,1)S(1)}, bf16[1,64,128]{2,1,0:T(8,128)(2,1)S(1)}, u32[]{:S(2)}, u32[]{:S(2)}) collective-permute-start(bf16[1,64,128]{2,1,0:T(8,128)(2,1)S(1)} %get-tuple-element.79), channel_id=1, source_target_pairs={{0,2},{1,3},{2,0},{3,1},{4,6},{5,7},{6,4},{7,5},{8,10},{9,11},{10,... | collective-permute-start | bytes 49160 | tf_op jit(solution)/shard_map/ppermute | solution.py:443
  33.2 1.5 %collective-permute-start.10 = (bf16[1,256,128]{2,1,0:T(8,128)(2,1)S(1)}, bf16[1,256,128]{2,1,0:T(8,128)(2,1)S(1)}, u32[]{:S(2)}, u32[]{:S(2)}) collective-permute-start(bf16[1,256,128]{2,1,0:T(8,128)(2,1)S(1)} %get-tuple-element.78), channel_id=1, source_target_pairs={{0,8},{4,12},{8,0},{12,4},{1,9},{5,13},{9,1},{13,5},{2,10},{6,14},... | collective-permute-start | bytes 196616 | tf_op jit(solution)/shard_map/ppermute | solution.py:443
  34.8 3.1 %pair.1 = (bf16[64,64,128]{2,1,0:T(8,128)(2,1)}, f32[16,2048]{1,0:T(8,128)}) custom-call(f32[1,256,128]{2,1,0:T(8,128)S(1)} %get-tuple-element.72.refs_0_, f32[64,128]{1,0:T(8,128)S(1)} %get-tuple-element.53.refs_1_, bf16[64,64,1024]{2,1,0:T(8,128)(2,1)S(1)} %get-tuple-element.73.refs_2_, bf16[1024,128]{1,0:T(8,128)(2,1)S(1)} %get-tuple-element.46.wp_ref.refs_3_, ...), custom_call_target="tpu_custom_call" | custom-call | flops 8589934592 | bytes 1048576 | tf_op jit(solution)/shard_map/pair/pallas_call | solution.py:675
  37.9 0.7 %final_sums.1 = (f32[16,2048]{1,0:T(8,128)}, f32[64,128]{1,0:T(8,128)}) custom-call(bf16[64,64,128]{2,1,0:T(8,128)(2,1)} %get-tuple-element.39.after, f32[64,128]{1,0:T(8,128)S(1)} %get-tuple-element.47.rj_ref, f32[1,2048]{1,0:T(1,128)S(1)} %get-tuple-element.48.keep_ref.refs_2_.refs_5_, f32[1,256,128]{2,1,0:T(8,128)S(1)} %get-tuple-element.72.refs_0_, ...), custom_call_target="tpu_custom_call" | custom-call | flops 1000 | bytes 1000 | tf_op jit(solution)/shard_map/final_sums/pallas_call | solution.py:695
  (19 shorter events, 0.2 us)
Async XLA Ops:
  0.6 8.7 %collective-permute-start = (bf16[1,16,2048]{2,1,0:T(8,128)(2,1)}, bf16[1,16,2048]{2,1,0:T(8,128)(2,1)S(1)}, u32[]{:S(2)}, u32[]{:S(2)}) collective-permute-start(bf16[1,16,2048]{2,1,0:T(8,128)(2,1)} %bitcast.4), channel_id=1, source_target_pairs={{0,2},{1,3},{2,0},{3,1},{4,6},{5,7},{6,4},{7,5},{8,10},{9,11},{10,... | collective-permute-start | bytes 196616 | tf_op jit(solution)/shard_map/ppermute | solution.py:443
  4.7 6.2 %collective-permute-start.1 = (bf16[1,16,2048]{2,1,0:T(8,128)(2,1)}, bf16[1,16,2048]{2,1,0:T(8,128)(2,1)S(1)}, u32[]{:S(2)}, u32[]{:S(2)}) collective-permute-start(bf16[1,16,2048]{2,1,0:T(8,128)(2,1)} %bitcast.5), channel_id=1, source_target_pairs={{0,8},{4,12},{8,0},{12,4},{1,9},{5,13},{9,1},{13,5},{2,10},{6,14},... | collective-permute-start | bytes 196616 | tf_op jit(solution)/shard_map/ppermute | solution.py:443
  9.3 7.0 %collective-permute-start.3 = (bf16[2,16,2048]{2,1,0:T(8,128)(2,1)S(1)}, bf16[2,16,2048]{2,1,0:T(8,128)(2,1)S(1)}, u32[]{:S(2)}, u32[]{:S(2)}) collective-permute-start(bf16[2,16,2048]{2,1,0:T(8,128)(2,1)S(1)} %join.2.after.refs_5_), channel_id=1, source_target_pairs={{0,1},{1,0},{2,3},{3,2},{4,5},{5,4},{6,7},{7,6},{8,9},{9,8},{10,11... | collective-permute-start | bytes 393224 | tf_op jit(solution)/shard_map/ppermute | solution.py:443
  11.0 1.6 %collective-permute-start.2 = (bf16[2,16,2048]{2,1,0:T(8,128)(2,1)S(1)}, bf16[2,16,2048]{2,1,0:T(8,128)(2,1)S(1)}, u32[]{:S(2)}, u32[]{:S(2)}) collective-permute-start(bf16[2,16,2048]{2,1,0:T(8,128)(2,1)S(1)} %join.3.after.right_held), channel_id=1, source_target_pairs={{0,4},{4,0},{8,12},{12,8},{1,5},{5,1},{9,13},{13,9},{2,6},{6,2},{1... | collective-permute-start | bytes 393224 | tf_op jit(solution)/shard_map/ppermute | solution.py:443
  15.8 6.0 %collective-permute-start.4 = (bf16[2,256,128]{2,1,0:T(8,128)(2,1)S(1)}, bf16[2,256,128]{2,1,0:T(8,128)(2,1)S(1)}, u32[]{:S(2)}, u32[]{:S(2)}) collective-permute-start(bf16[2,256,128]{2,1,0:T(8,128)(2,1)S(1)} %get-tuple-element.55), channel_id=1, source_target_pairs={{0,1},{1,0},{2,3},{3,2},{4,5},{5,4},{6,7},{7,6},{8,9},{9,8},{10,11... | collective-permute-start | bytes 393224 | tf_op jit(solution)/shard_map/ppermute | solution.py:443
  21.3 1.4 %collective-permute-start.5 = (bf16[2,256,128]{2,1,0:T(8,128)(2,1)S(1)}, bf16[2,256,128]{2,1,0:T(8,128)(2,1)S(1)}, u32[]{:S(2)}, u32[]{:S(2)}) collective-permute-start(bf16[2,256,128]{2,1,0:T(8,128)(2,1)S(1)} %get-tuple-element.58), channel_id=1, source_target_pairs={{0,4},{4,0},{8,12},{12,8},{1,5},{5,1},{9,13},{13,9},{2,6},{6,2},{1... | collective-permute-start | bytes 393224 | tf_op jit(solution)/shard_map/ppermute | solution.py:443
  22.7 4.3 %collective-permute-start.6 = (bf16[1,256,128]{2,1,0:T(8,128)(2,1)S(1)}, bf16[1,256,128]{2,1,0:T(8,128)(2,1)S(1)}, u32[]{:S(2)}, u32[]{:S(2)}) collective-permute-start(bf16[1,256,128]{2,1,0:T(8,128)(2,1)S(1)} %get-tuple-element.62), channel_id=1, source_target_pairs={{0,8},{4,12},{8,0},{12,4},{1,9},{5,13},{9,1},{13,5},{2,10},{6,14},... | collective-permute-start | bytes 196616 | tf_op jit(solution)/shard_map/ppermute | solution.py:443
  23.8 11.0 %collective-permute-start.9 = (bf16[1,256,128]{2,1,0:T(8,128)(2,1)S(1)}, bf16[1,256,128]{2,1,0:T(8,128)(2,1)S(1)}, u32[]{:S(2)}, u32[]{:S(2)}) collective-permute-start(bf16[1,256,128]{2,1,0:T(8,128)(2,1)S(1)} %get-tuple-element.75), channel_id=1, source_target_pairs={{0,2},{1,3},{2,0},{3,1},{4,6},{5,7},{6,4},{7,5},{8,10},{9,11},{10,... | collective-permute-start | bytes 196616 | tf_op jit(solution)/shard_map/ppermute | solution.py:443
  27.1 4.2 %collective-permute-start.7 = (bf16[2,64,128]{2,1,0:T(8,128)(2,1)S(1)}, bf16[2,64,128]{2,1,0:T(8,128)(2,1)S(1)}, u32[]{:S(2)}, u32[]{:S(2)}) collective-permute-start(bf16[2,64,128]{2,1,0:T(8,128)(2,1)S(1)} %get-tuple-element.65), channel_id=1, source_target_pairs={{0,1},{1,0},{2,3},{3,2},{4,5},{5,4},{6,7},{7,6},{8,9},{9,8},{10,11... | collective-permute-start | bytes 98312 | tf_op jit(solution)/shard_map/ppermute | solution.py:443
  31.4 1.8 %collective-permute-start.8 = (bf16[2,256,128]{2,1,0:T(8,128)(2,1)S(1)}, bf16[2,256,128]{2,1,0:T(8,128)(2,1)S(1)}, u32[]{:S(2)}, u32[]{:S(2)}) collective-permute-start(bf16[2,256,128]{2,1,0:T(8,128)(2,1)S(1)} %get-tuple-element.71), channel_id=1, source_target_pairs={{0,4},{4,0},{8,12},{12,8},{1,5},{5,1},{9,13},{13,9},{2,6},{6,2},{1... | collective-permute-start | bytes 393224 | tf_op jit(solution)/shard_map/ppermute | solution.py:443
  31.4 6.5 %collective-permute-start.11 = (bf16[1,64,128]{2,1,0:T(8,128)(2,1)S(1)}, bf16[1,64,128]{2,1,0:T(8,128)(2,1)S(1)}, u32[]{:S(2)}, u32[]{:S(2)}) collective-permute-start(bf16[1,64,128]{2,1,0:T(8,128)(2,1)S(1)} %get-tuple-element.79), channel_id=1, source_target_pairs={{0,2},{1,3},{2,0},{3,1},{4,6},{5,7},{6,4},{7,5},{8,10},{9,11},{10,... | collective-permute-start | bytes 49160 | tf_op jit(solution)/shard_map/ppermute | solution.py:443
  33.2 4.7 %collective-permute-start.10 = (bf16[1,256,128]{2,1,0:T(8,128)(2,1)S(1)}, bf16[1,256,128]{2,1,0:T(8,128)(2,1)S(1)}, u32[]{:S(2)}, u32[]{:S(2)}) collective-permute-start(bf16[1,256,128]{2,1,0:T(8,128)(2,1)S(1)} %get-tuple-element.78), channel_id=1, source_target_pairs={{0,8},{4,12},{8,0},{12,4},{1,9},{5,13},{9,1},{13,5},{2,10},{6,14},... | collective-permute-start | bytes 196616 | tf_op jit(solution)/shard_map/ppermute | solution.py:443
